TPU v7x, 32 devices: a whole 2x2x4 slice. The times are simulated.
32 devices in a mesh: photo: 4 (over y, x), tile: 8 (over z, core).
Axes of the slice: x: 2, y: 2, z: 4, core: 2. Of those that a mesh axis runs over, the one named last changes fastest.
Arguments:
- photos: bfloat16 [64, 128, 4096], P('photo', 'tile'), may hold values from 0.25 to 64, as said below
- camera_id: int32 [64], P('photo'), may hold values from 0 to 31, never falling along the last dimension, each value on 1 to 4 neighbouring positions
Outputs:
- fingerprints: float32 [32, 128, 4096], P(None, 'tile', 'photo')
- correlation: float32 [32, 32], replicated
Inputs may be any that keep to these rules, and one draw needn't show every extreme that they name: `photos`: values are positive intensities. `camera_id`: photos are ordered by camera: ids never fall, every camera has 1 to 4 photos, and one has exactly 4.
All inputs are finite; a program needn't handle non-finite values.
Results may differ from a plain program's by a relative error of at most 0.0026.
Values may be sent and summed in bfloat16 or wider, within the bound.
No kernel may reach another device: no remote copies, remote signals or barrier semaphores. Data moves between devices by JAX's collectives and lax.ppermute only.
A program may use at most 192 MiB of HBM per device.

v0:
```python
import jax
import jax.numpy as jnp
from jax import lax
from jax.sharding import PartitionSpec as P

CAMS = 32


noise_power = 1.0
var_eps = 1e-06


def extended(shard, sides, width):
    for axis, dim in sides:
        size, length = (lax.axis_size(axis), shard.shape[dim])
        up = [(i, (i + 1) % size) for i in range(size - 1)]
        down = [(j, i) for i, j in up]
        last = lax.slice_in_dim(shard, length - width, length, axis=dim)
        leading = lax.slice_in_dim(shard, 0, width, axis=dim)
        before = lax.ppermute(last, axis, up)
        after = lax.ppermute(leading, axis, down)
        shard = jnp.concatenate([before, shard, after], axis=dim)
    return shard


def forward_haar(field):
    top_left = field[..., 0::2, 0::2]
    top_right = field[..., 0::2, 1::2]
    low_left = field[..., 1::2, 0::2]
    low_right = field[..., 1::2, 1::2]
    horiz = (top_left + top_right - low_left - low_right) * 0.5
    vertic = (top_left - top_right + low_left - low_right) * 0.5
    diagon = (top_left - top_right - low_left + low_right) * 0.5
    return jnp.stack([horiz, vertic, diagon])


def inverse_haar(bands):
    horiz, vertic, diagon = (bands[0], bands[1], bands[2])
    top_left = (horiz + vertic + diagon) * 0.5
    top_right = (horiz - vertic - diagon) * 0.5
    low_left = (vertic - horiz - diagon) * 0.5
    low_right = (diagon - horiz - vertic) * 0.5
    upper = jnp.stack([top_left, top_right], -1).reshape(top_left.shape[:-1] + (-1,))
    lower = jnp.stack([low_left, low_right], -1).reshape(low_left.shape[:-1] + (-1,))
    joined = jnp.stack([upper, lower], -2)
    return joined.reshape(upper.shape[:-2] + (-1, upper.shape[-1]))


def local_variance(padded, rows, cols):
    squares = padded * padded
    column_box = squares[..., :, 4 : 4 + cols]
    lowest = None
    for radius in range(1, 5):
        column_box = (
            column_box
            + squares[..., :, 4 - radius : 4 - radius + cols]
            + squares[..., :, 4 + radius : 4 + radius + cols]
        )
        row_box = column_box[..., 4 : 4 + rows, :]
        for offset in range(1, radius + 1):
            row_box = (
                row_box
                + column_box[..., 4 - offset : 4 - offset + rows, :]
                + column_box[..., 4 + offset : 4 + offset + rows, :]
            )
        mean_square = row_box / float((2 * radius + 1) ** 2)
        lowest = mean_square if lowest is None else jnp.minimum(lowest, mean_square)
    return lowest


def camera_totals(selector, noise_part, image_part):
    field = image_part.astype(jnp.float32)
    product = noise_part.astype(jnp.float32) * field
    weighted_part = jnp.einsum(
        "cp,prw->crw",
        selector,
        product,
        precision=lax.Precision.HIGHEST,
        preferred_element_type=jnp.float32,
    )
    energy_part = jnp.einsum(
        "cp,prw->crw",
        selector,
        field * field,
        precision=lax.Precision.HIGHEST,
        preferred_element_type=jnp.float32,
    )
    return (weighted_part, energy_part)


def on_device(photos, camera_id):
    tile_rows = photos.shape[1]
    width_all = photos.shape[2]
    half_rows = tile_rows // 2
    half_cols = width_all // 2
    bands_own = forward_haar(photos.astype(jnp.float32))
    bands_ext = extended(bands_own, (("tile", 2),), 4)
    centre = bands_ext[:, :, 4 : 4 + half_rows, :]
    padded = jnp.pad(bands_ext, ((0, 0), (0, 0), (0, 0), (4, 4)))
    variance = local_variance(padded, half_rows, half_cols)
    gain = noise_power / jnp.maximum(variance, noise_power)
    noise_map = inverse_haar(centre * gain).astype(jnp.bfloat16)
    cameras = jnp.arange(CAMS, dtype=jnp.int32)
    all_ids = lax.all_gather(camera_id, "photo", axis=0, tiled=True)
    selector_all = (cameras[:, None] == all_ids[None, :]).astype(jnp.float32)
    weighted, energy = camera_totals(
        selector_all,
        lax.all_to_all(noise_map, "photo", split_axis=2, concat_axis=0, tiled=True),
        lax.all_to_all(photos, "photo", split_axis=2, concat_axis=0, tiled=True),
    )
    fingerprints = weighted / energy
    flat = fingerprints.reshape(CAMS, -1)
    gram_local = jnp.dot(
        flat, flat.T, precision=lax.Precision.HIGHEST, preferred_element_type=jnp.float32
    )
    totals_local = jnp.sum(flat, axis=1)
    gram, totals = lax.psum((gram_local, totals_local), ("photo", "tile"))
    pixel_count = float(tile_rows * lax.axis_size("tile") * width_all)
    average = totals / pixel_count
    covar = gram / pixel_count - average[:, None] * average[None, :]
    spread = jnp.diagonal(covar) + var_eps
    correlation = covar / jnp.sqrt(spread[:, None] * spread[None, :])
    return (fingerprints, correlation)


def solution(mesh):
    placed = (P("photo", "tile", None), P("photo"))
    return jax.shard_map(
        on_device,
        mesh=mesh,
        in_specs=placed,
        out_specs=(P(None, "tile", "photo"), P()),
        check_vma=False,
    )
```

profile of v0, /device:TPU:0, one launch (start us, length us, event | category | flops | bytes accessed | tf_op | source)
XLA Modules:
  0.0 550.2 jit_solution(18331604786342072489)
XLA Ops:
  0.6 36.9 %slice.126 = f32[16,8,2048]{2,1,0:T(8,128)} slice(bf16[16,16,4096]{2,1,0:T(8,128)(2,1)} %param.2), slice={[0:16:1], [0:16:2], [0:4096:2]} | slice | bytes 2097152 | tf_op jit(solution)/shard_map/slice | solution.py:27
  37.5 36.7 %slice.127 = f32[16,8,2048]{2,1,0:T(8,128)} slice(bf16[16,16,4096]{2,1,0:T(8,128)(2,1)} %param.2), slice={[0:16:1], [0:16:2], [1:4096:2]} | slice | bytes 2097152 | tf_op jit(solution)/shard_map/slice | solution.py:28
  74.2 18.9 %slice.128 = f32[16,8,2048]{2,1,0:T(8,128)} slice(bf16[16,16,4096]{2,1,0:T(8,128)(2,1)S(1)} %copy-done), slice={[0:16:1], [1:16:2], [0:4096:2]} | slice | bytes 2097152 | tf_op jit(solution)/shard_map/slice | solution.py:29
  93.1 19.4 %slice.129 = f32[16,8,2048]{2,1,0:T(8,128)} slice(bf16[16,16,4096]{2,1,0:T(8,128)(2,1)S(1)} %copy-done), slice={[0:16:1], [1:16:2], [1:4096:2]} | slice | bytes 2097152 | tf_op jit(solution)/shard_map/slice | solution.py:30
  112.5 2.7 multiply_bitcast_fusion.2
  116.8 2.5 fusion.18
  119.3 3.5 collective-permute-start
  124.1 14.2 %copy.33 = bf16[16,16,4096]{0,1,2:T(8,128)(2,1)} copy(bf16[16,16,4096]{2,1,0:T(8,128)(2,1)S(1)} %copy-done) | data formatting | bytes 4194304 | tf_op args[0]
  138.4 20.3 %reshape.157 = bf16[4,2,131072]{2,1,0:T(2,128)(2,1)} reshape(bf16[4096,16,16]{2,1,0:T(8,128)(2,1)} %bitcast.71) | data formatting | bytes 4194304
  158.7 4.9 all-to-all-start.1
  163.6 8.6 %fusion = f32[3,16,16,2056]{3,2,1,0:T(8,128)} fusion(f32[3,16,4,2048]{3,2,1,0:T(4,128)} %collective-permute-done.1, f32[3,16,4,2048]{3,2,1,0:T(4,128)} %collective-permute-done, f32[1,16,8,2048]{3,2,1,0:T(8,128)S(1)} %copy-done.2, f32[1,16,8,2048]{3,2,1,0:T(8,128)S(1)} %copy-done.4, f32[1,16,8,2048]{3,2,1,0:T(8,128)S(1)} %get-tuple-element.20), kind=kLoop, calls=%fused_computation.7 | loop fusion | flops 20527104 | bytes 12607488 | tf_op jit(solution)/shard_map/mul | solution.py:50
  172.3 38.2 %slice_add_fusion = (f32[3,16,16,2048]{3,2,1,0:T(8,128)}, f32[3,16,16,2048]{3,2,1,0:T(8,128)}, f32[3,16,16,2048]{3,2,1,0:T(8,128)}, f32[3,16,16,2048]{3,2,1,0:T(8,128)}) fusion(f32[3,16,16,2056]{3,2,1,0:T(8,128)} %fusion), kind=kLoop, calls=%fused_computation.12 | loop fusion | flops 12582912 | bytes 81788928 | tf_op jit(solution)/shard_map/add | solution.py:55
  210.5 66.0 %fusion.6 = f32[3,16,8,2048]{3,2,1,0:T(8,128)} fusion(f32[3,16,16,2048]{3,2,1,0:T(8,128)} %get-tuple-element.14, f32[3,16,16,2048]{3,2,1,0:T(8,128)} %get-tuple-element.15, f32[3,16,16,2048]{3,2,1,0:T(8,128)} %get-tuple-element.16, f32[3,16,16,2048]{3,2,1,0:T(8,128)} %get-tuple-element.17, f32[1,16,8,2048]{3,2,1,0:T(8,128)S(1)} %copy-done.2, ...), kind=kLoop, calls=%fused_computation.25 | loop fusion | flops 25165824 | bytes 81788928 | tf_op jit(solution)/shard_map/mul | solution.py:102
  276.5 2.4 multiply_convert_fusion.3
  279.1 9.0 %copy.29 = bf16[16,8,2048,2]{0,1,3,2:T(8,128)(2,1)} copy(bf16[16,8,2048,2]{2,1,0,3:T(8,128)(2,1)S(1)} %get-tuple-element.31) | data formatting | bytes 2097152 | tf_op jit(solution)/shard_map/stack | solution.py:43
  288.1 8.7 %copy.30 = bf16[16,8,2048,2]{0,1,3,2:T(8,128)(2,1)} copy(bf16[16,8,2048,2]{2,1,0,3:T(8,128)(2,1)S(1)} %get-tuple-element.32) | data formatting | bytes 2097152 | tf_op jit(solution)/shard_map/stack | solution.py:44
  296.8 14.7 %pad_maximum_fusion = bf16[16,8,2,4096]{0,1,3,2:T(8,128)(2,1)} fusion(bf16[16,8,1,4096]{0,1,3,2:T(8,128)(2,1)} %bitcast.73, bf16[16,8,1,4096]{0,1,3,2:T(8,128)(2,1)} %bitcast.72), kind=kLoop, calls=%fused_computation.3 | loop fusion | flops 1048576 | bytes 4194304 | tf_op jit(solution)/shard_map/stack | solution.py:45
  311.5 15.2 %copy.31 = bf16[16,8,2,4096]{3,0,2,1:T(8,128)(2,1)S(1)} copy(bf16[16,8,2,4096]{0,1,3,2:T(8,128)(2,1)} %pad_maximum_fusion) | data formatting | bytes 4194304 | tf_op jit(solution)/shard_map/stack | solution.py:45
  326.7 14.1 %copy.32 = bf16[16,16,4096]{0,1,2:T(8,128)(2,1)} copy(bf16[16,16,4096]{2,0,1:T(8,128)(2,1)S(1)} %bitcast.76) | data formatting | bytes 4194304 | tf_op jit(solution)/shard_map/convert_element_type | solution.py:102
  340.8 20.3 %reshape.159 = bf16[4,2,131072]{2,1,0:T(2,128)(2,1)} reshape(bf16[4096,16,16]{2,1,0:T(8,128)(2,1)} %bitcast.70) | data formatting | bytes 4194304
  361.2 4.6 all-to-all-start
  367.2 27.6 %all-reduce.1 = s32[64]{0:T(128)S(1)} all-reduce(s32[64]{0:T(128)S(1)} %dynamic-update-slice), channel_id=1, replica_groups=mesh['photo'=4,'tile'=8] {'photo'}, use_global_device_ids=true, to_apply=%add.1 | all-reduce | flops 64 | bytes 512
  394.9 14.7 %reshape.158 = bf16[4096,16,16]{2,1,0:T(8,128)(2,1)} reshape(bf16[4,2,131072]{2,1,0:T(2,128)(2,1)} %all-to-all-done.1) | data formatting | bytes 4194304
  409.5 13.5 %reshape.160 = bf16[4096,16,16]{2,1,0:T(8,128)(2,1)} reshape(bf16[4,2,131072]{2,1,0:T(2,128)(2,1)S(1)} %all-to-all-done) | data formatting | bytes 4194304
  423.0 33.0 %convert_multiply_fusion = (f32[16,16,4096]{0,1,2:T(8,128)}, f32[16,16,4096]{0,1,2:T(8,128)}) fusion(bf16[4096,16,16]{2,1,0:T(8,128)(2,1)} %reshape.160, bf16[4096,16,16]{2,1,0:T(8,128)(2,1)} %reshape.158), kind=kLoop, calls=%fused_computation.1 | loop fusion | flops 4194304 | bytes 12582912 | tf_op jit(solution)/shard_map/mul | solution.py:84
  456.1 20.6 %copy.34 = f32[4,16,16,1024]{3,1,0,2:T(8,128)} copy(f32[4,16,16,1024]{1,2,3,0:T(8,128)} %bitcast.69) | data formatting | bytes 8388608 | tf_op jit(solution)/shard_map/mul | solution.py:73
  476.7 20.8 %copy.35 = f32[4,16,16,1024]{3,1,0,2:T(8,128)} copy(f32[4,16,16,1024]{1,2,3,0:T(8,128)} %bitcast.68) | data formatting | bytes 8388608 | tf_op jit(solution)/shard_map/mul | solution.py:84
  497.5 3.9 fusion.14
  501.5 2.1 fusion.19
  503.6 1.8 convolution_bitcast_fusion
  505.4 2.5 copy.36
  507.9 40.3 %all-reduce.2 = (f32[32,32]{1,0:T(8,128)S(1)}, f32[32]{0:T(128)S(1)}) all-reduce(f32[32,32]{1,0:T(8,128)S(1)} %convolution_bitcast_fusion, f32[32]{0:T(128)S(1)} %get-tuple-element.29), channel_id=1, replica_groups=mesh['photo'=4,'tile'=8] {'photo','tile'}, use_global_device_ids=true, to_apply=%region_0.1 | all-reduce | flops 1056 | bytes 8448 | tf_op jit(solution)/shard_map/psum | solution.py:117
  (32 shorter events, 5.4 us)
Async XLA Ops:
  0.6 73.6 %copy-start = (bf16[16,16,4096]{2,1,0:T(8,128)(2,1)S(1)}, bf16[16,16,4096]{2,1,0:T(8,128)(2,1)}, u32[]{:S(2)}) copy-start(bf16[16,16,4096]{2,1,0:T(8,128)(2,1)} %param.2) | copy-start | bytes 6291460
  115.2 1.0 copy-start.1
  115.2 1.4 copy-start.3
  119.3 44.2 %collective-permute-start = (f32[3,16,4,2048]{3,2,1,0:T(4,128)}, f32[3,16,4,2048]{3,2,1,0:T(4,128)}, u32[]{:S(2)}, u32[]{:S(2)}) collective-permute-start(f32[3,16,4,2048]{3,2,1,0:T(4,128)} %get-tuple-element.27), channel_id=1, source_target_pairs={{0,1},{1,2},{2,3},{3,4},{4,5},{5,6},{6,7},{8,9},{9,10},{10,11},{11... | collective-permute-start | bytes 4718600 | tf_op jit(solution)/shard_map/ppermute | solution.py:20
  122.8 40.8 %collective-permute-start.1 = (f32[3,16,4,2048]{3,2,1,0:T(4,128)}, f32[3,16,4,2048]{3,2,1,0:T(4,128)}, u32[]{:S(2)}, u32[]{:S(2)}) collective-permute-start(f32[3,16,4,2048]{3,2,1,0:T(4,128)} %get-tuple-element.28), channel_id=1, source_target_pairs={{1,0},{2,1},{3,2},{4,3},{5,4},{6,5},{7,6},{9,8},{10,9},{11,10},{12... | collective-permute-start | bytes 4718600 | tf_op jit(solution)/shard_map/ppermute | solution.py:21
  158.7 4.9 copy-start.2
  158.7 4.9 copy-start.4
  158.7 202.4 %all-to-all-start.1 = ((bf16[4,2,131072]{2,1,0:T(2,128)(2,1)}), bf16[4,2,131072]{2,1,0:T(2,128)(2,1)}, u32[]{:S(2)}, u32[]{:S(2)}) async-start(bf16[4,2,131072]{2,1,0:T(2,128)(2,1)} %reshape.157), calls=%async_computation.1 | async-start | bytes 4194304 | tf_op jit(solution)/shard_map/all_to_all | solution.py:109
  361.2 4.6 copy-start.7
  361.2 5.8 %copy-start.6 = (s32[16]{0:T(128)S(1)}, s32[16]{0:T(128)}, u32[]{:S(2)}) copy-start(s32[16]{0:T(128)} %param.3) | copy-start | bytes 196
  361.2 48.4 %all-to-all-start = ((bf16[4,2,131072]{2,1,0:T(2,128)(2,1)}), bf16[4,2,131072]{2,1,0:T(2,128)(2,1)S(1)}, u32[]{:S(2)}, u32[]{:S(2)}) async-start(bf16[4,2,131072]{2,1,0:T(2,128)(2,1)} %reshape.159), calls=%async_computation | async-start | bytes 4194304 | tf_op jit(solution)/shard_map/all_to_all | solution.py:108
  497.5 3.9 copy-start.5
where the time goes:
time: 559 us; the launch traced here: 550 us
  local copies, waits for them, and re-layouts  291 us (52%)
  other arithmetic  167 us (30%)
  blocking collectives  67.9 us (12%)
  starting transfers between devices  14.2 us (3%)
  matrix products  7.82 us (1%)
    unnamed x25, local copies, waits for them, and re-layouts  87.8 us
    mul x1, other arithmetic, on_device(): noise_map = inverse_haar(centre * gain).astype(jnp.bfloat16)  66 us
    psum x1, blocking collectives, on_device(): gram, totals = lax.psum((gram_local, totals_local), ('photo', 'tile'))  40.3 us
    add x1, other arithmetic, local_variance(): column_box + squares[..., :, 4 - radius:4 - radius + cols]  38.2 us
    slice x1, local copies, waits for them, and re-layouts, forward_haar(): top_left = field[..., 0::2, 0::2]  36.9 us
    slice x1, local copies, waits for them, and re-layouts, forward_haar(): top_right = field[..., 0::2, 1::2]  36.7 us
    mul x1, other arithmetic, camera_totals(): field * field  33 us
    unnamed x1, blocking collectives  27.6 us
  transfers between devices with their start and end apart: 4, of which 0 were waited for; matrix products, arithmetic and copies ran while one was open for 45% of the time, Pallas kernels for 0%

commit v1 on v0

v1 whole, which is shorter than its diff:
```python
import functools

import jax
import jax.numpy as jnp
import numpy as np
from jax import lax
from jax.experimental import pallas as pl
from jax.experimental.pallas import tpu as pltpu
from jax.sharding import PartitionSpec as P

CAMS = 32
RADII = 4
LANES = 128

noise_power = 1.0
var_eps = 1e-06

f32 = jnp.float32
bf16 = jnp.bfloat16


def log2(value):
    return value.bit_length() - 1


def row_permutation(photos, rows):
    size = photos * rows
    matrix = np.zeros((size, size), np.float32)
    for photo in range(photos):
        for row in range(rows):
            matrix[row * photos + photo, photo * rows + row] = 1.0
    return jnp.asarray(matrix, bf16)


def column_split():
    matrix = np.zeros((2 * LANES, 2 * LANES), np.float32)
    for cell in range(LANES):
        matrix[2 * cell, cell] = 1.0
        matrix[2 * cell + 1, LANES + cell] = 1.0
    return matrix


def box_matrices():
    source = np.arange(4 * LANES)[:, None] - LANES
    target = np.arange(2 * LANES)[None, :]
    distance = np.abs(source - target)
    return jnp.asarray(
        np.stack([(distance <= radius).astype(np.float32) for radius in range(1, RADII + 1)]), bf16
    )


def haar_rows(even0, odd0, even1, odd1):
    low0, low1 = even0 + odd0, even1 + odd1
    high0, high1 = even0 - odd0, even1 - odd1
    return (low0 - low1, high0 + high1, high0 - high1)


def halves(value):
    upper = value.astype(bf16)
    lower = (value - upper.astype(f32)).astype(bf16)
    return upper, lower


def prepare_kernel(ids, photos, perm, split, sorted_out, up_out, down_out, first_out, last_out):
    count, rows, width = photos.shape
    cells = rows // 2
    flat = photos[...].reshape(count * rows, width)
    by_row = jnp.dot(perm[...], flat, preferred_element_type=f32).astype(bf16)

    lane = lax.broadcasted_iota(jnp.int32, (2 * rows, count * rows), 1)
    sub = lax.broadcasted_iota(jnp.int32, (2 * rows, count * rows), 0)
    lane_photo = lane & (count - 1)
    lane_id = jnp.zeros_like(lane)
    for photo in range(count):
        lane_id = jnp.where(lane_photo == photo, ids[photo], lane_id)
    wanted = jnp.where(sub < rows, ids[0], ids[count - 1])
    chosen = (lane_id == wanted) & ((sub & (rows - 1)) == (lane >> log2(count)))
    edge_select = jnp.where(chosen, 1.0, 0.0).astype(bf16)

    for block in range(width // (2 * LANES)):
        cols = slice(block * 2 * LANES, (block + 1) * 2 * LANES)
        cell_cols = slice(block * LANES, (block + 1) * LANES)
        parted = jnp.dot(by_row[:, cols], split[...], preferred_element_type=f32)
        sorted_out[:, cols] = parted.astype(bf16)
        upper, lower = halves(parted * parted)
        edge = jnp.dot(edge_select, upper, preferred_element_type=f32) + jnp.dot(
            edge_select, lower, preferred_element_type=f32
        )
        first_out[:rows, cols] = edge[:rows]
        last_out[:rows, cols] = edge[rows:]
        for i in range(cells):
            if RADII <= i < cells - RADII:
                continue
            top = parted[2 * i * count : (2 * i + 1) * count]
            low = parted[(2 * i + 1) * count : (2 * i + 2) * count]
            bands = haar_rows(top[:, :LANES], top[:, LANES:], low[:, :LANES], low[:, LANES:])
            for band in range(3):
                square = (bands[band] * bands[band]).astype(bf16)
                if i < RADII:
                    start = (band * RADII + i) * count
                    up_out[start : start + count, cell_cols] = square
                if i >= cells - RADII:
                    start = (band * RADII + i - (cells - RADII)) * count
                    down_out[start : start + count, cell_cols] = square
    first_out[rows:, :] = jnp.full((8, width), ids[0].astype(f32))
    last_out[rows:, :] = jnp.full((8, width), ids[count - 1].astype(f32))


def prepare(ids, photos):
    count, rows, width = photos.shape
    step = min(width, 1024)
    size = count * rows
    halo = 3 * RADII * count
    whole = lambda i, ids: (0, 0)
    along = lambda i, ids: (0, i)
    return pl.pallas_call(
        prepare_kernel,
        grid_spec=pltpu.PrefetchScalarGridSpec(
            num_scalar_prefetch=1,
            grid=(width // step,),
            in_specs=[
                pl.BlockSpec((count, rows, step), lambda i, ids: (0, 0, i)),
                pl.BlockSpec((size, size), whole),
                pl.BlockSpec((2 * LANES, 2 * LANES), whole),
            ],
            out_specs=[
                pl.BlockSpec((size, step), along),
                pl.BlockSpec((halo, step // 2), along),
                pl.BlockSpec((halo, step // 2), along),
                pl.BlockSpec((rows + 8, step), along),
                pl.BlockSpec((rows + 8, step), along),
            ],
        ),
        out_shape=[
            jax.ShapeDtypeStruct((size, width), bf16),
            jax.ShapeDtypeStruct((halo, width // 2), bf16),
            jax.ShapeDtypeStruct((halo, width // 2), bf16),
            jax.ShapeDtypeStruct((rows + 8, width), f32),
            jax.ShapeDtypeStruct((rows + 8, width), f32),
        ],
        compiler_params=pltpu.CompilerParams(vmem_limit_bytes=24 * 2**20),
        cost_estimate=pl.CostEstimate(flops=10**9, bytes_accessed=8 * 2**20, transcendentals=0),
        name="prepare",
    )(ids, photos, row_permutation(count, rows), jnp.asarray(column_split(), bf16))


def main_kernel(
    count, rows, blocks_all,
    where, ids,
    own, own_l, own_r, above, above_l, above_r, below, below_l, below_r,
    before, after, box, merge,
    out,
    sums, least, product, square, energy,
):
    cells = rows // 2
    size = count * rows
    width = own.shape[1]
    blocks = width // (2 * LANES)
    chunk = where[0]
    left_ok = jnp.where(chunk > 0, 1.0, 0.0).astype(f32)
    right_ok = jnp.where((chunk + 1) * blocks < blocks_all, 1.0, 0.0).astype(f32)

    for block in range(-1, blocks + 1):
        if block < 0:
            mine, over, under, factor, at = own_l, above_l, below_l, left_ok, 0
        elif block == blocks:
            mine, over, under, factor, at = own_r, above_r, below_r, right_ok, 0
        else:
            mine, over, under, factor, at = own, above, below, None, block
        even = slice(2 * at * LANES, (2 * at + 1) * LANES)
        odd = slice((2 * at + 1) * LANES, (2 * at + 2) * LANES)
        cols = slice(at * LANES, (at + 1) * LANES)
        place = slice((block + 1) * LANES, (block + 2) * LANES)
        squares = [[], [], []]
        for i in range(cells):
            top = slice(2 * i * count, (2 * i + 1) * count)
            low = slice((2 * i + 1) * count, (2 * i + 2) * count)
            bands = haar_rows(
                mine[top, even].astype(f32),
                mine[top, odd].astype(f32),
                mine[low, even].astype(f32),
                mine[low, odd].astype(f32),
            )
            for band in range(3):
                squares[band].append(bands[band] * bands[band])
        for band in range(3):
            start = band * RADII * count
            outer = [
                over[start + i * count : start + (i + 1) * count, cols].astype(f32)
                for i in range(RADII)
            ]
            inner = [
                under[start + i * count : start + (i + 1) * count, cols].astype(f32)
                for i in range(RADII)
            ]
            column = outer + squares[band] + inner
            if factor is not None:
                column = [value * factor for value in column]
            for i in range(cells):
                total = column[i + RADII]
                at_row = (band * cells + i) * count
                for radius in range(1, RADII + 1):
                    total = total + (column[i + RADII - radius] + column[i + RADII + radius])
                    sums[radius - 1, at_row : at_row + count, place] = total.astype(bf16)

    for group in range(blocks // 2):
        window = slice(2 * group * LANES, (2 * group + 4) * LANES)
        for radius in range(1, RADII + 1):
            wide = jnp.dot(sums[radius - 1, :, window], box[radius - 1], preferred_element_type=f32)
            mean = wide * (1.0 / float((2 * radius + 1) ** 2))
            least[...] = mean if radius == 1 else jnp.minimum(least[...], mean)
        for half in range(2):
            block = 2 * group + half
            even = slice(2 * block * LANES, (2 * block + 1) * LANES)
            odd = slice((2 * block + 1) * LANES, (2 * block + 2) * LANES)
            lanes = slice(half * LANES, (half + 1) * LANES)
            for i in range(cells):
                top = slice(2 * i * count, (2 * i + 1) * count)
                low = slice((2 * i + 1) * count, (2 * i + 2) * count)
                pixels = (
                    own[top, even].astype(f32),
                    own[top, odd].astype(f32),
                    own[low, even].astype(f32),
                    own[low, odd].astype(f32),
                )
                bands = haar_rows(*pixels)
                shrunk = []
                for band in range(3):
                    at_row = (band * cells + i) * count
                    variance = least[at_row : at_row + count, lanes]
                    gain = 1.0 / jnp.maximum(variance, 4.0 * noise_power)
                    shrunk.append(bands[band] * (gain * noise_power))
                horiz, vertic, diagon = shrunk
                both, cross = vertic + diagon, vertic - diagon
                noise = (horiz + both, horiz - both, cross - horiz, -horiz - cross)
                for (rows_at, cols_at), pixel, part in zip(
                    ((top, even), (top, odd), (low, even), (low, odd)), pixels, noise
                ):
                    start, stop = rows_at.start, rows_at.stop
                    upper, lower = halves(part.astype(bf16).astype(f32) * pixel)
                    product[start:stop, cols_at] = upper
                    product[size + start : size + stop, cols_at] = lower
                    upper, lower = halves(pixel * pixel)
                    square[start:stop, cols_at] = upper
                    square[size + start : size + stop, cols_at] = lower

    lane = lax.broadcasted_iota(jnp.int32, (size, size), 1)
    sub = lax.broadcasted_iota(jnp.int32, (size, size), 0)
    lane_photo = lane & (count - 1)
    lane_rank = jnp.zeros_like(lane)
    slot_lane = lax.broadcasted_iota(jnp.int32, (rows, size), 1) >> log2(rows)
    slot_id = jnp.full((rows, size), -1, jnp.int32)
    rank = jnp.int32(0)
    for photo in range(count):
        if photo:
            rank = rank + jnp.where(ids[photo] != ids[photo - 1], 1, 0)
        lane_rank = jnp.where(lane_photo == photo, rank, lane_rank)
        slot_id = jnp.where(slot_lane == rank, ids[photo], slot_id)
    chosen = (lane_rank == (sub >> log2(rows))) & ((sub & (rows - 1)) == (lane >> log2(count)))
    select = jnp.where(chosen, 1.0, 0.0).astype(bf16)
    select = jnp.concatenate([select, select], axis=1)
    out[size:, :] = jnp.zeros((rows, width), bf16)
    out[size:, :size] = slot_id.astype(f32).astype(bf16)
    first_id = ids[0].astype(f32)
    last_id = ids[count - 1].astype(f32)
    for block in range(blocks):
        cols = slice(2 * block * LANES, (2 * block + 2) * LANES)
        weighted = jnp.dot(select, product[:, cols], preferred_element_type=f32)
        energy[...] = jnp.dot(select, square[:, cols], preferred_element_type=f32)
        shared = jnp.where(before[rows : rows + 1, cols] == first_id, before[:rows, cols], 0.0)
        energy[:rows, :] += shared
        shared = jnp.where(after[rows : rows + 1, cols] == last_id, after[:rows, cols], 0.0)
        tail = pl.ds(pl.multiple_of(rank * rows, rows), rows)
        energy[tail, :] += shared
        part = (weighted / jnp.maximum(energy[...], 2.0**-20)).astype(bf16)
        out[:size, cols] = jnp.dot(part, merge[...], preferred_element_type=f32).astype(bf16)


def main_part(chunk, ids, own, above, below, before, after, rows, pieces):
    size, width_all = own.shape
    count = size // rows
    width = width_all // pieces
    halo = above.shape[0]
    blocks_all = width_all // (2 * LANES)
    blocks = width // (2 * LANES)
    here = lambda i, where, ids: (0, where[0])
    left = lambda i, where, ids: (0, jnp.maximum(where[0] * blocks - 1, 0))
    right = lambda i, where, ids: (0, jnp.minimum((where[0] + 1) * blocks, blocks_all - 1))
    cell_rows = 3 * (rows // 2) * count
    halo_specs = [
        pl.BlockSpec((halo, width // 2), here),
        pl.BlockSpec((halo, LANES), left),
        pl.BlockSpec((halo, LANES), right),
    ]
    return pl.pallas_call(
        functools.partial(main_kernel, count, rows, blocks_all),
        grid_spec=pltpu.PrefetchScalarGridSpec(
            num_scalar_prefetch=2,
            grid=(1,),
            in_specs=[
                pl.BlockSpec((size, width), here),
                pl.BlockSpec((size, 2 * LANES), left),
                pl.BlockSpec((size, 2 * LANES), right),
                *halo_specs,
                *halo_specs,
                pl.BlockSpec((rows + 8, width), here),
                pl.BlockSpec((rows + 8, width), here),
                pl.BlockSpec((RADII, 4 * LANES, 2 * LANES), lambda i, where, ids: (0, 0, 0)),
                pl.BlockSpec((2 * LANES, 2 * LANES), lambda i, where, ids: (0, 0)),
            ],
            out_specs=pl.BlockSpec((size + rows, width), lambda i, where, ids: (0, 0)),
            scratch_shapes=[
                pltpu.VMEM((RADII, cell_rows, width // 2 + 2 * LANES), bf16),
                pltpu.VMEM((cell_rows, 2 * LANES), f32),
                pltpu.VMEM((2 * size, width), bf16),
                pltpu.VMEM((2 * size, width), bf16),
                pltpu.VMEM((size, 2 * LANES), f32),
            ],
        ),
        out_shape=jax.ShapeDtypeStruct((size + rows, width), bf16),
        compiler_params=pltpu.CompilerParams(vmem_limit_bytes=32 * 2**20),
        cost_estimate=pl.CostEstimate(
            flops=2 * 10**9, bytes_accessed=4 * 2**20, transcendentals=0
        ),
        name="residual",
    )(
        chunk, ids, own, own, own, above, above, above, below, below, below, before, after,
        box_matrices(), jnp.asarray(column_split().T, bf16),
    )


def assemble_kernel(rows, *refs):
    pieces = len(refs) - 3
    parts, (prints, partial, flat) = refs[:pieces], refs[pieces:]
    size = parts[0].shape[0] - rows
    width = parts[0].shape[1]
    tall = CAMS * rows
    sub = lax.broadcasted_iota(jnp.int32, (tall, size), 0)
    lane = lax.broadcasted_iota(jnp.int32, (tall, size), 1)
    same_row = (sub & (rows - 1)) == (lane & (rows - 1))
    camera = (sub >> log2(rows)).astype(f32)
    selects = []
    for part in parts:
        slot_id = part[size : size + rows, :size].astype(f32)[:1]
        selects.append(jnp.where((camera == slot_id) & same_row, 1.0, 0.0).astype(bf16))
    total = jnp.zeros((tall, 1), f32)
    for block in range(width // (2 * LANES)):
        cols = slice(block * 2 * LANES, (block + 1) * 2 * LANES)
        joined = jnp.zeros((tall, 2 * LANES), f32)
        for select, part in zip(selects, parts):
            joined = joined + jnp.dot(select, part[:size, cols], preferred_element_type=f32)
        prints[:, :, cols] = joined.reshape(CAMS, rows, 2 * LANES)
        flat[:, cols] = joined.astype(bf16)
        total = total + jnp.sum(joined, axis=1, keepdims=True)
    gram = lax.dot_general(
        flat[...], flat[...], (((1,), (1,)), ((), ())), preferred_element_type=f32
    )
    sub = lax.broadcasted_iota(jnp.int32, (tall, tall), 0)
    lane = lax.broadcasted_iota(jnp.int32, (tall, tall), 1)
    gram = jnp.where((sub & (rows - 1)) == (lane & (rows - 1)), gram, 0.0)
    gram = jnp.sum(gram.reshape(CAMS, rows, tall), axis=1)
    sub = lax.broadcasted_iota(jnp.int32, (tall, LANES), 0)
    lane = lax.broadcasted_iota(jnp.int32, (tall, LANES), 1)
    gather = jnp.where((sub >> log2(rows)) == lane, 1.0, 0.0).astype(f32)
    gram = jnp.dot(gram, gather, precision=lax.Precision.HIGHEST, preferred_element_type=f32)
    total = jnp.sum(total.reshape(CAMS, rows, 1), axis=1)
    lane = lax.broadcasted_iota(jnp.int32, (CAMS, LANES), 1)
    partial[...] = jnp.where(lane == CAMS, total, gram)


def assemble(parts, rows):
    width = parts[0].shape[1]
    return pl.pallas_call(
        functools.partial(assemble_kernel, rows),
        out_shape=[
            jax.ShapeDtypeStruct((CAMS, rows, width), f32),
            jax.ShapeDtypeStruct((CAMS, LANES), f32),
        ],
        scratch_shapes=[pltpu.VMEM((CAMS * rows, width), bf16)],
        compiler_params=pltpu.CompilerParams(vmem_limit_bytes=32 * 2**20),
        cost_estimate=pl.CostEstimate(
            flops=2 * 10**9, bytes_accessed=4 * 2**20, transcendentals=0
        ),
        name="assemble",
    )(*parts)


def correlate_kernel(pixels, *refs):
    parts, out = refs[:-1], refs[-1]
    whole = parts[0][...]
    for part in parts[1:]:
        whole = whole + part[...]
    gram = whole[:, :CAMS]
    mean = whole[:, CAMS : CAMS + 1] / pixels
    sub = lax.broadcasted_iota(jnp.int32, (CAMS, CAMS), 0)
    lane = lax.broadcasted_iota(jnp.int32, (CAMS, CAMS), 1)
    diagonal = sub == lane
    mean_row = jnp.sum(jnp.where(diagonal, mean, 0.0), axis=0, keepdims=True)
    covar = gram / pixels - mean * mean_row
    only = jnp.where(diagonal, covar, 0.0)
    spread = jnp.sum(only, axis=1, keepdims=True) + var_eps
    spread_row = jnp.sum(only, axis=0, keepdims=True) + var_eps
    out[...] = covar / jnp.sqrt(spread * spread_row)


def correlate(parts, pixels):
    return pl.pallas_call(
        functools.partial(correlate_kernel, pixels),
        out_shape=jax.ShapeDtypeStruct((CAMS, CAMS), f32),
        name="correlate",
    )(*parts)


def exchange(array, axis, distance):
    size = lax.axis_size(axis)
    return lax.ppermute(array, axis, [(i, i ^ distance) for i in range(size)])


def on_device(photos, camera_id):
    rows, width = photos.shape[1:]
    pieces, tiles = lax.axis_size("photo"), lax.axis_size("tile")
    own, up, down, first, last = prepare(camera_id, photos)
    above = lax.ppermute(down, "tile", [(i, i + 1) for i in range(tiles - 1)])
    below = lax.ppermute(up, "tile", [(i + 1, i) for i in range(tiles - 1)])
    before = lax.ppermute(last, "photo", [(i, i + 1) for i in range(pieces - 1)])
    after = lax.ppermute(first, "photo", [(i + 1, i) for i in range(pieces - 1)])
    me = lax.axis_index("photo").astype(jnp.int32)
    parts = []
    for distance in reversed(range(pieces)):
        chunk = (me ^ distance).reshape(1)
        part = main_part(chunk, camera_id, own, above, below, before, after, rows, pieces)
        parts.append(exchange(part, "photo", distance) if distance else part)
    prints, partial = assemble(parts, rows)
    total = partial
    for distance in range(1, pieces):
        total = total + exchange(partial, "photo", distance)
    sums = [total] + [exchange(total, "tile", distance) for distance in range(1, tiles)]
    return prints, correlate(sums, float(rows * tiles * width))


def solution(mesh):
    return jax.shard_map(
        on_device,
        mesh=mesh,
        in_specs=(P("photo", "tile", None), P("photo")),
        out_specs=(P(None, "tile", "photo"), P()),
        check_vma=False,
    )
```

time: 559 us -> 94.9 us (0.17); the launches traced: 550 us -> 94.5 us
  local copies, waits for them, and re-layouts: 291 us -> 6.47 us
  other arithmetic: 167 us -> 0.01 us
  blocking collectives: 67.9 us -> 0 us
  waiting for transfers between devices: 0.01 us -> 33.2 us
  Pallas kernels: 0 us -> 28.9 us
  starting transfers between devices: 14.2 us -> 25.1 us
  matrix products: 7.82 us -> 0 us
    slice x5 -> x0, local copies, waits for them, and re-layouts: 114 us -> none  [the longest x1 36.9 us: forward_haar(): top_left = field[..., 0::2, 0::2]]
    mul x3 -> x0, other arithmetic: 108 us -> none  [the longest x1 66 us: on_device(): noise_map = inverse_haar(centre * gain).astype(jnp.bfloat16)]
    unnamed x25 -> x32, local copies, waits for them, and re-layouts: 87.8 us -> 6.47 us
    mul x2 -> x0, local copies, waits for them, and re-layouts: 41.4 us -> none  [the longest x1 20.8 us: camera_totals(): field * field]
    psum x1 -> x0, blocking collectives: 40.3 us -> none  [on_device(): gram, totals = lax.psum((gram_local, totals_local), ('photo', 'tile'))]
    add x2 -> x1, other arithmetic: 38.2 us -> 0.01 us  [on_device(): total = total + exchange(partial, 'photo', distance)]
    ppermute x2 -> x17, waiting for transfers between devices: 0.01 us -> 33.2 us  [the longest x13 15.9 us: exchange(): return lax.ppermute(array, axis, [(i, i ^ distance) for i in range(size)])]
    another operation x3 -> x0, local copies, waits for them, and re-layouts: 32.9 us -> none  [the longest x1 15.2 us: inverse_haar(): joined = jnp.stack([upper, lower], -2)]
  transfers between devices with their start and end apart: 4 -> 17, of which waited for: 0 -> 9; matrix products, arithmetic and copies ran while one was open for 45% -> 0% of each run, Pallas kernels for 0% -> 16%
where the time goes in v1:
time: 94.9 us; the launch traced here: 94.5 us
  waiting for transfers between devices  33.2 us (35%)
  Pallas kernels  28.9 us (30%)
  starting transfers between devices  25.1 us (26%)
  local copies, waits for them, and re-layouts  6.47 us (7%)
    pallas_call x4, Pallas kernels, main_part(): pl.pallas_call(functools.partial(main_kernel, count, rows, blocks_all), g...  19.8 us
    ppermute x13, starting transfers between devices, exchange(): return lax.ppermute(array, axis, [(i, i ^ distance) for i in range(size)])  15.9 us
    ppermute x13, waiting for transfers between devices, exchange(): return lax.ppermute(array, axis, [(i, i ^ distance) for i in range(size)])  15.9 us
    ppermute x1, waiting for transfers between devices, on_device(): lax.ppermute(first, 'photo', [(i + 1, i) for i in range(pieces - 1)])  10.4 us
    ppermute x1, waiting for transfers between devices, on_device(): lax.ppermute(last, 'photo', [(i, i + 1) for i in range(pieces - 1)])  6.94 us
    unnamed x32, local copies, waits for them, and re-layouts  6.47 us
    pallas_call x1, Pallas kernels, prepare(): pl.pallas_call(prepare_kernel, grid_spec=pltpu.PrefetchScalarGridSpec(num...  4.71 us
    ppermute x1, starting transfers between devices, on_device(): lax.ppermute(last, 'photo', [(i, i + 1) for i in range(pieces - 1)])  4.25 us
  transfers between devices with their start and end apart: 17, of which 9 were waited for; matrix products, arithmetic and copies ran while one was open for 0% of the time, Pallas kernels for 16%

profile of v1, /device:TPU:0, one launch (start us, length us, event | category | flops | bytes accessed | tf_op | source)
XLA Modules:
  0.0 94.5 jit_solution(2537155235434172387)
XLA Ops:
  0.7 0.7 copy-done.3
  1.3 1.6 %copy-done.5 = bf16[16,16,4096]{2,1,0:T(8,128)(2,1)S(1)} copy-done((bf16[16,16,4096]{2,1,0:T(8,128)(2,1)S(1)}, bf16[16,16,4096]{2,1,0:T(8,128)(2,1)}, u32[]{:S(2)}) %copy-start.5) | copy-done | bytes 2097176
  2.9 0.9 copy-done.6
  3.8 0.9 copy-done.7
  4.7 4.7 %prepare.1 = (bf16[256,4096]{1,0:T(8,128)(2,1)S(1)}, bf16[192,2048]{1,0:T(8,128)(2,1)}, bf16[192,2048]{1,0:T(8,128)(2,1)}, f32[24,4096]{1,0:T(8,128)}, f32[24,4096]{1,0:T(8,128)}) custom-call(s32[16]{0:T(128)S(1)} %copy-done.3, bf16[16,16,4096]{2,1,0:T(8,128)(2,1)S(1)} %copy-done.5, bf16[256,256]{1,0:T(8,128)(2,1)S(1)} %copy-done.7, ...), custom_call_target="tpu_custom_call" | custom-call | flops 1000000000 | bytes 8388608 | tf_op jit(solution)/shard_map/prepare/pallas_call | solution.py:116
  9.4 2.4 %collective-permute-start = (bf16[192,2048]{1,0:T(8,128)(2,1)}, bf16[192,2048]{1,0:T(8,128)(2,1)S(1)}, u32[]{:S(2)}, u32[]{:S(2)}) collective-permute-start(bf16[192,2048]{1,0:T(8,128)(2,1)} %get-tuple-element.10), channel_id=1, source_target_pairs={{0,1},{1,2},{2,3},{3,4},{4,5},{5,6},{6,7},{8,9},{9,10},{10,11},{11... | collective-permute-start | bytes 2359304 | tf_op jit(solution)/shard_map/ppermute | solution.py:423
  11.8 1.3 %collective-permute-start.1 = (bf16[192,2048]{1,0:T(8,128)(2,1)}, bf16[192,2048]{1,0:T(8,128)(2,1)}, u32[]{:S(2)}, u32[]{:S(2)}) collective-permute-start(bf16[192,2048]{1,0:T(8,128)(2,1)} %get-tuple-element.11), channel_id=1, source_target_pairs={{1,0},{2,1},{3,2},{4,3},{5,4},{6,5},{7,6},{9,8},{10,9},{11,10},{12... | collective-permute-start | bytes 2359304 | tf_op jit(solution)/shard_map/ppermute | solution.py:424
  13.1 4.3 %collective-permute-start.2 = (f32[24,4096]{1,0:T(8,128)}, f32[24,4096]{1,0:T(8,128)S(1)}, u32[]{:S(2)}, u32[]{:S(2)}) collective-permute-start(f32[24,4096]{1,0:T(8,128)} %get-tuple-element.12), channel_id=1, source_target_pairs={{0,8},{8,16},{16,24},{1,9},{9,17},{17,25},{2,10},{10,18},{18,26},{... | collective-permute-start | bytes 1179656 | tf_op jit(solution)/shard_map/ppermute | solution.py:425
  17.4 1.3 %collective-permute-start.3 = (f32[24,4096]{1,0:T(8,128)}, f32[24,4096]{1,0:T(8,128)}, u32[]{:S(2)}, u32[]{:S(2)}) collective-permute-start(f32[24,4096]{1,0:T(8,128)} %get-tuple-element.13), channel_id=1, source_target_pairs={{8,0},{16,8},{24,16},{9,1},{17,9},{25,17},{10,2},{18,10},{26,18},{... | collective-permute-start | bytes 1179656 | tf_op jit(solution)/shard_map/ppermute | solution.py:426
  18.7 6.9 %collective-permute-done.2.before = f32[24,4096]{1,0:T(8,128)S(1)} collective-permute-done((f32[24,4096]{1,0:T(8,128)}, f32[24,4096]{1,0:T(8,128)S(1)}, u32[]{:S(2)}, u32[]{:S(2)}) %collective-permute-start.2) | collective-permute-done | bytes 393248 | tf_op jit(solution)/shard_map/ppermute | solution.py:425
  25.6 10.4 %collective-permute-done.3.after = f32[24,4096]{1,0:T(8,128)} collective-permute-done((f32[24,4096]{1,0:T(8,128)}, f32[24,4096]{1,0:T(8,128)}, u32[]{:S(2)}, u32[]{:S(2)}) %collective-permute-start.3) | collective-permute-done | bytes 393248 | tf_op jit(solution)/shard_map/ppermute | solution.py:426
  36.1 1.2 %copy-done = bf16[4,512,256]{2,1,0:T(8,128)(2,1)S(1)} copy-done((bf16[4,512,256]{2,1,0:T(8,128)(2,1)S(1)}, bf16[4,512,256]{2,1,0:T(8,128)(2,1)}, u32[]{:S(2)}) %copy-start) | copy-done | bytes 1048600
  37.3 4.9 %residual.4 = bf16[272,1024]{1,0:T(8,128)(2,1)S(1)} custom-call(s32[1]{0:T(128)} %bitcast.where, s32[16]{0:T(128)S(1)} %copy-done.4, bf16[256,4096]{1,0:T(8,128)(2,1)S(1)} %get-tuple-element.9.own.own_l.own_r, bf16[256,4096]{1,0:T(8,128)(2,1)S(1)} %get-tuple-element.9.own.own_l.own_r, bf16[256,4096]{1,0:T(8,128)(2,1)S(1)} %get-tuple-element.9.own.own_l.own_r, ...), custom_call_target="tpu_custom_call" | custom-call | flops 2000000000 | bytes 4194304 | tf_op jit(solution)/shard_map/residual/pallas_call | solution.py:295
  42.3 4.9 %residual.5 = bf16[272,1024]{1,0:T(8,128)(2,1)S(1)} custom-call(s32[1]{0:T(128)} %bitcast.1.where, s32[16]{0:T(128)S(1)} %copy-done.4, bf16[256,4096]{1,0:T(8,128)(2,1)S(1)} %get-tuple-element.9.own.own_l.own_r, bf16[256,4096]{1,0:T(8,128)(2,1)S(1)} %get-tuple-element.9.own.own_l.own_r, bf16[256,4096]{1,0:T(8,128)(2,1)S(1)} %get-tuple-element.9.own.own_l.own_r, ...), custom_call_target="tpu_custom_call" | custom-call | flops 2000000000 | bytes 4194304 | tf_op jit(solution)/shard_map/residual/pallas_call | solution.py:295
  47.3 3.0 %collective-permute-start.5 = (bf16[272,1024]{1,0:T(8,128)(2,1)S(1)}, bf16[272,1024]{1,0:T(8,128)(2,1)S(1)}, u32[]{:S(2)}, u32[]{:S(2)}) collective-permute-start(bf16[272,1024]{1,0:T(8,128)(2,1)S(1)} %residual.5), channel_id=1, source_target_pairs={{0,16},{8,24},{16,0},{24,8},{1,17},{9,25},{17,1},{25,9},{2,18},{10... | collective-permute-start | bytes 1671176 | tf_op jit(solution)/shard_map/ppermute | solution.py:416
  50.3 4.9 %residual.6 = bf16[272,1024]{1,0:T(8,128)(2,1)S(1)} custom-call(s32[1]{0:T(128)} %bitcast.2.where, s32[16]{0:T(128)S(1)} %copy-done.4, bf16[256,4096]{1,0:T(8,128)(2,1)S(1)} %get-tuple-element.9.own.own_l.own_r, bf16[256,4096]{1,0:T(8,128)(2,1)S(1)} %get-tuple-element.9.own.own_l.own_r, bf16[256,4096]{1,0:T(8,128)(2,1)S(1)} %get-tuple-element.9.own.own_l.own_r, ...), custom_call_target="tpu_custom_call" | custom-call | flops 2000000000 | bytes 4194304 | tf_op jit(solution)/shard_map/residual/pallas_call | solution.py:295
  55.8 4.9 %residual.7.refs_3_ = bf16[272,1024]{1,0:T(8,128)(2,1)S(1)} custom-call(s32[1]{0:T(128)} %bitcast.3.where, s32[16]{0:T(128)S(1)} %copy-done.4, bf16[256,4096]{1,0:T(8,128)(2,1)S(1)} %get-tuple-element.9.own.own_l.own_r, bf16[256,4096]{1,0:T(8,128)(2,1)S(1)} %get-tuple-element.9.own.own_l.own_r, bf16[256,4096]{1,0:T(8,128)(2,1)S(1)} %get-tuple-element.9.own.own_l.own_r, ...), custom_call_target="tpu_custom_call" | custom-call | flops 2000000000 | bytes 4194304 | tf_op jit(solution)/shard_map/residual/pallas_call | solution.py:295
  60.8 9.8 %collective-permute-done.5.refs_1_ = bf16[272,1024]{1,0:T(8,128)(2,1)S(1)} collective-permute-done((bf16[272,1024]{1,0:T(8,128)(2,1)S(1)}, bf16[272,1024]{1,0:T(8,128)(2,1)S(1)}, u32[]{:S(2)}, u32[]{:S(2)}) %collective-permute-start.5) | collective-permute-done | bytes 557088 | tf_op jit(solution)/shard_map/ppermute | solution.py:416
  70.6 2.8 %assemble.1 = (f32[32,16,1024]{2,1,0:T(8,128)}, f32[32,128]{1,0:T(8,128)S(1)}) custom-call(bf16[272,1024]{1,0:T(8,128)(2,1)S(1)} %collective-permute-done.4.refs_0_, bf16[272,1024]{1,0:T(8,128)(2,1)S(1)} %collective-permute-done.5.refs_1_, bf16[272,1024]{1,0:T(8,128)(2,1)S(1)} %collective-permute-done.6.refs_2_, bf16[272,1024]{1,0:T(8,128)(2,1)S(1)} %residual.7.refs_3_), custom_call_target="tpu_custom_call" | custom-call | flops 2000000000 | bytes 4194304 | tf_op jit(solution)/shard_map/assemble/pallas_call | solution.py:373
  73.4 1.3 %collective-permute-start.9 = (f32[32,128]{1,0:T(8,128)S(1)}, f32[32,128]{1,0:T(8,128)S(1)}, u32[]{:S(2)}, u32[]{:S(2)}) collective-permute-start(f32[32,128]{1,0:T(8,128)S(1)} %get-tuple-element.15), channel_id=1, source_target_pairs={{0,24},{8,16},{16,8},{24,0},{1,25},{9,17},{17,9},{25,1},{2,26},{10... | collective-permute-start | bytes 49160 | tf_op jit(solution)/shard_map/ppermute | solution.py:416
  74.6 1.7 %collective-permute-start.8 = (f32[32,128]{1,0:T(8,128)S(1)}, f32[32,128]{1,0:T(8,128)S(1)}, u32[]{:S(2)}, u32[]{:S(2)}) collective-permute-start(f32[32,128]{1,0:T(8,128)S(1)} %get-tuple-element.15), channel_id=1, source_target_pairs={{0,16},{8,24},{16,0},{24,8},{1,17},{9,25},{17,1},{25,9},{2,18},{10... | collective-permute-start | bytes 49160 | tf_op jit(solution)/shard_map/ppermute | solution.py:416
  76.9 1.1 %collective-permute-done.9 = f32[32,128]{1,0:T(8,128)S(1)} collective-permute-done((f32[32,128]{1,0:T(8,128)S(1)}, f32[32,128]{1,0:T(8,128)S(1)}, u32[]{:S(2)}, u32[]{:S(2)}) %collective-permute-start.9) | collective-permute-done | bytes 16416 | tf_op jit(solution)/shard_map/ppermute | solution.py:416
  78.4 1.7 %collective-permute-done.7 = f32[32,128]{1,0:T(8,128)S(1)} collective-permute-done((f32[32,128]{1,0:T(8,128)S(1)}, f32[32,128]{1,0:T(8,128)S(1)}, u32[]{:S(2)}, u32[]{:S(2)}) %collective-permute-start.7) | collective-permute-done | bytes 16416 | tf_op jit(solution)/shard_map/ppermute | solution.py:416
  80.1 2.4 %collective-permute-start.16 = (f32[32,128]{1,0:T(8,128)S(1)}, f32[32,128]{1,0:T(8,128)S(1)}, u32[]{:S(2)}, u32[]{:S(2)}) collective-permute-start(f32[32,128]{1,0:T(8,128)S(1)} %add_add_fusion.refs_0_), channel_id=1, source_target_pairs={{0,7},{1,6},{2,5},{3,4},{4,3},{5,2},{6,1},{7,0},{8,15},{9,14},{10,... | collective-permute-start | bytes 49160 | tf_op jit(solution)/shard_map/ppermute | solution.py:416
  82.5 1.9 %collective-permute-start.15 = (f32[32,128]{1,0:T(8,128)S(1)}, f32[32,128]{1,0:T(8,128)S(1)}, u32[]{:S(2)}, u32[]{:S(2)}) collective-permute-start(f32[32,128]{1,0:T(8,128)S(1)} %add_add_fusion.refs_0_), channel_id=1, source_target_pairs={{0,6},{1,7},{2,4},{3,5},{4,2},{5,3},{6,0},{7,1},{8,14},{9,15},{10,... | collective-permute-start | bytes 49160 | tf_op jit(solution)/shard_map/ppermute | solution.py:416
  84.4 1.0 %collective-permute-start.14 = (f32[32,128]{1,0:T(8,128)S(1)}, f32[32,128]{1,0:T(8,128)S(1)}, u32[]{:S(2)}, u32[]{:S(2)}) collective-permute-start(f32[32,128]{1,0:T(8,128)S(1)} %add_add_fusion.refs_0_), channel_id=1, source_target_pairs={{0,5},{1,4},{2,7},{3,6},{4,1},{5,0},{6,3},{7,2},{8,13},{9,12},{10,... | collective-permute-start | bytes 49160 | tf_op jit(solution)/shard_map/ppermute | solution.py:416
  85.4 1.6 %collective-permute-start.13 = (f32[32,128]{1,0:T(8,128)S(1)}, f32[32,128]{1,0:T(8,128)S(1)}, u32[]{:S(2)}, u32[]{:S(2)}) collective-permute-start(f32[32,128]{1,0:T(8,128)S(1)} %add_add_fusion.refs_0_), channel_id=1, source_target_pairs={{0,4},{1,5},{2,6},{3,7},{4,0},{5,1},{6,2},{7,3},{8,12},{9,13},{10,... | collective-permute-start | bytes 49160 | tf_op jit(solution)/shard_map/ppermute | solution.py:416
  86.9 0.9 collective-permute-start.12
  87.9 0.9 collective-permute-start.11
  88.8 1.3 %collective-permute-done.13.refs_4_ = f32[32,128]{1,0:T(8,128)S(1)} collective-permute-done((f32[32,128]{1,0:T(8,128)S(1)}, f32[32,128]{1,0:T(8,128)S(1)}, u32[]{:S(2)}, u32[]{:S(2)}) %collective-permute-start.13) | collective-permute-done | bytes 16416 | tf_op jit(solution)/shard_map/ppermute | solution.py:416
  90.2 1.4 %collective-permute-done.11.refs_2_ = f32[32,128]{1,0:T(8,128)S(1)} collective-permute-done((f32[32,128]{1,0:T(8,128)S(1)}, f32[32,128]{1,0:T(8,128)S(1)}, u32[]{:S(2)}, u32[]{:S(2)}) %collective-permute-start.11) | collective-permute-done | bytes 16416 | tf_op jit(solution)/shard_map/ppermute | solution.py:416
  92.8 1.6 %correlate.1 = f32[32,32]{1,0:T(8,128)} custom-call(f32[32,128]{1,0:T(8,128)} %copy-done.8, f32[32,128]{1,0:T(8,128)} %copy-done.15, f32[32,128]{1,0:T(8,128)} %copy-done.14, f32[32,128]{1,0:T(8,128)} %copy-done.13, f32[32,128]{1,0:T(8,128)} %copy-done.12, f32[32,128]{1,0:T(8,128)} %copy-done.11, f32[32,128]{1,0:T(8,128)} %copy-done.10, f32[32,128]{1,0:T(8,128)} %copy-done.9), custom_call_target="tpu_custom_call" | custom-call | tf_op jit(solution)/shard_map/correlate/pallas_call | solution.py:407
  (42 shorter events, 2.9 us)
Async XLA Ops:
  0.6 35.4 %copy-start.2 = (bf16[256,256]{1,0:T(8,128)(2,1)S(1)}, bf16[256,256]{1,0:T(8,128)(2,1)}, u32[]{:S(2)}) copy-start(bf16[256,256]{1,0:T(8,128)(2,1)} %constant.22.clone.merge) | copy-start | bytes 393220
  0.6 0.7 copy-start.3
  1.3 1.6 %copy-start.5 = (bf16[16,16,4096]{2,1,0:T(8,128)(2,1)S(1)}, bf16[16,16,4096]{2,1,0:T(8,128)(2,1)}, u32[]{:S(2)}) copy-start(bf16[16,16,4096]{2,1,0:T(8,128)(2,1)} %photos.1) | copy-start | bytes 6291460
  2.9 0.9 copy-start.6
  3.8 0.9 copy-start.7
  4.7 31.3 %copy-start.4 = (s32[16]{0:T(128)S(1)}, s32[16]{0:T(128)}, u32[]{:S(2)}) copy-start(s32[16]{0:T(128)} %ids.9) | copy-start | bytes 196
  9.4 26.6 %collective-permute-start = (bf16[192,2048]{1,0:T(8,128)(2,1)}, bf16[192,2048]{1,0:T(8,128)(2,1)S(1)}, u32[]{:S(2)}, u32[]{:S(2)}) collective-permute-start(bf16[192,2048]{1,0:T(8,128)(2,1)} %get-tuple-element.10), channel_id=1, source_target_pairs={{0,1},{1,2},{2,3},{3,4},{4,5},{5,6},{6,7},{8,9},{9,10},{10,11},{11... | collective-permute-start | bytes 2359304 | tf_op jit(solution)/shard_map/ppermute | solution.py:423
  11.8 24.2 %collective-permute-start.1 = (bf16[192,2048]{1,0:T(8,128)(2,1)}, bf16[192,2048]{1,0:T(8,128)(2,1)}, u32[]{:S(2)}, u32[]{:S(2)}) collective-permute-start(bf16[192,2048]{1,0:T(8,128)(2,1)} %get-tuple-element.11), channel_id=1, source_target_pairs={{1,0},{2,1},{3,2},{4,3},{5,4},{6,5},{7,6},{9,8},{10,9},{11,10},{12... | collective-permute-start | bytes 2359304 | tf_op jit(solution)/shard_map/ppermute | solution.py:424
  13.1 12.5 %collective-permute-start.2 = (f32[24,4096]{1,0:T(8,128)}, f32[24,4096]{1,0:T(8,128)S(1)}, u32[]{:S(2)}, u32[]{:S(2)}) collective-permute-start(f32[24,4096]{1,0:T(8,128)} %get-tuple-element.12), channel_id=1, source_target_pairs={{0,8},{8,16},{16,24},{1,9},{9,17},{17,25},{2,10},{10,18},{18,26},{... | collective-permute-start | bytes 1179656 | tf_op jit(solution)/shard_map/ppermute | solution.py:425
  17.4 18.6 %collective-permute-start.3 = (f32[24,4096]{1,0:T(8,128)}, f32[24,4096]{1,0:T(8,128)}, u32[]{:S(2)}, u32[]{:S(2)}) collective-permute-start(f32[24,4096]{1,0:T(8,128)} %get-tuple-element.13), channel_id=1, source_target_pairs={{8,0},{16,8},{24,16},{9,1},{17,9},{25,17},{10,2},{18,10},{26,18},{... | collective-permute-start | bytes 1179656 | tf_op jit(solution)/shard_map/ppermute | solution.py:426
  36.0 1.2 %copy-start = (bf16[4,512,256]{2,1,0:T(8,128)(2,1)S(1)}, bf16[4,512,256]{2,1,0:T(8,128)(2,1)}, u32[]{:S(2)}) copy-start(bf16[4,512,256]{2,1,0:T(8,128)(2,1)} %constant.21.clone.box) | copy-start | bytes 3145732
  37.3 5.0 %copy-start.1 = (bf16[4,512,256]{2,1,0:T(8,128)(2,1)S(1)}, bf16[4,512,256]{2,1,0:T(8,128)(2,1)}, u32[]{:S(2)}) copy-start(bf16[4,512,256]{2,1,0:T(8,128)(2,1)} %constant.21.clone.box) | copy-start | bytes 3145732
  42.2 18.5 %collective-permute-start.4 = (bf16[272,1024]{1,0:T(8,128)(2,1)S(1)}, bf16[272,1024]{1,0:T(8,128)(2,1)S(1)}, u32[]{:S(2)}, u32[]{:S(2)}) collective-permute-start(bf16[272,1024]{1,0:T(8,128)(2,1)S(1)} %residual.4), channel_id=1, source_target_pairs={{0,24},{8,16},{16,8},{24,0},{1,25},{9,17},{17,9},{25,1},{2,26},{10... | collective-permute-start | bytes 1671176 | tf_op jit(solution)/shard_map/ppermute | solution.py:416
  47.3 23.3 %collective-permute-start.5 = (bf16[272,1024]{1,0:T(8,128)(2,1)S(1)}, bf16[272,1024]{1,0:T(8,128)(2,1)S(1)}, u32[]{:S(2)}, u32[]{:S(2)}) collective-permute-start(bf16[272,1024]{1,0:T(8,128)(2,1)S(1)} %residual.5), channel_id=1, source_target_pairs={{0,16},{8,24},{16,0},{24,8},{1,17},{9,25},{17,1},{25,9},{2,18},{10... | collective-permute-start | bytes 1671176 | tf_op jit(solution)/shard_map/ppermute | solution.py:416
  55.2 15.4 %collective-permute-start.6 = (bf16[272,1024]{1,0:T(8,128)(2,1)S(1)}, bf16[272,1024]{1,0:T(8,128)(2,1)S(1)}, u32[]{:S(2)}, u32[]{:S(2)}) collective-permute-start(bf16[272,1024]{1,0:T(8,128)(2,1)S(1)} %residual.6), channel_id=1, source_target_pairs={{0,8},{8,0},{16,24},{24,16},{1,9},{9,1},{17,25},{25,17},{2,10},{10... | collective-permute-start | bytes 1671176 | tf_op jit(solution)/shard_map/ppermute | solution.py:416
  73.4 4.6 %collective-permute-start.9 = (f32[32,128]{1,0:T(8,128)S(1)}, f32[32,128]{1,0:T(8,128)S(1)}, u32[]{:S(2)}, u32[]{:S(2)}) collective-permute-start(f32[32,128]{1,0:T(8,128)S(1)} %get-tuple-element.15), channel_id=1, source_target_pairs={{0,24},{8,16},{16,8},{24,0},{1,25},{9,17},{17,9},{25,1},{2,26},{10... | collective-permute-start | bytes 49160 | tf_op jit(solution)/shard_map/ppermute | solution.py:416
  74.6 3.7 %collective-permute-start.8 = (f32[32,128]{1,0:T(8,128)S(1)}, f32[32,128]{1,0:T(8,128)S(1)}, u32[]{:S(2)}, u32[]{:S(2)}) collective-permute-start(f32[32,128]{1,0:T(8,128)S(1)} %get-tuple-element.15), channel_id=1, source_target_pairs={{0,16},{8,24},{16,0},{24,8},{1,17},{9,25},{17,1},{25,9},{2,18},{10... | collective-permute-start | bytes 49160 | tf_op jit(solution)/shard_map/ppermute | solution.py:416
  76.3 3.7 %collective-permute-start.7 = (f32[32,128]{1,0:T(8,128)S(1)}, f32[32,128]{1,0:T(8,128)S(1)}, u32[]{:S(2)}, u32[]{:S(2)}) collective-permute-start(f32[32,128]{1,0:T(8,128)S(1)} %get-tuple-element.15), channel_id=1, source_target_pairs={{0,8},{8,0},{16,24},{24,16},{1,9},{9,1},{17,25},{25,17},{2,10},{10... | collective-permute-start | bytes 49160 | tf_op jit(solution)/shard_map/ppermute | solution.py:416
  80.1 11.6 %copy-start.8 = (f32[32,128]{1,0:T(8,128)}, f32[32,128]{1,0:T(8,128)S(1)}, u32[]{:S(2)}) copy-start(f32[32,128]{1,0:T(8,128)S(1)} %add_add_fusion.refs_0_) | copy-start | bytes 49156
  80.1 7.8 %collective-permute-start.16 = (f32[32,128]{1,0:T(8,128)S(1)}, f32[32,128]{1,0:T(8,128)S(1)}, u32[]{:S(2)}, u32[]{:S(2)}) collective-permute-start(f32[32,128]{1,0:T(8,128)S(1)} %add_add_fusion.refs_0_), channel_id=1, source_target_pairs={{0,7},{1,6},{2,5},{3,4},{4,3},{5,2},{6,1},{7,0},{8,15},{9,14},{10,... | collective-permute-start | bytes 49160 | tf_op jit(solution)/shard_map/ppermute | solution.py:416
  82.5 6.3 %collective-permute-start.15 = (f32[32,128]{1,0:T(8,128)S(1)}, f32[32,128]{1,0:T(8,128)S(1)}, u32[]{:S(2)}, u32[]{:S(2)}) collective-permute-start(f32[32,128]{1,0:T(8,128)S(1)} %add_add_fusion.refs_0_), channel_id=1, source_target_pairs={{0,6},{1,7},{2,4},{3,5},{4,2},{5,3},{6,0},{7,1},{8,14},{9,15},{10,... | collective-permute-start | bytes 49160 | tf_op jit(solution)/shard_map/ppermute | solution.py:416
  84.4 4.4 %collective-permute-start.14 = (f32[32,128]{1,0:T(8,128)S(1)}, f32[32,128]{1,0:T(8,128)S(1)}, u32[]{:S(2)}, u32[]{:S(2)}) collective-permute-start(f32[32,128]{1,0:T(8,128)S(1)} %add_add_fusion.refs_0_), channel_id=1, source_target_pairs={{0,5},{1,4},{2,7},{3,6},{4,1},{5,0},{6,3},{7,2},{8,13},{9,12},{10,... | collective-permute-start | bytes 49160 | tf_op jit(solution)/shard_map/ppermute | solution.py:416
  85.4 4.8 %collective-permute-start.13 = (f32[32,128]{1,0:T(8,128)S(1)}, f32[32,128]{1,0:T(8,128)S(1)}, u32[]{:S(2)}, u32[]{:S(2)}) collective-permute-start(f32[32,128]{1,0:T(8,128)S(1)} %add_add_fusion.refs_0_), channel_id=1, source_target_pairs={{0,4},{1,5},{2,6},{3,7},{4,0},{5,1},{6,2},{7,3},{8,12},{9,13},{10,... | collective-permute-start | bytes 49160 | tf_op jit(solution)/shard_map/ppermute | solution.py:416
  86.9 3.2 %collective-permute-start.12 = (f32[32,128]{1,0:T(8,128)S(1)}, f32[32,128]{1,0:T(8,128)S(1)}, u32[]{:S(2)}, u32[]{:S(2)}) collective-permute-start(f32[32,128]{1,0:T(8,128)S(1)} %add_add_fusion.refs_0_), channel_id=1, source_target_pairs={{0,3},{1,2},{2,1},{3,0},{4,7},{5,6},{6,5},{7,4},{8,11},{9,10},{10,... | collective-permute-start | bytes 49160 | tf_op jit(solution)/shard_map/ppermute | solution.py:416
  87.9 3.8 %copy-start.9 = (f32[32,128]{1,0:T(8,128)}, f32[32,128]{1,0:T(8,128)S(1)}, u32[]{:S(2)}) copy-start(f32[32,128]{1,0:T(8,128)S(1)} %collective-permute-done.16.refs_7_) | copy-start | bytes 49156
  87.9 3.8 %collective-permute-start.11 = (f32[32,128]{1,0:T(8,128)S(1)}, f32[32,128]{1,0:T(8,128)S(1)}, u32[]{:S(2)}, u32[]{:S(2)}) collective-permute-start(f32[32,128]{1,0:T(8,128)S(1)} %add_add_fusion.refs_0_), channel_id=1, source_target_pairs={{0,2},{1,3},{2,0},{3,1},{4,6},{5,7},{6,4},{7,5},{8,10},{9,11},{10,... | collective-permute-start | bytes 49160 | tf_op jit(solution)/shard_map/ppermute | solution.py:416
  88.8 2.9 %copy-start.10 = (f32[32,128]{1,0:T(8,128)}, f32[32,128]{1,0:T(8,128)S(1)}, u32[]{:S(2)}) copy-start(f32[32,128]{1,0:T(8,128)S(1)} %collective-permute-done.15.refs_6_) | copy-start | bytes 49156
  88.8 2.9 %collective-permute-start.10 = (f32[32,128]{1,0:T(8,128)S(1)}, f32[32,128]{1,0:T(8,128)S(1)}, u32[]{:S(2)}, u32[]{:S(2)}) collective-permute-start(f32[32,128]{1,0:T(8,128)S(1)} %add_add_fusion.refs_0_), channel_id=1, source_target_pairs={{0,1},{1,0},{2,3},{3,2},{4,5},{5,4},{6,7},{7,6},{8,9},{9,8},{10,11... | collective-permute-start | bytes 49160 | tf_op jit(solution)/shard_map/ppermute | solution.py:416
  88.8 2.8 %copy-start.11 = (f32[32,128]{1,0:T(8,128)}, f32[32,128]{1,0:T(8,128)S(1)}, u32[]{:S(2)}) copy-start(f32[32,128]{1,0:T(8,128)S(1)} %collective-permute-done.14.refs_5_) | copy-start | bytes 49156
  90.1 1.6 %copy-start.12 = (f32[32,128]{1,0:T(8,128)}, f32[32,128]{1,0:T(8,128)S(1)}, u32[]{:S(2)}) copy-start(f32[32,128]{1,0:T(8,128)S(1)} %collective-permute-done.13.refs_4_) | copy-start | bytes 49156
  90.2 1.5 %copy-start.13 = (f32[32,128]{1,0:T(8,128)}, f32[32,128]{1,0:T(8,128)S(1)}, u32[]{:S(2)}) copy-start(f32[32,128]{1,0:T(8,128)S(1)} %collective-permute-done.12.refs_3_) | copy-start | bytes 49156
  91.6 0.6 copy-start.14
  (1 other events, 0.6 us)

commit v2 on v1

v2 whole, which is shorter than its diff:
```python
import functools

import jax
import jax.numpy as jnp
from jax import lax
from jax.experimental import pallas as pl
from jax.experimental.pallas import tpu as pltpu
from jax.sharding import PartitionSpec as P

CAMS = 32
RADII = 4
FINE = 2
LANES = 128

noise_power = 1.0
var_eps = 1e-06

f32 = jnp.float32
bf16 = jnp.bfloat16


def log2(value):
    return value.bit_length() - 1


def indicator(condition):
    return jnp.where(condition, 1.0, 0.0).astype(bf16)


def iotas(shape):
    return (
        lax.broadcasted_iota(jnp.int32, shape, len(shape) - 2),
        lax.broadcasted_iota(jnp.int32, shape, len(shape) - 1),
    )


def row_permutation(photos, rows):
    sub, lane = iotas((photos * rows, photos * rows))
    same_row = (sub >> log2(photos)) == (lane & (rows - 1))
    same_photo = (sub & (photos - 1)) == (lane >> log2(rows))
    return indicator(same_row & same_photo)


def column_split():
    sub, lane = iotas((2 * LANES, 2 * LANES))
    return indicator(sub == 2 * (lane & (LANES - 1)) + (lane >> log2(LANES)))


def column_merge():
    sub, lane = iotas((2 * LANES, 2 * LANES))
    return indicator(lane == 2 * (sub & (LANES - 1)) + (sub >> log2(LANES)))


def box_matrix(radius):
    sub, lane = iotas((4 * LANES, 2 * LANES))
    return indicator(jnp.abs(sub - LANES - lane) <= radius)


def haar_rows(even0, odd0, even1, odd1):
    low0, low1 = even0 + odd0, even1 + odd1
    high0, high1 = even0 - odd0, even1 - odd1
    return (low0 - low1, high0 + high1, high0 - high1)


def halves(value):
    upper = value.astype(bf16)
    lower = (value - upper.astype(f32)).astype(bf16)
    return upper, lower


def prepare_kernel(photos, sorted_out, up_out, down_out, buffer, arrived):
    count, rows, width = photos.shape
    cells = rows // 2
    step = width // arrived.shape[0]
    copies = []
    for part in range(width // step):
        cols = pl.ds(part * step, step)
        copies.append(
            pltpu.make_async_copy(photos.at[:, :, cols], buffer.at[:, :, cols], arrived.at[part])
        )
        copies[-1].start()
    perm = row_permutation(count, rows)
    split = column_split()
    for part in range(width // step):
        copies[part].wait()
        flat = buffer[:, :, part * step : (part + 1) * step].reshape(count * rows, step)
        by_row = jnp.dot(perm, flat, preferred_element_type=f32).astype(bf16)
        for inner in range(step // (2 * LANES)):
            block = part * (step // (2 * LANES)) + inner
            cols = slice(block * 2 * LANES, (block + 1) * 2 * LANES)
            cell_cols = slice(block * LANES, (block + 1) * LANES)
            pixels = by_row[:, inner * 2 * LANES : (inner + 1) * 2 * LANES]
            parted = jnp.dot(pixels, split, preferred_element_type=f32)
            sorted_out[:, cols] = parted.astype(bf16)
            for i in range(cells):
                if RADII <= i < cells - RADII:
                    continue
                top = parted[2 * i * count : (2 * i + 1) * count]
                low = parted[(2 * i + 1) * count : (2 * i + 2) * count]
                bands = haar_rows(top[:, :LANES], top[:, LANES:], low[:, :LANES], low[:, LANES:])
                for band in range(3):
                    square = (bands[band] * bands[band]).astype(bf16)
                    if i < RADII:
                        start = (band * RADII + i) * count
                        up_out[start : start + count, cell_cols] = square
                    if i >= cells - RADII:
                        start = (band * RADII + i - (cells - RADII)) * count
                        down_out[start : start + count, cell_cols] = square


def prepare(photos):
    count, rows, width = photos.shape
    step = min(width, 1024)
    size = count * rows
    halo = 3 * RADII * count
    vmem = pl.BlockSpec(memory_space=pltpu.VMEM)
    return pl.pallas_call(
        prepare_kernel,
        in_specs=[pl.BlockSpec(memory_space=pltpu.HBM)],
        out_specs=[vmem] * 3,
        out_shape=[
            jax.ShapeDtypeStruct((size, width), bf16),
            jax.ShapeDtypeStruct((halo, width // 2), bf16),
            jax.ShapeDtypeStruct((halo, width // 2), bf16),
        ],
        scratch_shapes=[
            pltpu.VMEM((count, rows, width), bf16),
            pltpu.SemaphoreType.DMA((width // step,)),
        ],
        compiler_params=pltpu.CompilerParams(vmem_limit_bytes=24 * 2**20),
        cost_estimate=pl.CostEstimate(flops=10**9, bytes_accessed=8 * 2**20, transcendentals=0),
        name="prepare",
    )(photos)


def energy_kernel(count, rows, me, ids, own, inverse, select_out, box_out, merge_out, *extras):
    size, width_all = own.shape
    width = width_all // len(extras)
    ranks = [jnp.int32(0)]
    for photo in range(1, count):
        ranks.append(ranks[-1] + jnp.where(ids[photo] != ids[photo - 1], 1, 0))
    last = ranks[-1]
    slots = [jnp.where(rank == 0, 0, jnp.where(rank == last, 1, rank + 1)) for rank in ranks]

    sub, lane = iotas((size, size))
    lane_photo = lane & (count - 1)
    lane_slot = jnp.zeros_like(lane)
    for photo in range(count):
        lane_slot = jnp.where(lane_photo == photo, slots[photo], lane_slot)
    in_slot = lane_slot == (sub >> log2(rows))
    same_row = (sub & (rows - 1)) == (lane >> log2(count))
    select = indicator(in_slot & same_row)
    select = jnp.concatenate([select, select], axis=1)
    select_out[...] = select
    for radius in range(1, RADII + 1):
        box_out[radius - 1] = box_matrix(radius)
    merge = column_merge()
    merge_out[...] = merge

    sub, lane = iotas((rows, width))
    slot_id = jnp.full((rows, width), -1, jnp.int32)
    for photo in range(count):
        slot_id = jnp.where((lane >> log2(rows)) == slots[photo], ids[photo], slot_id)
    notes = jnp.where(sub == 0, ids[0], jnp.where(sub == 1, ids[count - 1], slot_id))
    notes = jnp.where(sub == 3, last + 1, notes).astype(f32).astype(bf16)

    for distance, extra in enumerate(extras):
        base = (me[0] ^ distance) * width
        extra[2 * rows :, :] = notes
        for block in range(width // (2 * LANES)):
            cols = pl.ds(pl.multiple_of(base + block * 2 * LANES, 2 * LANES), 2 * LANES)
            pixel = own[:, cols].astype(f32)
            pair = jnp.concatenate(halves(pixel * pixel), axis=0)
            energy = jnp.dot(select, pair, preferred_element_type=f32)
            inverse[:, cols] = 1.0 / jnp.maximum(energy, 2.0**-20)
            edges = jnp.dot(
                energy[: 2 * rows].astype(bf16), merge, preferred_element_type=f32
            )
            extra[: 2 * rows, block * 2 * LANES : (block + 1) * 2 * LANES] = edges.astype(bf16)


def energies(me, ids, own, rows, pieces):
    size, width = own.shape
    vmem = pl.BlockSpec(memory_space=pltpu.VMEM)
    smem = pl.BlockSpec(memory_space=pltpu.SMEM)
    return pl.pallas_call(
        functools.partial(energy_kernel, size // rows, rows),
        in_specs=[smem, smem, vmem],
        out_specs=[vmem] * (4 + pieces),
        out_shape=[
            jax.ShapeDtypeStruct((size, width), f32),
            jax.ShapeDtypeStruct((size, 2 * size), bf16),
            jax.ShapeDtypeStruct((RADII, 4 * LANES, 2 * LANES), bf16),
            jax.ShapeDtypeStruct((2 * LANES, 2 * LANES), bf16),
        ]
        + [jax.ShapeDtypeStruct((3 * rows, width // pieces), bf16)] * pieces,
        compiler_params=pltpu.CompilerParams(vmem_limit_bytes=24 * 2**20),
        cost_estimate=pl.CostEstimate(flops=10**9, bytes_accessed=8 * 2**20, transcendentals=0),
        name="energies",
    )(me, ids, own)


def blend_kernel(rows, me, *refs):
    pieces = (len(refs) - 4) // 1
    extras, (select, share, most, held) = refs[:pieces], refs[pieces:]
    size = select.shape[2]
    tall = CAMS * rows
    sub, lane = iotas((tall, size))
    same_row = (sub & (rows - 1)) == (lane & (rows - 1))
    camera = (sub >> log2(rows)).astype(f32)
    highest = jnp.float32(0)
    for distance, extra in enumerate(extras):
        notes = extra[2 * rows :, :].astype(f32)
        select[distance] = indicator((camera == notes[2:3, :size]) & same_row)
        highest = jnp.maximum(highest, jnp.max(notes[3:4, :LANES]))
        held[me[0] ^ distance] = extra[...].astype(f32)
    most[0, 0] = highest.astype(jnp.int32)
    ones = jnp.ones((rows, share.shape[3]), f32)
    for device in range(pieces):
        if device == 0:
            share[me[0] ^ device, 0] = ones
        if device == pieces - 1:
            share[me[0] ^ device, 1] = ones
            continue
        late = held[device, rows : 2 * rows]
        early = held[device + 1, :rows]
        crosses = held[device, 2 * rows + 1 : 2 * rows + 2] == held[device + 1, 2 * rows : 2 * rows + 1]
        joint = 1.0 / (late + early)
        share[me[0] ^ device, 1] = jnp.where(crosses, late * joint, 1.0)
        share[me[0] ^ (device + 1), 0] = jnp.where(crosses, early * joint, 1.0)


def blend(me, extras, rows, size):
    pieces, width = len(extras), extras[0].shape[1]
    vmem = pl.BlockSpec(memory_space=pltpu.VMEM)
    smem = pl.BlockSpec(memory_space=pltpu.SMEM)
    return pl.pallas_call(
        functools.partial(blend_kernel, rows),
        in_specs=[smem] + [vmem] * pieces,
        out_specs=[vmem, vmem, smem],
        out_shape=[
            jax.ShapeDtypeStruct((pieces, CAMS * rows, size), bf16),
            jax.ShapeDtypeStruct((pieces, 2, rows, width), f32),
            jax.ShapeDtypeStruct((1, 1), jnp.int32),
        ],
        scratch_shapes=[pltpu.VMEM((pieces, 3 * rows, width), f32)],
        compiler_params=pltpu.CompilerParams(vmem_limit_bytes=24 * 2**20),
        name="blend",
    )(me, *extras)


def main_kernel(
    count, rows, blocks_all,
    where,
    own, own_l, own_r, above, above_l, above_r, below, below_l, below_r,
    inverse, select, box, merge,
    out,
    sums, rest, least, product,
):
    cells = rows // 2
    size = count * rows
    width = own.shape[1]
    blocks = width // (2 * LANES)
    chunk = where[0]
    left_ok = jnp.where(chunk > 0, 1.0, 0.0).astype(f32)
    right_ok = jnp.where((chunk + 1) * blocks < blocks_all, 1.0, 0.0).astype(f32)

    for block in range(-1, blocks + 1):
        if block < 0:
            mine, over, under, factor, at = own_l, above_l, below_l, left_ok, 0
        elif block == blocks:
            mine, over, under, factor, at = own_r, above_r, below_r, right_ok, 0
        else:
            mine, over, under, factor, at = own, above, below, None, block
        even = slice(2 * at * LANES, (2 * at + 1) * LANES)
        odd = slice((2 * at + 1) * LANES, (2 * at + 2) * LANES)
        cols = slice(at * LANES, (at + 1) * LANES)
        place = slice((block + 1) * LANES, (block + 2) * LANES)
        squares = [[], [], []]
        for i in range(cells):
            top = slice(2 * i * count, (2 * i + 1) * count)
            low = slice((2 * i + 1) * count, (2 * i + 2) * count)
            bands = haar_rows(
                mine[top, even].astype(f32),
                mine[top, odd].astype(f32),
                mine[low, even].astype(f32),
                mine[low, odd].astype(f32),
            )
            for band in range(3):
                squares[band].append(bands[band] * bands[band])
        for band in range(3):
            start = band * RADII * count
            outer = [
                over[start + i * count : start + (i + 1) * count, cols].astype(f32)
                for i in range(RADII)
            ]
            inner = [
                under[start + i * count : start + (i + 1) * count, cols].astype(f32)
                for i in range(RADII)
            ]
            column = outer + squares[band] + inner
            if factor is not None:
                column = [value * factor for value in column]
            for i in range(cells):
                total = column[i + RADII]
                at_row = (band * cells + i) * count
                for radius in range(1, RADII + 1):
                    total = total + (column[i + RADII - radius] + column[i + RADII + radius])
                    upper = total.astype(bf16)
                    sums[radius - 1, at_row : at_row + count, place] = upper
                    if radius <= FINE and factor is None:
                        lower = (total - upper.astype(f32)).astype(bf16)
                        rest[radius - 1, at_row : at_row + count, cols] = lower

    for group in range(blocks // 2):
        window = slice(2 * group * LANES, (2 * group + 4) * LANES)
        for radius in range(1, RADII + 1):
            narrow, weights = sums[radius - 1, :, window], box[radius - 1]
            if radius <= FINE:
                middle = slice(2 * group * LANES, (2 * group + 2) * LANES)
                narrow = jnp.concatenate([narrow, rest[radius - 1, :, middle]], axis=1)
                weights = jnp.concatenate([weights, weights[LANES : 3 * LANES]], axis=0)
            wide = jnp.dot(narrow, weights, preferred_element_type=f32)
            mean = wide * (1.0 / float((2 * radius + 1) ** 2))
            least[...] = mean if radius == 1 else jnp.minimum(least[...], mean)
        for half in range(2):
            block = 2 * group + half
            even = slice(2 * block * LANES, (2 * block + 1) * LANES)
            odd = slice((2 * block + 1) * LANES, (2 * block + 2) * LANES)
            lanes = slice(half * LANES, (half + 1) * LANES)
            for i in range(cells):
                top = slice(2 * i * count, (2 * i + 1) * count)
                low = slice((2 * i + 1) * count, (2 * i + 2) * count)
                pixels = (
                    own[top, even].astype(f32),
                    own[top, odd].astype(f32),
                    own[low, even].astype(f32),
                    own[low, odd].astype(f32),
                )
                bands = haar_rows(*pixels)
                shrunk = []
                for band in range(3):
                    at_row = (band * cells + i) * count
                    variance = least[at_row : at_row + count, lanes]
                    gain = 1.0 / jnp.maximum(variance, 4.0 * noise_power)
                    shrunk.append(bands[band] * (gain * noise_power))
                horiz, vertic, diagon = shrunk
                both, cross = vertic + diagon, vertic - diagon
                noise = (horiz + both, horiz - both, cross - horiz, -horiz - cross)
                for (rows_at, cols_at), pixel, part in zip(
                    ((top, even), (top, odd), (low, even), (low, odd)), pixels, noise
                ):
                    start, stop = rows_at.start, rows_at.stop
                    upper, lower = halves(part.astype(bf16).astype(f32) * pixel)
                    product[start:stop, cols_at] = upper
                    product[size + start : size + stop, cols_at] = lower

    for block in range(blocks):
        cols = slice(2 * block * LANES, (2 * block + 2) * LANES)
        weighted = jnp.dot(select[...], product[:, cols], preferred_element_type=f32)
        part = (weighted * inverse[:, cols]).astype(bf16)
        out[:, cols] = jnp.dot(part, merge[...], preferred_element_type=f32).astype(bf16)


def main_part(chunk, own, above, below, inverse, select, box, merge, rows, pieces, slots):
    size, width_all = own.shape
    count = size // rows
    width = width_all // pieces
    halo = above.shape[0]
    blocks_all = width_all // (2 * LANES)
    blocks = width // (2 * LANES)
    here = lambda i, where: (0, where[0])
    left = lambda i, where: (0, jnp.maximum(where[0] * blocks - 1, 0))
    right = lambda i, where: (0, jnp.minimum((where[0] + 1) * blocks, blocks_all - 1))
    cell_rows = 3 * (rows // 2) * count
    halo_specs = [
        pl.BlockSpec((halo, width // 2), here),
        pl.BlockSpec((halo, LANES), left),
        pl.BlockSpec((halo, LANES), right),
    ]
    return pl.pallas_call(
        functools.partial(main_kernel, count, rows, blocks_all),
        grid_spec=pltpu.PrefetchScalarGridSpec(
            num_scalar_prefetch=1,
            grid=(1,),
            in_specs=[
                pl.BlockSpec((size, width), here),
                pl.BlockSpec((size, 2 * LANES), left),
                pl.BlockSpec((size, 2 * LANES), right),
                *halo_specs,
                *halo_specs,
                pl.BlockSpec((slots * rows, width), here),
                pl.BlockSpec((slots * rows, 2 * size), lambda i, where: (0, 0)),
                pl.BlockSpec((RADII, 4 * LANES, 2 * LANES), lambda i, where: (0, 0, 0)),
                pl.BlockSpec((2 * LANES, 2 * LANES), lambda i, where: (0, 0)),
            ],
            out_specs=pl.BlockSpec((slots * rows, width), lambda i, where: (0, 0)),
            scratch_shapes=[
                pltpu.VMEM((RADII, cell_rows, width // 2 + 2 * LANES), bf16),
                pltpu.VMEM((FINE, cell_rows, width // 2), bf16),
                pltpu.VMEM((cell_rows, 2 * LANES), f32),
                pltpu.VMEM((2 * size, width), bf16),
            ],
        ),
        out_shape=jax.ShapeDtypeStruct((slots * rows, width), bf16),
        compiler_params=pltpu.CompilerParams(vmem_limit_bytes=32 * 2**20),
        cost_estimate=pl.CostEstimate(
            flops=2 * 10**9, bytes_accessed=4 * 2**20, transcendentals=0
        ),
        name="residual",
    )(
        chunk, own, own, own, above, above, above, below, below, below, inverse, select, box, merge,
    )


def assemble_kernel(rows, select, share, *refs):
    pieces = len(refs) - 4
    parts, (prints, partial, flat, scaled) = refs[:pieces], refs[pieces:]
    size, width = parts[0].shape
    tall = CAMS * rows
    for place, part in enumerate(parts):
        edges = part[: 2 * rows, :].astype(f32) * share[place].reshape(2 * rows, width)
        scaled[place, : 2 * rows, :] = edges.astype(bf16)
    total = jnp.zeros((tall, 1), f32)
    for block in range(width // (2 * LANES)):
        cols = slice(block * 2 * LANES, (block + 1) * 2 * LANES)
        joined = jnp.zeros((tall, 2 * LANES), f32)
        for place, part in enumerate(parts):
            source = jnp.concatenate([scaled[place, :, cols], part[2 * rows :, cols]], axis=0)
            joined = joined + jnp.dot(
                select[place, :, :size], source, preferred_element_type=f32
            )
        prints[:, :, cols] = joined.reshape(CAMS, rows, 2 * LANES)
        flat[:, cols] = joined.astype(bf16)
        total = total + jnp.sum(joined, axis=1, keepdims=True)
    gram = lax.dot_general(
        flat[...], flat[...], (((1,), (1,)), ((), ())), preferred_element_type=f32
    )
    sub = lax.broadcasted_iota(jnp.int32, (tall, tall), 0)
    lane = lax.broadcasted_iota(jnp.int32, (tall, tall), 1)
    gram = jnp.where((sub & (rows - 1)) == (lane & (rows - 1)), gram, 0.0)
    gram = jnp.sum(gram.reshape(CAMS, rows, tall), axis=1)
    sub = lax.broadcasted_iota(jnp.int32, (tall, LANES), 0)
    lane = lax.broadcasted_iota(jnp.int32, (tall, LANES), 1)
    gather = jnp.where((sub >> log2(rows)) == lane, 1.0, 0.0).astype(f32)
    gram = jnp.dot(gram, gather, precision=lax.Precision.HIGHEST, preferred_element_type=f32)
    total = jnp.sum(total.reshape(CAMS, rows, 1), axis=1)
    lane = lax.broadcasted_iota(jnp.int32, (CAMS, LANES), 1)
    partial[...] = jnp.where(lane == CAMS, total, gram)


def assemble(select, share, parts, rows):
    width = parts[0].shape[1]
    return pl.pallas_call(
        functools.partial(assemble_kernel, rows),
        out_shape=[
            jax.ShapeDtypeStruct((CAMS, rows, width), f32),
            jax.ShapeDtypeStruct((CAMS, LANES), f32),
        ],
        scratch_shapes=[
            pltpu.VMEM((CAMS * rows, width), bf16),
            pltpu.VMEM((len(parts), 2 * rows, width), bf16),
        ],
        compiler_params=pltpu.CompilerParams(vmem_limit_bytes=32 * 2**20),
        cost_estimate=pl.CostEstimate(
            flops=2 * 10**9, bytes_accessed=4 * 2**20, transcendentals=0
        ),
        name="assemble",
    )(select, share, *parts)


def correlate_kernel(pixels, *refs):
    parts, out = refs[:-1], refs[-1]
    whole = parts[0][...]
    for part in parts[1:]:
        whole = whole + part[...]
    gram = whole[:, :CAMS]
    mean = whole[:, CAMS : CAMS + 1] / pixels
    sub = lax.broadcasted_iota(jnp.int32, (CAMS, CAMS), 0)
    lane = lax.broadcasted_iota(jnp.int32, (CAMS, CAMS), 1)
    diagonal = sub == lane
    mean_row = jnp.sum(jnp.where(diagonal, mean, 0.0), axis=0, keepdims=True)
    covar = gram / pixels - mean * mean_row
    only = jnp.where(diagonal, covar, 0.0)
    spread = jnp.sum(only, axis=1, keepdims=True) + var_eps
    spread_row = jnp.sum(only, axis=0, keepdims=True) + var_eps
    out[...] = covar / jnp.sqrt(spread * spread_row)


def correlate(parts, pixels):
    return pl.pallas_call(
        functools.partial(correlate_kernel, pixels),
        out_shape=jax.ShapeDtypeStruct((CAMS, CAMS), f32),
        name="correlate",
    )(*parts)


def exchange(array, axis, distance):
    size = lax.axis_size(axis)
    return lax.ppermute(array, axis, [(i, i ^ distance) for i in range(size)])


def gathered(array, axis):
    size = lax.axis_size(axis)
    return lax.all_to_all(
        jnp.broadcast_to(array, (size,) + array.shape), axis, split_axis=0, concat_axis=0
    )


def on_device(photos, camera_id):
    count, rows, width = photos.shape
    pieces, tiles = lax.axis_size("photo"), lax.axis_size("tile")
    me = lax.axis_index("photo").astype(jnp.int32)
    own, up, down = prepare(photos)
    above = lax.ppermute(down, "tile", [(i, i + 1) for i in range(tiles - 1)])
    below = lax.ppermute(up, "tile", [(i + 1, i) for i in range(tiles - 1)])
    inverse, select, box, merge, *extras = energies(
        me.reshape(1), camera_id, own, rows, pieces
    )
    extras = [
        exchange(extra, "photo", distance) if distance else extra
        for distance, extra in enumerate(extras)
    ]
    place, share, most = blend(me.reshape(1), extras, rows, count * rows)

    def finish(slots):
        parts = [None] * pieces
        for distance in reversed(range(pieces)):
            part = main_part(
                (me ^ distance).reshape(1), own, above, below, inverse, select, box, merge,
                rows, pieces, slots,
            )
            parts[distance] = exchange(part, "photo", distance) if distance else part
        return assemble(place, share, parts, rows)

    few = max(2, 3 * count // 4)
    prints, partial = lax.cond(
        most[0, 0] > few, lambda: finish(count), lambda: finish(few)
    )
    total = jnp.sum(gathered(partial, "photo"), axis=0)
    sums = gathered(total, "tile")
    return prints, correlate([sums[i] for i in range(tiles)], float(rows * tiles * width))


def solution(mesh):
    return jax.shard_map(
        on_device,
        mesh=mesh,
        in_specs=(P("photo", "tile", None), P("photo")),
        out_specs=(P(None, "tile", "photo"), P()),
        check_vma=False,
    )
```

time: 94.9 us -> 83.3 us (0.88)
  blocking collectives: 0 us -> 18.9 us
  waiting for transfers between devices: 33.2 us -> 14.4 us
  starting transfers between devices: 25.1 us -> 11.2 us
  Pallas kernels: 28.9 us -> 34.3 us
  local copies, waits for them, and re-layouts: 6.47 us -> 2.29 us
    all_to_all x0 -> x2, blocking collectives: none -> 18.9 us  [gathered(): lax.all_to_all(jnp.broadcast_to(array, (size,) + array.shape), axis, spli...]
    ppermute x2 -> x0, waiting for transfers between devices: 17.3 us -> none  [the longest x1 10.4 us: on_device(): lax.ppermute(first, 'photo', [(i + 1, i) for i in range(pieces - 1)])]
    ppermute x13 -> x6, starting transfers between devices: 15.9 us -> 7.52 us  [exchange(): return lax.ppermute(array, axis, [(i, i ^ distance) for i in range(size)])]
    pallas_call x1 -> x3, Pallas kernels: 4.71 us -> 12.5 us  [the longest x1 7.41 us: energies(): pl.pallas_call(functools.partial(energy_kernel, size // rows, rows), in_s...]
    ppermute x2 -> x0, starting transfers between devices: 5.54 us -> none  [the longest x1 4.25 us: on_device(): lax.ppermute(last, 'photo', [(i, i + 1) for i in range(pieces - 1)])]
    unnamed x32 -> x4, local copies, waits for them, and re-layouts: 6.47 us -> 1.59 us
    pallas_call x4, Pallas kernels: 19.8 us -> 17.7 us  [main_part(): pl.pallas_call(functools.partial(main_kernel, count, rows, blocks_all), g...]
    ppermute x13 -> x6, waiting for transfers between devices: 15.9 us -> 14.4 us  [exchange(): return lax.ppermute(array, axis, [(i, i ^ distance) for i in range(size)])]
  transfers between devices with their start and end apart: 17 -> 8, of which waited for: 9 -> 4; matrix products, arithmetic and copies ran while one was open for 0% -> 0% of each run, Pallas kernels for 16% -> 27%
where the time goes in v2:
time: 83.3 us; the launch traced here: 82.8 us
  Pallas kernels  34.3 us (41%)
  blocking collectives  18.9 us (23%)
  waiting for transfers between devices  14.4 us (17%)
  starting transfers between devices  11.2 us (13%)
  local copies, waits for them, and re-layouts  2.29 us (3%)
  between operations  1.36 us (2%)
    all_to_all x2, blocking collectives, gathered(): lax.all_to_all(jnp.broadcast_to(array, (size,) + array.shape), axis, spli...  18.9 us
    pallas_call x4, Pallas kernels, main_part(): pl.pallas_call(functools.partial(main_kernel, count, rows, blocks_all), g...  17.7 us
    ppermute x6, waiting for transfers between devices, exchange(): return lax.ppermute(array, axis, [(i, i ^ distance) for i in range(size)])  14.4 us
    ppermute x6, starting transfers between devices, exchange(): return lax.ppermute(array, axis, [(i, i ^ distance) for i in range(size)])  7.52 us
    pallas_call x1, Pallas kernels, energies(): pl.pallas_call(functools.partial(energy_kernel, size // rows, rows), in_s...  7.41 us
    pallas_call x1, Pallas kernels, prepare(): pl.pallas_call(prepare_kernel, in_specs=[pl.BlockSpec(memory_space=pltpu....  3.52 us
    pallas_call x1, Pallas kernels, assemble(): pl.pallas_call(functools.partial(assemble_kernel, rows), out_shape=[jax.S...  2.57 us
    ppermute x1, starting transfers between devices, on_device(): above = lax.ppermute(down, 'tile', [(i, i + 1) for i in range(tiles - 1)])  2.41 us
  transfers between devices with their start and end apart: 8, of which 4 were waited for; matrix products, arithmetic and copies ran while one was open for 0% of the time, Pallas kernels for 27%

profile of v2, /device:TPU:0, one launch (start us, length us, event | category | flops | bytes accessed | tf_op | source)
XLA Modules:
  0.0 82.8 jit_solution(4539545490286385251)
XLA Ops:
  0.6 0.0 copy-start
  0.6 1.6 %copy-done = bf16[16,16,4096]{2,1,0:T(8,128)(2,1)S(1)} copy-done((bf16[16,16,4096]{2,1,0:T(8,128)(2,1)S(1)}, bf16[16,16,4096]{2,1,0:T(8,128)(2,1)}, u32[]{:S(2)}) %copy-start) | copy-done | bytes 2097176
  2.2 3.5 %prepare.1 = (bf16[256,4096]{1,0:T(8,128)(2,1)}, bf16[192,2048]{1,0:T(8,128)(2,1)S(1)}, bf16[192,2048]{1,0:T(8,128)(2,1)S(1)}) custom-call(bf16[16,16,4096]{2,1,0:T(8,128)(2,1)S(1)} %copy-done), custom_call_target="tpu_custom_call" | custom-call | flops 1000000000 | bytes 8388608 | tf_op jit(solution)/shard_map/prepare/pallas_call | solution.py:117
  5.8 2.4 %collective-permute-start.9 = (bf16[192,2048]{1,0:T(8,128)(2,1)S(1)}, bf16[192,2048]{1,0:T(8,128)(2,1)S(1)}, u32[]{:S(2)}, u32[]{:S(2)}) collective-permute-start(bf16[192,2048]{1,0:T(8,128)(2,1)S(1)} %get-tuple-element.84), channel_id=1, source_target_pairs={{0,1},{1,2},{2,3},{3,4},{4,5},{5,6},{6,7},{8,9},{9,10},{10,11},{11... | collective-permute-start | bytes 2359304 | tf_op jit(solution)/shard_map/ppermute | solution.py:515
  8.2 1.3 %collective-permute-start.10 = (bf16[192,2048]{1,0:T(8,128)(2,1)S(1)}, bf16[192,2048]{1,0:T(8,128)(2,1)}, u32[]{:S(2)}, u32[]{:S(2)}) collective-permute-start(bf16[192,2048]{1,0:T(8,128)(2,1)S(1)} %get-tuple-element.85), channel_id=1, source_target_pairs={{1,0},{2,1},{3,2},{4,3},{5,4},{6,5},{7,6},{9,8},{10,9},{11,10},{12... | collective-permute-start | bytes 2359304 | tf_op jit(solution)/shard_map/ppermute | solution.py:516
  9.5 7.4 %energies.1 = (f32[256,4096]{1,0:T(8,128)}, bf16[256,512]{1,0:T(8,128)(2,1)}, bf16[4,512,256]{2,1,0:T(8,128)(2,1)S(1)}, bf16[256,256]{1,0:T(8,128)(2,1)S(1)}, bf...) custom-call(s32[1]{0:T(128)} %bitcast.8.me, ...), custom_call_target="tpu_custom_call" | custom-call | flops 1000000000 | bytes 8388608 | tf_op jit(solution)/shard_map/energies/pallas_call | solution.py:186
  16.9 2.3 %collective-permute-start.6 = (bf16[48,1024]{1,0:T(8,128)(2,1)S(1)}, bf16[48,1024]{1,0:T(8,128)(2,1)S(1)}, u32[]{:S(2)}, u32[]{:S(2)}) collective-permute-start(bf16[48,1024]{1,0:T(8,128)(2,1)S(1)} %get-tuple-element.80), channel_id=1, source_target_pairs={{0,8},{8,0},{16,24},{24,16},{1,9},{9,1},{17,25},{25,17},{2,10},{10... | collective-permute-start | bytes 294920 | tf_op jit(solution)/shard_map/ppermute | solution.py:500
  19.2 1.5 %collective-permute-start.7 = (bf16[48,1024]{1,0:T(8,128)(2,1)S(1)}, bf16[48,1024]{1,0:T(8,128)(2,1)S(1)}, u32[]{:S(2)}, u32[]{:S(2)}) collective-permute-start(bf16[48,1024]{1,0:T(8,128)(2,1)S(1)} %get-tuple-element.81), channel_id=1, source_target_pairs={{0,16},{8,24},{16,0},{24,8},{1,17},{9,25},{17,1},{25,9},{2,18},{10... | collective-permute-start | bytes 294920 | tf_op jit(solution)/shard_map/ppermute | solution.py:500
  20.7 0.0 collective-permute-start.8
  20.7 1.1 %collective-permute-done.6.refs_1_ = bf16[48,1024]{1,0:T(8,128)(2,1)S(1)} collective-permute-done((bf16[48,1024]{1,0:T(8,128)(2,1)S(1)}, bf16[48,1024]{1,0:T(8,128)(2,1)S(1)}, u32[]{:S(2)}, u32[]{:S(2)}) %collective-permute-start.6) | collective-permute-done | bytes 98336 | tf_op jit(solution)/shard_map/ppermute | solution.py:500
  21.8 2.0 %collective-permute-done.7.refs_2_ = bf16[48,1024]{1,0:T(8,128)(2,1)S(1)} collective-permute-done((bf16[48,1024]{1,0:T(8,128)(2,1)S(1)}, bf16[48,1024]{1,0:T(8,128)(2,1)S(1)}, u32[]{:S(2)}, u32[]{:S(2)}) %collective-permute-start.7) | collective-permute-done | bytes 98336 | tf_op jit(solution)/shard_map/ppermute | solution.py:500
  23.8 2.6 %collective-permute-done.8.refs_3_ = bf16[48,1024]{1,0:T(8,128)(2,1)S(1)} collective-permute-done((bf16[48,1024]{1,0:T(8,128)(2,1)S(1)}, bf16[48,1024]{1,0:T(8,128)(2,1)S(1)}, u32[]{:S(2)}, u32[]{:S(2)}) %collective-permute-start.8) | collective-permute-done | bytes 98336 | tf_op jit(solution)/shard_map/ppermute | solution.py:500
  26.4 1.5 %blend.1 = (bf16[4,512,256]{2,1,0:T(8,128)(2,1)}, f32[4,2,16,1024]{3,2,1,0:T(8,128)}, s32[1,1]{1,0:T(1,128)}) custom-call(s32[1]{0:T(128)} %bitcast.8.me, bf16[48,1024]{1,0:T(8,128)(2,1)S(1)} %get-tuple-element.79.refs_0_, bf16[48,1024]{1,0:T(8,128)(2,1)S(1)} %collective-permute-done.6.refs_1_, bf16[48,1024]{1,0:T(8,128)(2,1)S(1)} %collective-permute-done.7.refs_2_, ...), custom_call_target="tpu_custom_call" | custom-call | tf_op jit(solution)/shard_map/blend/pallas_call | solution.py:237
  28.6 0.0 collective-permute-done.9
  28.6 0.0 collective-permute-done.10
  28.6 33.0 %conditional.1 = ((f32[32,16,1024]{2,1,0:T(8,128)}, f32[32,128]{1,0:T(8,128)S(1)})) conditional(s32[]{:T(128)} %bitcast.9, (s32[]{:T(128)}, bf16[256,4096]{1,0:T(8,128)(2,1)}, bf16[192,2048]{1,0:T(8,128)(2,1)S(1)}, bf16[192,2048]{1,0:T(8,128)(2,1)}, f32[256,4096]{1,0:T(8,128)}, /*index=5*/bf16[256,512]{1,0:T(8,128)(2,1)}, ...), branch_computations={%region_0.0_spmd, %region_1.0_spmd} | conditional | flops 10000000000 | bytes 68157800 | solution.py:537
  28.8 4.6 %residual.9 = bf16[192,1024]{1,0:T(8,128)(2,1)S(1)} custom-call(s32[1]{0:T(128)} %bitcast.1.where, bf16[256,4096]{1,0:T(8,128)(2,1)} %get-tuple-element.43.own.own_l.own_r, bf16[256,4096]{1,0:T(8,128)(2,1)} %get-tuple-element.43.own.own_l.own_r, bf16[256,4096]{1,0:T(8,128)(2,1)} %get-tuple-element.43.own.own_l.own_r, ...), custom_call_target="tpu_custom_call" | custom-call | flops 2000000000 | bytes 4194304 | tf_op jit(solution)/shard_map/cond/branch_0_fun/residual/pallas_call | solution.py:381
  33.4 1.4 %collective-permute-start = (bf16[192,1024]{1,0:T(8,128)(2,1)S(1)}, bf16[192,1024]{1,0:T(8,128)(2,1)S(1)}, u32[]{:S(2)}, u32[]{:S(2)}) collective-permute-start(bf16[192,1024]{1,0:T(8,128)(2,1)S(1)} %residual.9), channel_id=1, source_target_pairs={{0,8},{8,0},{16,24},{24,16},{1,9},{9,1},{17,25},{25,17},{2,10},{10... | collective-permute-start | bytes 1179656 | tf_op jit(solution)/shard_map/cond/branch_0_fun/ppermute | solution.py:500
  34.8 0.0 copy-done.8
  34.8 4.5 %residual.10 = bf16[192,1024]{1,0:T(8,128)(2,1)S(1)} custom-call(s32[1]{0:T(128)} %bitcast.2.where, bf16[256,4096]{1,0:T(8,128)(2,1)} %get-tuple-element.43.own.own_l.own_r, bf16[256,4096]{1,0:T(8,128)(2,1)} %get-tuple-element.43.own.own_l.own_r, bf16[256,4096]{1,0:T(8,128)(2,1)} %get-tuple-element.43.own.own_l.own_r, ...), custom_call_target="tpu_custom_call" | custom-call | flops 2000000000 | bytes 4194304 | tf_op jit(solution)/shard_map/cond/branch_0_fun/residual/pallas_call | solution.py:381
  39.3 0.3 collective-permute-start.1
  39.6 4.7 %residual.11 = bf16[192,1024]{1,0:T(8,128)(2,1)S(1)} custom-call(s32[1]{0:T(128)} %bitcast.3.where, bf16[256,4096]{1,0:T(8,128)(2,1)} %get-tuple-element.43.own.own_l.own_r, bf16[256,4096]{1,0:T(8,128)(2,1)} %get-tuple-element.43.own.own_l.own_r, bf16[256,4096]{1,0:T(8,128)(2,1)} %get-tuple-element.43.own.own_l.own_r, ...), custom_call_target="tpu_custom_call" | custom-call | flops 2000000000 | bytes 4194304 | tf_op jit(solution)/shard_map/cond/branch_0_fun/residual/pallas_call | solution.py:381
  44.3 2.0 %collective-permute-start.2 = (bf16[192,1024]{1,0:T(8,128)(2,1)S(1)}, bf16[192,1024]{1,0:T(8,128)(2,1)S(1)}, u32[]{:S(2)}, u32[]{:S(2)}) collective-permute-start(bf16[192,1024]{1,0:T(8,128)(2,1)S(1)} %residual.11), channel_id=1, source_target_pairs={{0,24},{8,16},{16,8},{24,0},{1,25},{9,17},{17,9},{25,1},{2,26},{10... | collective-permute-start | bytes 1179656 | tf_op jit(solution)/shard_map/cond/branch_0_fun/ppermute | solution.py:500
  46.3 4.0 %residual.8.refs_0_ = bf16[192,1024]{1,0:T(8,128)(2,1)S(1)} custom-call(s32[1]{0:T(128)} %bitcast.where, bf16[256,4096]{1,0:T(8,128)(2,1)S(1)} %copy-done.2, bf16[256,4096]{1,0:T(8,128)(2,1)S(1)} %copy-done.2, bf16[256,4096]{1,0:T(8,128)(2,1)S(1)} %copy-done.2, bf16[192,2048]{1,0:T(8,128)(2,1)S(1)} %get-tuple-element.44.above.above_l.above_r, ...), custom_call_target="tpu_custom_call" | custom-call | flops 2000000000 | bytes 4194304 | tf_op jit(solution)/shard_map/cond/branch_0_fun/residual/pallas_call | solution.py:381
  50.2 0.0 collective-permute-done.refs_1_
  50.3 8.7 %collective-permute-done.1.refs_2_ = bf16[192,1024]{1,0:T(8,128)(2,1)S(1)} collective-permute-done((bf16[192,1024]{1,0:T(8,128)(2,1)S(1)}, bf16[192,1024]{1,0:T(8,128)(2,1)S(1)}, u32[]{:S(2)}, u32[]{:S(2)}) %collective-permute-start.1) | collective-permute-done | bytes 393248 | tf_op jit(solution)/shard_map/cond/branch_0_fun/ppermute | solution.py:500
  59.0 0.0 collective-permute-done.2.refs_3_
  59.0 2.6 %assemble.2 = (f32[32,16,1024]{2,1,0:T(8,128)}, f32[32,128]{1,0:T(8,128)S(1)}) custom-call(bf16[4,512,256]{2,1,0:T(8,128)(2,1)S(1)} %copy-done.11, f32[4,2,16,1024]{3,2,1,0:T(8,128)S(1)} %copy-done.13, bf16[192,1024]{1,0:T(8,128)(2,1)S(1)} %residual.8.refs_0_, bf16[192,1024]{1,0:T(8,128)(2,1)S(1)} %collective-permute-done.refs_1_, ...), custom_call_target="tpu_custom_call" | custom-call | flops 2000000000 | bytes 4194304 | tf_op jit(solution)/shard_map/cond/branch_0_fun/assemble/pallas_call | solution.py:454
  61.6 7.2 %all_to_all.10 = f32[4,32,128]{2,1,0:T(8,128)S(1)} all-to-all(f32[4,32,128]{2,1,0:T(8,128)S(1)} %broadcast_in_dim.6), channel_id=1, replica_groups=mesh['photo'=4,'tile'=8] {'photo'}, dimensions={0} | all-to-all | bytes 131072 | tf_op jit(solution)/shard_map/all_to_all | solution.py:505
  68.8 11.7 %all_to_all.11 = f32[8,32,128]{2,1,0:T(8,128)S(1)} all-to-all(f32[8,32,128]{2,1,0:T(8,128)S(1)} %broadcast_in_dim.7), channel_id=1, replica_groups=mesh['photo'=4,'tile'=8] {'tile'}, dimensions={0} | all-to-all | bytes 262144 | tf_op jit(solution)/shard_map/all_to_all | solution.py:505
  80.6 0.7 slice_bitcast_fusion
  81.2 1.6 %correlate.1 = f32[32,32]{1,0:T(8,128)} custom-call(f32[32,128]{1,0:T(8,128)} %get-tuple-element.101.refs_0_, f32[32,128]{1,0:T(8,128)} %get-tuple-element.100.refs_1_, f32[32,128]{1,0:T(8,128)} %get-tuple-element.99.refs_2_, f32[32,128]{1,0:T(8,128)} %get-tuple-element.98.refs_3_, f32[32,128]{1,0:T(8,128)} %get-tuple-element.97.refs_4_, ...), custom_call_target="tpu_custom_call" | custom-call | tf_op jit(solution)/shard_map/correlate/pallas_call | solution.py:491
  (16 shorter events, 0.0 us)
Async XLA Ops:
  0.6 1.6 %copy-start = (bf16[16,16,4096]{2,1,0:T(8,128)(2,1)S(1)}, bf16[16,16,4096]{2,1,0:T(8,128)(2,1)}, u32[]{:S(2)}) copy-start(bf16[16,16,4096]{2,1,0:T(8,128)(2,1)} %photos.1) | copy-start | bytes 6291460
  2.2 7.3 %copy-start.1 = (s32[16]{0:T(128)S(1)}, s32[16]{0:T(128)}, u32[]{:S(2)}) copy-start(s32[16]{0:T(128)} %ids.1) | copy-start | bytes 196
  5.8 22.8 %collective-permute-start.9 = (bf16[192,2048]{1,0:T(8,128)(2,1)S(1)}, bf16[192,2048]{1,0:T(8,128)(2,1)S(1)}, u32[]{:S(2)}, u32[]{:S(2)}) collective-permute-start(bf16[192,2048]{1,0:T(8,128)(2,1)S(1)} %get-tuple-element.84), channel_id=1, source_target_pairs={{0,1},{1,2},{2,3},{3,4},{4,5},{5,6},{6,7},{8,9},{9,10},{10,11},{11... | collective-permute-start | bytes 2359304 | tf_op jit(solution)/shard_map/ppermute | solution.py:515
  8.2 20.4 %collective-permute-start.10 = (bf16[192,2048]{1,0:T(8,128)(2,1)S(1)}, bf16[192,2048]{1,0:T(8,128)(2,1)}, u32[]{:S(2)}, u32[]{:S(2)}) collective-permute-start(bf16[192,2048]{1,0:T(8,128)(2,1)S(1)} %get-tuple-element.85), channel_id=1, source_target_pairs={{1,0},{2,1},{3,2},{4,3},{5,4},{6,5},{7,6},{9,8},{10,9},{11,10},{12... | collective-permute-start | bytes 2359304 | tf_op jit(solution)/shard_map/ppermute | solution.py:516
  16.9 4.9 %collective-permute-start.6 = (bf16[48,1024]{1,0:T(8,128)(2,1)S(1)}, bf16[48,1024]{1,0:T(8,128)(2,1)S(1)}, u32[]{:S(2)}, u32[]{:S(2)}) collective-permute-start(bf16[48,1024]{1,0:T(8,128)(2,1)S(1)} %get-tuple-element.80), channel_id=1, source_target_pairs={{0,8},{8,0},{16,24},{24,16},{1,9},{9,1},{17,25},{25,17},{2,10},{10... | collective-permute-start | bytes 294920 | tf_op jit(solution)/shard_map/ppermute | solution.py:500
  19.2 4.6 %collective-permute-start.7 = (bf16[48,1024]{1,0:T(8,128)(2,1)S(1)}, bf16[48,1024]{1,0:T(8,128)(2,1)S(1)}, u32[]{:S(2)}, u32[]{:S(2)}) collective-permute-start(bf16[48,1024]{1,0:T(8,128)(2,1)S(1)} %get-tuple-element.81), channel_id=1, source_target_pairs={{0,16},{8,24},{16,0},{24,8},{1,17},{9,25},{17,1},{25,9},{2,18},{10... | collective-permute-start | bytes 294920 | tf_op jit(solution)/shard_map/ppermute | solution.py:500
  20.7 5.7 %collective-permute-start.8 = (bf16[48,1024]{1,0:T(8,128)(2,1)S(1)}, bf16[48,1024]{1,0:T(8,128)(2,1)S(1)}, u32[]{:S(2)}, u32[]{:S(2)}) collective-permute-start(bf16[48,1024]{1,0:T(8,128)(2,1)S(1)} %get-tuple-element.82), channel_id=1, source_target_pairs={{0,24},{8,16},{16,8},{24,0},{1,25},{9,17},{17,9},{25,1},{2,26},{10... | collective-permute-start | bytes 294920 | tf_op jit(solution)/shard_map/ppermute | solution.py:500
  28.8 6.0 %copy-start.8 = (bf16[256,512]{1,0:T(8,128)(2,1)S(1)}, bf16[256,512]{1,0:T(8,128)(2,1)}, u32[]{:S(2)}) copy-start(bf16[256,512]{1,0:T(8,128)(2,1)} %get-tuple-element.47.select) | copy-start | bytes 786436 | tf_op jit(solution)/shard_map/cond
  33.4 16.9 %collective-permute-start = (bf16[192,1024]{1,0:T(8,128)(2,1)S(1)}, bf16[192,1024]{1,0:T(8,128)(2,1)S(1)}, u32[]{:S(2)}, u32[]{:S(2)}) collective-permute-start(bf16[192,1024]{1,0:T(8,128)(2,1)S(1)} %residual.9), channel_id=1, source_target_pairs={{0,8},{8,0},{16,24},{24,16},{1,9},{9,1},{17,25},{25,17},{2,10},{10... | collective-permute-start | bytes 1179656 | tf_op jit(solution)/shard_map/cond/branch_0_fun/ppermute | solution.py:500
  39.3 19.7 %collective-permute-start.1 = (bf16[192,1024]{1,0:T(8,128)(2,1)S(1)}, bf16[192,1024]{1,0:T(8,128)(2,1)S(1)}, u32[]{:S(2)}, u32[]{:S(2)}) collective-permute-start(bf16[192,1024]{1,0:T(8,128)(2,1)S(1)} %residual.10), channel_id=1, source_target_pairs={{0,16},{8,24},{16,0},{24,8},{1,17},{9,25},{17,1},{25,9},{2,18},{10... | collective-permute-start | bytes 1179656 | tf_op jit(solution)/shard_map/cond/branch_0_fun/ppermute | solution.py:500
  39.6 6.7 %copy-start.2 = (bf16[256,4096]{1,0:T(8,128)(2,1)S(1)}, bf16[256,4096]{1,0:T(8,128)(2,1)}, u32[]{:S(2)}) copy-start(bf16[256,4096]{1,0:T(8,128)(2,1)} %get-tuple-element.43.own.own_l.own_r) | copy-start | bytes 6291460 | tf_op jit(solution)/shard_map/cond
  39.6 6.7 %copy-start.4 = (f32[256,4096]{1,0:T(8,128)S(1)}, f32[256,4096]{1,0:T(8,128)}, u32[]{:S(2)}) copy-start(f32[256,4096]{1,0:T(8,128)} %get-tuple-element.46.inverse) | copy-start | bytes 12582916 | tf_op jit(solution)/shard_map/cond
  39.6 6.7 %copy-start.9 = (bf16[256,512]{1,0:T(8,128)(2,1)S(1)}, bf16[256,512]{1,0:T(8,128)(2,1)}, u32[]{:S(2)}) copy-start(bf16[256,512]{1,0:T(8,128)(2,1)} %get-tuple-element.47.select) | copy-start | bytes 786436 | tf_op jit(solution)/shard_map/cond
  44.3 14.7 %collective-permute-start.2 = (bf16[192,1024]{1,0:T(8,128)(2,1)S(1)}, bf16[192,1024]{1,0:T(8,128)(2,1)S(1)}, u32[]{:S(2)}, u32[]{:S(2)}) collective-permute-start(bf16[192,1024]{1,0:T(8,128)(2,1)S(1)} %residual.11), channel_id=1, source_target_pairs={{0,24},{8,16},{16,8},{24,0},{1,25},{9,17},{17,9},{25,1},{2,26},{10... | collective-permute-start | bytes 1179656 | tf_op jit(solution)/shard_map/cond/branch_0_fun/ppermute | solution.py:500
  46.3 12.7 %copy-start.11 = (bf16[4,512,256]{2,1,0:T(8,128)(2,1)S(1)}, bf16[4,512,256]{2,1,0:T(8,128)(2,1)}, u32[]{:S(2)}) copy-start(bf16[4,512,256]{2,1,0:T(8,128)(2,1)} %get-tuple-element.40.select) | copy-start | bytes 3145732 | tf_op jit(solution)/shard_map/cond
  46.3 12.7 %copy-start.13 = (f32[4,2,16,1024]{3,2,1,0:T(8,128)S(1)}, f32[4,2,16,1024]{3,2,1,0:T(8,128)}, u32[]{:S(2)}) copy-start(f32[4,2,16,1024]{3,2,1,0:T(8,128)} %get-tuple-element.41.share) | copy-start | bytes 1572868 | tf_op jit(solution)/shard_map/cond

commit v3 on v2

--- a/solution.py
+++ b/solution.py
@@ -68,29 +68,56 @@
     return upper, lower
 
 
-def prepare_kernel(photos, sorted_out, up_out, down_out, buffer, arrived):
+def slot_numbers(ids, count):
+    ranks = [jnp.int32(0)]
+    for photo in range(1, count):
+        ranks.append(ranks[-1] + jnp.where(ids[photo] != ids[photo - 1], 1, 0))
+    last = ranks[-1]
+    slots = [jnp.where(rank == 0, 0, jnp.where(rank == last, 1, rank + 1)) for rank in ranks]
+    return slots, last + 1
+
+
+def prepare_kernel(me, ids, photos, sorted_out, up_out, down_out, *refs):
+    extras, (buffer, arrived) = refs[:-2], refs[-2:]
     count, rows, width = photos.shape
     cells = rows // 2
-    step = width // arrived.shape[0]
+    pieces = len(extras)
+    step = width // pieces
+    bases = [pl.multiple_of((me[0] ^ distance) * step, step) for distance in range(pieces)]
     copies = []
-    for part in range(width // step):
-        cols = pl.ds(part * step, step)
+    for distance in range(pieces):
+        cols = pl.ds(bases[distance], step)
         copies.append(
-            pltpu.make_async_copy(photos.at[:, :, cols], buffer.at[:, :, cols], arrived.at[part])
+            pltpu.make_async_copy(
+                photos.at[:, :, cols], buffer.at[distance], arrived.at[distance]
+            )
         )
         copies[-1].start()
     perm = row_permutation(count, rows)
     split = column_split()
-    for part in range(width // step):
-        copies[part].wait()
-        flat = buffer[:, :, part * step : (part + 1) * step].reshape(count * rows, step)
+
+    slots, cameras = slot_numbers(ids, count)
+    sub, lane = iotas((rows, step))
+    slot_id = jnp.full((rows, step), -1, jnp.int32)
+    in_first, in_last = jnp.int32(0), jnp.int32(0)
+    for photo in range(count):
+        slot_id = jnp.where((lane >> log2(rows)) == slots[photo], ids[photo], slot_id)
+        in_first = in_first + jnp.where(ids[photo] == ids[0], 1, 0)
+        in_last = in_last + jnp.where(ids[photo] == ids[count - 1], 1, 0)
+    notes = jnp.where(sub == 0, ids[0], jnp.where(sub == 1, ids[count - 1], slot_id))
+    notes = jnp.where(sub == 3, cameras, notes).astype(f32).astype(bf16)
+
+    for distance in range(pieces):
+        copies[distance].wait()
+        flat = buffer[distance].reshape(count * rows, step)
         by_row = jnp.dot(perm, flat, preferred_element_type=f32).astype(bf16)
         for inner in range(step // (2 * LANES)):
-            block = part * (step // (2 * LANES)) + inner
-            cols = slice(block * 2 * LANES, (block + 1) * 2 * LANES)
-            cell_cols = slice(block * LANES, (block + 1) * LANES)
-            pixels = by_row[:, inner * 2 * LANES : (inner + 1) * 2 * LANES]
-            parted = jnp.dot(pixels, split, preferred_element_type=f32)
+            at = inner * 2 * LANES
+            cols = pl.ds(pl.multiple_of(bases[distance] + at, 2 * LANES), 2 * LANES)
+            cell_cols = pl.ds(
+                pl.multiple_of((me[0] ^ distance) * (step // 2) + at // 2, LANES), LANES
+            )
+            parted = jnp.dot(by_row[:, at : at + 2 * LANES], split, preferred_element_type=f32)
             sorted_out[:, cols] = parted.astype(bf16)
             for i in range(cells):
                 if RADII <= i < cells - RADII:
@@ -107,41 +134,47 @@
                         start = (band * RADII + i - (cells - RADII)) * count
                         down_out[start : start + count, cell_cols] = square
 
-
-def prepare(photos):
+        def add(photo, total):
+            pixel = buffer[distance, photo].astype(f32)
+            return total + pixel * pixel
+
+        none = jnp.zeros((rows, step), f32)
+        extra = extras[distance]
+        extra[:rows, :] = lax.fori_loop(0, in_first, add, none).astype(bf16)
+        extra[rows : 2 * rows, :] = lax.fori_loop(count - in_last, count, add, none).astype(bf16)
+        extra[2 * rows :, :] = notes
+
+
+def prepare(me, ids, photos, pieces):
     count, rows, width = photos.shape
-    step = min(width, 1024)
+    step = width // pieces
     size = count * rows
     halo = 3 * RADII * count
     vmem = pl.BlockSpec(memory_space=pltpu.VMEM)
+    smem = pl.BlockSpec(memory_space=pltpu.SMEM)
     return pl.pallas_call(
         prepare_kernel,
-        in_specs=[pl.BlockSpec(memory_space=pltpu.HBM)],
-        out_specs=[vmem] * 3,
+        in_specs=[smem, smem, pl.BlockSpec(memory_space=pltpu.HBM)],
+        out_specs=[vmem] * (3 + pieces),
         out_shape=[
             jax.ShapeDtypeStruct((size, width), bf16),
             jax.ShapeDtypeStruct((halo, width // 2), bf16),
             jax.ShapeDtypeStruct((halo, width // 2), bf16),
+        ]
+        + [jax.ShapeDtypeStruct((3 * rows, step), bf16)] * pieces,
+        scratch_shapes=[
+            pltpu.VMEM((pieces, count, rows, step), bf16),
+            pltpu.SemaphoreType.DMA((pieces,)),
         ],
-        scratch_shapes=[
-            pltpu.VMEM((count, rows, width), bf16),
-            pltpu.SemaphoreType.DMA((width // step,)),
-        ],
-        compiler_params=pltpu.CompilerParams(vmem_limit_bytes=24 * 2**20),
+        compiler_params=pltpu.CompilerParams(vmem_limit_bytes=20 * 2**20),
         cost_estimate=pl.CostEstimate(flops=10**9, bytes_accessed=8 * 2**20, transcendentals=0),
         name="prepare",
-    )(photos)
-
-
-def energy_kernel(count, rows, me, ids, own, inverse, select_out, box_out, merge_out, *extras):
-    size, width_all = own.shape
-    width = width_all // len(extras)
-    ranks = [jnp.int32(0)]
-    for photo in range(1, count):
-        ranks.append(ranks[-1] + jnp.where(ids[photo] != ids[photo - 1], 1, 0))
-    last = ranks[-1]
-    slots = [jnp.where(rank == 0, 0, jnp.where(rank == last, 1, rank + 1)) for rank in ranks]
-
+    )(me, ids, photos)
+
+
+def energy_kernel(count, rows, ids, own, inverse, select_out, box_out, merge_out):
+    size, width = own.shape
+    slots, _ = slot_numbers(ids, count)
     sub, lane = iotas((size, size))
     lane_photo = lane & (count - 1)
     lane_slot = jnp.zeros_like(lane)
@@ -154,54 +187,37 @@
     select_out[...] = select
     for radius in range(1, RADII + 1):
         box_out[radius - 1] = box_matrix(radius)
-    merge = column_merge()
-    merge_out[...] = merge
-
-    sub, lane = iotas((rows, width))
-    slot_id = jnp.full((rows, width), -1, jnp.int32)
-    for photo in range(count):
-        slot_id = jnp.where((lane >> log2(rows)) == slots[photo], ids[photo], slot_id)
-    notes = jnp.where(sub == 0, ids[0], jnp.where(sub == 1, ids[count - 1], slot_id))
-    notes = jnp.where(sub == 3, last + 1, notes).astype(f32).astype(bf16)
-
-    for distance, extra in enumerate(extras):
-        base = (me[0] ^ distance) * width
-        extra[2 * rows :, :] = notes
-        for block in range(width // (2 * LANES)):
-            cols = pl.ds(pl.multiple_of(base + block * 2 * LANES, 2 * LANES), 2 * LANES)
-            pixel = own[:, cols].astype(f32)
-            pair = jnp.concatenate(halves(pixel * pixel), axis=0)
-            energy = jnp.dot(select, pair, preferred_element_type=f32)
-            inverse[:, cols] = 1.0 / jnp.maximum(energy, 2.0**-20)
-            edges = jnp.dot(
-                energy[: 2 * rows].astype(bf16), merge, preferred_element_type=f32
-            )
-            extra[: 2 * rows, block * 2 * LANES : (block + 1) * 2 * LANES] = edges.astype(bf16)
-
-
-def energies(me, ids, own, rows, pieces):
+    merge_out[...] = column_merge()
+    for block in range(width // (2 * LANES)):
+        cols = slice(block * 2 * LANES, (block + 1) * 2 * LANES)
+        pixel = own[:, cols].astype(f32)
+        pair = jnp.concatenate(halves(pixel * pixel), axis=0)
+        energy = jnp.dot(select, pair, preferred_element_type=f32)
+        inverse[:, cols] = 1.0 / jnp.maximum(energy, 2.0**-20)
+
+
+def energies(ids, own, rows):
     size, width = own.shape
     vmem = pl.BlockSpec(memory_space=pltpu.VMEM)
     smem = pl.BlockSpec(memory_space=pltpu.SMEM)
     return pl.pallas_call(
         functools.partial(energy_kernel, size // rows, rows),
-        in_specs=[smem, smem, vmem],
-        out_specs=[vmem] * (4 + pieces),
+        in_specs=[smem, vmem],
+        out_specs=[vmem] * 4,
         out_shape=[
             jax.ShapeDtypeStruct((size, width), f32),
             jax.ShapeDtypeStruct((size, 2 * size), bf16),
             jax.ShapeDtypeStruct((RADII, 4 * LANES, 2 * LANES), bf16),
             jax.ShapeDtypeStruct((2 * LANES, 2 * LANES), bf16),
-        ]
-        + [jax.ShapeDtypeStruct((3 * rows, width // pieces), bf16)] * pieces,
-        compiler_params=pltpu.CompilerParams(vmem_limit_bytes=24 * 2**20),
+        ],
+        compiler_params=pltpu.CompilerParams(vmem_limit_bytes=20 * 2**20),
         cost_estimate=pl.CostEstimate(flops=10**9, bytes_accessed=8 * 2**20, transcendentals=0),
         name="energies",
-    )(me, ids, own)
+    )(ids, own)
 
 
 def blend_kernel(rows, me, *refs):
-    pieces = (len(refs) - 4) // 1
+    pieces = len(refs) - 4
     extras, (select, share, most, held) = refs[:pieces], refs[pieces:]
     size = select.shape[2]
     tall = CAMS * rows
@@ -244,60 +260,58 @@
             jax.ShapeDtypeStruct((1, 1), jnp.int32),
         ],
         scratch_shapes=[pltpu.VMEM((pieces, 3 * rows, width), f32)],
-        compiler_params=pltpu.CompilerParams(vmem_limit_bytes=24 * 2**20),
+        compiler_params=pltpu.CompilerParams(vmem_limit_bytes=20 * 2**20),
         name="blend",
     )(me, *extras)
 
 
 def main_kernel(
-    count, rows, blocks_all,
-    where,
-    own, own_l, own_r, above, above_l, above_r, below, below_l, below_r,
-    inverse, select, box, merge,
-    out,
+    count, rows, width, where, own, above, below, inverse, select, box, merge, out,
     sums, rest, least, product,
 ):
     cells = rows // 2
     size = count * rows
-    width = own.shape[1]
+    width_all = own.shape[1]
     blocks = width // (2 * LANES)
-    chunk = where[0]
-    left_ok = jnp.where(chunk > 0, 1.0, 0.0).astype(f32)
-    right_ok = jnp.where((chunk + 1) * blocks < blocks_all, 1.0, 0.0).astype(f32)
+    slot_rows = out.shape[0]
+    base = where[0] * width
+    left_ok = jnp.where(base > 0, 1.0, 0.0).astype(f32)
+    right_ok = jnp.where(base + width < width_all, 1.0, 0.0).astype(f32)
+
+    def pixels_of(i, start):
+        top = slice(2 * i * count, (2 * i + 1) * count)
+        low = slice((2 * i + 1) * count, (2 * i + 2) * count)
+        even = pl.ds(pl.multiple_of(start, 2 * LANES), LANES)
+        odd = pl.ds(pl.multiple_of(start + LANES, LANES), LANES)
+        return tuple(
+            own[at, cols].astype(f32)
+            for at, cols in ((top, even), (top, odd), (low, even), (low, odd))
+        )
 
     for block in range(-1, blocks + 1):
+        start = base + block * 2 * LANES
+        factor = None
         if block < 0:
-            mine, over, under, factor, at = own_l, above_l, below_l, left_ok, 0
+            start, factor = jnp.maximum(start, 0), left_ok
         elif block == blocks:
-            mine, over, under, factor, at = own_r, above_r, below_r, right_ok, 0
-        else:
-            mine, over, under, factor, at = own, above, below, None, block
-        even = slice(2 * at * LANES, (2 * at + 1) * LANES)
-        odd = slice((2 * at + 1) * LANES, (2 * at + 2) * LANES)
-        cols = slice(at * LANES, (at + 1) * LANES)
+            start, factor = jnp.minimum(start, width_all - 2 * LANES), right_ok
         place = slice((block + 1) * LANES, (block + 2) * LANES)
+        cols = slice(block * LANES, (block + 1) * LANES)
+        cell_cols = pl.ds(pl.multiple_of(lax.shift_right_arithmetic(start, 1), LANES), LANES)
         squares = [[], [], []]
         for i in range(cells):
-            top = slice(2 * i * count, (2 * i + 1) * count)
-            low = slice((2 * i + 1) * count, (2 * i + 2) * count)
-            bands = haar_rows(
-                mine[top, even].astype(f32),
-                mine[top, odd].astype(f32),
-                mine[low, even].astype(f32),
-                mine[low, odd].astype(f32),
-            )
+            bands = haar_rows(*pixels_of(i, start))
             for band in range(3):
                 squares[band].append(bands[band] * bands[band])
         for band in range(3):
-            start = band * RADII * count
-            outer = [
-                over[start + i * count : start + (i + 1) * count, cols].astype(f32)
-                for i in range(RADII)
-            ]
-            inner = [
-                under[start + i * count : start + (i + 1) * count, cols].astype(f32)
-                for i in range(RADII)
-            ]
+            first = band * RADII * count
+            outer, inner = (
+                [
+                    halo[first + i * count : first + (i + 1) * count, cell_cols].astype(f32)
+                    for i in range(RADII)
+                ]
+                for halo in (above, below)
+            )
             column = outer + squares[band] + inner
             if factor is not None:
                 column = [value * factor for value in column]
@@ -331,12 +345,7 @@
             for i in range(cells):
                 top = slice(2 * i * count, (2 * i + 1) * count)
                 low = slice((2 * i + 1) * count, (2 * i + 2) * count)
-                pixels = (
-                    own[top, even].astype(f32),
-                    own[top, odd].astype(f32),
-                    own[low, even].astype(f32),
-                    own[low, odd].astype(f32),
-                )
+                pixels = pixels_of(i, base + block * 2 * LANES)
                 bands = haar_rows(*pixels)
                 shrunk = []
                 for band in range(3):
@@ -357,8 +366,11 @@
 
     for block in range(blocks):
         cols = slice(2 * block * LANES, (2 * block + 2) * LANES)
-        weighted = jnp.dot(select[...], product[:, cols], preferred_element_type=f32)
-        part = (weighted * inverse[:, cols]).astype(bf16)
+        there = pl.ds(pl.multiple_of(base + block * 2 * LANES, 2 * LANES), 2 * LANES)
+        weighted = jnp.dot(
+            select[:slot_rows, :], product[:, cols], preferred_element_type=f32
+        )
+        part = (weighted * inverse[:slot_rows, there]).astype(bf16)
         out[:, cols] = jnp.dot(part, merge[...], preferred_element_type=f32).astype(bf16)
 
 
@@ -366,51 +378,26 @@
     size, width_all = own.shape
     count = size // rows
     width = width_all // pieces
-    halo = above.shape[0]
-    blocks_all = width_all // (2 * LANES)
-    blocks = width // (2 * LANES)
-    here = lambda i, where: (0, where[0])
-    left = lambda i, where: (0, jnp.maximum(where[0] * blocks - 1, 0))
-    right = lambda i, where: (0, jnp.minimum((where[0] + 1) * blocks, blocks_all - 1))
     cell_rows = 3 * (rows // 2) * count
-    halo_specs = [
-        pl.BlockSpec((halo, width // 2), here),
-        pl.BlockSpec((halo, LANES), left),
-        pl.BlockSpec((halo, LANES), right),
-    ]
+    vmem = pl.BlockSpec(memory_space=pltpu.VMEM)
+    smem = pl.BlockSpec(memory_space=pltpu.SMEM)
     return pl.pallas_call(
-        functools.partial(main_kernel, count, rows, blocks_all),
-        grid_spec=pltpu.PrefetchScalarGridSpec(
-            num_scalar_prefetch=1,
-            grid=(1,),
-            in_specs=[
-                pl.BlockSpec((size, width), here),
-                pl.BlockSpec((size, 2 * LANES), left),
-                pl.BlockSpec((size, 2 * LANES), right),
-                *halo_specs,
-                *halo_specs,
-                pl.BlockSpec((slots * rows, width), here),
-                pl.BlockSpec((slots * rows, 2 * size), lambda i, where: (0, 0)),
-                pl.BlockSpec((RADII, 4 * LANES, 2 * LANES), lambda i, where: (0, 0, 0)),
-                pl.BlockSpec((2 * LANES, 2 * LANES), lambda i, where: (0, 0)),
-            ],
-            out_specs=pl.BlockSpec((slots * rows, width), lambda i, where: (0, 0)),
-            scratch_shapes=[
-                pltpu.VMEM((RADII, cell_rows, width // 2 + 2 * LANES), bf16),
-                pltpu.VMEM((FINE, cell_rows, width // 2), bf16),
-                pltpu.VMEM((cell_rows, 2 * LANES), f32),
-                pltpu.VMEM((2 * size, width), bf16),
-            ],
-        ),
+        functools.partial(main_kernel, count, rows, width),
+        in_specs=[smem] + [vmem] * 7,
+        out_specs=vmem,
+        scratch_shapes=[
+            pltpu.VMEM((RADII, cell_rows, width // 2 + 2 * LANES), bf16),
+            pltpu.VMEM((FINE, cell_rows, width // 2), bf16),
+            pltpu.VMEM((cell_rows, 2 * LANES), f32),
+            pltpu.VMEM((2 * size, width), bf16),
+        ],
         out_shape=jax.ShapeDtypeStruct((slots * rows, width), bf16),
-        compiler_params=pltpu.CompilerParams(vmem_limit_bytes=32 * 2**20),
+        compiler_params=pltpu.CompilerParams(vmem_limit_bytes=20 * 2**20),
         cost_estimate=pl.CostEstimate(
             flops=2 * 10**9, bytes_accessed=4 * 2**20, transcendentals=0
         ),
         name="residual",
-    )(
-        chunk, own, own, own, above, above, above, below, below, below, inverse, select, box, merge,
-    )
+    )(chunk, own, above, below, inverse, select, box, merge)
 
 
 def assemble_kernel(rows, select, share, *refs):
@@ -461,7 +448,7 @@
             pltpu.VMEM((CAMS * rows, width), bf16),
             pltpu.VMEM((len(parts), 2 * rows, width), bf16),
         ],
-        compiler_params=pltpu.CompilerParams(vmem_limit_bytes=32 * 2**20),
+        compiler_params=pltpu.CompilerParams(vmem_limit_bytes=20 * 2**20),
         cost_estimate=pl.CostEstimate(
             flops=2 * 10**9, bytes_accessed=4 * 2**20, transcendentals=0
         ),
@@ -500,27 +487,18 @@
     return lax.ppermute(array, axis, [(i, i ^ distance) for i in range(size)])
 
 
-def gathered(array, axis):
-    size = lax.axis_size(axis)
-    return lax.all_to_all(
-        jnp.broadcast_to(array, (size,) + array.shape), axis, split_axis=0, concat_axis=0
-    )
-
-
 def on_device(photos, camera_id):
     count, rows, width = photos.shape
     pieces, tiles = lax.axis_size("photo"), lax.axis_size("tile")
     me = lax.axis_index("photo").astype(jnp.int32)
-    own, up, down = prepare(photos)
+    own, up, down, *extras = prepare(me.reshape(1), camera_id, photos, pieces)
     above = lax.ppermute(down, "tile", [(i, i + 1) for i in range(tiles - 1)])
     below = lax.ppermute(up, "tile", [(i + 1, i) for i in range(tiles - 1)])
-    inverse, select, box, merge, *extras = energies(
-        me.reshape(1), camera_id, own, rows, pieces
-    )
     extras = [
         exchange(extra, "photo", distance) if distance else extra
         for distance, extra in enumerate(extras)
     ]
+    inverse, select, box, merge = energies(camera_id, own, rows)
     place, share, most = blend(me.reshape(1), extras, rows, count * rows)
 
     def finish(slots):
@@ -537,9 +515,16 @@
     prints, partial = lax.cond(
         most[0, 0] > few, lambda: finish(count), lambda: finish(few)
     )
-    total = jnp.sum(gathered(partial, "photo"), axis=0)
-    sums = gathered(total, "tile")
-    return prints, correlate([sums[i] for i in range(tiles)], float(rows * tiles * width))
+    terms = [partial] + [exchange(partial, "photo", i) for i in range(1, pieces)]
+    while len(terms) > 1:
+        terms = [terms[i] + terms[i + 1] for i in range(0, len(terms), 2)]
+    total = terms[0]
+    distance = 1
+    while 2 * distance < tiles:
+        total = total + exchange(total, "tile", distance)
+        distance *= 2
+    sums = [total, exchange(total, "tile", distance)]
+    return prints, correlate(sums, float(rows * tiles * width))
 
 
 def solution(mesh):

time: 83.3 us -> 79.3 us (0.952)
  blocking collectives: 18.9 us -> 0 us
  starting transfers between devices: 11.2 us -> 20.9 us
  Pallas kernels: 34.3 us -> 37.8 us
  waiting for transfers between devices: 14.4 us -> 15.9 us
    all_to_all x2 -> x0, blocking collectives: 18.9 us -> none  [gathered(): lax.all_to_all(jnp.broadcast_to(array, (size,) + array.shape), axis, spli...]
    ppermute x6 -> x12, starting transfers between devices: 7.52 us -> 16.3 us  [exchange(): return lax.ppermute(array, axis, [(i, i ^ distance) for i in range(size)])]
    pallas_call x5, Pallas kernels: 21.2 us -> 27.8 us  [the longest x4 24.7 us: main_part(): pl.pallas_call(functools.partial(main_kernel, count, rows, width), in_spe...]
    pallas_call x1, Pallas kernels: 7.41 us -> 4.39 us  [energies(): pl.pallas_call(functools.partial(energy_kernel, size // rows, rows), in_s...]
    ppermute x6 -> x12, waiting for transfers between devices: 14.4 us -> 15.9 us  [exchange(): return lax.ppermute(array, axis, [(i, i ^ distance) for i in range(size)])]
    unnamed x4 -> x8, local copies, waits for them, and re-layouts: 1.59 us -> 2.84 us
    ppermute x1, starting transfers between devices: 2.41 us -> 3.24 us  [on_device(): above = lax.ppermute(down, 'tile', [(i, i + 1) for i in range(tiles - 1)])]
  transfers between devices with their start and end apart: 8 -> 14, of which waited for: 4 -> 8; matrix products, arithmetic and copies ran while one was open for 0% -> 0% of each run, Pallas kernels for 27% -> 30%
where the time goes in v3:
time: 79.3 us; the launch traced here: 79.1 us
  Pallas kernels  37.8 us (48%)
  starting transfers between devices  20.9 us (26%)
  waiting for transfers between devices  15.9 us (20%)
  local copies, waits for them, and re-layouts  2.87 us (4%)
  between operations  1.35 us (2%)
    pallas_call x4, Pallas kernels, main_part(): pl.pallas_call(functools.partial(main_kernel, count, rows, width), in_spe...  24.7 us
    ppermute x12, starting transfers between devices, exchange(): return lax.ppermute(array, axis, [(i, i ^ distance) for i in range(size)])  16.3 us
    ppermute x12, waiting for transfers between devices, exchange(): return lax.ppermute(array, axis, [(i, i ^ distance) for i in range(size)])  15.9 us
    pallas_call x1, Pallas kernels, energies(): pl.pallas_call(functools.partial(energy_kernel, size // rows, rows), in_s...  4.39 us
    ppermute x1, starting transfers between devices, on_device(): above = lax.ppermute(down, 'tile', [(i, i + 1) for i in range(tiles - 1)])  3.24 us
    pallas_call x1, Pallas kernels, prepare(): pl.pallas_call(prepare_kernel, in_specs=[smem, smem, pl.BlockSpec(memory_...  3.1 us
    unnamed x8, local copies, waits for them, and re-layouts  2.84 us
    pallas_call x1, Pallas kernels, assemble(): pl.pallas_call(functools.partial(assemble_kernel, rows), out_shape=[jax.S...  2.56 us
  transfers between devices with their start and end apart: 14, of which 8 were waited for; matrix products, arithmetic and copies ran while one was open for 0% of the time, Pallas kernels for 30%

profile of v3, /device:TPU:0, one launch (start us, length us, event | category | flops | bytes accessed | tf_op | source)
XLA Modules:
  0.0 79.1 jit_solution(7270570966708681056)
XLA Ops:
  0.6 1.6 %copy-done = bf16[16,16,4096]{2,1,0:T(8,128)(2,1)S(1)} copy-done((bf16[16,16,4096]{2,1,0:T(8,128)(2,1)S(1)}, bf16[16,16,4096]{2,1,0:T(8,128)(2,1)}, u32[]{:S(2)}) %copy-start) | copy-done | bytes 2097176
  2.2 0.7 copy-done.1
  2.9 3.1 %prepare.1 = (bf16[256,4096]{1,0:T(8,128)(2,1)S(1)}, bf16[192,2048]{1,0:T(8,128)(2,1)S(1)}, bf16[192,2048]{1,0:T(8,128)(2,1)S(1)}, bf16[48,1024]{1,0:T(8,128)(2,...) custom-call(s32[1]{0:T(128)} %bitcast.8.me, s32[16]{0:T(128)S(1)} %copy-done.1, ...), custom_call_target="tpu_custom_call" | custom-call | flops 1000000000 | bytes 8388608 | tf_op jit(solution)/shard_map/prepare/pallas_call | solution.py:155
  6.0 3.2 %collective-permute-start.9 = (bf16[192,2048]{1,0:T(8,128)(2,1)S(1)}, bf16[192,2048]{1,0:T(8,128)(2,1)}, u32[]{:S(2)}, u32[]{:S(2)}) collective-permute-start(bf16[192,2048]{1,0:T(8,128)(2,1)S(1)} %get-tuple-element.84), channel_id=1, source_target_pairs={{0,1},{1,2},{2,3},{3,4},{4,5},{5,6},{6,7},{8,9},{9,10},{10,11},{11... | collective-permute-start | bytes 2359304 | tf_op jit(solution)/shard_map/ppermute | solution.py:495
  9.2 1.3 %collective-permute-start.10 = (bf16[192,2048]{1,0:T(8,128)(2,1)S(1)}, bf16[192,2048]{1,0:T(8,128)(2,1)}, u32[]{:S(2)}, u32[]{:S(2)}) collective-permute-start(bf16[192,2048]{1,0:T(8,128)(2,1)S(1)} %get-tuple-element.85), channel_id=1, source_target_pairs={{1,0},{2,1},{3,2},{4,3},{5,4},{6,5},{7,6},{9,8},{10,9},{11,10},{12... | collective-permute-start | bytes 2359304 | tf_op jit(solution)/shard_map/ppermute | solution.py:496
  10.5 2.3 %collective-permute-start.6 = (bf16[48,1024]{1,0:T(8,128)(2,1)S(1)}, bf16[48,1024]{1,0:T(8,128)(2,1)S(1)}, u32[]{:S(2)}, u32[]{:S(2)}) collective-permute-start(bf16[48,1024]{1,0:T(8,128)(2,1)S(1)} %get-tuple-element.79), channel_id=1, source_target_pairs={{0,8},{8,0},{16,24},{24,16},{1,9},{9,1},{17,25},{25,17},{2,10},{10... | collective-permute-start | bytes 294920 | tf_op jit(solution)/shard_map/ppermute | solution.py:487
  12.9 1.5 %collective-permute-start.7 = (bf16[48,1024]{1,0:T(8,128)(2,1)S(1)}, bf16[48,1024]{1,0:T(8,128)(2,1)S(1)}, u32[]{:S(2)}, u32[]{:S(2)}) collective-permute-start(bf16[48,1024]{1,0:T(8,128)(2,1)S(1)} %get-tuple-element.80), channel_id=1, source_target_pairs={{0,16},{8,24},{16,0},{24,8},{1,17},{9,25},{17,1},{25,9},{2,18},{10... | collective-permute-start | bytes 294920 | tf_op jit(solution)/shard_map/ppermute | solution.py:487
  14.5 4.4 %energies.1 = (f32[256,4096]{1,0:T(8,128)}, bf16[256,512]{1,0:T(8,128)(2,1)S(1)}, bf16[4,512,256]{2,1,0:T(8,128)(2,1)}, bf16[256,256]{1,0:T(8,128)(2,1)S(1)}) custom-call(s32[16]{0:T(128)S(1)} %copy-done.1, bf16[256,4096]{1,0:T(8,128)(2,1)S(1)} %get-tuple-element.83.own), custom_call_target="tpu_custom_call" | custom-call | flops 1000000000 | bytes 8388608 | tf_op jit(solution)/shard_map/energies/pallas_call | solution.py:203
  18.9 1.9 %collective-permute-done.8.refs_3_ = bf16[48,1024]{1,0:T(8,128)(2,1)S(1)} collective-permute-done((bf16[48,1024]{1,0:T(8,128)(2,1)S(1)}, bf16[48,1024]{1,0:T(8,128)(2,1)S(1)}, u32[]{:S(2)}, u32[]{:S(2)}) %collective-permute-start.8) | collective-permute-done | bytes 98336 | tf_op jit(solution)/shard_map/ppermute | solution.py:487
  20.9 1.6 %blend.1 = (bf16[4,512,256]{2,1,0:T(8,128)(2,1)}, f32[4,2,16,1024]{3,2,1,0:T(8,128)}, s32[1,1]{1,0:T(1,128)}) custom-call(s32[1]{0:T(128)} %bitcast.8.me, bf16[48,1024]{1,0:T(8,128)(2,1)S(1)} %get-tuple-element.78.refs_0_, bf16[48,1024]{1,0:T(8,128)(2,1)S(1)} %collective-permute-done.6.refs_1_, bf16[48,1024]{1,0:T(8,128)(2,1)S(1)} %collective-permute-done.7.refs_2_, ...), custom_call_target="tpu_custom_call" | custom-call | tf_op jit(solution)/shard_map/blend/pallas_call | solution.py:253
  23.1 36.9 %conditional.1 = ((f32[32,16,1024]{2,1,0:T(8,128)}, f32[32,128]{1,0:T(8,128)S(1)})) conditional(s32[]{:T(128)} %bitcast.9, (s32[]{:T(128)}, bf16[256,4096]{1,0:T(8,128)(2,1)S(1)}, bf16[192,2048]{1,0:T(8,128)(2,1)}, bf16[192,2048]{1,0:T(8,128)(2,1)}, f32[256,4096]{1,0:T(8,128)}, /*index=5*/bf16[256,512]{1,0:T(8,128)(2,1)S(1)}, ...), branch_computations={%region_0.0_spmd, %region_1.0_spmd} | conditional | flops 10000000000 | bytes 71303496 | solution.py:515
  23.3 6.8 %residual.9 = bf16[192,1024]{1,0:T(8,128)(2,1)S(1)} custom-call(s32[1]{0:T(128)} %bitcast.1.where, bf16[256,4096]{1,0:T(8,128)(2,1)S(1)} %get-tuple-element.43.own, bf16[192,2048]{1,0:T(8,128)(2,1)} %get-tuple-element.44.above, bf16[192,2048]{1,0:T(8,128)(2,1)} %get-tuple-element.45.below, f32[256,4096]{1,0:T(8,128)} %get-tuple-element.46.inverse, ...), custom_call_target="tpu_custom_call" | custom-call | flops 2000000000 | bytes 4194304 | tf_op jit(solution)/shard_map/cond/branch_0_fun/residual/pallas_call | solution.py:384
  30.1 0.7 collective-permute-start
  30.8 6.6 %residual.10 = bf16[192,1024]{1,0:T(8,128)(2,1)S(1)} custom-call(s32[1]{0:T(128)} %bitcast.2.where, bf16[256,4096]{1,0:T(8,128)(2,1)} %copy-done.4, bf16[192,2048]{1,0:T(8,128)(2,1)} %get-tuple-element.44.above, bf16[192,2048]{1,0:T(8,128)(2,1)} %get-tuple-element.45.below, f32[256,4096]{1,0:T(8,128)} %get-tuple-element.46.inverse, ...), custom_call_target="tpu_custom_call" | custom-call | flops 2000000000 | bytes 4194304 | tf_op jit(solution)/shard_map/cond/branch_0_fun/residual/pallas_call | solution.py:384
  37.4 1.1 %collective-permute-start.1 = (bf16[192,1024]{1,0:T(8,128)(2,1)S(1)}, bf16[192,1024]{1,0:T(8,128)(2,1)S(1)}, u32[]{:S(2)}, u32[]{:S(2)}) collective-permute-start(bf16[192,1024]{1,0:T(8,128)(2,1)S(1)} %residual.10), channel_id=1, source_target_pairs={{0,16},{8,24},{16,0},{24,8},{1,17},{9,25},{17,1},{25,9},{2,18},{10... | collective-permute-start | bytes 1179656 | tf_op jit(solution)/shard_map/cond/branch_0_fun/ppermute | solution.py:487
  38.5 6.8 %residual.11 = bf16[192,1024]{1,0:T(8,128)(2,1)S(1)} custom-call(s32[1]{0:T(128)} %bitcast.3.where, bf16[256,4096]{1,0:T(8,128)(2,1)} %copy-done.4, bf16[192,2048]{1,0:T(8,128)(2,1)} %get-tuple-element.44.above, bf16[192,2048]{1,0:T(8,128)(2,1)} %get-tuple-element.45.below, f32[256,4096]{1,0:T(8,128)} %get-tuple-element.46.inverse, ...), custom_call_target="tpu_custom_call" | custom-call | flops 2000000000 | bytes 4194304 | tf_op jit(solution)/shard_map/cond/branch_0_fun/residual/pallas_call | solution.py:384
  45.3 1.8 %collective-permute-start.2 = (bf16[192,1024]{1,0:T(8,128)(2,1)S(1)}, bf16[192,1024]{1,0:T(8,128)(2,1)S(1)}, u32[]{:S(2)}, u32[]{:S(2)}) collective-permute-start(bf16[192,1024]{1,0:T(8,128)(2,1)S(1)} %residual.11), channel_id=1, source_target_pairs={{0,24},{8,16},{16,8},{24,0},{1,25},{9,17},{17,9},{25,1},{2,26},{10... | collective-permute-start | bytes 1179656 | tf_op jit(solution)/shard_map/cond/branch_0_fun/ppermute | solution.py:487
  47.2 4.5 %residual.8.refs_0_ = bf16[192,1024]{1,0:T(8,128)(2,1)S(1)} custom-call(s32[1]{0:T(128)} %bitcast.where, bf16[256,4096]{1,0:T(8,128)(2,1)S(1)} %copy-done.5, bf16[192,2048]{1,0:T(8,128)(2,1)} %get-tuple-element.44.above, bf16[192,2048]{1,0:T(8,128)(2,1)} %get-tuple-element.45.below, f32[256,4096]{1,0:T(8,128)S(1)} %copy-done.2, ...), custom_call_target="tpu_custom_call" | custom-call | flops 2000000000 | bytes 4194304 | tf_op jit(solution)/shard_map/cond/branch_0_fun/residual/pallas_call | solution.py:384
  51.7 5.7 %collective-permute-done.2.refs_3_ = bf16[192,1024]{1,0:T(8,128)(2,1)S(1)} collective-permute-done((bf16[192,1024]{1,0:T(8,128)(2,1)S(1)}, bf16[192,1024]{1,0:T(8,128)(2,1)S(1)}, u32[]{:S(2)}, u32[]{:S(2)}) %collective-permute-start.2) | collective-permute-done | bytes 393248 | tf_op jit(solution)/shard_map/cond/branch_0_fun/ppermute | solution.py:487
  57.4 2.6 %assemble.2 = (f32[32,16,1024]{2,1,0:T(8,128)}, f32[32,128]{1,0:T(8,128)S(1)}) custom-call(bf16[4,512,256]{2,1,0:T(8,128)(2,1)S(1)} %copy-done.12, f32[4,2,16,1024]{3,2,1,0:T(8,128)S(1)} %copy-done.14, bf16[192,1024]{1,0:T(8,128)(2,1)S(1)} %residual.8.refs_0_, bf16[192,1024]{1,0:T(8,128)(2,1)S(1)} %collective-permute-done.refs_1_, ...), custom_call_target="tpu_custom_call" | custom-call | flops 2000000000 | bytes 4194304 | tf_op jit(solution)/shard_map/cond/branch_0_fun/assemble/pallas_call | solution.py:441
  60.0 2.3 %collective-permute-start.13 = (f32[32,128]{1,0:T(8,128)S(1)}, f32[32,128]{1,0:T(8,128)S(1)}, u32[]{:S(2)}, u32[]{:S(2)}) collective-permute-start(f32[32,128]{1,0:T(8,128)S(1)} %get-tuple-element.93), channel_id=1, source_target_pairs={{0,24},{8,16},{16,8},{24,0},{1,25},{9,17},{17,9},{25,1},{2,26},{10... | collective-permute-start | bytes 49160 | tf_op jit(solution)/shard_map/ppermute | solution.py:487
  62.3 1.1 %collective-permute-start.12 = (f32[32,128]{1,0:T(8,128)S(1)}, f32[32,128]{1,0:T(8,128)S(1)}, u32[]{:S(2)}, u32[]{:S(2)}) collective-permute-start(f32[32,128]{1,0:T(8,128)S(1)} %get-tuple-element.93), channel_id=1, source_target_pairs={{0,16},{8,24},{16,0},{24,8},{1,17},{9,25},{17,1},{25,9},{2,18},{10... | collective-permute-start | bytes 49160 | tf_op jit(solution)/shard_map/ppermute | solution.py:487
  63.5 1.3 %collective-permute-done.13 = f32[32,128]{1,0:T(8,128)S(1)} collective-permute-done((f32[32,128]{1,0:T(8,128)S(1)}, f32[32,128]{1,0:T(8,128)S(1)}, u32[]{:S(2)}, u32[]{:S(2)}) %collective-permute-start.13) | collective-permute-done | bytes 16416 | tf_op jit(solution)/shard_map/ppermute | solution.py:487
  64.7 1.3 %collective-permute-done.12 = f32[32,128]{1,0:T(8,128)S(1)} collective-permute-done((f32[32,128]{1,0:T(8,128)S(1)}, f32[32,128]{1,0:T(8,128)S(1)}, u32[]{:S(2)}, u32[]{:S(2)}) %collective-permute-start.12) | collective-permute-done | bytes 16416 | tf_op jit(solution)/shard_map/ppermute | solution.py:487
  66.1 1.1 %collective-permute-done.11 = f32[32,128]{1,0:T(8,128)S(1)} collective-permute-done((f32[32,128]{1,0:T(8,128)S(1)}, f32[32,128]{1,0:T(8,128)S(1)}, u32[]{:S(2)}, u32[]{:S(2)}) %collective-permute-start.11) | collective-permute-done | bytes 16416 | tf_op jit(solution)/shard_map/ppermute | solution.py:487
  67.2 1.2 %collective-permute-done.14 = f32[32,128]{1,0:T(8,128)S(1)} collective-permute-done((f32[32,128]{1,0:T(8,128)S(1)}, f32[32,128]{1,0:T(8,128)S(1)}, u32[]{:S(2)}, u32[]{:S(2)}) %collective-permute-start.14) | collective-permute-done | bytes 16416 | tf_op jit(solution)/shard_map/ppermute | solution.py:487
  68.4 2.1 %collective-permute-start.15 = (f32[32,128]{1,0:T(8,128)S(1)}, f32[32,128]{1,0:T(8,128)S(1)}, u32[]{:S(2)}, u32[]{:S(2)}) collective-permute-start(f32[32,128]{1,0:T(8,128)S(1)} %add.18), channel_id=1, source_target_pairs={{0,2},{1,3},{2,0},{3,1},{4,6},{5,7},{6,4},{7,5},{8,10},{9,11},{10,... | collective-permute-start | bytes 49160 | tf_op jit(solution)/shard_map/ppermute | solution.py:487
  70.5 1.7 %collective-permute-done.15 = f32[32,128]{1,0:T(8,128)S(1)} collective-permute-done((f32[32,128]{1,0:T(8,128)S(1)}, f32[32,128]{1,0:T(8,128)S(1)}, u32[]{:S(2)}, u32[]{:S(2)}) %collective-permute-start.15) | collective-permute-done | bytes 16416 | tf_op jit(solution)/shard_map/ppermute | solution.py:487
  72.2 3.0 %collective-permute-start.16 = (f32[32,128]{1,0:T(8,128)S(1)}, f32[32,128]{1,0:T(8,128)S(1)}, u32[]{:S(2)}, u32[]{:S(2)}) collective-permute-start(f32[32,128]{1,0:T(8,128)S(1)} %add.19.refs_0_), channel_id=1, source_target_pairs={{0,4},{1,5},{2,6},{3,7},{4,0},{5,1},{6,2},{7,3},{8,12},{9,13},{10,... | collective-permute-start | bytes 49160 | tf_op jit(solution)/shard_map/ppermute | solution.py:487
  75.2 1.7 %collective-permute-done.16.refs_1_ = f32[32,128]{1,0:T(8,128)S(1)} collective-permute-done((f32[32,128]{1,0:T(8,128)S(1)}, f32[32,128]{1,0:T(8,128)S(1)}, u32[]{:S(2)}, u32[]{:S(2)}) %collective-permute-start.16) | collective-permute-done | bytes 16416 | tf_op jit(solution)/shard_map/ppermute | solution.py:487
  76.9 0.6 copy-done.11
  77.5 1.5 %correlate.1 = f32[32,32]{1,0:T(8,128)} custom-call(f32[32,128]{1,0:T(8,128)} %copy-done.10, f32[32,128]{1,0:T(8,128)} %copy-done.11), custom_call_target="tpu_custom_call" | custom-call | tf_op jit(solution)/shard_map/correlate/pallas_call | solution.py:478
  (29 shorter events, 0.3 us)
Async XLA Ops:
  0.6 1.6 %copy-start = (bf16[16,16,4096]{2,1,0:T(8,128)(2,1)S(1)}, bf16[16,16,4096]{2,1,0:T(8,128)(2,1)}, u32[]{:S(2)}) copy-start(bf16[16,16,4096]{2,1,0:T(8,128)(2,1)} %photos.1) | copy-start | bytes 6291460
  2.2 0.7 copy-start.1
  6.0 17.1 %collective-permute-start.9 = (bf16[192,2048]{1,0:T(8,128)(2,1)S(1)}, bf16[192,2048]{1,0:T(8,128)(2,1)}, u32[]{:S(2)}, u32[]{:S(2)}) collective-permute-start(bf16[192,2048]{1,0:T(8,128)(2,1)S(1)} %get-tuple-element.84), channel_id=1, source_target_pairs={{0,1},{1,2},{2,3},{3,4},{4,5},{5,6},{6,7},{8,9},{9,10},{10,11},{11... | collective-permute-start | bytes 2359304 | tf_op jit(solution)/shard_map/ppermute | solution.py:495
  9.2 13.9 %collective-permute-start.10 = (bf16[192,2048]{1,0:T(8,128)(2,1)S(1)}, bf16[192,2048]{1,0:T(8,128)(2,1)}, u32[]{:S(2)}, u32[]{:S(2)}) collective-permute-start(bf16[192,2048]{1,0:T(8,128)(2,1)S(1)} %get-tuple-element.85), channel_id=1, source_target_pairs={{1,0},{2,1},{3,2},{4,3},{5,4},{6,5},{7,6},{9,8},{10,9},{11,10},{12... | collective-permute-start | bytes 2359304 | tf_op jit(solution)/shard_map/ppermute | solution.py:496
  10.5 8.4 %collective-permute-start.6 = (bf16[48,1024]{1,0:T(8,128)(2,1)S(1)}, bf16[48,1024]{1,0:T(8,128)(2,1)S(1)}, u32[]{:S(2)}, u32[]{:S(2)}) collective-permute-start(bf16[48,1024]{1,0:T(8,128)(2,1)S(1)} %get-tuple-element.79), channel_id=1, source_target_pairs={{0,8},{8,0},{16,24},{24,16},{1,9},{9,1},{17,25},{25,17},{2,10},{10... | collective-permute-start | bytes 294920 | tf_op jit(solution)/shard_map/ppermute | solution.py:487
  12.9 6.0 %collective-permute-start.7 = (bf16[48,1024]{1,0:T(8,128)(2,1)S(1)}, bf16[48,1024]{1,0:T(8,128)(2,1)S(1)}, u32[]{:S(2)}, u32[]{:S(2)}) collective-permute-start(bf16[48,1024]{1,0:T(8,128)(2,1)S(1)} %get-tuple-element.80), channel_id=1, source_target_pairs={{0,16},{8,24},{16,0},{24,8},{1,17},{9,25},{17,1},{25,9},{2,18},{10... | collective-permute-start | bytes 294920 | tf_op jit(solution)/shard_map/ppermute | solution.py:487
  14.4 6.5 %collective-permute-start.8 = (bf16[48,1024]{1,0:T(8,128)(2,1)S(1)}, bf16[48,1024]{1,0:T(8,128)(2,1)S(1)}, u32[]{:S(2)}, u32[]{:S(2)}) collective-permute-start(bf16[48,1024]{1,0:T(8,128)(2,1)S(1)} %get-tuple-element.81), channel_id=1, source_target_pairs={{0,24},{8,16},{16,8},{24,0},{1,25},{9,17},{17,9},{25,1},{2,26},{10... | collective-permute-start | bytes 294920 | tf_op jit(solution)/shard_map/ppermute | solution.py:487
  23.3 7.5 %copy-start.4 = (bf16[256,4096]{1,0:T(8,128)(2,1)}, bf16[256,4096]{1,0:T(8,128)(2,1)S(1)}, u32[]{:S(2)}) copy-start(bf16[256,4096]{1,0:T(8,128)(2,1)S(1)} %get-tuple-element.43.own) | copy-start | bytes 6291460 | tf_op jit(solution)/shard_map/cond
  30.1 21.6 %collective-permute-start = (bf16[192,1024]{1,0:T(8,128)(2,1)S(1)}, bf16[192,1024]{1,0:T(8,128)(2,1)S(1)}, u32[]{:S(2)}, u32[]{:S(2)}) collective-permute-start(bf16[192,1024]{1,0:T(8,128)(2,1)S(1)} %residual.9), channel_id=1, source_target_pairs={{0,8},{8,0},{16,24},{24,16},{1,9},{9,1},{17,25},{25,17},{2,10},{10... | collective-permute-start | bytes 1179656 | tf_op jit(solution)/shard_map/cond/branch_0_fun/ppermute | solution.py:487
  37.4 14.3 %collective-permute-start.1 = (bf16[192,1024]{1,0:T(8,128)(2,1)S(1)}, bf16[192,1024]{1,0:T(8,128)(2,1)S(1)}, u32[]{:S(2)}, u32[]{:S(2)}) collective-permute-start(bf16[192,1024]{1,0:T(8,128)(2,1)S(1)} %residual.10), channel_id=1, source_target_pairs={{0,16},{8,24},{16,0},{24,8},{1,17},{9,25},{17,1},{25,9},{2,18},{10... | collective-permute-start | bytes 1179656 | tf_op jit(solution)/shard_map/cond/branch_0_fun/ppermute | solution.py:487
  38.5 8.6 %copy-start.2 = (f32[256,4096]{1,0:T(8,128)S(1)}, f32[256,4096]{1,0:T(8,128)}, u32[]{:S(2)}) copy-start(f32[256,4096]{1,0:T(8,128)} %get-tuple-element.46.inverse) | copy-start | bytes 12582916 | tf_op jit(solution)/shard_map/cond
  38.5 8.6 %copy-start.5 = (bf16[256,4096]{1,0:T(8,128)(2,1)S(1)}, bf16[256,4096]{1,0:T(8,128)(2,1)}, u32[]{:S(2)}) copy-start(bf16[256,4096]{1,0:T(8,128)(2,1)} %copy-done.4) | copy-start | bytes 6291460 | tf_op jit(solution)/shard_map/cond
  38.5 8.6 %copy-start.8 = (bf16[4,512,256]{2,1,0:T(8,128)(2,1)S(1)}, bf16[4,512,256]{2,1,0:T(8,128)(2,1)}, u32[]{:S(2)}) copy-start(bf16[4,512,256]{2,1,0:T(8,128)(2,1)} %get-tuple-element.48.box) | copy-start | bytes 3145732 | tf_op jit(solution)/shard_map/cond
  45.3 12.1 %collective-permute-start.2 = (bf16[192,1024]{1,0:T(8,128)(2,1)S(1)}, bf16[192,1024]{1,0:T(8,128)(2,1)S(1)}, u32[]{:S(2)}, u32[]{:S(2)}) collective-permute-start(bf16[192,1024]{1,0:T(8,128)(2,1)S(1)} %residual.11), channel_id=1, source_target_pairs={{0,24},{8,16},{16,8},{24,0},{1,25},{9,17},{17,9},{25,1},{2,26},{10... | collective-permute-start | bytes 1179656 | tf_op jit(solution)/shard_map/cond/branch_0_fun/ppermute | solution.py:487
  47.2 10.2 %copy-start.12 = (bf16[4,512,256]{2,1,0:T(8,128)(2,1)S(1)}, bf16[4,512,256]{2,1,0:T(8,128)(2,1)}, u32[]{:S(2)}) copy-start(bf16[4,512,256]{2,1,0:T(8,128)(2,1)} %get-tuple-element.40.select) | copy-start | bytes 3145732 | tf_op jit(solution)/shard_map/cond
  47.2 10.2 %copy-start.14 = (f32[4,2,16,1024]{3,2,1,0:T(8,128)S(1)}, f32[4,2,16,1024]{3,2,1,0:T(8,128)}, u32[]{:S(2)}) copy-start(f32[4,2,16,1024]{3,2,1,0:T(8,128)} %get-tuple-element.41.share) | copy-start | bytes 1572868 | tf_op jit(solution)/shard_map/cond
  60.0 4.7 %collective-permute-start.13 = (f32[32,128]{1,0:T(8,128)S(1)}, f32[32,128]{1,0:T(8,128)S(1)}, u32[]{:S(2)}, u32[]{:S(2)}) collective-permute-start(f32[32,128]{1,0:T(8,128)S(1)} %get-tuple-element.93), channel_id=1, source_target_pairs={{0,24},{8,16},{16,8},{24,0},{1,25},{9,17},{17,9},{25,1},{2,26},{10... | collective-permute-start | bytes 49160 | tf_op jit(solution)/shard_map/ppermute | solution.py:487
  62.3 3.7 %collective-permute-start.12 = (f32[32,128]{1,0:T(8,128)S(1)}, f32[32,128]{1,0:T(8,128)S(1)}, u32[]{:S(2)}, u32[]{:S(2)}) collective-permute-start(f32[32,128]{1,0:T(8,128)S(1)} %get-tuple-element.93), channel_id=1, source_target_pairs={{0,16},{8,24},{16,0},{24,8},{1,17},{9,25},{17,1},{25,9},{2,18},{10... | collective-permute-start | bytes 49160 | tf_op jit(solution)/shard_map/ppermute | solution.py:487
  63.4 3.7 %collective-permute-start.11 = (f32[32,128]{1,0:T(8,128)S(1)}, f32[32,128]{1,0:T(8,128)S(1)}, u32[]{:S(2)}, u32[]{:S(2)}) collective-permute-start(f32[32,128]{1,0:T(8,128)S(1)} %get-tuple-element.93), channel_id=1, source_target_pairs={{0,8},{8,0},{16,24},{24,16},{1,9},{9,1},{17,25},{25,17},{2,10},{10... | collective-permute-start | bytes 49160 | tf_op jit(solution)/shard_map/ppermute | solution.py:487
  67.1 1.2 %collective-permute-start.14 = (f32[32,128]{1,0:T(8,128)S(1)}, f32[32,128]{1,0:T(8,128)S(1)}, u32[]{:S(2)}, u32[]{:S(2)}) collective-permute-start(f32[32,128]{1,0:T(8,128)S(1)} %add_add_fusion), channel_id=1, source_target_pairs={{0,1},{1,0},{2,3},{3,2},{4,5},{5,4},{6,7},{7,6},{8,9},{9,8},{10,11... | collective-permute-start | bytes 49160 | tf_op jit(solution)/shard_map/ppermute | solution.py:487
  68.4 3.8 %collective-permute-start.15 = (f32[32,128]{1,0:T(8,128)S(1)}, f32[32,128]{1,0:T(8,128)S(1)}, u32[]{:S(2)}, u32[]{:S(2)}) collective-permute-start(f32[32,128]{1,0:T(8,128)S(1)} %add.18), channel_id=1, source_target_pairs={{0,2},{1,3},{2,0},{3,1},{4,6},{5,7},{6,4},{7,5},{8,10},{9,11},{10,... | collective-permute-start | bytes 49160 | tf_op jit(solution)/shard_map/ppermute | solution.py:487
  72.2 4.8 %copy-start.10 = (f32[32,128]{1,0:T(8,128)}, f32[32,128]{1,0:T(8,128)S(1)}, u32[]{:S(2)}) copy-start(f32[32,128]{1,0:T(8,128)S(1)} %add.19.refs_0_) | copy-start | bytes 49156
  72.2 4.8 %collective-permute-start.16 = (f32[32,128]{1,0:T(8,128)S(1)}, f32[32,128]{1,0:T(8,128)S(1)}, u32[]{:S(2)}, u32[]{:S(2)}) collective-permute-start(f32[32,128]{1,0:T(8,128)S(1)} %add.19.refs_0_), channel_id=1, source_target_pairs={{0,4},{1,5},{2,6},{3,7},{4,0},{5,1},{6,2},{7,3},{8,12},{9,13},{10,... | collective-permute-start | bytes 49160 | tf_op jit(solution)/shard_map/ppermute | solution.py:487
  76.9 0.6 copy-start.11

commit v4 on v3

--- a/solution.py
+++ b/solution.py
@@ -66,6 +66,11 @@
     upper = value.astype(bf16)
     lower = (value - upper.astype(f32)).astype(bf16)
     return upper, lower
+
+
+def inverted(value):
+    guess = pl.reciprocal(value, approx=True)
+    return guess * (2.0 - value * guess)
 
 
 def slot_numbers(ids, count):
@@ -78,21 +83,16 @@
 
 
 def prepare_kernel(me, ids, photos, sorted_out, up_out, down_out, *refs):
-    extras, (buffer, arrived) = refs[:-2], refs[-2:]
+    extras, (buffer, by_row, arrived) = refs[:-3], refs[-3:]
     count, rows, width = photos.shape
     cells = rows // 2
     pieces = len(extras)
     step = width // pieces
-    bases = [pl.multiple_of((me[0] ^ distance) * step, step) for distance in range(pieces)]
-    copies = []
     for distance in range(pieces):
-        cols = pl.ds(bases[distance], step)
-        copies.append(
-            pltpu.make_async_copy(
-                photos.at[:, :, cols], buffer.at[distance], arrived.at[distance]
-            )
-        )
-        copies[-1].start()
+        cols = pl.ds(pl.multiple_of((me[0] ^ distance) * step, step), step)
+        pltpu.make_async_copy(
+            photos.at[:, :, cols], buffer.at[distance], arrived.at[distance]
+        ).start()
     perm = row_permutation(count, rows)
     split = column_split()
 
@@ -107,17 +107,23 @@
     notes = jnp.where(sub == 0, ids[0], jnp.where(sub == 1, ids[count - 1], slot_id))
     notes = jnp.where(sub == 3, cameras, notes).astype(f32).astype(bf16)
 
-    for distance in range(pieces):
-        copies[distance].wait()
+    @pl.loop(0, pieces)
+    def _(distance):
+        piece = me[0] ^ distance
+        cols = pl.ds(pl.multiple_of(piece * step, step), step)
+        pltpu.make_async_copy(
+            photos.at[:, :, cols], buffer.at[distance], arrived.at[distance]
+        ).wait()
         flat = buffer[distance].reshape(count * rows, step)
-        by_row = jnp.dot(perm, flat, preferred_element_type=f32).astype(bf16)
-        for inner in range(step // (2 * LANES)):
-            at = inner * 2 * LANES
-            cols = pl.ds(pl.multiple_of(bases[distance] + at, 2 * LANES), 2 * LANES)
-            cell_cols = pl.ds(
-                pl.multiple_of((me[0] ^ distance) * (step // 2) + at // 2, LANES), LANES
-            )
-            parted = jnp.dot(by_row[:, at : at + 2 * LANES], split, preferred_element_type=f32)
+        by_row[...] = jnp.dot(perm, flat, preferred_element_type=f32).astype(bf16)
+
+        @pl.loop(0, step // (2 * LANES))
+        def _(inner):
+            block = piece * (step // (2 * LANES)) + inner
+            cols = pl.ds(pl.multiple_of(block * 2 * LANES, 2 * LANES), 2 * LANES)
+            cell_cols = pl.ds(pl.multiple_of(block * LANES, LANES), LANES)
+            local = pl.ds(pl.multiple_of(inner * 2 * LANES, 2 * LANES), 2 * LANES)
+            parted = jnp.dot(by_row[:, local], split, preferred_element_type=f32)
             sorted_out[:, cols] = parted.astype(bf16)
             for i in range(cells):
                 if RADII <= i < cells - RADII:
@@ -134,12 +140,13 @@
                         start = (band * RADII + i - (cells - RADII)) * count
                         down_out[start : start + count, cell_cols] = square
 
+    none = jnp.zeros((rows, step), f32)
+    for distance, extra in enumerate(extras):
+
         def add(photo, total):
             pixel = buffer[distance, photo].astype(f32)
             return total + pixel * pixel
 
-        none = jnp.zeros((rows, step), f32)
-        extra = extras[distance]
         extra[:rows, :] = lax.fori_loop(0, in_first, add, none).astype(bf16)
         extra[rows : 2 * rows, :] = lax.fori_loop(count - in_last, count, add, none).astype(bf16)
         extra[2 * rows :, :] = notes
@@ -164,6 +171,7 @@
         + [jax.ShapeDtypeStruct((3 * rows, step), bf16)] * pieces,
         scratch_shapes=[
             pltpu.VMEM((pieces, count, rows, step), bf16),
+            pltpu.VMEM((size, step), bf16),
             pltpu.SemaphoreType.DMA((pieces,)),
         ],
         compiler_params=pltpu.CompilerParams(vmem_limit_bytes=20 * 2**20),
@@ -188,12 +196,14 @@
     for radius in range(1, RADII + 1):
         box_out[radius - 1] = box_matrix(radius)
     merge_out[...] = column_merge()
-    for block in range(width // (2 * LANES)):
-        cols = slice(block * 2 * LANES, (block + 1) * 2 * LANES)
+
+    @pl.loop(0, width // (2 * LANES))
+    def _(block):
+        cols = pl.ds(pl.multiple_of(block * 2 * LANES, 2 * LANES), 2 * LANES)
         pixel = own[:, cols].astype(f32)
         pair = jnp.concatenate(halves(pixel * pixel), axis=0)
         energy = jnp.dot(select, pair, preferred_element_type=f32)
-        inverse[:, cols] = 1.0 / jnp.maximum(energy, 2.0**-20)
+        inverse[:, cols] = inverted(jnp.maximum(energy, 2.0**-20))
 
 
 def energies(ids, own, rows):
@@ -217,20 +227,17 @@
 
 
 def blend_kernel(rows, me, *refs):
-    pieces = len(refs) - 4
-    extras, (select, share, most, held) = refs[:pieces], refs[pieces:]
+    pieces = len(refs) - 3
+    extras, (select, share, held) = refs[:pieces], refs[pieces:]
     size = select.shape[2]
     tall = CAMS * rows
     sub, lane = iotas((tall, size))
     same_row = (sub & (rows - 1)) == (lane & (rows - 1))
     camera = (sub >> log2(rows)).astype(f32)
-    highest = jnp.float32(0)
     for distance, extra in enumerate(extras):
         notes = extra[2 * rows :, :].astype(f32)
         select[distance] = indicator((camera == notes[2:3, :size]) & same_row)
-        highest = jnp.maximum(highest, jnp.max(notes[3:4, :LANES]))
         held[me[0] ^ distance] = extra[...].astype(f32)
-    most[0, 0] = highest.astype(jnp.int32)
     ones = jnp.ones((rows, share.shape[3]), f32)
     for device in range(pieces):
         if device == 0:
@@ -253,11 +260,10 @@
     return pl.pallas_call(
         functools.partial(blend_kernel, rows),
         in_specs=[smem] + [vmem] * pieces,
-        out_specs=[vmem, vmem, smem],
+        out_specs=[vmem, vmem],
         out_shape=[
             jax.ShapeDtypeStruct((pieces, CAMS * rows, size), bf16),
             jax.ShapeDtypeStruct((pieces, 2, rows, width), f32),
-            jax.ShapeDtypeStruct((1, 1), jnp.int32),
         ],
         scratch_shapes=[pltpu.VMEM((pieces, 3 * rows, width), f32)],
         compiler_params=pltpu.CompilerParams(vmem_limit_bytes=20 * 2**20),
@@ -266,17 +272,48 @@
 
 
 def main_kernel(
-    count, rows, width, where, own, above, below, inverse, select, box, merge, out,
-    sums, rest, least, product,
+    count, rows, chunk, own_all, above_all, below_all, inverse, select, box, merge, out,
+    own, above, below, sums, rest, least, product, scale, select_in, box_in, merge_in,
+    arrived, ready,
 ):
     cells = rows // 2
     size = count * rows
-    width_all = own.shape[1]
+    width = out.shape[1]
     blocks = width // (2 * LANES)
     slot_rows = out.shape[0]
-    base = where[0] * width
-    left_ok = jnp.where(base > 0, 1.0, 0.0).astype(f32)
-    right_ok = jnp.where(base + width < width_all, 1.0, 0.0).astype(f32)
+    base = chunk[0] * width
+    inner = []
+    edges = ([], [])
+    for at, (whole, local, lanes) in enumerate(
+        ((own_all, own, 2 * LANES), (above_all, above, LANES), (below_all, below, LANES))
+    ):
+        length = blocks * lanes
+        start = chunk[0] * length
+        for place, size_here, offset, group in (
+            (start, length, lanes, inner),
+            (jnp.maximum(start - lanes, 0), lanes, 0, edges[0]),
+            (jnp.minimum(start + length, whole.shape[1] - lanes), lanes, lanes + length, edges[1]),
+        ):
+            index = 3 * at + (0 if group is inner else 1 if group is edges[0] else 2)
+            group.append(
+                pltpu.make_async_copy(
+                    whole.at[:, pl.ds(pl.multiple_of(place, lanes), size_here)],
+                    local.at[:, pl.ds(offset, size_here)],
+                    arrived.at[index],
+                )
+            )
+    late = [
+        pltpu.make_async_copy(box, box_in, ready.at[0]),
+        pltpu.make_async_copy(select.at[pl.ds(0, slot_rows)], select_in, ready.at[1]),
+        pltpu.make_async_copy(
+            inverse.at[pl.ds(0, slot_rows), pl.ds(pl.multiple_of(base, width), width)],
+            scale,
+            ready.at[2],
+        ),
+        pltpu.make_async_copy(merge, merge_in, ready.at[3]),
+    ]
+    for copy in inner + edges[0] + edges[1] + late:
+        copy.start()
 
     def pixels_of(i, start):
         top = slice(2 * i * count, (2 * i + 1) * count)
@@ -288,108 +325,131 @@
             for at, cols in ((top, even), (top, odd), (low, even), (low, odd))
         )
 
-    for block in range(-1, blocks + 1):
-        start = base + block * 2 * LANES
-        factor = None
-        if block < 0:
-            start, factor = jnp.maximum(start, 0), left_ok
-        elif block == blocks:
-            start, factor = jnp.minimum(start, width_all - 2 * LANES), right_ok
-        place = slice((block + 1) * LANES, (block + 2) * LANES)
-        cols = slice(block * LANES, (block + 1) * LANES)
-        cell_cols = pl.ds(pl.multiple_of(lax.shift_right_arithmetic(start, 1), LANES), LANES)
+    def add_up(block, fine):
+        cols = pl.ds(pl.multiple_of(block * LANES, LANES), LANES)
         squares = [[], [], []]
         for i in range(cells):
-            bands = haar_rows(*pixels_of(i, start))
+            bands = haar_rows(*pixels_of(i, block * 2 * LANES))
             for band in range(3):
                 squares[band].append(bands[band] * bands[band])
         for band in range(3):
             first = band * RADII * count
-            outer, inner = (
+            over, under = (
                 [
-                    halo[first + i * count : first + (i + 1) * count, cell_cols].astype(f32)
+                    halo[first + i * count : first + (i + 1) * count, cols].astype(f32)
                     for i in range(RADII)
                 ]
                 for halo in (above, below)
             )
-            column = outer + squares[band] + inner
-            if factor is not None:
-                column = [value * factor for value in column]
+            column = over + squares[band] + under
             for i in range(cells):
                 total = column[i + RADII]
                 at_row = (band * cells + i) * count
                 for radius in range(1, RADII + 1):
                     total = total + (column[i + RADII - radius] + column[i + RADII + radius])
                     upper = total.astype(bf16)
-                    sums[radius - 1, at_row : at_row + count, place] = upper
-                    if radius <= FINE and factor is None:
+                    sums[radius - 1, at_row : at_row + count, cols] = upper
+                    if radius <= FINE and fine:
                         lower = (total - upper.astype(f32)).astype(bf16)
                         rest[radius - 1, at_row : at_row + count, cols] = lower
 
-    for group in range(blocks // 2):
-        window = slice(2 * group * LANES, (2 * group + 4) * LANES)
+    for copy in inner:
+        copy.wait()
+
+    @pl.loop(1, blocks + 1)
+    def _(block):
+        add_up(block, True)
+
+    for copy in edges[0] + edges[1]:
+        copy.wait()
+
+    @pl.loop(0, 2)
+    def _(side):
+        add_up(side * (blocks + 1), False)
+
+    for side, outside in enumerate((base == 0, base + width == own_all.shape[1])):
+
+        @pl.when(outside)
+        def _():
+            at = side * (blocks + 1) * LANES
+            sums[:, :, at : at + LANES] = jnp.zeros(sums.shape[:2] + (LANES,), bf16)
+
+    late[0].wait()
+
+    @pl.loop(0, blocks // 2)
+    def _(group):
+        first = pl.multiple_of(group * 2 * LANES, 2 * LANES)
+        window = pl.ds(first, 4 * LANES)
+        middle = pl.ds(pl.multiple_of(first + LANES, LANES), 2 * LANES)
         for radius in range(1, RADII + 1):
-            narrow, weights = sums[radius - 1, :, window], box[radius - 1]
+            narrow, weights = sums[radius - 1, :, window], box_in[radius - 1]
             if radius <= FINE:
-                middle = slice(2 * group * LANES, (2 * group + 2) * LANES)
                 narrow = jnp.concatenate([narrow, rest[radius - 1, :, middle]], axis=1)
                 weights = jnp.concatenate([weights, weights[LANES : 3 * LANES]], axis=0)
             wide = jnp.dot(narrow, weights, preferred_element_type=f32)
             mean = wide * (1.0 / float((2 * radius + 1) ** 2))
             least[...] = mean if radius == 1 else jnp.minimum(least[...], mean)
+
         for half in range(2):
-            block = 2 * group + half
-            even = slice(2 * block * LANES, (2 * block + 1) * LANES)
-            odd = slice((2 * block + 1) * LANES, (2 * block + 2) * LANES)
+            start = pl.multiple_of((2 * group + half) * 2 * LANES, 2 * LANES)
+            even = pl.ds(start, LANES)
+            odd = pl.ds(pl.multiple_of(start + LANES, LANES), LANES)
             lanes = slice(half * LANES, (half + 1) * LANES)
             for i in range(cells):
-                top = slice(2 * i * count, (2 * i + 1) * count)
-                low = slice((2 * i + 1) * count, (2 * i + 2) * count)
-                pixels = pixels_of(i, base + block * 2 * LANES)
+                top, low = 2 * i * count, (2 * i + 1) * count
+                pixels = pixels_of(i, start + 2 * LANES)
                 bands = haar_rows(*pixels)
                 shrunk = []
                 for band in range(3):
                     at_row = (band * cells + i) * count
                     variance = least[at_row : at_row + count, lanes]
-                    gain = 1.0 / jnp.maximum(variance, 4.0 * noise_power)
-                    shrunk.append(bands[band] * (gain * noise_power))
+                    bound = jnp.maximum(variance, 4.0 * noise_power)
+                    shrunk.append(bands[band] * (noise_power * inverted(bound)))
                 horiz, vertic, diagon = shrunk
                 both, cross = vertic + diagon, vertic - diagon
                 noise = (horiz + both, horiz - both, cross - horiz, -horiz - cross)
-                for (rows_at, cols_at), pixel, part in zip(
-                    ((top, even), (top, odd), (low, even), (low, odd)), pixels, noise
+                for at, cols, pixel, part in zip(
+                    (top, top, low, low), (even, odd, even, odd), pixels, noise
                 ):
-                    start, stop = rows_at.start, rows_at.stop
                     upper, lower = halves(part.astype(bf16).astype(f32) * pixel)
-                    product[start:stop, cols_at] = upper
-                    product[size + start : size + stop, cols_at] = lower
-
-    for block in range(blocks):
-        cols = slice(2 * block * LANES, (2 * block + 2) * LANES)
-        there = pl.ds(pl.multiple_of(base + block * 2 * LANES, 2 * LANES), 2 * LANES)
-        weighted = jnp.dot(
-            select[:slot_rows, :], product[:, cols], preferred_element_type=f32
-        )
-        part = (weighted * inverse[:slot_rows, there]).astype(bf16)
-        out[:, cols] = jnp.dot(part, merge[...], preferred_element_type=f32).astype(bf16)
+                    product[at : at + count, cols] = upper
+                    product[size + at : size + at + count, cols] = lower
+
+    for copy in late[1:]:
+        copy.wait()
+
+    @pl.loop(0, blocks)
+    def _(block):
+        cols = pl.ds(pl.multiple_of(block * 2 * LANES, 2 * LANES), 2 * LANES)
+        weighted = jnp.dot(select_in[...], product[:, cols], preferred_element_type=f32)
+        part = (weighted * scale[:, cols]).astype(bf16)
+        out[:, cols] = jnp.dot(part, merge_in[...], preferred_element_type=f32).astype(bf16)
 
 
 def main_part(chunk, own, above, below, inverse, select, box, merge, rows, pieces, slots):
     size, width_all = own.shape
     count = size // rows
     width = width_all // pieces
+    halo = above.shape[0]
     cell_rows = 3 * (rows // 2) * count
-    vmem = pl.BlockSpec(memory_space=pltpu.VMEM)
-    smem = pl.BlockSpec(memory_space=pltpu.SMEM)
     return pl.pallas_call(
-        functools.partial(main_kernel, count, rows, width),
-        in_specs=[smem] + [vmem] * 7,
-        out_specs=vmem,
+        functools.partial(main_kernel, count, rows),
+        in_specs=[pl.BlockSpec(memory_space=pltpu.SMEM)] + [pl.BlockSpec(memory_space=pl.ANY)] * 7,
+        out_specs=pl.BlockSpec(memory_space=pltpu.VMEM),
         scratch_shapes=[
+            pltpu.VMEM((size, width + 4 * LANES), bf16),
+            pltpu.VMEM((halo, width // 2 + 2 * LANES), bf16),
+            pltpu.VMEM((halo, width // 2 + 2 * LANES), bf16),
             pltpu.VMEM((RADII, cell_rows, width // 2 + 2 * LANES), bf16),
-            pltpu.VMEM((FINE, cell_rows, width // 2), bf16),
+            pltpu.VMEM((FINE, cell_rows, width // 2 + 2 * LANES), bf16),
             pltpu.VMEM((cell_rows, 2 * LANES), f32),
             pltpu.VMEM((2 * size, width), bf16),
+            pltpu.VMEM((slots * rows, width), f32),
+            pltpu.VMEM((slots * rows, 2 * size), bf16),
+            pltpu.VMEM((RADII, 4 * LANES, 2 * LANES), bf16),
+            pltpu.VMEM((2 * LANES, 2 * LANES), bf16),
+            pltpu.SemaphoreType.DMA((9,)),
+            pltpu.SemaphoreType.DMA((4,)),
         ],
         out_shape=jax.ShapeDtypeStruct((slots * rows, width), bf16),
         compiler_params=pltpu.CompilerParams(vmem_limit_bytes=20 * 2**20),
@@ -400,26 +460,48 @@
     )(chunk, own, above, below, inverse, select, box, merge)
 
 
+def most_kernel(*refs):
+    notes, most = refs[:-1], refs[-1]
+    highest = notes[0][...].astype(f32)
+    for note in notes[1:]:
+        highest = jnp.maximum(highest, note[...].astype(f32))
+    most[0, 0] = jnp.max(highest[3:4]).astype(jnp.int32)
+
+
+def most_cameras(extras, rows):
+    return pl.pallas_call(
+        most_kernel,
+        grid=(1,),
+        in_specs=[pl.BlockSpec((rows, LANES), lambda i: (2, 0))] * len(extras),
+        out_specs=pl.BlockSpec(memory_space=pltpu.SMEM),
+        out_shape=jax.ShapeDtypeStruct((1, 1), jnp.int32),
+        compiler_params=pltpu.CompilerParams(vmem_limit_bytes=4 * 2**20),
+        name="most_cameras",
+    )(*extras)[0, 0]
+
+
 def assemble_kernel(rows, select, share, *refs):
     pieces = len(refs) - 4
-    parts, (prints, partial, flat, scaled) = refs[:pieces], refs[pieces:]
+    parts, (flat, partial, scaled, total) = refs[:pieces], refs[pieces:]
     size, width = parts[0].shape
     tall = CAMS * rows
     for place, part in enumerate(parts):
         edges = part[: 2 * rows, :].astype(f32) * share[place].reshape(2 * rows, width)
         scaled[place, : 2 * rows, :] = edges.astype(bf16)
-    total = jnp.zeros((tall, 1), f32)
-    for block in range(width // (2 * LANES)):
-        cols = slice(block * 2 * LANES, (block + 1) * 2 * LANES)
+    total[...] = jnp.zeros((tall, LANES), f32)
+
+    @pl.loop(0, width // (2 * LANES))
+    def _(block):
+        cols = pl.ds(pl.multiple_of(block * 2 * LANES, 2 * LANES), 2 * LANES)
         joined = jnp.zeros((tall, 2 * LANES), f32)
         for place, part in enumerate(parts):
             source = jnp.concatenate([scaled[place, :, cols], part[2 * rows :, cols]], axis=0)
             joined = joined + jnp.dot(
                 select[place, :, :size], source, preferred_element_type=f32
             )
-        prints[:, :, cols] = joined.reshape(CAMS, rows, 2 * LANES)
         flat[:, cols] = joined.astype(bf16)
-        total = total + jnp.sum(joined, axis=1, keepdims=True)
+        total[...] += joined[:, :LANES] + joined[:, LANES:]
+
     gram = lax.dot_general(
         flat[...], flat[...], (((1,), (1,)), ((), ())), preferred_element_type=f32
     )
@@ -431,9 +513,10 @@
     lane = lax.broadcasted_iota(jnp.int32, (tall, LANES), 1)
     gather = jnp.where((sub >> log2(rows)) == lane, 1.0, 0.0).astype(f32)
     gram = jnp.dot(gram, gather, precision=lax.Precision.HIGHEST, preferred_element_type=f32)
-    total = jnp.sum(total.reshape(CAMS, rows, 1), axis=1)
+    sums = jnp.sum(total[...], axis=1, keepdims=True)
+    sums = jnp.sum(sums.reshape(CAMS, rows, 1), axis=1)
     lane = lax.broadcasted_iota(jnp.int32, (CAMS, LANES), 1)
-    partial[...] = jnp.where(lane == CAMS, total, gram)
+    partial[...] = jnp.where(lane == CAMS, sums, gram)
 
 
 def assemble(select, share, parts, rows):
@@ -441,12 +524,12 @@
     return pl.pallas_call(
         functools.partial(assemble_kernel, rows),
         out_shape=[
-            jax.ShapeDtypeStruct((CAMS, rows, width), f32),
+            jax.ShapeDtypeStruct((CAMS * rows, width), bf16),
             jax.ShapeDtypeStruct((CAMS, LANES), f32),
         ],
         scratch_shapes=[
-            pltpu.VMEM((CAMS * rows, width), bf16),
             pltpu.VMEM((len(parts), 2 * rows, width), bf16),
+            pltpu.VMEM((CAMS * rows, LANES), f32),
         ],
         compiler_params=pltpu.CompilerParams(vmem_limit_bytes=20 * 2**20),
         cost_estimate=pl.CostEstimate(
@@ -478,6 +561,7 @@
     return pl.pallas_call(
         functools.partial(correlate_kernel, pixels),
         out_shape=jax.ShapeDtypeStruct((CAMS, CAMS), f32),
+        compiler_params=pltpu.CompilerParams(vmem_limit_bytes=4 * 2**20),
         name="correlate",
     )(*parts)
 
@@ -485,6 +569,13 @@
 def exchange(array, axis, distance):
     size = lax.axis_size(axis)
     return lax.ppermute(array, axis, [(i, i ^ distance) for i in range(size)])
+
+
+def summed(array, axis, distances):
+    terms = [array] + [exchange(array, axis, distance) for distance in distances]
+    while len(terms) > 1:
+        terms = [terms[i] + terms[i + 1] for i in range(0, len(terms), 2)]
+    return terms[0]
 
 
 def on_device(photos, camera_id):
@@ -499,7 +590,6 @@
         for distance, extra in enumerate(extras)
     ]
     inverse, select, box, merge = energies(camera_id, own, rows)
-    place, share, most = blend(me.reshape(1), extras, rows, count * rows)
 
     def finish(slots):
         parts = [None] * pieces
@@ -509,22 +599,20 @@
                 rows, pieces, slots,
             )
             parts[distance] = exchange(part, "photo", distance) if distance else part
+        place, share = blend(me.reshape(1), extras, rows, count * rows)
         return assemble(place, share, parts, rows)
 
-    few = max(2, 3 * count // 4)
-    prints, partial = lax.cond(
-        most[0, 0] > few, lambda: finish(count), lambda: finish(few)
-    )
-    terms = [partial] + [exchange(partial, "photo", i) for i in range(1, pieces)]
-    while len(terms) > 1:
-        terms = [terms[i] + terms[i + 1] for i in range(0, len(terms), 2)]
-    total = terms[0]
-    distance = 1
-    while 2 * distance < tiles:
-        total = total + exchange(total, "tile", distance)
-        distance *= 2
-    sums = [total, exchange(total, "tile", distance)]
-    return prints, correlate(sums, float(rows * tiles * width))
+    most = most_cameras(extras, rows)
+    sizes = sorted({max(2, count * part // 16) for part in (10, 12, 16)})
+    branch = sum((most > size).astype(jnp.int32) for size in sizes[:-1])
+    flat, partial = lax.switch(branch, [functools.partial(finish, size) for size in sizes])
+    flat, partial = lax.optimization_barrier((flat, partial))
+    prints = flat.reshape(CAMS, rows, width // pieces).astype(f32)
+
+    total = summed(partial, "tile", (1,))
+    total = summed(total, "photo", range(1, pieces))
+    total = summed(total, "tile", range(2, tiles, 2))
+    return prints, correlate([total], float(rows * tiles * width))
 
 
 def solution(mesh):

time: 79.3 us -> 78.1 us (0.985)
  waiting for transfers between devices: 15.9 us -> 9.42 us
  other arithmetic: 0.02 us -> 2.82 us
  Pallas kernels: 37.8 us -> 40.5 us
  starting transfers between devices: 20.9 us -> 19.5 us
    ppermute x12 -> x13, waiting for transfers between devices: 15.9 us -> 9.42 us  [exchange(): return lax.ppermute(array, axis, [(i, i ^ distance) for i in range(size)])]
    pallas_call x1, Pallas kernels: 3.1 us -> 6.28 us  [prepare(): pl.pallas_call(prepare_kernel, in_specs=[smem, smem, pl.BlockSpec(memory_...]
    convert_element_type x0 -> x1, other arithmetic: none -> 2.8 us  [on_device(): prints = flat.reshape(CAMS, rows, width // pieces).astype(f32)]
    pallas_call x1, Pallas kernels: 4.39 us -> 7.01 us  [energies(): pl.pallas_call(functools.partial(energy_kernel, size // rows, rows), in_s...]
    pallas_call x4 -> x5, Pallas kernels: 24.7 us -> 23.1 us  [the longest x4 21.8 us: main_part(): pl.pallas_call(functools.partial(main_kernel, count, rows), in_specs=[pl....]
    pallas_call x1, Pallas kernels: 1.57 us -> 0.42 us  [blend(): pl.pallas_call(functools.partial(blend_kernel, rows), in_specs=[smem] + [...]
    ppermute x1, starting transfers between devices: 3.24 us -> 2.4 us  [on_device(): above = lax.ppermute(down, 'tile', [(i, i + 1) for i in range(tiles - 1)])]
    unnamed x8 -> x4, local copies, waits for them, and re-layouts: 2.84 us -> 2.24 us
  transfers between devices with their start and end apart: 14 -> 15, of which waited for: 8 -> 5; matrix products, arithmetic and copies ran while one was open for 0% -> 4% of each run, Pallas kernels for 30% -> 32%
where the time goes in v4:
time: 78.1 us; the launch traced here: 77.7 us
  Pallas kernels  40.5 us (52%)
  starting transfers between devices  19.5 us (25%)
  waiting for transfers between devices  9.42 us (12%)
  local copies, waits for them, and re-layouts  3.05 us (4%)
  other arithmetic  2.82 us (4%)
  between operations  2.03 us (3%)
    pallas_call x4, Pallas kernels, main_part(): pl.pallas_call(functools.partial(main_kernel, count, rows), in_specs=[pl....  21.8 us
    ppermute x13, starting transfers between devices, exchange(): return lax.ppermute(array, axis, [(i, i ^ distance) for i in range(size)])  15.8 us
    ppermute x13, waiting for transfers between devices, exchange(): return lax.ppermute(array, axis, [(i, i ^ distance) for i in range(size)])  9.42 us
    pallas_call x1, Pallas kernels, energies(): pl.pallas_call(functools.partial(energy_kernel, size // rows, rows), in_s...  7.01 us
    pallas_call x1, Pallas kernels, prepare(): pl.pallas_call(prepare_kernel, in_specs=[smem, smem, pl.BlockSpec(memory_...  6.28 us
    pallas_call x1, Pallas kernels, assemble(): pl.pallas_call(functools.partial(assemble_kernel, rows), out_shape=[jax.S...  2.86 us
    convert_element_type x1, other arithmetic, on_device(): prints = flat.reshape(CAMS, rows, width // pieces).astype(f32)  2.8 us
    ppermute x1, starting transfers between devices, on_device(): above = lax.ppermute(down, 'tile', [(i, i + 1) for i in range(tiles - 1)])  2.4 us
  transfers between devices with their start and end apart: 15, of which 5 were waited for; matrix products, arithmetic and copies ran while one was open for 4% of the time, Pallas kernels for 32%

profile of v4, /device:TPU:0, one launch (start us, length us, event | category | flops | bytes accessed | tf_op | source)
XLA Modules:
  0.0 77.7 jit_solution(17031297207291256061)
XLA Ops:
  0.6 1.6 %copy-done = bf16[16,16,4096]{2,1,0:T(8,128)(2,1)S(1)} copy-done((bf16[16,16,4096]{2,1,0:T(8,128)(2,1)S(1)}, bf16[16,16,4096]{2,1,0:T(8,128)(2,1)}, u32[]{:S(2)}) %copy-start) | copy-done | bytes 2097176
  2.2 0.7 copy-done.1
  2.9 6.3 %prepare.1 = (bf16[256,4096]{1,0:T(8,128)(2,1)S(1)}, bf16[192,2048]{1,0:T(8,128)(2,1)S(1)}, bf16[192,2048]{1,0:T(8,128)(2,1)S(1)}, bf16[48,1024]{1,0:T(8,128)(2,...) custom-call(s32[1]{0:T(128)} %bitcast.12.me, s32[16]{0:T(128)S(1)} %copy-done.1, ...), custom_call_target="tpu_custom_call" | custom-call | flops 1000000000 | bytes 8388608 | tf_op jit(solution)/shard_map/prepare/pallas_call | solution.py:162
  9.2 2.4 %collective-permute-start.12 = (bf16[192,2048]{1,0:T(8,128)(2,1)S(1)}, bf16[192,2048]{1,0:T(8,128)(2,1)S(1)}, u32[]{:S(2)}, u32[]{:S(2)}) collective-permute-start(bf16[192,2048]{1,0:T(8,128)(2,1)S(1)} %get-tuple-element.134), channel_id=1, source_target_pairs={{0,1},{1,2},{2,3},{3,4},{4,5},{5,6},{6,7},{8,9},{9,10},{10,11},{11... | collective-permute-start | bytes 2359304 | tf_op jit(solution)/shard_map/ppermute | solution.py:586
  11.6 1.3 %collective-permute-start.13 = (bf16[192,2048]{1,0:T(8,128)(2,1)S(1)}, bf16[192,2048]{1,0:T(8,128)(2,1)}, u32[]{:S(2)}, u32[]{:S(2)}) collective-permute-start(bf16[192,2048]{1,0:T(8,128)(2,1)S(1)} %get-tuple-element.135), channel_id=1, source_target_pairs={{1,0},{2,1},{3,2},{4,3},{5,4},{6,5},{7,6},{9,8},{10,9},{11,10},{12... | collective-permute-start | bytes 2359304 | tf_op jit(solution)/shard_map/ppermute | solution.py:587
  12.9 2.3 %collective-permute-start.9 = (bf16[48,1024]{1,0:T(8,128)(2,1)S(1)}, bf16[48,1024]{1,0:T(8,128)(2,1)S(1)}, u32[]{:S(2)}, u32[]{:S(2)}) collective-permute-start(bf16[48,1024]{1,0:T(8,128)(2,1)S(1)} %get-tuple-element.130), channel_id=1, source_target_pairs={{0,8},{8,0},{16,24},{24,16},{1,9},{9,1},{17,25},{25,17},{2,10},{10... | collective-permute-start | bytes 294920 | tf_op jit(solution)/shard_map/ppermute | solution.py:571
  15.1 1.7 %collective-permute-start.10 = (bf16[48,1024]{1,0:T(8,128)(2,1)S(1)}, bf16[48,1024]{1,0:T(8,128)(2,1)S(1)}, u32[]{:S(2)}, u32[]{:S(2)}) collective-permute-start(bf16[48,1024]{1,0:T(8,128)(2,1)S(1)} %get-tuple-element.131), channel_id=1, source_target_pairs={{0,16},{8,24},{16,0},{24,8},{1,17},{9,25},{17,1},{25,9},{2,18},{10... | collective-permute-start | bytes 294920 | tf_op jit(solution)/shard_map/ppermute | solution.py:571
  16.8 7.0 %energies.1 = (f32[256,4096]{1,0:T(8,128)}, bf16[256,512]{1,0:T(8,128)(2,1)S(1)}, bf16[4,512,256]{2,1,0:T(8,128)(2,1)}, bf16[256,256]{1,0:T(8,128)(2,1)}) custom-call(s32[16]{0:T(128)S(1)} %copy-done.1, bf16[256,4096]{1,0:T(8,128)(2,1)S(1)} %get-tuple-element.133.own), custom_call_target="tpu_custom_call" | custom-call | flops 1000000000 | bytes 8388608 | tf_op jit(solution)/shard_map/energies/pallas_call | solution.py:213
  23.9 1.3 %most_cameras.1 = s32[1,1]{1,0:T(1,128)} custom-call(bf16[48,1024]{1,0:T(8,128)(2,1)} %get-tuple-element.129.refs_0_, bf16[48,1024]{1,0:T(8,128)(2,1)S(1)} %collective-permute-done.9.refs_1_, bf16[48,1024]{1,0:T(8,128)(2,1)S(1)} %collective-permute-done.10.refs_2_, bf16[48,1024]{1,0:T(8,128)(2,1)S(1)} %collective-permute-done.11.refs_3_), custom_call_target="tpu_custom_call" | custom-call | tf_op jit(solution)/shard_map/most_cameras/pallas_call | solution.py:472
  26.5 35.5 %conditional.1 = ((bf16[512,1024]{1,0:T(8,128)(2,1)}, f32[32,128]{1,0:T(8,128)S(1)})) conditional(s32[]{:T(128)} %bitcast.13, (s32[]{:T(128)}, bf16[48,1024]{1,0:T(8,128)(2,1)}, bf16[48,1024]{1,0:T(8,128)(2,1)S(1)}, bf16[48,1024]{1,0:T(8,128)(2,1)S(1)}, bf16[48,1024]{1,0:T(8,128)(2,1)S(1)}, ...), branch_computations={%region_0.0_spmd, %region_1.0_spmd, %region_2.0_spmd} | conditional | flops 10000000000 | bytes 76677728 | solution.py:608
  26.6 0.6 copy-done.30
  27.2 0.1 copy-done.18
  27.3 5.3 %residual.13 = bf16[160,1024]{1,0:T(8,128)(2,1)S(1)} custom-call(s32[1]{0:T(128)} %bitcast.1.chunk, bf16[256,4096]{1,0:T(8,128)(2,1)S(1)} %get-tuple-element.79.own_all, bf16[192,2048]{1,0:T(8,128)(2,1)S(1)} %get-tuple-element.80.above_all, bf16[192,2048]{1,0:T(8,128)(2,1)} %get-tuple-element.81.below_all, f32[256,4096]{1,0:T(8,128)} %get-tuple-element.82.inverse, ...), custom_call_target="tpu_custom_call" | custom-call | flops 2000000000 | bytes 4194304 | tf_op jit(solution)/shard_map/cond/branch_0_fun/residual/pallas_call | solution.py:435
  32.7 1.9 %collective-permute-start = (bf16[160,1024]{1,0:T(8,128)(2,1)S(1)}, bf16[160,1024]{1,0:T(8,128)(2,1)S(1)}, u32[]{:S(2)}, u32[]{:S(2)}) collective-permute-start(bf16[160,1024]{1,0:T(8,128)(2,1)S(1)} %residual.13), channel_id=1, source_target_pairs={{0,8},{8,0},{16,24},{24,16},{1,9},{9,1},{17,25},{25,17},{2,10},{10... | collective-permute-start | bytes 983048 | tf_op jit(solution)/shard_map/cond/branch_0_fun/ppermute | solution.py:571
  34.6 5.4 %residual.14 = bf16[160,1024]{1,0:T(8,128)(2,1)S(1)} custom-call(s32[1]{0:T(128)} %bitcast.2.chunk, bf16[256,4096]{1,0:T(8,128)(2,1)S(1)} %get-tuple-element.79.own_all, bf16[192,2048]{1,0:T(8,128)(2,1)} %copy-done.12, bf16[192,2048]{1,0:T(8,128)(2,1)} %get-tuple-element.81.below_all, f32[256,4096]{1,0:T(8,128)} %get-tuple-element.82.inverse, ...), custom_call_target="tpu_custom_call" | custom-call | flops 2000000000 | bytes 4194304 | tf_op jit(solution)/shard_map/cond/branch_0_fun/residual/pallas_call | solution.py:435
  40.0 1.8 %collective-permute-start.1 = (bf16[160,1024]{1,0:T(8,128)(2,1)S(1)}, bf16[160,1024]{1,0:T(8,128)(2,1)S(1)}, u32[]{:S(2)}, u32[]{:S(2)}) collective-permute-start(bf16[160,1024]{1,0:T(8,128)(2,1)S(1)} %residual.14), channel_id=1, source_target_pairs={{0,16},{8,24},{16,0},{24,8},{1,17},{9,25},{17,1},{25,9},{2,18},{10... | collective-permute-start | bytes 983048 | tf_op jit(solution)/shard_map/cond/branch_0_fun/ppermute | solution.py:571
  41.9 5.6 %residual.15 = bf16[160,1024]{1,0:T(8,128)(2,1)S(1)} custom-call(s32[1]{0:T(128)} %bitcast.3.chunk, bf16[256,4096]{1,0:T(8,128)(2,1)S(1)} %get-tuple-element.79.own_all, bf16[192,2048]{1,0:T(8,128)(2,1)} %copy-done.12, bf16[192,2048]{1,0:T(8,128)(2,1)} %get-tuple-element.81.below_all, f32[256,4096]{1,0:T(8,128)} %get-tuple-element.82.inverse, ...), custom_call_target="tpu_custom_call" | custom-call | flops 2000000000 | bytes 4194304 | tf_op jit(solution)/shard_map/cond/branch_0_fun/residual/pallas_call | solution.py:435
  47.6 0.4 blend.3
  48.1 5.4 %residual.12.refs_0_ = bf16[160,1024]{1,0:T(8,128)(2,1)S(1)} custom-call(s32[1]{0:T(128)} %bitcast.me.chunk, bf16[256,4096]{1,0:T(8,128)(2,1)S(1)} %get-tuple-element.79.own_all, bf16[192,2048]{1,0:T(8,128)(2,1)S(1)} %copy-done.13, bf16[192,2048]{1,0:T(8,128)(2,1)} %get-tuple-element.81.below_all, f32[256,4096]{1,0:T(8,128)S(1)} %copy-done.2, ...), custom_call_target="tpu_custom_call" | custom-call | flops 2000000000 | bytes 4194304 | tf_op jit(solution)/shard_map/cond/branch_0_fun/residual/pallas_call | solution.py:435
  53.5 5.5 %collective-permute-done.2.refs_3_ = bf16[160,1024]{1,0:T(8,128)(2,1)S(1)} collective-permute-done((bf16[160,1024]{1,0:T(8,128)(2,1)S(1)}, bf16[160,1024]{1,0:T(8,128)(2,1)S(1)}, u32[]{:S(2)}, u32[]{:S(2)}) %collective-permute-start.2) | collective-permute-done | bytes 327712 | tf_op jit(solution)/shard_map/cond/branch_0_fun/ppermute | solution.py:571
  59.0 2.9 %assemble.3 = (bf16[512,1024]{1,0:T(8,128)(2,1)}, f32[32,128]{1,0:T(8,128)S(1)}) custom-call(bf16[4,512,256]{2,1,0:T(8,128)(2,1)S(1)} %get-tuple-element.77.select, f32[4,2,16,1024]{3,2,1,0:T(8,128)S(1)} %get-tuple-element.78.share, bf16[160,1024]{1,0:T(8,128)(2,1)S(1)} %residual.12.refs_0_, bf16[160,1024]{1,0:T(8,128)(2,1)S(1)} %collective-permute-done.refs_1_, ...), custom_call_target="tpu_custom_call" | custom-call | flops 2000000000 | bytes 4194304 | tf_op jit(solution)/shard_map/cond/branch_0_fun/assemble/pallas_call | solution.py:524
  62.1 0.2 collective-permute-start.14
  62.2 1.1 %collective-permute-done.14 = f32[32,128]{1,0:T(8,128)S(1)} collective-permute-done((f32[32,128]{1,0:T(8,128)S(1)}, f32[32,128]{1,0:T(8,128)S(1)}, u32[]{:S(2)}, u32[]{:S(2)}) %collective-permute-start.14) | collective-permute-done | bytes 16416 | tf_op jit(solution)/shard_map/ppermute | solution.py:571
  63.3 1.8 %collective-permute-start.16 = (f32[32,128]{1,0:T(8,128)S(1)}, f32[32,128]{1,0:T(8,128)S(1)}, u32[]{:S(2)}, u32[]{:S(2)}) collective-permute-start(f32[32,128]{1,0:T(8,128)S(1)} %add.26), channel_id=1, source_target_pairs={{0,16},{8,24},{16,0},{24,8},{1,17},{9,25},{17,1},{25,9},{2,18},{10... | collective-permute-start | bytes 49160 | tf_op jit(solution)/shard_map/ppermute | solution.py:571
  65.1 1.7 %collective-permute-start.15 = (f32[32,128]{1,0:T(8,128)S(1)}, f32[32,128]{1,0:T(8,128)S(1)}, u32[]{:S(2)}, u32[]{:S(2)}) collective-permute-start(f32[32,128]{1,0:T(8,128)S(1)} %add.26), channel_id=1, source_target_pairs={{0,8},{8,0},{16,24},{24,16},{1,9},{9,1},{17,25},{25,17},{2,10},{10... | collective-permute-start | bytes 49160 | tf_op jit(solution)/shard_map/ppermute | solution.py:571
  66.8 1.1 %collective-permute-done.17 = f32[32,128]{1,0:T(8,128)S(1)} collective-permute-done((f32[32,128]{1,0:T(8,128)S(1)}, f32[32,128]{1,0:T(8,128)S(1)}, u32[]{:S(2)}, u32[]{:S(2)}) %collective-permute-start.17) | collective-permute-done | bytes 16416 | tf_op jit(solution)/shard_map/ppermute | solution.py:571
  68.0 0.9 %collective-permute-done.15 = f32[32,128]{1,0:T(8,128)S(1)} collective-permute-done((f32[32,128]{1,0:T(8,128)S(1)}, f32[32,128]{1,0:T(8,128)S(1)}, u32[]{:S(2)}, u32[]{:S(2)}) %collective-permute-start.15) | collective-permute-done | bytes 16416 | tf_op jit(solution)/shard_map/ppermute | solution.py:571
  68.8 3.5 %collective-permute-start.20 = (f32[32,128]{1,0:T(8,128)S(1)}, f32[32,128]{1,0:T(8,128)S(1)}, u32[]{:S(2)}, u32[]{:S(2)}) collective-permute-start(f32[32,128]{1,0:T(8,128)S(1)} %add_add_fusion.1), channel_id=1, source_target_pairs={{0,6},{1,7},{2,4},{3,5},{4,2},{5,3},{6,0},{7,1},{8,14},{9,15},{10,... | collective-permute-start | bytes 49160 | tf_op jit(solution)/shard_map/ppermute | solution.py:571
  72.3 1.0 %collective-permute-start.18 = (f32[32,128]{1,0:T(8,128)S(1)}, f32[32,128]{1,0:T(8,128)S(1)}, u32[]{:S(2)}, u32[]{:S(2)}) collective-permute-start(f32[32,128]{1,0:T(8,128)S(1)} %add_add_fusion.1), channel_id=1, source_target_pairs={{0,2},{1,3},{2,0},{3,1},{4,6},{5,7},{6,4},{7,5},{8,10},{9,11},{10,... | collective-permute-start | bytes 49160 | tf_op jit(solution)/shard_map/ppermute | solution.py:571
  73.3 2.8 %convert.1 = f32[32,16,1024]{2,1,0:T(8,128)} convert(bf16[32,16,1024]{2,1,0:T(8,128)(2,1)} %bitcast.15) | non-fusion elementwise | flops 524288 | bytes 3145728 | tf_op jit(solution)/shard_map/convert_element_type | solution.py:610
  76.1 0.9 %collective-permute-done.19 = f32[32,128]{1,0:T(8,128)S(1)} collective-permute-done((f32[32,128]{1,0:T(8,128)S(1)}, f32[32,128]{1,0:T(8,128)S(1)}, u32[]{:S(2)}, u32[]{:S(2)}) %collective-permute-start.19) | collective-permute-done | bytes 16416 | tf_op jit(solution)/shard_map/ppermute | solution.py:571
  76.9 0.8 %correlate.1 = f32[32,32]{1,0:T(8,128)} custom-call(f32[32,128]{1,0:T(8,128)S(1)} %add_add_fusion.refs_0_), custom_call_target="tpu_custom_call" | custom-call | tf_op jit(solution)/shard_map/correlate/pallas_call | solution.py:561
  (45 shorter events, 0.3 us)
Async XLA Ops:
  0.6 1.6 %copy-start = (bf16[16,16,4096]{2,1,0:T(8,128)(2,1)S(1)}, bf16[16,16,4096]{2,1,0:T(8,128)(2,1)}, u32[]{:S(2)}) copy-start(bf16[16,16,4096]{2,1,0:T(8,128)(2,1)} %photos.1) | copy-start | bytes 6291460
  2.2 0.7 copy-start.1
  9.2 17.3 %collective-permute-start.12 = (bf16[192,2048]{1,0:T(8,128)(2,1)S(1)}, bf16[192,2048]{1,0:T(8,128)(2,1)S(1)}, u32[]{:S(2)}, u32[]{:S(2)}) collective-permute-start(bf16[192,2048]{1,0:T(8,128)(2,1)S(1)} %get-tuple-element.134), channel_id=1, source_target_pairs={{0,1},{1,2},{2,3},{3,4},{4,5},{5,6},{6,7},{8,9},{9,10},{10,11},{11... | collective-permute-start | bytes 2359304 | tf_op jit(solution)/shard_map/ppermute | solution.py:586
  11.6 14.9 %collective-permute-start.13 = (bf16[192,2048]{1,0:T(8,128)(2,1)S(1)}, bf16[192,2048]{1,0:T(8,128)(2,1)}, u32[]{:S(2)}, u32[]{:S(2)}) collective-permute-start(bf16[192,2048]{1,0:T(8,128)(2,1)S(1)} %get-tuple-element.135), channel_id=1, source_target_pairs={{1,0},{2,1},{3,2},{4,3},{5,4},{6,5},{7,6},{9,8},{10,9},{11,10},{12... | collective-permute-start | bytes 2359304 | tf_op jit(solution)/shard_map/ppermute | solution.py:587
  12.9 11.0 %collective-permute-start.9 = (bf16[48,1024]{1,0:T(8,128)(2,1)S(1)}, bf16[48,1024]{1,0:T(8,128)(2,1)S(1)}, u32[]{:S(2)}, u32[]{:S(2)}) collective-permute-start(bf16[48,1024]{1,0:T(8,128)(2,1)S(1)} %get-tuple-element.130), channel_id=1, source_target_pairs={{0,8},{8,0},{16,24},{24,16},{1,9},{9,1},{17,25},{25,17},{2,10},{10... | collective-permute-start | bytes 294920 | tf_op jit(solution)/shard_map/ppermute | solution.py:571
  15.1 8.7 %collective-permute-start.10 = (bf16[48,1024]{1,0:T(8,128)(2,1)S(1)}, bf16[48,1024]{1,0:T(8,128)(2,1)S(1)}, u32[]{:S(2)}, u32[]{:S(2)}) collective-permute-start(bf16[48,1024]{1,0:T(8,128)(2,1)S(1)} %get-tuple-element.131), channel_id=1, source_target_pairs={{0,16},{8,24},{16,0},{24,8},{1,17},{9,25},{17,1},{25,9},{2,18},{10... | collective-permute-start | bytes 294920 | tf_op jit(solution)/shard_map/ppermute | solution.py:571
  16.8 7.0 %collective-permute-start.11 = (bf16[48,1024]{1,0:T(8,128)(2,1)S(1)}, bf16[48,1024]{1,0:T(8,128)(2,1)S(1)}, u32[]{:S(2)}, u32[]{:S(2)}) collective-permute-start(bf16[48,1024]{1,0:T(8,128)(2,1)S(1)} %get-tuple-element.132), channel_id=1, source_target_pairs={{0,24},{8,16},{16,8},{24,0},{1,25},{9,17},{17,9},{25,1},{2,26},{10... | collective-permute-start | bytes 294920 | tf_op jit(solution)/shard_map/ppermute | solution.py:571
  26.5 0.6 copy-start.30
  26.5 0.7 copy-start.36
  26.5 0.7 copy-start.42
  26.5 0.8 %copy-start.18 = (bf16[256,512]{1,0:T(8,128)(2,1)}, bf16[256,512]{1,0:T(8,128)(2,1)S(1)}, u32[]{:S(2)}) copy-start(bf16[256,512]{1,0:T(8,128)(2,1)S(1)} %get-tuple-element.83.select) | copy-start | bytes 786436 | tf_op jit(solution)/shard_map/cond
  26.6 8.0 %copy-start.12 = (bf16[192,2048]{1,0:T(8,128)(2,1)}, bf16[192,2048]{1,0:T(8,128)(2,1)S(1)}, u32[]{:S(2)}) copy-start(bf16[192,2048]{1,0:T(8,128)(2,1)S(1)} %get-tuple-element.80.above_all) | copy-start | bytes 2359300 | tf_op jit(solution)/shard_map/cond
  32.7 20.8 %collective-permute-start = (bf16[160,1024]{1,0:T(8,128)(2,1)S(1)}, bf16[160,1024]{1,0:T(8,128)(2,1)S(1)}, u32[]{:S(2)}, u32[]{:S(2)}) collective-permute-start(bf16[160,1024]{1,0:T(8,128)(2,1)S(1)} %residual.13), channel_id=1, source_target_pairs={{0,8},{8,0},{16,24},{24,16},{1,9},{9,1},{17,25},{25,17},{2,10},{10... | collective-permute-start | bytes 983048 | tf_op jit(solution)/shard_map/cond/branch_0_fun/ppermute | solution.py:571
  34.6 7.2 %copy-start.24 = (bf16[256,256]{1,0:T(8,128)(2,1)S(1)}, bf16[256,256]{1,0:T(8,128)(2,1)}, u32[]{:S(2)}) copy-start(bf16[256,256]{1,0:T(8,128)(2,1)} %get-tuple-element.85.merge) | copy-start | bytes 393220 | tf_op jit(solution)/shard_map/cond
  40.0 13.5 %collective-permute-start.1 = (bf16[160,1024]{1,0:T(8,128)(2,1)S(1)}, bf16[160,1024]{1,0:T(8,128)(2,1)S(1)}, u32[]{:S(2)}, u32[]{:S(2)}) collective-permute-start(bf16[160,1024]{1,0:T(8,128)(2,1)S(1)} %residual.14), channel_id=1, source_target_pairs={{0,16},{8,24},{16,0},{24,8},{1,17},{9,25},{17,1},{25,9},{2,18},{10... | collective-permute-start | bytes 983048 | tf_op jit(solution)/shard_map/cond/branch_0_fun/ppermute | solution.py:571
  41.8 5.8 %copy-start.27 = (bf16[48,1024]{1,0:T(8,128)(2,1)S(1)}, bf16[48,1024]{1,0:T(8,128)(2,1)}, u32[]{:S(2)}) copy-start(bf16[48,1024]{1,0:T(8,128)(2,1)} %get-tuple-element.73.refs_0_) | copy-start | bytes 294916 | tf_op jit(solution)/shard_map/cond
  41.8 5.8 %copy-start.31 = (bf16[48,1024]{1,0:T(8,128)(2,1)S(1)}, bf16[48,1024]{1,0:T(8,128)(2,1)}, u32[]{:S(2)}) copy-start(bf16[48,1024]{1,0:T(8,128)(2,1)} %copy-done.30) | copy-start | bytes 294916 | tf_op jit(solution)/shard_map/cond
  41.8 5.8 %copy-start.37 = (bf16[48,1024]{1,0:T(8,128)(2,1)S(1)}, bf16[48,1024]{1,0:T(8,128)(2,1)}, u32[]{:S(2)}) copy-start(bf16[48,1024]{1,0:T(8,128)(2,1)} %copy-done.36) | copy-start | bytes 294916 | tf_op jit(solution)/shard_map/cond
  41.8 5.8 %copy-start.43 = (bf16[48,1024]{1,0:T(8,128)(2,1)S(1)}, bf16[48,1024]{1,0:T(8,128)(2,1)}, u32[]{:S(2)}) copy-start(bf16[48,1024]{1,0:T(8,128)(2,1)} %copy-done.42) | copy-start | bytes 294916 | tf_op jit(solution)/shard_map/cond
  41.8 6.2 %copy-start.2 = (f32[256,4096]{1,0:T(8,128)S(1)}, f32[256,4096]{1,0:T(8,128)}, u32[]{:S(2)}) copy-start(f32[256,4096]{1,0:T(8,128)} %get-tuple-element.82.inverse) | copy-start | bytes 12582916 | tf_op jit(solution)/shard_map/cond
  41.8 6.2 %copy-start.9 = (bf16[4,512,256]{2,1,0:T(8,128)(2,1)S(1)}, bf16[4,512,256]{2,1,0:T(8,128)(2,1)}, u32[]{:S(2)}) copy-start(bf16[4,512,256]{2,1,0:T(8,128)(2,1)} %get-tuple-element.84.box) | copy-start | bytes 3145732 | tf_op jit(solution)/shard_map/cond
  41.8 6.2 %copy-start.13 = (bf16[192,2048]{1,0:T(8,128)(2,1)S(1)}, bf16[192,2048]{1,0:T(8,128)(2,1)}, u32[]{:S(2)}) copy-start(bf16[192,2048]{1,0:T(8,128)(2,1)} %copy-done.12) | copy-start | bytes 2359300 | tf_op jit(solution)/shard_map/cond
  41.9 6.2 %copy-start.19 = (bf16[256,512]{1,0:T(8,128)(2,1)S(1)}, bf16[256,512]{1,0:T(8,128)(2,1)}, u32[]{:S(2)}) copy-start(bf16[256,512]{1,0:T(8,128)(2,1)} %copy-done.18) | copy-start | bytes 786436 | tf_op jit(solution)/shard_map/cond
  47.5 11.5 %collective-permute-start.2 = (bf16[160,1024]{1,0:T(8,128)(2,1)S(1)}, bf16[160,1024]{1,0:T(8,128)(2,1)S(1)}, u32[]{:S(2)}, u32[]{:S(2)}) collective-permute-start(bf16[160,1024]{1,0:T(8,128)(2,1)S(1)} %residual.15), channel_id=1, source_target_pairs={{0,24},{8,16},{16,8},{24,0},{1,25},{9,17},{17,9},{25,1},{2,26},{10... | collective-permute-start | bytes 983048 | tf_op jit(solution)/shard_map/cond/branch_0_fun/ppermute | solution.py:571
  62.1 1.2 %collective-permute-start.14 = (f32[32,128]{1,0:T(8,128)S(1)}, f32[32,128]{1,0:T(8,128)S(1)}, u32[]{:S(2)}, u32[]{:S(2)}) collective-permute-start(f32[32,128]{1,0:T(8,128)S(1)} %get-tuple-element.141), channel_id=1, source_target_pairs={{0,1},{1,0},{2,3},{3,2},{4,5},{5,4},{6,7},{7,6},{8,9},{9,8},{10,11... | collective-permute-start | bytes 49160 | tf_op jit(solution)/shard_map/ppermute | solution.py:571
  63.3 4.6 %collective-permute-start.17 = (f32[32,128]{1,0:T(8,128)S(1)}, f32[32,128]{1,0:T(8,128)S(1)}, u32[]{:S(2)}, u32[]{:S(2)}) collective-permute-start(f32[32,128]{1,0:T(8,128)S(1)} %add.26), channel_id=1, source_target_pairs={{0,24},{8,16},{16,8},{24,0},{1,25},{9,17},{17,9},{25,1},{2,26},{10... | collective-permute-start | bytes 49160 | tf_op jit(solution)/shard_map/ppermute | solution.py:571
  63.3 4.6 %collective-permute-start.16 = (f32[32,128]{1,0:T(8,128)S(1)}, f32[32,128]{1,0:T(8,128)S(1)}, u32[]{:S(2)}, u32[]{:S(2)}) collective-permute-start(f32[32,128]{1,0:T(8,128)S(1)} %add.26), channel_id=1, source_target_pairs={{0,16},{8,24},{16,0},{24,8},{1,17},{9,25},{17,1},{25,9},{2,18},{10... | collective-permute-start | bytes 49160 | tf_op jit(solution)/shard_map/ppermute | solution.py:571
  65.1 3.7 %collective-permute-start.15 = (f32[32,128]{1,0:T(8,128)S(1)}, f32[32,128]{1,0:T(8,128)S(1)}, u32[]{:S(2)}, u32[]{:S(2)}) collective-permute-start(f32[32,128]{1,0:T(8,128)S(1)} %add.26), channel_id=1, source_target_pairs={{0,8},{8,0},{16,24},{24,16},{1,9},{9,1},{17,25},{25,17},{2,10},{10... | collective-permute-start | bytes 49160 | tf_op jit(solution)/shard_map/ppermute | solution.py:571
  68.8 7.2 %collective-permute-start.20 = (f32[32,128]{1,0:T(8,128)S(1)}, f32[32,128]{1,0:T(8,128)S(1)}, u32[]{:S(2)}, u32[]{:S(2)}) collective-permute-start(f32[32,128]{1,0:T(8,128)S(1)} %add_add_fusion.1), channel_id=1, source_target_pairs={{0,6},{1,7},{2,4},{3,5},{4,2},{5,3},{6,0},{7,1},{8,14},{9,15},{10,... | collective-permute-start | bytes 49160 | tf_op jit(solution)/shard_map/ppermute | solution.py:571
  72.3 4.6 %collective-permute-start.19 = (f32[32,128]{1,0:T(8,128)S(1)}, f32[32,128]{1,0:T(8,128)S(1)}, u32[]{:S(2)}, u32[]{:S(2)}) collective-permute-start(f32[32,128]{1,0:T(8,128)S(1)} %add_add_fusion.1), channel_id=1, source_target_pairs={{0,4},{1,5},{2,6},{3,7},{4,0},{5,1},{6,2},{7,3},{8,12},{9,13},{10,... | collective-permute-start | bytes 49160 | tf_op jit(solution)/shard_map/ppermute | solution.py:571
  72.3 4.6 %collective-permute-start.18 = (f32[32,128]{1,0:T(8,128)S(1)}, f32[32,128]{1,0:T(8,128)S(1)}, u32[]{:S(2)}, u32[]{:S(2)}) collective-permute-start(f32[32,128]{1,0:T(8,128)S(1)} %add_add_fusion.1), channel_id=1, source_target_pairs={{0,2},{1,3},{2,0},{3,1},{4,6},{5,7},{6,4},{7,5},{8,10},{9,11},{10,... | collective-permute-start | bytes 49160 | tf_op jit(solution)/shard_map/ppermute | solution.py:571

commit v5 on v4

--- a/solution.py
+++ b/solution.py
@@ -82,17 +82,11 @@
     return slots, last + 1
 
 
-def prepare_kernel(me, ids, photos, sorted_out, up_out, down_out, *refs):
-    extras, (buffer, by_row, arrived) = refs[:-3], refs[-3:]
+def prepare_kernel(me, ids, photos, sorted_out, up_out, down_out, *extras):
     count, rows, width = photos.shape
     cells = rows // 2
     pieces = len(extras)
     step = width // pieces
-    for distance in range(pieces):
-        cols = pl.ds(pl.multiple_of((me[0] ^ distance) * step, step), step)
-        pltpu.make_async_copy(
-            photos.at[:, :, cols], buffer.at[distance], arrived.at[distance]
-        ).start()
     perm = row_permutation(count, rows)
     split = column_split()
 
@@ -107,23 +101,15 @@
     notes = jnp.where(sub == 0, ids[0], jnp.where(sub == 1, ids[count - 1], slot_id))
     notes = jnp.where(sub == 3, cameras, notes).astype(f32).astype(bf16)
 
-    @pl.loop(0, pieces)
-    def _(distance):
-        piece = me[0] ^ distance
-        cols = pl.ds(pl.multiple_of(piece * step, step), step)
-        pltpu.make_async_copy(
-            photos.at[:, :, cols], buffer.at[distance], arrived.at[distance]
-        ).wait()
-        flat = buffer[distance].reshape(count * rows, step)
-        by_row[...] = jnp.dot(perm, flat, preferred_element_type=f32).astype(bf16)
-
-        @pl.loop(0, step // (2 * LANES))
-        def _(inner):
+    for piece in range(pieces):
+        flat = photos[:, :, piece * step : (piece + 1) * step].reshape(count * rows, step)
+        by_row = jnp.dot(perm, flat, preferred_element_type=f32).astype(bf16)
+        for inner in range(step // (2 * LANES)):
             block = piece * (step // (2 * LANES)) + inner
-            cols = pl.ds(pl.multiple_of(block * 2 * LANES, 2 * LANES), 2 * LANES)
-            cell_cols = pl.ds(pl.multiple_of(block * LANES, LANES), LANES)
-            local = pl.ds(pl.multiple_of(inner * 2 * LANES, 2 * LANES), 2 * LANES)
-            parted = jnp.dot(by_row[:, local], split, preferred_element_type=f32)
+            cols = slice(block * 2 * LANES, (block + 1) * 2 * LANES)
+            cell_cols = slice(block * LANES, (block + 1) * LANES)
+            pixels = by_row[:, inner * 2 * LANES : (inner + 1) * 2 * LANES]
+            parted = jnp.dot(pixels, split, preferred_element_type=f32)
             sorted_out[:, cols] = parted.astype(bf16)
             for i in range(cells):
                 if RADII <= i < cells - RADII:
@@ -142,9 +128,10 @@
 
     none = jnp.zeros((rows, step), f32)
     for distance, extra in enumerate(extras):
+        cols = pl.ds(pl.multiple_of((me[0] ^ distance) * step, step), step)
 
         def add(photo, total):
-            pixel = buffer[distance, photo].astype(f32)
+            pixel = photos[photo, :, cols].astype(f32)
             return total + pixel * pixel
 
         extra[:rows, :] = lax.fori_loop(0, in_first, add, none).astype(bf16)
@@ -161,7 +148,7 @@
     smem = pl.BlockSpec(memory_space=pltpu.SMEM)
     return pl.pallas_call(
         prepare_kernel,
-        in_specs=[smem, smem, pl.BlockSpec(memory_space=pltpu.HBM)],
+        in_specs=[smem, smem, vmem],
         out_specs=[vmem] * (3 + pieces),
         out_shape=[
             jax.ShapeDtypeStruct((size, width), bf16),
@@ -169,11 +156,6 @@
             jax.ShapeDtypeStruct((halo, width // 2), bf16),
         ]
         + [jax.ShapeDtypeStruct((3 * rows, step), bf16)] * pieces,
-        scratch_shapes=[
-            pltpu.VMEM((pieces, count, rows, step), bf16),
-            pltpu.VMEM((size, step), bf16),
-            pltpu.SemaphoreType.DMA((pieces,)),
-        ],
         compiler_params=pltpu.CompilerParams(vmem_limit_bytes=20 * 2**20),
         cost_estimate=pl.CostEstimate(flops=10**9, bytes_accessed=8 * 2**20, transcendentals=0),
         name="prepare",
@@ -197,9 +179,8 @@
         box_out[radius - 1] = box_matrix(radius)
     merge_out[...] = column_merge()
 
-    @pl.loop(0, width // (2 * LANES))
-    def _(block):
-        cols = pl.ds(pl.multiple_of(block * 2 * LANES, 2 * LANES), 2 * LANES)
+    for block in range(width // (2 * LANES)):
+        cols = slice(block * 2 * LANES, (block + 1) * 2 * LANES)
         pixel = own[:, cols].astype(f32)
         pair = jnp.concatenate(halves(pixel * pixel), axis=0)
         energy = jnp.dot(select, pair, preferred_element_type=f32)
@@ -272,7 +253,7 @@
 
 
 def main_kernel(
-    count, rows, chunk, own_all, above_all, below_all, inverse, select, box, merge, out,
+    count, rows, chunk, own_all, above_all, below_all, inverse, select, box, merge, out, other,
     own, above, below, sums, rest, least, product, scale, select_in, box_in, merge_in,
     arrived, ready,
 ):
@@ -304,9 +285,9 @@
             )
     late = [
         pltpu.make_async_copy(box, box_in, ready.at[0]),
-        pltpu.make_async_copy(select.at[pl.ds(0, slot_rows)], select_in, ready.at[1]),
+        pltpu.make_async_copy(select, select_in, ready.at[1]),
         pltpu.make_async_copy(
-            inverse.at[pl.ds(0, slot_rows), pl.ds(pl.multiple_of(base, width), width)],
+            inverse.at[:, pl.ds(pl.multiple_of(base, width), width)],
             scale,
             ready.at[2],
         ),
@@ -318,15 +299,14 @@
     def pixels_of(i, start):
         top = slice(2 * i * count, (2 * i + 1) * count)
         low = slice((2 * i + 1) * count, (2 * i + 2) * count)
-        even = pl.ds(pl.multiple_of(start, 2 * LANES), LANES)
-        odd = pl.ds(pl.multiple_of(start + LANES, LANES), LANES)
+        even, odd = slice(start, start + LANES), slice(start + LANES, start + 2 * LANES)
         return tuple(
             own[at, cols].astype(f32)
             for at, cols in ((top, even), (top, odd), (low, even), (low, odd))
         )
 
     def add_up(block, fine):
-        cols = pl.ds(pl.multiple_of(block * LANES, LANES), LANES)
+        cols = slice(block * LANES, (block + 1) * LANES)
         squares = [[], [], []]
         for i in range(cells):
             bands = haar_rows(*pixels_of(i, block * 2 * LANES))
@@ -356,16 +336,14 @@
     for copy in inner:
         copy.wait()
 
-    @pl.loop(1, blocks + 1)
-    def _(block):
+    for block in range(1, blocks + 1):
         add_up(block, True)
 
     for copy in edges[0] + edges[1]:
         copy.wait()
 
-    @pl.loop(0, 2)
-    def _(side):
-        add_up(side * (blocks + 1), False)
+    add_up(0, False)
+    add_up(blocks + 1, False)
 
     for side, outside in enumerate((base == 0, base + width == own_all.shape[1])):
 
@@ -376,11 +354,10 @@
 
     late[0].wait()
 
-    @pl.loop(0, blocks // 2)
-    def _(group):
-        first = pl.multiple_of(group * 2 * LANES, 2 * LANES)
-        window = pl.ds(first, 4 * LANES)
-        middle = pl.ds(pl.multiple_of(first + LANES, LANES), 2 * LANES)
+    for group in range(blocks // 2):
+        first = group * 2 * LANES
+        window = slice(first, first + 4 * LANES)
+        middle = slice(first + LANES, first + 3 * LANES)
         for radius in range(1, RADII + 1):
             narrow, weights = sums[radius - 1, :, window], box_in[radius - 1]
             if radius <= FINE:
@@ -391,9 +368,9 @@
             least[...] = mean if radius == 1 else jnp.minimum(least[...], mean)
 
         for half in range(2):
-            start = pl.multiple_of((2 * group + half) * 2 * LANES, 2 * LANES)
-            even = pl.ds(start, LANES)
-            odd = pl.ds(pl.multiple_of(start + LANES, LANES), LANES)
+            start = (2 * group + half) * 2 * LANES
+            even = slice(start, start + LANES)
+            odd = slice(start + LANES, start + 2 * LANES)
             lanes = slice(half * LANES, (half + 1) * LANES)
             for i in range(cells):
                 top, low = 2 * i * count, (2 * i + 1) * count
@@ -418,12 +395,13 @@
     for copy in late[1:]:
         copy.wait()
 
-    @pl.loop(0, blocks)
-    def _(block):
-        cols = pl.ds(pl.multiple_of(block * 2 * LANES, 2 * LANES), 2 * LANES)
+    for block in range(blocks):
+        cols = slice(2 * block * LANES, (2 * block + 2) * LANES)
         weighted = jnp.dot(select_in[...], product[:, cols], preferred_element_type=f32)
         part = (weighted * scale[:, cols]).astype(bf16)
-        out[:, cols] = jnp.dot(part, merge_in[...], preferred_element_type=f32).astype(bf16)
+        both = jnp.dot(part, merge_in[...], preferred_element_type=f32).astype(bf16)
+        out[:, cols] = both[:slot_rows]
+        other[:, cols] = both[slot_rows:]
 
 
 def main_part(chunk, own, above, below, inverse, select, box, merge, rows, pieces, slots):
@@ -435,7 +413,7 @@
     return pl.pallas_call(
         functools.partial(main_kernel, count, rows),
         in_specs=[pl.BlockSpec(memory_space=pltpu.SMEM)] + [pl.BlockSpec(memory_space=pl.ANY)] * 7,
-        out_specs=pl.BlockSpec(memory_space=pltpu.VMEM),
+        out_specs=[pl.BlockSpec(memory_space=pltpu.VMEM)] * 2,
         scratch_shapes=[
             pltpu.VMEM((size, width + 4 * LANES), bf16),
             pltpu.VMEM((halo, width // 2 + 2 * LANES), bf16),
@@ -444,14 +422,17 @@
             pltpu.VMEM((FINE, cell_rows, width // 2 + 2 * LANES), bf16),
             pltpu.VMEM((cell_rows, 2 * LANES), f32),
             pltpu.VMEM((2 * size, width), bf16),
-            pltpu.VMEM((slots * rows, width), f32),
-            pltpu.VMEM((slots * rows, 2 * size), bf16),
+            pltpu.VMEM((size, width), f32),
+            pltpu.VMEM((size, 2 * size), bf16),
             pltpu.VMEM((RADII, 4 * LANES, 2 * LANES), bf16),
             pltpu.VMEM((2 * LANES, 2 * LANES), bf16),
             pltpu.SemaphoreType.DMA((9,)),
             pltpu.SemaphoreType.DMA((4,)),
         ],
-        out_shape=jax.ShapeDtypeStruct((slots * rows, width), bf16),
+        out_shape=[
+            jax.ShapeDtypeStruct((slots * rows, width), bf16),
+            jax.ShapeDtypeStruct((size - slots * rows, width), bf16),
+        ],
         compiler_params=pltpu.CompilerParams(vmem_limit_bytes=20 * 2**20),
         cost_estimate=pl.CostEstimate(
             flops=2 * 10**9, bytes_accessed=4 * 2**20, transcendentals=0
@@ -480,28 +461,36 @@
     )(*extras)[0, 0]
 
 
-def assemble_kernel(rows, select, share, *refs):
-    pieces = len(refs) - 4
-    parts, (flat, partial, scaled, total) = refs[:pieces], refs[pieces:]
-    size, width = parts[0].shape
+def assemble_kernel(rows, pieces, select, share, *refs):
+    parts, others = refs[:pieces], refs[pieces:-7]
+    prints, partial, flat, scaled, wide, total, sent = refs[-7:]
+    width = parts[0].shape[1]
+    size = parts[0].shape[0] + sum(other.shape[0] for other in others[:1])
     tall = CAMS * rows
     for place, part in enumerate(parts):
         edges = part[: 2 * rows, :].astype(f32) * share[place].reshape(2 * rows, width)
         scaled[place, : 2 * rows, :] = edges.astype(bf16)
     total[...] = jnp.zeros((tall, LANES), f32)
-
-    @pl.loop(0, width // (2 * LANES))
-    def _(block):
-        cols = pl.ds(pl.multiple_of(block * 2 * LANES, 2 * LANES), 2 * LANES)
+    copies = []
+    for block in range(width // (2 * LANES)):
+        cols = slice(block * 2 * LANES, (block + 1) * 2 * LANES)
         joined = jnp.zeros((tall, 2 * LANES), f32)
         for place, part in enumerate(parts):
-            source = jnp.concatenate([scaled[place, :, cols], part[2 * rows :, cols]], axis=0)
+            pieces_of = [scaled[place, :, cols], part[2 * rows :, cols]]
+            if others:
+                pieces_of.append(others[place][:, cols])
+            source = jnp.concatenate(pieces_of, axis=0)
             joined = joined + jnp.dot(
                 select[place, :, :size], source, preferred_element_type=f32
             )
         flat[:, cols] = joined.astype(bf16)
         total[...] += joined[:, :LANES] + joined[:, LANES:]
-
+        wide[:, :, cols] = joined.reshape(CAMS, rows, 2 * LANES)
+        there = pl.ds(block * 2 * LANES, 2 * LANES)
+        copies.append(
+            pltpu.make_async_copy(wide.at[:, :, there], prints.at[:, :, there], sent.at[block])
+        )
+        copies[-1].start()
     gram = lax.dot_general(
         flat[...], flat[...], (((1,), (1,)), ((), ())), preferred_element_type=f32
     )
@@ -517,26 +506,35 @@
     sums = jnp.sum(sums.reshape(CAMS, rows, 1), axis=1)
     lane = lax.broadcasted_iota(jnp.int32, (CAMS, LANES), 1)
     partial[...] = jnp.where(lane == CAMS, sums, gram)
-
-
-def assemble(select, share, parts, rows):
+    for copy in copies:
+        copy.wait()
+
+
+def assemble(select, share, parts, others, rows):
     width = parts[0].shape[1]
+    tall = CAMS * rows
+    vmem = pl.BlockSpec(memory_space=pltpu.VMEM)
     return pl.pallas_call(
-        functools.partial(assemble_kernel, rows),
+        functools.partial(assemble_kernel, rows, len(parts)),
+        in_specs=[vmem] * (2 + len(parts) + len(others)),
+        out_specs=[pl.BlockSpec(memory_space=pl.ANY), vmem],
         out_shape=[
-            jax.ShapeDtypeStruct((CAMS * rows, width), bf16),
+            jax.ShapeDtypeStruct((CAMS, rows, width), f32),
             jax.ShapeDtypeStruct((CAMS, LANES), f32),
         ],
         scratch_shapes=[
+            pltpu.VMEM((tall, width), bf16),
             pltpu.VMEM((len(parts), 2 * rows, width), bf16),
-            pltpu.VMEM((CAMS * rows, LANES), f32),
+            pltpu.VMEM((CAMS, rows, width), f32),
+            pltpu.VMEM((tall, LANES), f32),
+            pltpu.SemaphoreType.DMA((width // (2 * LANES),)),
         ],
         compiler_params=pltpu.CompilerParams(vmem_limit_bytes=20 * 2**20),
         cost_estimate=pl.CostEstimate(
             flops=2 * 10**9, bytes_accessed=4 * 2**20, transcendentals=0
         ),
         name="assemble",
-    )(select, share, *parts)
+    )(select, share, *parts, *others)
 
 
 def correlate_kernel(pixels, *refs):
@@ -591,23 +589,28 @@
     ]
     inverse, select, box, merge = energies(camera_id, own, rows)
 
-    def finish(slots):
-        parts = [None] * pieces
-        for distance in reversed(range(pieces)):
-            part = main_part(
-                (me ^ distance).reshape(1), own, above, below, inverse, select, box, merge,
-                rows, pieces, slots,
-            )
-            parts[distance] = exchange(part, "photo", distance) if distance else part
-        place, share = blend(me.reshape(1), extras, rows, count * rows)
-        return assemble(place, share, parts, rows)
-
-    most = most_cameras(extras, rows)
-    sizes = sorted({max(2, count * part // 16) for part in (10, 12, 16)})
-    branch = sum((most > size).astype(jnp.int32) for size in sizes[:-1])
-    flat, partial = lax.switch(branch, [functools.partial(finish, size) for size in sizes])
-    flat, partial = lax.optimization_barrier((flat, partial))
-    prints = flat.reshape(CAMS, rows, width // pieces).astype(f32)
+    few = max(2, 11 * count // 16)
+    parts, others = [None] * pieces, [None] * pieces
+    for distance in reversed(range(pieces)):
+        part, other = main_part(
+            (me ^ distance).reshape(1), own, above, below, inverse, select, box, merge,
+            rows, pieces, few,
+        )
+        parts[distance] = exchange(part, "photo", distance) if distance else part
+        others[distance] = other
+    place, share = blend(me.reshape(1), extras, rows, count * rows)
+
+    def finish_few():
+        return assemble(place, share, parts, [], rows)
+
+    def finish_all():
+        late = [
+            exchange(other, "photo", distance) if distance else other
+            for distance, other in enumerate(others)
+        ]
+        return assemble(place, share, parts, late, rows)
+
+    prints, partial = lax.cond(most_cameras(extras, rows) > few, finish_all, finish_few)
 
     total = summed(partial, "tile", (1,))
     total = summed(total, "photo", range(1, pieces))

time: 78.1 us -> 81 us (1.037)
  starting transfers between devices: 19.5 us -> 32.9 us
  Pallas kernels: 40.5 us -> 30.2 us
  waiting for transfers between devices: 9.42 us -> 13.7 us
  other arithmetic: 2.82 us -> 0.02 us
    ppermute x13, starting transfers between devices: 15.8 us -> 29.3 us  [exchange(): return lax.ppermute(array, axis, [(i, i ^ distance) for i in range(size)])]
    pallas_call x1, Pallas kernels: 7.01 us -> 2.6 us  [energies(): pl.pallas_call(functools.partial(energy_kernel, size // rows, rows), in_s...]
    ppermute x13, waiting for transfers between devices: 9.42 us -> 13.3 us  [exchange(): return lax.ppermute(array, axis, [(i, i ^ distance) for i in range(size)])]
    pallas_call x2, Pallas kernels: 9.13 us -> 5.61 us  [the longest x1 3.31 us: prepare(): pl.pallas_call(prepare_kernel, in_specs=[smem, smem, vmem], out_specs=[vm...]
    convert_element_type x1 -> x0, other arithmetic: 2.8 us -> none  [on_device(): prints = flat.reshape(CAMS, rows, width // pieces).astype(f32)]
    pallas_call x4, Pallas kernels: 21.8 us -> 20.1 us  [main_part(): pl.pallas_call(functools.partial(main_kernel, count, rows), in_specs=[pl....]
    cond x28 -> x0, local copies, waits for them, and re-layouts: 0.81 us -> none
    unnamed x4 -> x8, local copies, waits for them, and re-layouts: 2.24 us -> 2.25 us
  transfers between devices with their start and end apart: 15 -> 15, of which waited for: 5 -> 9; matrix products, arithmetic and copies ran while one was open for 4% -> 0% of each run, Pallas kernels for 32% -> 29%
where the time goes in v5:
time: 81 us; the launch traced here: 80.7 us
  starting transfers between devices  32.9 us (41%)
  Pallas kernels  30.2 us (37%)
  waiting for transfers between devices  13.7 us (17%)
  local copies, waits for them, and re-layouts  2.25 us (3%)
  between operations  1.42 us (2%)
    ppermute x13, starting transfers between devices, exchange(): return lax.ppermute(array, axis, [(i, i ^ distance) for i in range(size)])  29.3 us
    pallas_call x4, Pallas kernels, main_part(): pl.pallas_call(functools.partial(main_kernel, count, rows), in_specs=[pl....  20.1 us
    ppermute x13, waiting for transfers between devices, exchange(): return lax.ppermute(array, axis, [(i, i ^ distance) for i in range(size)])  13.3 us
    pallas_call x1, Pallas kernels, prepare(): pl.pallas_call(prepare_kernel, in_specs=[smem, smem, vmem], out_specs=[vm...  3.31 us
    pallas_call x1, Pallas kernels, energies(): pl.pallas_call(functools.partial(energy_kernel, size // rows, rows), in_s...  2.6 us
    ppermute x1, starting transfers between devices, on_device(): above = lax.ppermute(down, 'tile', [(i, i + 1) for i in range(tiles - 1)])  2.39 us
    pallas_call x1, Pallas kernels, assemble(): pl.pallas_call(functools.partial(assemble_kernel, rows, len(parts)), in_s...  2.3 us
    unnamed x8, local copies, waits for them, and re-layouts  2.25 us
  transfers between devices with their start and end apart: 15, of which 9 were waited for; matrix products, arithmetic and copies ran while one was open for 0% of the time, Pallas kernels for 29%

profile of v5, /device:TPU:0, one launch (start us, length us, event | category | flops | bytes accessed | tf_op | source)
XLA Modules:
  0.0 80.7 jit_solution(4054644811442610137)
XLA Ops:
  0.7 1.6 %copy-done = bf16[16,16,4096]{2,1,0:T(8,128)(2,1)S(1)} copy-done((bf16[16,16,4096]{2,1,0:T(8,128)(2,1)S(1)}, bf16[16,16,4096]{2,1,0:T(8,128)(2,1)}, u32[]{:S(2)}) %copy-start) | copy-done | bytes 2097176
  2.2 0.7 copy-done.1
  2.9 3.3 %prepare.1 = (bf16[256,4096]{1,0:T(8,128)(2,1)S(1)}, bf16[192,2048]{1,0:T(8,128)(2,1)}, bf16[192,2048]{1,0:T(8,128)(2,1)}, bf16[48,1024]{1,0:T(8,128)(2,1)S(1)},...) custom-call(s32[1]{0:T(128)} %bitcast.me.chunk, s32[16]{0:T(128)S(1)} %copy-done.1, ...), custom_call_target="tpu_custom_call" | custom-call | flops 1000000000 | bytes 8388608 | tf_op jit(solution)/shard_map/prepare/pallas_call | solution.py:149
  6.2 2.4 %collective-permute-start.6 = (bf16[192,2048]{1,0:T(8,128)(2,1)}, bf16[192,2048]{1,0:T(8,128)(2,1)S(1)}, u32[]{:S(2)}, u32[]{:S(2)}) collective-permute-start(bf16[192,2048]{1,0:T(8,128)(2,1)} %get-tuple-element.80), channel_id=1, source_target_pairs={{0,1},{1,2},{2,3},{3,4},{4,5},{5,6},{6,7},{8,9},{9,10},{10,11},{11... | collective-permute-start | bytes 2359304 | tf_op jit(solution)/shard_map/ppermute | solution.py:584
  8.6 1.3 %collective-permute-start.7 = (bf16[192,2048]{1,0:T(8,128)(2,1)}, bf16[192,2048]{1,0:T(8,128)(2,1)}, u32[]{:S(2)}, u32[]{:S(2)}) collective-permute-start(bf16[192,2048]{1,0:T(8,128)(2,1)} %get-tuple-element.81), channel_id=1, source_target_pairs={{1,0},{2,1},{3,2},{4,3},{5,4},{6,5},{7,6},{9,8},{10,9},{11,10},{12... | collective-permute-start | bytes 2359304 | tf_op jit(solution)/shard_map/ppermute | solution.py:585
  9.9 2.4 %collective-permute-start.3 = (bf16[48,1024]{1,0:T(8,128)(2,1)S(1)}, bf16[48,1024]{1,0:T(8,128)(2,1)S(1)}, u32[]{:S(2)}, u32[]{:S(2)}) collective-permute-start(bf16[48,1024]{1,0:T(8,128)(2,1)S(1)} %get-tuple-element.74), channel_id=1, source_target_pairs={{0,8},{8,0},{16,24},{24,16},{1,9},{9,1},{17,25},{25,17},{2,10},{10... | collective-permute-start | bytes 294920 | tf_op jit(solution)/shard_map/ppermute | solution.py:569
  12.3 2.6 %energies.1 = (f32[256,4096]{1,0:T(8,128)S(1)}, bf16[256,512]{1,0:T(8,128)(2,1)S(1)}, bf16[4,512,256]{2,1,0:T(8,128)(2,1)S(1)}, bf16[256,256]{1,0:T(8,128)(2,1)S(1)}) custom-call(s32[16]{0:T(128)S(1)} %copy-done.2, bf16[256,4096]{1,0:T(8,128)(2,1)S(1)} %get-tuple-element.79.own.own_all), custom_call_target="tpu_custom_call" | custom-call | flops 1000000000 | bytes 8388608 | tf_op jit(solution)/shard_map/energies/pallas_call | solution.py:194
  15.3 4.8 %residual.7 = (bf16[176,1024]{1,0:T(8,128)(2,1)S(1)}, bf16[80,1024]{1,0:T(8,128)(2,1)S(1)}) custom-call(s32[1]{0:T(128)} %bitcast.4.chunk, bf16[256,4096]{1,0:T(8,128)(2,1)S(1)} %get-tuple-element.79.own.own_all, bf16[192,2048]{1,0:T(8,128)(2,1)S(1)} %collective-permute-done.6.above_all, bf16[192,2048]{1,0:T(8,128)(2,1)} %collective-permute-done.7.below_all, ...), custom_call_target="tpu_custom_call" | custom-call | flops 2000000000 | bytes 4194304 | tf_op jit(solution)/shard_map/residual/pallas_call | solution.py:413
  20.1 2.6 %collective-permute-start.10 = (bf16[176,1024]{1,0:T(8,128)(2,1)S(1)}, bf16[176,1024]{1,0:T(8,128)(2,1)S(1)}, u32[]{:S(2)}, u32[]{:S(2)}) collective-permute-start(bf16[176,1024]{1,0:T(8,128)(2,1)S(1)} %get-tuple-element.89), channel_id=1, source_target_pairs={{0,24},{8,16},{16,8},{24,0},{1,25},{9,17},{17,9},{25,1},{2,26},{10... | collective-permute-start | bytes 1081352 | tf_op jit(solution)/shard_map/ppermute | solution.py:569
  22.7 5.0 %residual.6 = (bf16[176,1024]{1,0:T(8,128)(2,1)S(1)}, bf16[80,1024]{1,0:T(8,128)(2,1)S(1)}) custom-call(s32[1]{0:T(128)} %bitcast.3.chunk, bf16[256,4096]{1,0:T(8,128)(2,1)S(1)} %get-tuple-element.79.own.own_all, bf16[192,2048]{1,0:T(8,128)(2,1)S(1)} %collective-permute-done.6.above_all, bf16[192,2048]{1,0:T(8,128)(2,1)} %collective-permute-done.7.below_all, ...), custom_call_target="tpu_custom_call" | custom-call | flops 2000000000 | bytes 4194304 | tf_op jit(solution)/shard_map/residual/pallas_call | solution.py:413
  27.7 0.5 collective-permute-start.9
  28.2 5.5 %residual.5 = (bf16[176,1024]{1,0:T(8,128)(2,1)S(1)}, bf16[80,1024]{1,0:T(8,128)(2,1)}) custom-call(s32[1]{0:T(128)} %bitcast.2.chunk, bf16[256,4096]{1,0:T(8,128)(2,1)S(1)} %get-tuple-element.79.own.own_all, bf16[192,2048]{1,0:T(8,128)(2,1)S(1)} %collective-permute-done.6.above_all, bf16[192,2048]{1,0:T(8,128)(2,1)} %collective-permute-done.7.below_all, ...), custom_call_target="tpu_custom_call" | custom-call | flops 2000000000 | bytes 4194304 | tf_op jit(solution)/shard_map/residual/pallas_call | solution.py:413
  33.6 0.6 collective-permute-start.8
  34.3 1.4 %collective-permute-start.4 = (bf16[48,1024]{1,0:T(8,128)(2,1)S(1)}, bf16[48,1024]{1,0:T(8,128)(2,1)S(1)}, u32[]{:S(2)}, u32[]{:S(2)}) collective-permute-start(bf16[48,1024]{1,0:T(8,128)(2,1)S(1)} %get-tuple-element.75), channel_id=1, source_target_pairs={{0,16},{8,24},{16,0},{24,8},{1,17},{9,25},{17,1},{25,9},{2,18},{10... | collective-permute-start | bytes 294920 | tf_op jit(solution)/shard_map/ppermute | solution.py:569
  35.7 1.5 %collective-permute-start.5 = (bf16[48,1024]{1,0:T(8,128)(2,1)S(1)}, bf16[48,1024]{1,0:T(8,128)(2,1)S(1)}, u32[]{:S(2)}, u32[]{:S(2)}) collective-permute-start(bf16[48,1024]{1,0:T(8,128)(2,1)S(1)} %get-tuple-element.76), channel_id=1, source_target_pairs={{0,24},{8,16},{16,8},{24,0},{1,25},{9,17},{17,9},{25,1},{2,26},{10... | collective-permute-start | bytes 294920 | tf_op jit(solution)/shard_map/ppermute | solution.py:569
  37.2 3.1 %collective-permute-done.4.refs_2_ = bf16[48,1024]{1,0:T(8,128)(2,1)S(1)} collective-permute-done((bf16[48,1024]{1,0:T(8,128)(2,1)S(1)}, bf16[48,1024]{1,0:T(8,128)(2,1)S(1)}, u32[]{:S(2)}, u32[]{:S(2)}) %collective-permute-start.4) | collective-permute-done | bytes 98336 | tf_op jit(solution)/shard_map/ppermute | solution.py:569
  40.3 3.1 %collective-permute-done.5.refs_3_ = bf16[48,1024]{1,0:T(8,128)(2,1)S(1)} collective-permute-done((bf16[48,1024]{1,0:T(8,128)(2,1)S(1)}, bf16[48,1024]{1,0:T(8,128)(2,1)S(1)}, u32[]{:S(2)}, u32[]{:S(2)}) %collective-permute-start.5) | collective-permute-done | bytes 98336 | tf_op jit(solution)/shard_map/ppermute | solution.py:569
  43.4 0.6 most_cameras.1
  45.1 4.8 %residual.4 = (bf16[176,1024]{1,0:T(8,128)(2,1)S(1)}, bf16[80,1024]{1,0:T(8,128)(2,1)S(1)}) custom-call(s32[1]{0:T(128)} %bitcast.me.chunk, bf16[256,4096]{1,0:T(8,128)(2,1)S(1)} %get-tuple-element.79.own.own_all, bf16[192,2048]{1,0:T(8,128)(2,1)S(1)} %collective-permute-done.6.above_all, bf16[192,2048]{1,0:T(8,128)(2,1)} %collective-permute-done.7.below_all, ...), custom_call_target="tpu_custom_call" | custom-call | flops 2000000000 | bytes 4194304 | tf_op jit(solution)/shard_map/residual/pallas_call | solution.py:413
  50.0 2.5 %conditional.1 = ((f32[32,16,1024]{2,1,0:T(8,128)}, f32[32,128]{1,0:T(8,128)S(1)})) conditional(s32[]{:T(128)} %bitcast.1, (bf16[4,512,256]{2,1,0:T(8,128)(2,1)S(1)}, f32[4,2,16,1024]{3,2,1,0:T(8,128)S(1)}, bf16[176,1024]{1,0:T(8,128)(2,1)S(1)}, bf16[176,1024]{1,0:T(8,128)(2,1)S(1)}, bf16[176,1024]{1,0:T(8,128)(2,1)S(1)}, ...), branch_computations={%region_0.0_spmd, %region_1.0_spmd} | conditional | flops 2000000000 | bytes 6160512 | solution.py:613
  50.0 2.3 %assemble.2 = (f32[32,16,1024]{2,1,0:T(8,128)}, f32[32,128]{1,0:T(8,128)S(1)}) custom-call(bf16[4,512,256]{2,1,0:T(8,128)(2,1)S(1)} %get-tuple-element.32.select, f32[4,2,16,1024]{3,2,1,0:T(8,128)S(1)} %get-tuple-element.33.share, bf16[176,1024]{1,0:T(8,128)(2,1)S(1)} %get-tuple-element.34.refs_0_, bf16[176,1024]{1,0:T(8,128)(2,1)S(1)} %get-tuple-element.35.refs_1_, ...), custom_call_target="tpu_custom_call" | custom-call | flops 2000000000 | bytes 4194304 | tf_op jit(solution)/shard_map/cond/branch_0_fun/assemble/pallas_call | solution.py:517
  52.5 8.0 %collective-permute-start.11 = (f32[32,128]{1,0:T(8,128)S(1)}, f32[32,128]{1,0:T(8,128)S(1)}, u32[]{:S(2)}, u32[]{:S(2)}) collective-permute-start(f32[32,128]{1,0:T(8,128)S(1)} %get-tuple-element.95), channel_id=1, source_target_pairs={{0,1},{1,0},{2,3},{3,2},{4,5},{5,4},{6,7},{7,6},{8,9},{9,8},{10,11... | collective-permute-start | bytes 49160 | tf_op jit(solution)/shard_map/ppermute | solution.py:569
  60.6 0.8 %collective-permute-done.11 = f32[32,128]{1,0:T(8,128)S(1)} collective-permute-done((f32[32,128]{1,0:T(8,128)S(1)}, f32[32,128]{1,0:T(8,128)S(1)}, u32[]{:S(2)}, u32[]{:S(2)}) %collective-permute-start.11) | collective-permute-done | bytes 16416 | tf_op jit(solution)/shard_map/ppermute | solution.py:569
  61.7 0.7 collective-permute-start.13
  62.4 2.5 %collective-permute-start.14 = (f32[32,128]{1,0:T(8,128)S(1)}, f32[32,128]{1,0:T(8,128)S(1)}, u32[]{:S(2)}, u32[]{:S(2)}) collective-permute-start(f32[32,128]{1,0:T(8,128)S(1)} %add.21), channel_id=1, source_target_pairs={{0,24},{8,16},{16,8},{24,0},{1,25},{9,17},{17,9},{25,1},{2,26},{10... | collective-permute-start | bytes 49160 | tf_op jit(solution)/shard_map/ppermute | solution.py:569
  65.5 1.6 %collective-permute-done.14 = f32[32,128]{1,0:T(8,128)S(1)} collective-permute-done((f32[32,128]{1,0:T(8,128)S(1)}, f32[32,128]{1,0:T(8,128)S(1)}, u32[]{:S(2)}, u32[]{:S(2)}) %collective-permute-start.14) | collective-permute-done | bytes 16416 | tf_op jit(solution)/shard_map/ppermute | solution.py:569
  67.0 6.2 %collective-permute-start.15 = (f32[32,128]{1,0:T(8,128)S(1)}, f32[32,128]{1,0:T(8,128)S(1)}, u32[]{:S(2)}, u32[]{:S(2)}) collective-permute-start(f32[32,128]{1,0:T(8,128)S(1)} %add_add_fusion.1), channel_id=1, source_target_pairs={{0,2},{1,3},{2,0},{3,1},{4,6},{5,7},{6,4},{7,5},{8,10},{9,11},{10,... | collective-permute-start | bytes 49160 | tf_op jit(solution)/shard_map/ppermute | solution.py:569
  73.3 1.1 %collective-permute-start.16 = (f32[32,128]{1,0:T(8,128)S(1)}, f32[32,128]{1,0:T(8,128)S(1)}, u32[]{:S(2)}, u32[]{:S(2)}) collective-permute-start(f32[32,128]{1,0:T(8,128)S(1)} %add_add_fusion.1), channel_id=1, source_target_pairs={{0,4},{1,5},{2,6},{3,7},{4,0},{5,1},{6,2},{7,3},{8,12},{9,13},{10,... | collective-permute-start | bytes 49160 | tf_op jit(solution)/shard_map/ppermute | solution.py:569
  74.4 1.4 %collective-permute-start.17 = (f32[32,128]{1,0:T(8,128)S(1)}, f32[32,128]{1,0:T(8,128)S(1)}, u32[]{:S(2)}, u32[]{:S(2)}) collective-permute-start(f32[32,128]{1,0:T(8,128)S(1)} %add_add_fusion.1), channel_id=1, source_target_pairs={{0,6},{1,7},{2,4},{3,5},{4,2},{5,3},{6,0},{7,1},{8,14},{9,15},{10,... | collective-permute-start | bytes 49160 | tf_op jit(solution)/shard_map/ppermute | solution.py:569
  75.7 2.2 %collective-permute-done.16 = f32[32,128]{1,0:T(8,128)S(1)} collective-permute-done((f32[32,128]{1,0:T(8,128)S(1)}, f32[32,128]{1,0:T(8,128)S(1)}, u32[]{:S(2)}, u32[]{:S(2)}) %collective-permute-start.16) | collective-permute-done | bytes 16416 | tf_op jit(solution)/shard_map/ppermute | solution.py:569
  77.9 2.0 %collective-permute-done.17 = f32[32,128]{1,0:T(8,128)S(1)} collective-permute-done((f32[32,128]{1,0:T(8,128)S(1)}, f32[32,128]{1,0:T(8,128)S(1)}, u32[]{:S(2)}, u32[]{:S(2)}) %collective-permute-start.17) | collective-permute-done | bytes 16416 | tf_op jit(solution)/shard_map/ppermute | solution.py:569
  79.9 0.8 correlate.1
  (20 shorter events, 1.7 us)
Async XLA Ops:
  0.6 11.7 %copy-start.2 = (s32[16]{0:T(128)S(1)}, s32[16]{0:T(128)}, u32[]{:S(2)}) copy-start(s32[16]{0:T(128)} %ids.3) | copy-start | bytes 196
  0.6 1.6 %copy-start = (bf16[16,16,4096]{2,1,0:T(8,128)(2,1)S(1)}, bf16[16,16,4096]{2,1,0:T(8,128)(2,1)}, u32[]{:S(2)}) copy-start(bf16[16,16,4096]{2,1,0:T(8,128)(2,1)} %photos.1) | copy-start | bytes 6291460
  2.2 0.7 copy-start.1
  6.2 8.7 %collective-permute-start.6 = (bf16[192,2048]{1,0:T(8,128)(2,1)}, bf16[192,2048]{1,0:T(8,128)(2,1)S(1)}, u32[]{:S(2)}, u32[]{:S(2)}) collective-permute-start(bf16[192,2048]{1,0:T(8,128)(2,1)} %get-tuple-element.80), channel_id=1, source_target_pairs={{0,1},{1,2},{2,3},{3,4},{4,5},{5,6},{6,7},{8,9},{9,10},{10,11},{11... | collective-permute-start | bytes 2359304 | tf_op jit(solution)/shard_map/ppermute | solution.py:584
  8.6 6.7 %collective-permute-start.7 = (bf16[192,2048]{1,0:T(8,128)(2,1)}, bf16[192,2048]{1,0:T(8,128)(2,1)}, u32[]{:S(2)}, u32[]{:S(2)}) collective-permute-start(bf16[192,2048]{1,0:T(8,128)(2,1)} %get-tuple-element.81), channel_id=1, source_target_pairs={{1,0},{2,1},{3,2},{4,3},{5,4},{6,5},{7,6},{9,8},{10,9},{11,10},{12... | collective-permute-start | bytes 2359304 | tf_op jit(solution)/shard_map/ppermute | solution.py:585
  9.9 25.8 %collective-permute-start.3 = (bf16[48,1024]{1,0:T(8,128)(2,1)S(1)}, bf16[48,1024]{1,0:T(8,128)(2,1)S(1)}, u32[]{:S(2)}, u32[]{:S(2)}) collective-permute-start(bf16[48,1024]{1,0:T(8,128)(2,1)S(1)} %get-tuple-element.74), channel_id=1, source_target_pairs={{0,8},{8,0},{16,24},{24,16},{1,9},{9,1},{17,25},{25,17},{2,10},{10... | collective-permute-start | bytes 294920 | tf_op jit(solution)/shard_map/ppermute | solution.py:569
  20.1 29.8 %collective-permute-start.10 = (bf16[176,1024]{1,0:T(8,128)(2,1)S(1)}, bf16[176,1024]{1,0:T(8,128)(2,1)S(1)}, u32[]{:S(2)}, u32[]{:S(2)}) collective-permute-start(bf16[176,1024]{1,0:T(8,128)(2,1)S(1)} %get-tuple-element.89), channel_id=1, source_target_pairs={{0,24},{8,16},{16,8},{24,0},{1,25},{9,17},{17,9},{25,1},{2,26},{10... | collective-permute-start | bytes 1081352 | tf_op jit(solution)/shard_map/ppermute | solution.py:569
  27.7 22.3 %collective-permute-start.9 = (bf16[176,1024]{1,0:T(8,128)(2,1)S(1)}, bf16[176,1024]{1,0:T(8,128)(2,1)S(1)}, u32[]{:S(2)}, u32[]{:S(2)}) collective-permute-start(bf16[176,1024]{1,0:T(8,128)(2,1)S(1)} %get-tuple-element.88), channel_id=1, source_target_pairs={{0,16},{8,24},{16,0},{24,8},{1,17},{9,25},{17,1},{25,9},{2,18},{10... | collective-permute-start | bytes 1081352 | tf_op jit(solution)/shard_map/ppermute | solution.py:569
  33.6 16.3 %collective-permute-start.8 = (bf16[176,1024]{1,0:T(8,128)(2,1)S(1)}, bf16[176,1024]{1,0:T(8,128)(2,1)S(1)}, u32[]{:S(2)}, u32[]{:S(2)}) collective-permute-start(bf16[176,1024]{1,0:T(8,128)(2,1)S(1)} %get-tuple-element.87), channel_id=1, source_target_pairs={{0,8},{8,0},{16,24},{24,16},{1,9},{9,1},{17,25},{25,17},{2,10},{10... | collective-permute-start | bytes 1081352 | tf_op jit(solution)/shard_map/ppermute | solution.py:569
  34.3 6.0 %collective-permute-start.4 = (bf16[48,1024]{1,0:T(8,128)(2,1)S(1)}, bf16[48,1024]{1,0:T(8,128)(2,1)S(1)}, u32[]{:S(2)}, u32[]{:S(2)}) collective-permute-start(bf16[48,1024]{1,0:T(8,128)(2,1)S(1)} %get-tuple-element.75), channel_id=1, source_target_pairs={{0,16},{8,24},{16,0},{24,8},{1,17},{9,25},{17,1},{25,9},{2,18},{10... | collective-permute-start | bytes 294920 | tf_op jit(solution)/shard_map/ppermute | solution.py:569
  35.7 7.7 %collective-permute-start.5 = (bf16[48,1024]{1,0:T(8,128)(2,1)S(1)}, bf16[48,1024]{1,0:T(8,128)(2,1)S(1)}, u32[]{:S(2)}, u32[]{:S(2)}) collective-permute-start(bf16[48,1024]{1,0:T(8,128)(2,1)S(1)} %get-tuple-element.76), channel_id=1, source_target_pairs={{0,24},{8,16},{16,8},{24,0},{1,25},{9,17},{17,9},{25,1},{2,26},{10... | collective-permute-start | bytes 294920 | tf_op jit(solution)/shard_map/ppermute | solution.py:569
  45.1 4.9 %copy-start.3 = (bf16[80,1024]{1,0:T(8,128)(2,1)S(1)}, bf16[80,1024]{1,0:T(8,128)(2,1)}, u32[]{:S(2)}) copy-start(bf16[80,1024]{1,0:T(8,128)(2,1)} %get-tuple-element.90) | copy-start | bytes 491524
  52.5 8.9 %collective-permute-start.11 = (f32[32,128]{1,0:T(8,128)S(1)}, f32[32,128]{1,0:T(8,128)S(1)}, u32[]{:S(2)}, u32[]{:S(2)}) collective-permute-start(f32[32,128]{1,0:T(8,128)S(1)} %get-tuple-element.95), channel_id=1, source_target_pairs={{0,1},{1,0},{2,3},{3,2},{4,5},{5,4},{6,7},{7,6},{8,9},{9,8},{10,11... | collective-permute-start | bytes 49160 | tf_op jit(solution)/shard_map/ppermute | solution.py:569
  61.4 3.7 %collective-permute-start.12 = (f32[32,128]{1,0:T(8,128)S(1)}, f32[32,128]{1,0:T(8,128)S(1)}, u32[]{:S(2)}, u32[]{:S(2)}) collective-permute-start(f32[32,128]{1,0:T(8,128)S(1)} %add.21), channel_id=1, source_target_pairs={{0,8},{8,0},{16,24},{24,16},{1,9},{9,1},{17,25},{25,17},{2,10},{10... | collective-permute-start | bytes 49160 | tf_op jit(solution)/shard_map/ppermute | solution.py:569
  61.7 3.7 %collective-permute-start.13 = (f32[32,128]{1,0:T(8,128)S(1)}, f32[32,128]{1,0:T(8,128)S(1)}, u32[]{:S(2)}, u32[]{:S(2)}) collective-permute-start(f32[32,128]{1,0:T(8,128)S(1)} %add.21), channel_id=1, source_target_pairs={{0,16},{8,24},{16,0},{24,8},{1,17},{9,25},{17,1},{25,9},{2,18},{10... | collective-permute-start | bytes 49160 | tf_op jit(solution)/shard_map/ppermute | solution.py:569
  62.4 4.6 %collective-permute-start.14 = (f32[32,128]{1,0:T(8,128)S(1)}, f32[32,128]{1,0:T(8,128)S(1)}, u32[]{:S(2)}, u32[]{:S(2)}) collective-permute-start(f32[32,128]{1,0:T(8,128)S(1)} %add.21), channel_id=1, source_target_pairs={{0,24},{8,16},{16,8},{24,0},{1,25},{9,17},{17,9},{25,1},{2,26},{10... | collective-permute-start | bytes 49160 | tf_op jit(solution)/shard_map/ppermute | solution.py:569
  67.0 8.7 %collective-permute-start.15 = (f32[32,128]{1,0:T(8,128)S(1)}, f32[32,128]{1,0:T(8,128)S(1)}, u32[]{:S(2)}, u32[]{:S(2)}) collective-permute-start(f32[32,128]{1,0:T(8,128)S(1)} %add_add_fusion.1), channel_id=1, source_target_pairs={{0,2},{1,3},{2,0},{3,1},{4,6},{5,7},{6,4},{7,5},{8,10},{9,11},{10,... | collective-permute-start | bytes 49160 | tf_op jit(solution)/shard_map/ppermute | solution.py:569
  73.3 4.6 %collective-permute-start.16 = (f32[32,128]{1,0:T(8,128)S(1)}, f32[32,128]{1,0:T(8,128)S(1)}, u32[]{:S(2)}, u32[]{:S(2)}) collective-permute-start(f32[32,128]{1,0:T(8,128)S(1)} %add_add_fusion.1), channel_id=1, source_target_pairs={{0,4},{1,5},{2,6},{3,7},{4,0},{5,1},{6,2},{7,3},{8,12},{9,13},{10,... | collective-permute-start | bytes 49160 | tf_op jit(solution)/shard_map/ppermute | solution.py:569
  74.4 5.5 %collective-permute-start.17 = (f32[32,128]{1,0:T(8,128)S(1)}, f32[32,128]{1,0:T(8,128)S(1)}, u32[]{:S(2)}, u32[]{:S(2)}) collective-permute-start(f32[32,128]{1,0:T(8,128)S(1)} %add_add_fusion.1), channel_id=1, source_target_pairs={{0,6},{1,7},{2,4},{3,5},{4,2},{5,3},{6,0},{7,1},{8,14},{9,15},{10,... | collective-permute-start | bytes 49160 | tf_op jit(solution)/shard_map/ppermute | solution.py:569

commit v6 on v5

--- a/solution.py
+++ b/solution.py
@@ -208,17 +208,20 @@
 
 
 def blend_kernel(rows, me, *refs):
-    pieces = len(refs) - 3
-    extras, (select, share, held) = refs[:pieces], refs[pieces:]
+    pieces = len(refs) - 4
+    extras, (select, share, most, held) = refs[:pieces], refs[pieces:]
     size = select.shape[2]
     tall = CAMS * rows
     sub, lane = iotas((tall, size))
     same_row = (sub & (rows - 1)) == (lane & (rows - 1))
     camera = (sub >> log2(rows)).astype(f32)
+    highest = jnp.float32(0)
     for distance, extra in enumerate(extras):
         notes = extra[2 * rows :, :].astype(f32)
+        highest = jnp.maximum(highest, jnp.max(notes[3:4, :LANES]))
         select[distance] = indicator((camera == notes[2:3, :size]) & same_row)
         held[me[0] ^ distance] = extra[...].astype(f32)
+    most[0] = highest.astype(jnp.int32)
     ones = jnp.ones((rows, share.shape[3]), f32)
     for device in range(pieces):
         if device == 0:
@@ -241,10 +244,11 @@
     return pl.pallas_call(
         functools.partial(blend_kernel, rows),
         in_specs=[smem] + [vmem] * pieces,
-        out_specs=[vmem, vmem],
+        out_specs=[vmem, vmem, smem],
         out_shape=[
             jax.ShapeDtypeStruct((pieces, CAMS * rows, size), bf16),
             jax.ShapeDtypeStruct((pieces, 2, rows, width), f32),
+            jax.ShapeDtypeStruct((1,), jnp.int32),
         ],
         scratch_shapes=[pltpu.VMEM((pieces, 3 * rows, width), f32)],
         compiler_params=pltpu.CompilerParams(vmem_limit_bytes=20 * 2**20),
@@ -253,7 +257,7 @@
 
 
 def main_kernel(
-    count, rows, chunk, own_all, above_all, below_all, inverse, select, box, merge, out, other,
+    count, rows, chunk, most, own_all, above_all, below_all, inverse, select, box, merge, out, other,
     own, above, below, sums, rest, least, product, scale, select_in, box_in, merge_in,
     arrived, ready,
 ):
@@ -404,7 +408,7 @@
         other[:, cols] = both[slot_rows:]
 
 
-def main_part(chunk, own, above, below, inverse, select, box, merge, rows, pieces, slots):
+def main_part(chunk, most, own, above, below, inverse, select, box, merge, rows, pieces, slots):
     size, width_all = own.shape
     count = size // rows
     width = width_all // pieces
@@ -412,7 +416,8 @@
     cell_rows = 3 * (rows // 2) * count
     return pl.pallas_call(
         functools.partial(main_kernel, count, rows),
-        in_specs=[pl.BlockSpec(memory_space=pltpu.SMEM)] + [pl.BlockSpec(memory_space=pl.ANY)] * 7,
+        in_specs=[pl.BlockSpec(memory_space=pltpu.SMEM)] * 2
+        + [pl.BlockSpec(memory_space=pl.ANY)] * 7,
         out_specs=[pl.BlockSpec(memory_space=pltpu.VMEM)] * 2,
         scratch_shapes=[
             pltpu.VMEM((size, width + 4 * LANES), bf16),
@@ -438,27 +443,7 @@
             flops=2 * 10**9, bytes_accessed=4 * 2**20, transcendentals=0
         ),
         name="residual",
-    )(chunk, own, above, below, inverse, select, box, merge)
-
-
-def most_kernel(*refs):
-    notes, most = refs[:-1], refs[-1]
-    highest = notes[0][...].astype(f32)
-    for note in notes[1:]:
-        highest = jnp.maximum(highest, note[...].astype(f32))
-    most[0, 0] = jnp.max(highest[3:4]).astype(jnp.int32)
-
-
-def most_cameras(extras, rows):
-    return pl.pallas_call(
-        most_kernel,
-        grid=(1,),
-        in_specs=[pl.BlockSpec((rows, LANES), lambda i: (2, 0))] * len(extras),
-        out_specs=pl.BlockSpec(memory_space=pltpu.SMEM),
-        out_shape=jax.ShapeDtypeStruct((1, 1), jnp.int32),
-        compiler_params=pltpu.CompilerParams(vmem_limit_bytes=4 * 2**20),
-        name="most_cameras",
-    )(*extras)[0, 0]
+    )(chunk, most, own, above, below, inverse, select, box, merge)
 
 
 def assemble_kernel(rows, pieces, select, share, *refs):
@@ -589,16 +574,16 @@
     ]
     inverse, select, box, merge = energies(camera_id, own, rows)
 
+    place, share, most = blend(me.reshape(1), extras, rows, count * rows)
     few = max(2, 11 * count // 16)
     parts, others = [None] * pieces, [None] * pieces
     for distance in reversed(range(pieces)):
         part, other = main_part(
-            (me ^ distance).reshape(1), own, above, below, inverse, select, box, merge,
+            (me ^ distance).reshape(1), most, own, above, below, inverse, select, box, merge,
             rows, pieces, few,
         )
         parts[distance] = exchange(part, "photo", distance) if distance else part
         others[distance] = other
-    place, share = blend(me.reshape(1), extras, rows, count * rows)
 
     def finish_few():
         return assemble(place, share, parts, [], rows)
@@ -610,7 +595,7 @@
         ]
         return assemble(place, share, parts, late, rows)
 
-    prints, partial = lax.cond(most_cameras(extras, rows) > few, finish_all, finish_few)
+    prints, partial = lax.cond(most[0] > few, finish_all, finish_few)
 
     total = summed(partial, "tile", (1,))
     total = summed(total, "photo", range(1, pieces))

time: 81 us -> 73.5 us (0.907)
  starting transfers between devices: 32.9 us -> 24.4 us
  Pallas kernels: 30.2 us -> 31.8 us
    ppermute x13, starting transfers between devices: 29.3 us -> 20.7 us  [exchange(): return lax.ppermute(array, axis, [(i, i ^ distance) for i in range(size)])]
    pallas_call x4, Pallas kernels: 20.1 us -> 21.9 us  [main_part(): pl.pallas_call(functools.partial(main_kernel, count, rows), in_specs=[pl....]
    unnamed x8 -> x6, local copies, waits for them, and re-layouts: 2.25 us -> 2.24 us
  transfers between devices with their start and end apart: 15 -> 15, of which waited for: 9 -> 9; matrix products, arithmetic and copies ran while one was open for 0% -> 0% of each run, Pallas kernels for 29% -> 27%
where the time goes in v6:
time: 73.5 us; the launch traced here: 73.2 us
  Pallas kernels  31.8 us (43%)
  starting transfers between devices  24.4 us (33%)
  waiting for transfers between devices  13.1 us (18%)
  local copies, waits for them, and re-layouts  2.24 us (3%)
  between operations  1.4 us (2%)
    pallas_call x4, Pallas kernels, main_part(): pl.pallas_call(functools.partial(main_kernel, count, rows), in_specs=[pl....  21.9 us
    ppermute x13, starting transfers between devices, exchange(): return lax.ppermute(array, axis, [(i, i ^ distance) for i in range(size)])  20.7 us
    ppermute x13, waiting for transfers between devices, exchange(): return lax.ppermute(array, axis, [(i, i ^ distance) for i in range(size)])  13.1 us
    pallas_call x1, Pallas kernels, prepare(): pl.pallas_call(prepare_kernel, in_specs=[smem, smem, vmem], out_specs=[vm...  3.32 us
    pallas_call x1, Pallas kernels, energies(): pl.pallas_call(functools.partial(energy_kernel, size // rows, rows), in_s...  2.59 us
    ppermute x1, starting transfers between devices, on_device(): above = lax.ppermute(down, 'tile', [(i, i + 1) for i in range(tiles - 1)])  2.39 us
    pallas_call x1, Pallas kernels, assemble(): pl.pallas_call(functools.partial(assemble_kernel, rows, len(parts)), in_s...  2.29 us
    unnamed x6, local copies, waits for them, and re-layouts  2.24 us
  transfers between devices with their start and end apart: 15, of which 9 were waited for; matrix products, arithmetic and copies ran while one was open for 0% of the time, Pallas kernels for 27%

profile of v6, /device:TPU:0, one launch (start us, length us, event | category | flops | bytes accessed | tf_op | source)
XLA Modules:
  0.0 73.2 jit_solution(14800911082914034447)
XLA Ops:
  0.7 1.6 %copy-done = bf16[16,16,4096]{2,1,0:T(8,128)(2,1)S(1)} copy-done((bf16[16,16,4096]{2,1,0:T(8,128)(2,1)S(1)}, bf16[16,16,4096]{2,1,0:T(8,128)(2,1)}, u32[]{:S(2)}) %copy-start) | copy-done | bytes 2097176
  2.9 3.3 %prepare.1 = (bf16[256,4096]{1,0:T(8,128)(2,1)S(1)}, bf16[192,2048]{1,0:T(8,128)(2,1)}, bf16[192,2048]{1,0:T(8,128)(2,1)}, bf16[48,1024]{1,0:T(8,128)(2,1)S(1)},...) custom-call(s32[1]{0:T(128)} %bitcast.me.chunk, s32[16]{0:T(128)S(1)} %copy-done.1, ...), custom_call_target="tpu_custom_call" | custom-call | flops 1000000000 | bytes 8388608 | tf_op jit(solution)/shard_map/prepare/pallas_call | solution.py:149
  6.2 2.4 %collective-permute-start.6 = (bf16[192,2048]{1,0:T(8,128)(2,1)}, bf16[192,2048]{1,0:T(8,128)(2,1)S(1)}, u32[]{:S(2)}, u32[]{:S(2)}) collective-permute-start(bf16[192,2048]{1,0:T(8,128)(2,1)} %get-tuple-element.82), channel_id=1, source_target_pairs={{0,1},{1,2},{2,3},{3,4},{4,5},{5,6},{6,7},{8,9},{9,10},{10,11},{11... | collective-permute-start | bytes 2359304 | tf_op jit(solution)/shard_map/ppermute | solution.py:569
  8.6 1.3 %collective-permute-start.7 = (bf16[192,2048]{1,0:T(8,128)(2,1)}, bf16[192,2048]{1,0:T(8,128)(2,1)}, u32[]{:S(2)}, u32[]{:S(2)}) collective-permute-start(bf16[192,2048]{1,0:T(8,128)(2,1)} %get-tuple-element.83), channel_id=1, source_target_pairs={{1,0},{2,1},{3,2},{4,3},{5,4},{6,5},{7,6},{9,8},{10,9},{11,10},{12... | collective-permute-start | bytes 2359304 | tf_op jit(solution)/shard_map/ppermute | solution.py:570
  9.9 2.3 %collective-permute-start.3 = (bf16[48,1024]{1,0:T(8,128)(2,1)}, bf16[48,1024]{1,0:T(8,128)(2,1)S(1)}, u32[]{:S(2)}, u32[]{:S(2)}) collective-permute-start(bf16[48,1024]{1,0:T(8,128)(2,1)} %get-tuple-element.75), channel_id=1, source_target_pairs={{0,8},{8,0},{16,24},{24,16},{1,9},{9,1},{17,25},{25,17},{2,10},{10... | collective-permute-start | bytes 294920 | tf_op jit(solution)/shard_map/ppermute | solution.py:554
  12.2 1.7 %collective-permute-start.4 = (bf16[48,1024]{1,0:T(8,128)(2,1)S(1)}, bf16[48,1024]{1,0:T(8,128)(2,1)S(1)}, u32[]{:S(2)}, u32[]{:S(2)}) collective-permute-start(bf16[48,1024]{1,0:T(8,128)(2,1)S(1)} %get-tuple-element.76), channel_id=1, source_target_pairs={{0,16},{8,24},{16,0},{24,8},{1,17},{9,25},{17,1},{25,9},{2,18},{10... | collective-permute-start | bytes 294920 | tf_op jit(solution)/shard_map/ppermute | solution.py:554
  13.9 2.6 %energies.1 = (f32[256,4096]{1,0:T(8,128)S(1)}, bf16[256,512]{1,0:T(8,128)(2,1)S(1)}, bf16[4,512,256]{2,1,0:T(8,128)(2,1)S(1)}, bf16[256,256]{1,0:T(8,128)(2,1)S(1)}) custom-call(s32[16]{0:T(128)S(1)} %copy-done.2, bf16[256,4096]{1,0:T(8,128)(2,1)S(1)} %get-tuple-element.81.own.own_all), custom_call_target="tpu_custom_call" | custom-call | flops 1000000000 | bytes 8388608 | tf_op jit(solution)/shard_map/energies/pallas_call | solution.py:194
  16.8 2.8 %collective-permute-done.5.refs_3_ = bf16[48,1024]{1,0:T(8,128)(2,1)S(1)} collective-permute-done((bf16[48,1024]{1,0:T(8,128)(2,1)S(1)}, bf16[48,1024]{1,0:T(8,128)(2,1)S(1)}, u32[]{:S(2)}, u32[]{:S(2)}) %collective-permute-start.5) | collective-permute-done | bytes 98336 | tf_op jit(solution)/shard_map/ppermute | solution.py:554
  19.6 0.9 %blend.1 = (bf16[4,512,256]{2,1,0:T(8,128)(2,1)S(1)}, f32[4,2,16,1024]{3,2,1,0:T(8,128)S(1)}, s32[1]{0:T(128)}) custom-call(s32[1]{0:T(128)} %bitcast.me.chunk, bf16[48,1024]{1,0:T(8,128)(2,1)S(1)} %get-tuple-element.74.refs_0_, bf16[48,1024]{1,0:T(8,128)(2,1)S(1)} %collective-permute-done.3.refs_1_, bf16[48,1024]{1,0:T(8,128)(2,1)S(1)} %collective-permute-done.4.refs_2_, ...), custom_call_target="tpu_custom_call" | custom-call | tf_op jit(solution)/shard_map/blend/pallas_call | solution.py:244
  20.5 5.5 %residual.7 = (bf16[176,1024]{1,0:T(8,128)(2,1)S(1)}, bf16[80,1024]{1,0:T(8,128)(2,1)S(1)}) custom-call(s32[1]{0:T(128)} %bitcast.4.chunk, s32[1]{0:T(128)} %get-tuple-element.78.most, bf16[256,4096]{1,0:T(8,128)(2,1)S(1)} %get-tuple-element.81.own.own_all, bf16[192,2048]{1,0:T(8,128)(2,1)S(1)} %collective-permute-done.6.above_all, ...), custom_call_target="tpu_custom_call" | custom-call | flops 2000000000 | bytes 4194304 | tf_op jit(solution)/shard_map/residual/pallas_call | solution.py:417
  26.0 1.1 %collective-permute-start.10 = (bf16[176,1024]{1,0:T(8,128)(2,1)S(1)}, bf16[176,1024]{1,0:T(8,128)(2,1)S(1)}, u32[]{:S(2)}, u32[]{:S(2)}) collective-permute-start(bf16[176,1024]{1,0:T(8,128)(2,1)S(1)} %get-tuple-element.91), channel_id=1, source_target_pairs={{0,24},{8,16},{16,8},{24,0},{1,25},{9,17},{17,9},{25,1},{2,26},{10... | collective-permute-start | bytes 1081352 | tf_op jit(solution)/shard_map/ppermute | solution.py:554
  27.0 5.6 %residual.6 = (bf16[176,1024]{1,0:T(8,128)(2,1)S(1)}, bf16[80,1024]{1,0:T(8,128)(2,1)S(1)}) custom-call(s32[1]{0:T(128)} %bitcast.3.chunk, s32[1]{0:T(128)} %get-tuple-element.78.most, bf16[256,4096]{1,0:T(8,128)(2,1)S(1)} %get-tuple-element.81.own.own_all, bf16[192,2048]{1,0:T(8,128)(2,1)S(1)} %collective-permute-done.6.above_all, ...), custom_call_target="tpu_custom_call" | custom-call | flops 2000000000 | bytes 4194304 | tf_op jit(solution)/shard_map/residual/pallas_call | solution.py:417
  32.6 1.9 %collective-permute-start.9 = (bf16[176,1024]{1,0:T(8,128)(2,1)S(1)}, bf16[176,1024]{1,0:T(8,128)(2,1)S(1)}, u32[]{:S(2)}, u32[]{:S(2)}) collective-permute-start(bf16[176,1024]{1,0:T(8,128)(2,1)S(1)} %get-tuple-element.90), channel_id=1, source_target_pairs={{0,16},{8,24},{16,0},{24,8},{1,17},{9,25},{17,1},{25,9},{2,18},{10... | collective-permute-start | bytes 1081352 | tf_op jit(solution)/shard_map/ppermute | solution.py:554
  34.5 5.4 %residual.5 = (bf16[176,1024]{1,0:T(8,128)(2,1)S(1)}, bf16[80,1024]{1,0:T(8,128)(2,1)S(1)}) custom-call(s32[1]{0:T(128)} %bitcast.2.chunk, s32[1]{0:T(128)} %get-tuple-element.78.most, bf16[256,4096]{1,0:T(8,128)(2,1)S(1)} %get-tuple-element.81.own.own_all, bf16[192,2048]{1,0:T(8,128)(2,1)S(1)} %collective-permute-done.6.above_all, ...), custom_call_target="tpu_custom_call" | custom-call | flops 2000000000 | bytes 4194304 | tf_op jit(solution)/shard_map/residual/pallas_call | solution.py:417
  39.9 0.8 %collective-permute-start.8 = (bf16[176,1024]{1,0:T(8,128)(2,1)S(1)}, bf16[176,1024]{1,0:T(8,128)(2,1)S(1)}, u32[]{:S(2)}, u32[]{:S(2)}) collective-permute-start(bf16[176,1024]{1,0:T(8,128)(2,1)S(1)} %get-tuple-element.89), channel_id=1, source_target_pairs={{0,8},{8,0},{16,24},{24,16},{1,9},{9,1},{17,25},{25,17},{2,10},{10... | collective-permute-start | bytes 1081352 | tf_op jit(solution)/shard_map/ppermute | solution.py:554
  41.3 5.5 %residual.4 = (bf16[176,1024]{1,0:T(8,128)(2,1)S(1)}, bf16[80,1024]{1,0:T(8,128)(2,1)S(1)}) custom-call(s32[1]{0:T(128)} %bitcast.me.chunk, s32[1]{0:T(128)} %get-tuple-element.78.most, bf16[256,4096]{1,0:T(8,128)(2,1)S(1)} %get-tuple-element.81.own.own_all, bf16[192,2048]{1,0:T(8,128)(2,1)S(1)} %collective-permute-done.6.above_all, ...), custom_call_target="tpu_custom_call" | custom-call | flops 2000000000 | bytes 4194304 | tf_op jit(solution)/shard_map/residual/pallas_call | solution.py:417
  46.8 1.5 %collective-permute-done.8 = bf16[176,1024]{1,0:T(8,128)(2,1)S(1)} collective-permute-done((bf16[176,1024]{1,0:T(8,128)(2,1)S(1)}, bf16[176,1024]{1,0:T(8,128)(2,1)S(1)}, u32[]{:S(2)}, u32[]{:S(2)}) %collective-permute-start.8) | collective-permute-done | bytes 360480 | tf_op jit(solution)/shard_map/ppermute | solution.py:554
  48.3 2.5 %conditional.1 = ((f32[32,16,1024]{2,1,0:T(8,128)}, f32[32,128]{1,0:T(8,128)S(1)})) conditional(s32[]{:T(128)} %bitcast.1, (bf16[4,512,256]{2,1,0:T(8,128)(2,1)S(1)}, f32[4,2,16,1024]{3,2,1,0:T(8,128)S(1)}, bf16[176,1024]{1,0:T(8,128)(2,1)S(1)}, bf16[176,1024]{1,0:T(8,128)(2,1)S(1)}, bf16[176,1024]{1,0:T(8,128)(2,1)S(1)}, ...), branch_computations={%region_0.0_spmd, %region_1.0_spmd} | conditional | flops 2000000000 | bytes 6160512 | solution.py:598
  48.4 2.3 %assemble.2 = (f32[32,16,1024]{2,1,0:T(8,128)}, f32[32,128]{1,0:T(8,128)S(1)}) custom-call(bf16[4,512,256]{2,1,0:T(8,128)(2,1)S(1)} %get-tuple-element.32.select, f32[4,2,16,1024]{3,2,1,0:T(8,128)S(1)} %get-tuple-element.33.share, bf16[176,1024]{1,0:T(8,128)(2,1)S(1)} %get-tuple-element.34.refs_0_, bf16[176,1024]{1,0:T(8,128)(2,1)S(1)} %get-tuple-element.35.refs_1_, ...), custom_call_target="tpu_custom_call" | custom-call | flops 2000000000 | bytes 4194304 | tf_op jit(solution)/shard_map/cond/branch_0_fun/assemble/pallas_call | solution.py:502
  50.9 2.8 %collective-permute-start.11 = (f32[32,128]{1,0:T(8,128)S(1)}, f32[32,128]{1,0:T(8,128)S(1)}, u32[]{:S(2)}, u32[]{:S(2)}) collective-permute-start(f32[32,128]{1,0:T(8,128)S(1)} %get-tuple-element.97), channel_id=1, source_target_pairs={{0,1},{1,0},{2,3},{3,2},{4,5},{5,4},{6,7},{7,6},{8,9},{9,8},{10,11... | collective-permute-start | bytes 49160 | tf_op jit(solution)/shard_map/ppermute | solution.py:554
  53.7 0.8 %collective-permute-done.11 = f32[32,128]{1,0:T(8,128)S(1)} collective-permute-done((f32[32,128]{1,0:T(8,128)S(1)}, f32[32,128]{1,0:T(8,128)S(1)}, u32[]{:S(2)}, u32[]{:S(2)}) %collective-permute-start.11) | collective-permute-done | bytes 16416 | tf_op jit(solution)/shard_map/ppermute | solution.py:554
  54.6 0.7 collective-permute-start.12
  55.2 1.7 %collective-permute-start.13 = (f32[32,128]{1,0:T(8,128)S(1)}, f32[32,128]{1,0:T(8,128)S(1)}, u32[]{:S(2)}, u32[]{:S(2)}) collective-permute-start(f32[32,128]{1,0:T(8,128)S(1)} %add.21), channel_id=1, source_target_pairs={{0,16},{8,24},{16,0},{24,8},{1,17},{9,25},{17,1},{25,9},{2,18},{10... | collective-permute-start | bytes 49160 | tf_op jit(solution)/shard_map/ppermute | solution.py:554
  56.9 1.1 %collective-permute-start.14 = (f32[32,128]{1,0:T(8,128)S(1)}, f32[32,128]{1,0:T(8,128)S(1)}, u32[]{:S(2)}, u32[]{:S(2)}) collective-permute-start(f32[32,128]{1,0:T(8,128)S(1)} %add.21), channel_id=1, source_target_pairs={{0,24},{8,16},{16,8},{24,0},{1,25},{9,17},{17,9},{25,1},{2,26},{10... | collective-permute-start | bytes 49160 | tf_op jit(solution)/shard_map/ppermute | solution.py:554
  58.3 0.7 collective-permute-done.13
  59.0 2.6 %collective-permute-done.14 = f32[32,128]{1,0:T(8,128)S(1)} collective-permute-done((f32[32,128]{1,0:T(8,128)S(1)}, f32[32,128]{1,0:T(8,128)S(1)}, u32[]{:S(2)}, u32[]{:S(2)}) %collective-permute-start.14) | collective-permute-done | bytes 16416 | tf_op jit(solution)/shard_map/ppermute | solution.py:554
  61.6 4.2 %collective-permute-start.15 = (f32[32,128]{1,0:T(8,128)S(1)}, f32[32,128]{1,0:T(8,128)S(1)}, u32[]{:S(2)}, u32[]{:S(2)}) collective-permute-start(f32[32,128]{1,0:T(8,128)S(1)} %add_add_fusion.1), channel_id=1, source_target_pairs={{0,2},{1,3},{2,0},{3,1},{4,6},{5,7},{6,4},{7,5},{8,10},{9,11},{10,... | collective-permute-start | bytes 49160 | tf_op jit(solution)/shard_map/ppermute | solution.py:554
  65.8 1.1 %collective-permute-start.16 = (f32[32,128]{1,0:T(8,128)S(1)}, f32[32,128]{1,0:T(8,128)S(1)}, u32[]{:S(2)}, u32[]{:S(2)}) collective-permute-start(f32[32,128]{1,0:T(8,128)S(1)} %add_add_fusion.1), channel_id=1, source_target_pairs={{0,4},{1,5},{2,6},{3,7},{4,0},{5,1},{6,2},{7,3},{8,12},{9,13},{10,... | collective-permute-start | bytes 49160 | tf_op jit(solution)/shard_map/ppermute | solution.py:554
  66.9 1.4 %collective-permute-start.17 = (f32[32,128]{1,0:T(8,128)S(1)}, f32[32,128]{1,0:T(8,128)S(1)}, u32[]{:S(2)}, u32[]{:S(2)}) collective-permute-start(f32[32,128]{1,0:T(8,128)S(1)} %add_add_fusion.1), channel_id=1, source_target_pairs={{0,6},{1,7},{2,4},{3,5},{4,2},{5,3},{6,0},{7,1},{8,14},{9,15},{10,... | collective-permute-start | bytes 49160 | tf_op jit(solution)/shard_map/ppermute | solution.py:554
  68.3 2.2 %collective-permute-done.16 = f32[32,128]{1,0:T(8,128)S(1)} collective-permute-done((f32[32,128]{1,0:T(8,128)S(1)}, f32[32,128]{1,0:T(8,128)S(1)}, u32[]{:S(2)}, u32[]{:S(2)}) %collective-permute-start.16) | collective-permute-done | bytes 16416 | tf_op jit(solution)/shard_map/ppermute | solution.py:554
  70.4 2.0 %collective-permute-done.17 = f32[32,128]{1,0:T(8,128)S(1)} collective-permute-done((f32[32,128]{1,0:T(8,128)S(1)}, f32[32,128]{1,0:T(8,128)S(1)}, u32[]{:S(2)}, u32[]{:S(2)}) %collective-permute-start.17) | collective-permute-done | bytes 16416 | tf_op jit(solution)/shard_map/ppermute | solution.py:554
  72.4 0.8 %correlate.1 = f32[32,32]{1,0:T(8,128)} custom-call(f32[32,128]{1,0:T(8,128)S(1)} %add_add_fusion.refs_0_), custom_call_target="tpu_custom_call" | custom-call | tf_op jit(solution)/shard_map/correlate/pallas_call | solution.py:544
  (17 shorter events, 1.2 us)
Async XLA Ops:
  0.6 13.3 %copy-start.2 = (s32[16]{0:T(128)S(1)}, s32[16]{0:T(128)}, u32[]{:S(2)}) copy-start(s32[16]{0:T(128)} %ids.3) | copy-start | bytes 196
  0.6 1.6 %copy-start = (bf16[16,16,4096]{2,1,0:T(8,128)(2,1)S(1)}, bf16[16,16,4096]{2,1,0:T(8,128)(2,1)}, u32[]{:S(2)}) copy-start(bf16[16,16,4096]{2,1,0:T(8,128)(2,1)} %photos.1) | copy-start | bytes 6291460
  2.2 0.7 copy-start.1
  6.2 14.3 %collective-permute-start.6 = (bf16[192,2048]{1,0:T(8,128)(2,1)}, bf16[192,2048]{1,0:T(8,128)(2,1)S(1)}, u32[]{:S(2)}, u32[]{:S(2)}) collective-permute-start(bf16[192,2048]{1,0:T(8,128)(2,1)} %get-tuple-element.82), channel_id=1, source_target_pairs={{0,1},{1,2},{2,3},{3,4},{4,5},{5,6},{6,7},{8,9},{9,10},{10,11},{11... | collective-permute-start | bytes 2359304 | tf_op jit(solution)/shard_map/ppermute | solution.py:569
  8.6 11.9 %collective-permute-start.7 = (bf16[192,2048]{1,0:T(8,128)(2,1)}, bf16[192,2048]{1,0:T(8,128)(2,1)}, u32[]{:S(2)}, u32[]{:S(2)}) collective-permute-start(bf16[192,2048]{1,0:T(8,128)(2,1)} %get-tuple-element.83), channel_id=1, source_target_pairs={{1,0},{2,1},{3,2},{4,3},{5,4},{6,5},{7,6},{9,8},{10,9},{11,10},{12... | collective-permute-start | bytes 2359304 | tf_op jit(solution)/shard_map/ppermute | solution.py:570
  9.9 6.6 %collective-permute-start.3 = (bf16[48,1024]{1,0:T(8,128)(2,1)}, bf16[48,1024]{1,0:T(8,128)(2,1)S(1)}, u32[]{:S(2)}, u32[]{:S(2)}) collective-permute-start(bf16[48,1024]{1,0:T(8,128)(2,1)} %get-tuple-element.75), channel_id=1, source_target_pairs={{0,8},{8,0},{16,24},{24,16},{1,9},{9,1},{17,25},{25,17},{2,10},{10... | collective-permute-start | bytes 294920 | tf_op jit(solution)/shard_map/ppermute | solution.py:554
  12.2 4.6 %collective-permute-start.4 = (bf16[48,1024]{1,0:T(8,128)(2,1)S(1)}, bf16[48,1024]{1,0:T(8,128)(2,1)S(1)}, u32[]{:S(2)}, u32[]{:S(2)}) collective-permute-start(bf16[48,1024]{1,0:T(8,128)(2,1)S(1)} %get-tuple-element.76), channel_id=1, source_target_pairs={{0,16},{8,24},{16,0},{24,8},{1,17},{9,25},{17,1},{25,9},{2,18},{10... | collective-permute-start | bytes 294920 | tf_op jit(solution)/shard_map/ppermute | solution.py:554
  13.9 5.7 %collective-permute-start.5 = (bf16[48,1024]{1,0:T(8,128)(2,1)S(1)}, bf16[48,1024]{1,0:T(8,128)(2,1)S(1)}, u32[]{:S(2)}, u32[]{:S(2)}) collective-permute-start(bf16[48,1024]{1,0:T(8,128)(2,1)S(1)} %get-tuple-element.77), channel_id=1, source_target_pairs={{0,24},{8,16},{16,8},{24,0},{1,25},{9,17},{17,9},{25,1},{2,26},{10... | collective-permute-start | bytes 294920 | tf_op jit(solution)/shard_map/ppermute | solution.py:554
  26.0 20.8 %collective-permute-start.10 = (bf16[176,1024]{1,0:T(8,128)(2,1)S(1)}, bf16[176,1024]{1,0:T(8,128)(2,1)S(1)}, u32[]{:S(2)}, u32[]{:S(2)}) collective-permute-start(bf16[176,1024]{1,0:T(8,128)(2,1)S(1)} %get-tuple-element.91), channel_id=1, source_target_pairs={{0,24},{8,16},{16,8},{24,0},{1,25},{9,17},{17,9},{25,1},{2,26},{10... | collective-permute-start | bytes 1081352 | tf_op jit(solution)/shard_map/ppermute | solution.py:554
  32.6 14.2 %collective-permute-start.9 = (bf16[176,1024]{1,0:T(8,128)(2,1)S(1)}, bf16[176,1024]{1,0:T(8,128)(2,1)S(1)}, u32[]{:S(2)}, u32[]{:S(2)}) collective-permute-start(bf16[176,1024]{1,0:T(8,128)(2,1)S(1)} %get-tuple-element.90), channel_id=1, source_target_pairs={{0,16},{8,24},{16,0},{24,8},{1,17},{9,25},{17,1},{25,9},{2,18},{10... | collective-permute-start | bytes 1081352 | tf_op jit(solution)/shard_map/ppermute | solution.py:554
  39.9 8.4 %collective-permute-start.8 = (bf16[176,1024]{1,0:T(8,128)(2,1)S(1)}, bf16[176,1024]{1,0:T(8,128)(2,1)S(1)}, u32[]{:S(2)}, u32[]{:S(2)}) collective-permute-start(bf16[176,1024]{1,0:T(8,128)(2,1)S(1)} %get-tuple-element.89), channel_id=1, source_target_pairs={{0,8},{8,0},{16,24},{24,16},{1,9},{9,1},{17,25},{25,17},{2,10},{10... | collective-permute-start | bytes 1081352 | tf_op jit(solution)/shard_map/ppermute | solution.py:554
  50.9 3.7 %collective-permute-start.11 = (f32[32,128]{1,0:T(8,128)S(1)}, f32[32,128]{1,0:T(8,128)S(1)}, u32[]{:S(2)}, u32[]{:S(2)}) collective-permute-start(f32[32,128]{1,0:T(8,128)S(1)} %get-tuple-element.97), channel_id=1, source_target_pairs={{0,1},{1,0},{2,3},{3,2},{4,5},{5,4},{6,7},{7,6},{8,9},{9,8},{10,11... | collective-permute-start | bytes 49160 | tf_op jit(solution)/shard_map/ppermute | solution.py:554
  54.6 3.7 %collective-permute-start.12 = (f32[32,128]{1,0:T(8,128)S(1)}, f32[32,128]{1,0:T(8,128)S(1)}, u32[]{:S(2)}, u32[]{:S(2)}) collective-permute-start(f32[32,128]{1,0:T(8,128)S(1)} %add.21), channel_id=1, source_target_pairs={{0,8},{8,0},{16,24},{24,16},{1,9},{9,1},{17,25},{25,17},{2,10},{10... | collective-permute-start | bytes 49160 | tf_op jit(solution)/shard_map/ppermute | solution.py:554
  55.2 3.7 %collective-permute-start.13 = (f32[32,128]{1,0:T(8,128)S(1)}, f32[32,128]{1,0:T(8,128)S(1)}, u32[]{:S(2)}, u32[]{:S(2)}) collective-permute-start(f32[32,128]{1,0:T(8,128)S(1)} %add.21), channel_id=1, source_target_pairs={{0,16},{8,24},{16,0},{24,8},{1,17},{9,25},{17,1},{25,9},{2,18},{10... | collective-permute-start | bytes 49160 | tf_op jit(solution)/shard_map/ppermute | solution.py:554
  56.9 4.6 %collective-permute-start.14 = (f32[32,128]{1,0:T(8,128)S(1)}, f32[32,128]{1,0:T(8,128)S(1)}, u32[]{:S(2)}, u32[]{:S(2)}) collective-permute-start(f32[32,128]{1,0:T(8,128)S(1)} %add.21), channel_id=1, source_target_pairs={{0,24},{8,16},{16,8},{24,0},{1,25},{9,17},{17,9},{25,1},{2,26},{10... | collective-permute-start | bytes 49160 | tf_op jit(solution)/shard_map/ppermute | solution.py:554
  61.6 6.7 %collective-permute-start.15 = (f32[32,128]{1,0:T(8,128)S(1)}, f32[32,128]{1,0:T(8,128)S(1)}, u32[]{:S(2)}, u32[]{:S(2)}) collective-permute-start(f32[32,128]{1,0:T(8,128)S(1)} %add_add_fusion.1), channel_id=1, source_target_pairs={{0,2},{1,3},{2,0},{3,1},{4,6},{5,7},{6,4},{7,5},{8,10},{9,11},{10,... | collective-permute-start | bytes 49160 | tf_op jit(solution)/shard_map/ppermute | solution.py:554
  65.8 4.6 %collective-permute-start.16 = (f32[32,128]{1,0:T(8,128)S(1)}, f32[32,128]{1,0:T(8,128)S(1)}, u32[]{:S(2)}, u32[]{:S(2)}) collective-permute-start(f32[32,128]{1,0:T(8,128)S(1)} %add_add_fusion.1), channel_id=1, source_target_pairs={{0,4},{1,5},{2,6},{3,7},{4,0},{5,1},{6,2},{7,3},{8,12},{9,13},{10,... | collective-permute-start | bytes 49160 | tf_op jit(solution)/shard_map/ppermute | solution.py:554
  66.9 5.5 %collective-permute-start.17 = (f32[32,128]{1,0:T(8,128)S(1)}, f32[32,128]{1,0:T(8,128)S(1)}, u32[]{:S(2)}, u32[]{:S(2)}) collective-permute-start(f32[32,128]{1,0:T(8,128)S(1)} %add_add_fusion.1), channel_id=1, source_target_pairs={{0,6},{1,7},{2,4},{3,5},{4,2},{5,3},{6,0},{7,1},{8,14},{9,15},{10,... | collective-permute-start | bytes 49160 | tf_op jit(solution)/shard_map/ppermute | solution.py:554

commit v7 on v6

--- a/solution.py
+++ b/solution.py
@@ -82,24 +82,17 @@
     return slots, last + 1
 
 
-def prepare_kernel(me, ids, photos, sorted_out, up_out, down_out, *extras):
+def prepare_kernel(ids_all, photos, sorted_out, up_out, down_out, *refs):
+    extras, (ids, ready) = refs[:-2], refs[-2:]
     count, rows, width = photos.shape
     cells = rows // 2
     pieces = len(extras)
     step = width // pieces
+    me = lax.axis_index("photo")
+    copy = pltpu.make_async_copy(ids_all, ids, ready)
+    copy.start()
     perm = row_permutation(count, rows)
     split = column_split()
-
-    slots, cameras = slot_numbers(ids, count)
-    sub, lane = iotas((rows, step))
-    slot_id = jnp.full((rows, step), -1, jnp.int32)
-    in_first, in_last = jnp.int32(0), jnp.int32(0)
-    for photo in range(count):
-        slot_id = jnp.where((lane >> log2(rows)) == slots[photo], ids[photo], slot_id)
-        in_first = in_first + jnp.where(ids[photo] == ids[0], 1, 0)
-        in_last = in_last + jnp.where(ids[photo] == ids[count - 1], 1, 0)
-    notes = jnp.where(sub == 0, ids[0], jnp.where(sub == 1, ids[count - 1], slot_id))
-    notes = jnp.where(sub == 3, cameras, notes).astype(f32).astype(bf16)
 
     for piece in range(pieces):
         flat = photos[:, :, piece * step : (piece + 1) * step].reshape(count * rows, step)
@@ -126,9 +119,21 @@
                         start = (band * RADII + i - (cells - RADII)) * count
                         down_out[start : start + count, cell_cols] = square
 
+    copy.wait()
+    slots, cameras = slot_numbers(ids, count)
+    sub, lane = iotas((rows, step))
+    slot_id = jnp.full((rows, step), -1, jnp.int32)
+    in_first, in_last = jnp.int32(0), jnp.int32(0)
+    for photo in range(count):
+        slot_id = jnp.where((lane >> log2(rows)) == slots[photo], ids[photo], slot_id)
+        in_first = in_first + jnp.where(ids[photo] == ids[0], 1, 0)
+        in_last = in_last + jnp.where(ids[photo] == ids[count - 1], 1, 0)
+    notes = jnp.where(sub == 0, ids[0], jnp.where(sub == 1, ids[count - 1], slot_id))
+    notes = jnp.where(sub == 3, cameras, notes).astype(f32).astype(bf16)
+
     none = jnp.zeros((rows, step), f32)
     for distance, extra in enumerate(extras):
-        cols = pl.ds(pl.multiple_of((me[0] ^ distance) * step, step), step)
+        cols = pl.ds(pl.multiple_of((me ^ distance) * step, step), step)
 
         def add(photo, total):
             pixel = photos[photo, :, cols].astype(f32)
@@ -139,16 +144,15 @@
         extra[2 * rows :, :] = notes
 
 
-def prepare(me, ids, photos, pieces):
+def prepare(ids, photos, pieces):
     count, rows, width = photos.shape
     step = width // pieces
     size = count * rows
     halo = 3 * RADII * count
     vmem = pl.BlockSpec(memory_space=pltpu.VMEM)
-    smem = pl.BlockSpec(memory_space=pltpu.SMEM)
     return pl.pallas_call(
         prepare_kernel,
-        in_specs=[smem, smem, vmem],
+        in_specs=[pl.BlockSpec(memory_space=pl.ANY), vmem],
         out_specs=[vmem] * (3 + pieces),
         out_shape=[
             jax.ShapeDtypeStruct((size, width), bf16),
@@ -156,10 +160,11 @@
             jax.ShapeDtypeStruct((halo, width // 2), bf16),
         ]
         + [jax.ShapeDtypeStruct((3 * rows, step), bf16)] * pieces,
+        scratch_shapes=[pltpu.SMEM((count,), jnp.int32), pltpu.SemaphoreType.DMA(())],
         compiler_params=pltpu.CompilerParams(vmem_limit_bytes=20 * 2**20),
         cost_estimate=pl.CostEstimate(flops=10**9, bytes_accessed=8 * 2**20, transcendentals=0),
         name="prepare",
-    )(me, ids, photos)
+    )(ids, photos)
 
 
 def energy_kernel(count, rows, ids, own, inverse, select_out, box_out, merge_out):
@@ -207,9 +212,10 @@
     )(ids, own)
 
 
-def blend_kernel(rows, me, *refs):
-    pieces = len(refs) - 4
-    extras, (select, share, most, held) = refs[:pieces], refs[pieces:]
+def blend_kernel(rows, *refs):
+    pieces = len(refs) - 5
+    me = lax.axis_index("photo")
+    extras, (select, share, most, most_row, held) = refs[:pieces], refs[pieces:]
     size = select.shape[2]
     tall = CAMS * rows
     sub, lane = iotas((tall, size))
@@ -220,45 +226,47 @@
         notes = extra[2 * rows :, :].astype(f32)
         highest = jnp.maximum(highest, jnp.max(notes[3:4, :LANES]))
         select[distance] = indicator((camera == notes[2:3, :size]) & same_row)
-        held[me[0] ^ distance] = extra[...].astype(f32)
+        held[me ^ distance] = extra[...].astype(f32)
     most[0] = highest.astype(jnp.int32)
+    most_row[...] = jnp.full(most_row.shape, highest)
     ones = jnp.ones((rows, share.shape[3]), f32)
     for device in range(pieces):
         if device == 0:
-            share[me[0] ^ device, 0] = ones
+            share[me ^ device, 0] = ones
         if device == pieces - 1:
-            share[me[0] ^ device, 1] = ones
+            share[me ^ device, 1] = ones
             continue
         late = held[device, rows : 2 * rows]
         early = held[device + 1, :rows]
         crosses = held[device, 2 * rows + 1 : 2 * rows + 2] == held[device + 1, 2 * rows : 2 * rows + 1]
         joint = 1.0 / (late + early)
-        share[me[0] ^ device, 1] = jnp.where(crosses, late * joint, 1.0)
-        share[me[0] ^ (device + 1), 0] = jnp.where(crosses, early * joint, 1.0)
-
-
-def blend(me, extras, rows, size):
+        share[me ^ device, 1] = jnp.where(crosses, late * joint, 1.0)
+        share[me ^ (device + 1), 0] = jnp.where(crosses, early * joint, 1.0)
+
+
+def blend(extras, rows, size):
     pieces, width = len(extras), extras[0].shape[1]
     vmem = pl.BlockSpec(memory_space=pltpu.VMEM)
     smem = pl.BlockSpec(memory_space=pltpu.SMEM)
     return pl.pallas_call(
         functools.partial(blend_kernel, rows),
-        in_specs=[smem] + [vmem] * pieces,
-        out_specs=[vmem, vmem, smem],
+        in_specs=[vmem] * pieces,
+        out_specs=[vmem, vmem, smem, vmem],
         out_shape=[
             jax.ShapeDtypeStruct((pieces, CAMS * rows, size), bf16),
             jax.ShapeDtypeStruct((pieces, 2, rows, width), f32),
             jax.ShapeDtypeStruct((1,), jnp.int32),
+            jax.ShapeDtypeStruct((8, LANES), f32),
         ],
         scratch_shapes=[pltpu.VMEM((pieces, 3 * rows, width), f32)],
         compiler_params=pltpu.CompilerParams(vmem_limit_bytes=20 * 2**20),
         name="blend",
-    )(me, *extras)
+    )(*extras)
 
 
 def main_kernel(
-    count, rows, chunk, most, own_all, above_all, below_all, inverse, select, box, merge, out, other,
-    own, above, below, sums, rest, least, product, scale, select_in, box_in, merge_in,
+    count, rows, distance, most, own_all, above_all, below_all, inverse, select, box, merge,
+    out, other, own, above, below, sums, rest, least, product, scale, scale_other, select_in, box_in, merge_in,
     arrived, ready,
 ):
     cells = rows // 2
@@ -266,14 +274,15 @@
     width = out.shape[1]
     blocks = width // (2 * LANES)
     slot_rows = out.shape[0]
-    base = chunk[0] * width
+    chunk = lax.axis_index("photo") ^ distance
+    base = chunk * width
     inner = []
     edges = ([], [])
     for at, (whole, local, lanes) in enumerate(
         ((own_all, own, 2 * LANES), (above_all, above, LANES), (below_all, below, LANES))
     ):
         length = blocks * lanes
-        start = chunk[0] * length
+        start = chunk * length
         for place, size_here, offset, group in (
             (start, length, lanes, inner),
             (jnp.maximum(start - lanes, 0), lanes, 0, edges[0]),
@@ -291,7 +300,7 @@
         pltpu.make_async_copy(box, box_in, ready.at[0]),
         pltpu.make_async_copy(select, select_in, ready.at[1]),
         pltpu.make_async_copy(
-            inverse.at[:, pl.ds(pl.multiple_of(base, width), width)],
+            inverse.at[pl.ds(0, slot_rows), pl.ds(pl.multiple_of(base, width), width)],
             scale,
             ready.at[2],
         ),
@@ -399,24 +408,44 @@
     for copy in late[1:]:
         copy.wait()
 
+    def fingerprints(cols, slot_slice, scale_here):
+        weighted = jnp.dot(
+            select_in[slot_slice, :], product[:, cols], preferred_element_type=f32
+        )
+        part = (weighted * scale_here[:, cols]).astype(bf16)
+        return jnp.dot(part, merge_in[...], preferred_element_type=f32).astype(bf16)
+
     for block in range(blocks):
         cols = slice(2 * block * LANES, (2 * block + 2) * LANES)
-        weighted = jnp.dot(select_in[...], product[:, cols], preferred_element_type=f32)
-        part = (weighted * scale[:, cols]).astype(bf16)
-        both = jnp.dot(part, merge_in[...], preferred_element_type=f32).astype(bf16)
-        out[:, cols] = both[:slot_rows]
-        other[:, cols] = both[slot_rows:]
-
-
-def main_part(chunk, most, own, above, below, inverse, select, box, merge, rows, pieces, slots):
+        out[:, cols] = fingerprints(cols, slice(0, slot_rows), scale)
+
+    @pl.when(jnp.max(most[...]) * rows > slot_rows)
+    def _():
+        copy = pltpu.make_async_copy(
+            inverse.at[
+                pl.ds(slot_rows, size - slot_rows), pl.ds(pl.multiple_of(base, width), width)
+            ],
+            scale_other,
+            ready.at[4],
+        )
+        copy.start()
+        copy.wait()
+
+        @pl.loop(0, blocks)
+        def _(block):
+            cols = pl.ds(pl.multiple_of(block * 2 * LANES, 2 * LANES), 2 * LANES)
+            other[:, cols] = fingerprints(cols, slice(slot_rows, size), scale_other)
+
+
+def main_part(distance, most, own, above, below, inverse, select, box, merge, rows, pieces, slots):
     size, width_all = own.shape
     count = size // rows
     width = width_all // pieces
     halo = above.shape[0]
     cell_rows = 3 * (rows // 2) * count
     return pl.pallas_call(
-        functools.partial(main_kernel, count, rows),
-        in_specs=[pl.BlockSpec(memory_space=pltpu.SMEM)] * 2
+        functools.partial(main_kernel, count, rows, distance),
+        in_specs=[pl.BlockSpec(memory_space=pltpu.VMEM)]
         + [pl.BlockSpec(memory_space=pl.ANY)] * 7,
         out_specs=[pl.BlockSpec(memory_space=pltpu.VMEM)] * 2,
         scratch_shapes=[
@@ -427,12 +456,13 @@
             pltpu.VMEM((FINE, cell_rows, width // 2 + 2 * LANES), bf16),
             pltpu.VMEM((cell_rows, 2 * LANES), f32),
             pltpu.VMEM((2 * size, width), bf16),
-            pltpu.VMEM((size, width), f32),
+            pltpu.VMEM((slots * rows, width), f32),
+            pltpu.VMEM((size - slots * rows, width), f32),
             pltpu.VMEM((size, 2 * size), bf16),
             pltpu.VMEM((RADII, 4 * LANES, 2 * LANES), bf16),
             pltpu.VMEM((2 * LANES, 2 * LANES), bf16),
             pltpu.SemaphoreType.DMA((9,)),
-            pltpu.SemaphoreType.DMA((4,)),
+            pltpu.SemaphoreType.DMA((5,)),
         ],
         out_shape=[
             jax.ShapeDtypeStruct((slots * rows, width), bf16),
@@ -443,7 +473,7 @@
             flops=2 * 10**9, bytes_accessed=4 * 2**20, transcendentals=0
         ),
         name="residual",
-    )(chunk, most, own, above, below, inverse, select, box, merge)
+    )(most, own, above, below, inverse, select, box, merge)
 
 
 def assemble_kernel(rows, pieces, select, share, *refs):
@@ -564,8 +594,7 @@
 def on_device(photos, camera_id):
     count, rows, width = photos.shape
     pieces, tiles = lax.axis_size("photo"), lax.axis_size("tile")
-    me = lax.axis_index("photo").astype(jnp.int32)
-    own, up, down, *extras = prepare(me.reshape(1), camera_id, photos, pieces)
+    own, up, down, *extras = prepare(camera_id, photos, pieces)
     above = lax.ppermute(down, "tile", [(i, i + 1) for i in range(tiles - 1)])
     below = lax.ppermute(up, "tile", [(i + 1, i) for i in range(tiles - 1)])
     extras = [
@@ -574,12 +603,12 @@
     ]
     inverse, select, box, merge = energies(camera_id, own, rows)
 
-    place, share, most = blend(me.reshape(1), extras, rows, count * rows)
+    place, share, most, most_row = blend(extras, rows, count * rows)
     few = max(2, 11 * count // 16)
     parts, others = [None] * pieces, [None] * pieces
     for distance in reversed(range(pieces)):
         part, other = main_part(
-            (me ^ distance).reshape(1), most, own, above, below, inverse, select, box, merge,
+            distance, most_row, own, above, below, inverse, select, box, merge,
             rows, pieces, few,
         )
         parts[distance] = exchange(part, "photo", distance) if distance else part

time: 73.5 us -> 65.1 us (0.89)
  Pallas kernels: 31.8 us -> 25.1 us
  starting transfers between devices: 24.4 us -> 23.4 us
    pallas_call x6, Pallas kernels: 26.1 us -> 19.4 us  [the longest x4 16.9 us: main_part(): pl.pallas_call(functools.partial(main_kernel, count, rows, distance), in_...]
    ppermute x13, starting transfers between devices: 20.7 us -> 19.7 us  [exchange(): return lax.ppermute(array, axis, [(i, i ^ distance) for i in range(size)])]
    unnamed x6 -> x4, local copies, waits for them, and re-layouts: 2.24 us -> 2.24 us
  transfers between devices with their start and end apart: 15 -> 15, of which waited for: 9 -> 9; matrix products, arithmetic and copies ran while one was open for 0% -> 0% of each run, Pallas kernels for 27% -> 25%
where the time goes in v7:
time: 65.1 us; the launch traced here: 64.8 us
  Pallas kernels  25.1 us (39%)
  starting transfers between devices  23.4 us (36%)
  waiting for transfers between devices  12.7 us (20%)
  local copies, waits for them, and re-layouts  2.24 us (3%)
  between operations  1.42 us (2%)
    ppermute x13, starting transfers between devices, exchange(): return lax.ppermute(array, axis, [(i, i ^ distance) for i in range(size)])  19.7 us
    pallas_call x4, Pallas kernels, main_part(): pl.pallas_call(functools.partial(main_kernel, count, rows, distance), in_...  16.9 us
    ppermute x13, waiting for transfers between devices, exchange(): return lax.ppermute(array, axis, [(i, i ^ distance) for i in range(size)])  12.7 us
    pallas_call x1, Pallas kernels, energies(): pl.pallas_call(functools.partial(energy_kernel, size // rows, rows), in_s...  2.59 us
    ppermute x1, starting transfers between devices, on_device(): above = lax.ppermute(down, 'tile', [(i, i + 1) for i in range(tiles - 1)])  2.41 us
    pallas_call x1, Pallas kernels, assemble(): pl.pallas_call(functools.partial(assemble_kernel, rows, len(parts)), in_s...  2.29 us
    unnamed x4, local copies, waits for them, and re-layouts  2.24 us
    pallas_call x1, Pallas kernels, prepare(): pl.pallas_call(prepare_kernel, in_specs=[pl.BlockSpec(memory_space=pl.ANY...  1.66 us
  transfers between devices with their start and end apart: 15, of which 9 were waited for; matrix products, arithmetic and copies ran while one was open for 0% of the time, Pallas kernels for 25%

profile of v7, /device:TPU:0, one launch (start us, length us, event | category | flops | bytes accessed | tf_op | source)
XLA Modules:
  0.0 64.8 jit_solution(7840002734773662907)
XLA Ops:
  0.6 1.6 %copy-done = bf16[16,16,4096]{2,1,0:T(8,128)(2,1)S(1)} copy-done((bf16[16,16,4096]{2,1,0:T(8,128)(2,1)S(1)}, bf16[16,16,4096]{2,1,0:T(8,128)(2,1)}, u32[]{:S(2)}) %copy-start) | copy-done | bytes 2097176
  2.9 1.7 %prepare.1 = (bf16[256,4096]{1,0:T(8,128)(2,1)S(1)}, bf16[192,2048]{1,0:T(8,128)(2,1)S(1)}, bf16[192,2048]{1,0:T(8,128)(2,1)S(1)}, bf16[48,1024]{1,0:T(8,128)(2,...) custom-call(s32[16]{0:T(128)S(1)} %copy-done.1, ...), custom_call_target="tpu_custom_call" | custom-call | flops 1000000000 | bytes 8388608 | tf_op jit(solution)/shard_map/prepare/pallas_call | solution.py:153
  4.5 2.4 %collective-permute-start.6 = (bf16[192,2048]{1,0:T(8,128)(2,1)S(1)}, bf16[192,2048]{1,0:T(8,128)(2,1)S(1)}, u32[]{:S(2)}, u32[]{:S(2)}) collective-permute-start(bf16[192,2048]{1,0:T(8,128)(2,1)S(1)} %get-tuple-element.84), channel_id=1, source_target_pairs={{0,1},{1,2},{2,3},{3,4},{4,5},{5,6},{6,7},{8,9},{9,10},{10,11},{11... | collective-permute-start | bytes 2359304 | tf_op jit(solution)/shard_map/ppermute | solution.py:598
  7.0 1.3 %collective-permute-start.7 = (bf16[192,2048]{1,0:T(8,128)(2,1)S(1)}, bf16[192,2048]{1,0:T(8,128)(2,1)S(1)}, u32[]{:S(2)}, u32[]{:S(2)}) collective-permute-start(bf16[192,2048]{1,0:T(8,128)(2,1)S(1)} %get-tuple-element.85), channel_id=1, source_target_pairs={{1,0},{2,1},{3,2},{4,3},{5,4},{6,5},{7,6},{9,8},{10,9},{11,10},{12... | collective-permute-start | bytes 2359304 | tf_op jit(solution)/shard_map/ppermute | solution.py:599
  8.3 2.4 %collective-permute-start.3 = (bf16[48,1024]{1,0:T(8,128)(2,1)S(1)}, bf16[48,1024]{1,0:T(8,128)(2,1)S(1)}, u32[]{:S(2)}, u32[]{:S(2)}) collective-permute-start(bf16[48,1024]{1,0:T(8,128)(2,1)S(1)} %get-tuple-element.76), channel_id=1, source_target_pairs={{0,8},{8,0},{16,24},{24,16},{1,9},{9,1},{17,25},{25,17},{2,10},{10... | collective-permute-start | bytes 294920 | tf_op jit(solution)/shard_map/ppermute | solution.py:584
  10.6 1.5 %collective-permute-start.4 = (bf16[48,1024]{1,0:T(8,128)(2,1)S(1)}, bf16[48,1024]{1,0:T(8,128)(2,1)S(1)}, u32[]{:S(2)}, u32[]{:S(2)}) collective-permute-start(bf16[48,1024]{1,0:T(8,128)(2,1)S(1)} %get-tuple-element.77), channel_id=1, source_target_pairs={{0,16},{8,24},{16,0},{24,8},{1,17},{9,25},{17,1},{25,9},{2,18},{10... | collective-permute-start | bytes 294920 | tf_op jit(solution)/shard_map/ppermute | solution.py:584
  12.2 2.6 %energies.1 = (f32[256,4096]{1,0:T(8,128)S(1)}, bf16[256,512]{1,0:T(8,128)(2,1)S(1)}, bf16[4,512,256]{2,1,0:T(8,128)(2,1)S(1)}, bf16[256,256]{1,0:T(8,128)(2,1)S(1)}) custom-call(s32[16]{0:T(128)S(1)} %copy-done.1, bf16[256,4096]{1,0:T(8,128)(2,1)S(1)} %get-tuple-element.83.own.own_all), custom_call_target="tpu_custom_call" | custom-call | flops 1000000000 | bytes 8388608 | tf_op jit(solution)/shard_map/energies/pallas_call | solution.py:199
  15.3 2.5 %collective-permute-done.5.refs_3_ = bf16[48,1024]{1,0:T(8,128)(2,1)S(1)} collective-permute-done((bf16[48,1024]{1,0:T(8,128)(2,1)S(1)}, bf16[48,1024]{1,0:T(8,128)(2,1)S(1)}, u32[]{:S(2)}, u32[]{:S(2)}) %collective-permute-start.5) | collective-permute-done | bytes 98336 | tf_op jit(solution)/shard_map/ppermute | solution.py:584
  17.8 0.9 %blend.1 = (bf16[4,512,256]{2,1,0:T(8,128)(2,1)S(1)}, f32[4,2,16,1024]{3,2,1,0:T(8,128)S(1)}, s32[1]{0:T(128)}, f32[8,128]{1,0:T(8,128)S(1)}) custom-call(bf16[48,1024]{1,0:T(8,128)(2,1)S(1)} %get-tuple-element.75.refs_0_, bf16[48,1024]{1,0:T(8,128)(2,1)S(1)} %collective-permute-done.3.refs_1_, bf16[48,1024]{1,0:T(8,128)(2,1)S(1)} %collective-permute-done.4.refs_2_, ...), custom_call_target="tpu_custom_call" | custom-call | tf_op jit(solution)/shard_map/blend/pallas_call | solution.py:251
  18.7 4.2 %residual.7 = (bf16[176,1024]{1,0:T(8,128)(2,1)S(1)}, bf16[80,1024]{1,0:T(8,128)(2,1)S(1)}) custom-call(f32[8,128]{1,0:T(8,128)S(1)} %get-tuple-element.82.most, bf16[256,4096]{1,0:T(8,128)(2,1)S(1)} %get-tuple-element.83.own.own_all, bf16[192,2048]{1,0:T(8,128)(2,1)S(1)} %collective-permute-done.6.above_all, ...), custom_call_target="tpu_custom_call" | custom-call | flops 2000000000 | bytes 4194304 | tf_op jit(solution)/shard_map/residual/pallas_call | solution.py:446
  22.9 1.1 %collective-permute-start.10 = (bf16[176,1024]{1,0:T(8,128)(2,1)S(1)}, bf16[176,1024]{1,0:T(8,128)(2,1)S(1)}, u32[]{:S(2)}, u32[]{:S(2)}) collective-permute-start(bf16[176,1024]{1,0:T(8,128)(2,1)S(1)} %get-tuple-element.93), channel_id=1, source_target_pairs={{0,24},{8,16},{16,8},{24,0},{1,25},{9,17},{17,9},{25,1},{2,26},{10... | collective-permute-start | bytes 1081352 | tf_op jit(solution)/shard_map/ppermute | solution.py:584
  24.0 4.3 %residual.6 = (bf16[176,1024]{1,0:T(8,128)(2,1)S(1)}, bf16[80,1024]{1,0:T(8,128)(2,1)S(1)}) custom-call(f32[8,128]{1,0:T(8,128)S(1)} %get-tuple-element.82.most, bf16[256,4096]{1,0:T(8,128)(2,1)S(1)} %get-tuple-element.83.own.own_all, bf16[192,2048]{1,0:T(8,128)(2,1)S(1)} %collective-permute-done.6.above_all, ...), custom_call_target="tpu_custom_call" | custom-call | flops 2000000000 | bytes 4194304 | tf_op jit(solution)/shard_map/residual/pallas_call | solution.py:446
  28.4 1.8 %collective-permute-start.9 = (bf16[176,1024]{1,0:T(8,128)(2,1)S(1)}, bf16[176,1024]{1,0:T(8,128)(2,1)S(1)}, u32[]{:S(2)}, u32[]{:S(2)}) collective-permute-start(bf16[176,1024]{1,0:T(8,128)(2,1)S(1)} %get-tuple-element.92), channel_id=1, source_target_pairs={{0,16},{8,24},{16,0},{24,8},{1,17},{9,25},{17,1},{25,9},{2,18},{10... | collective-permute-start | bytes 1081352 | tf_op jit(solution)/shard_map/ppermute | solution.py:584
  30.2 4.1 %residual.5 = (bf16[176,1024]{1,0:T(8,128)(2,1)S(1)}, bf16[80,1024]{1,0:T(8,128)(2,1)S(1)}) custom-call(f32[8,128]{1,0:T(8,128)S(1)} %get-tuple-element.82.most, bf16[256,4096]{1,0:T(8,128)(2,1)S(1)} %get-tuple-element.83.own.own_all, bf16[192,2048]{1,0:T(8,128)(2,1)S(1)} %collective-permute-done.6.above_all, ...), custom_call_target="tpu_custom_call" | custom-call | flops 2000000000 | bytes 4194304 | tf_op jit(solution)/shard_map/residual/pallas_call | solution.py:446
  34.4 0.8 %collective-permute-start.8 = (bf16[176,1024]{1,0:T(8,128)(2,1)S(1)}, bf16[176,1024]{1,0:T(8,128)(2,1)S(1)}, u32[]{:S(2)}, u32[]{:S(2)}) collective-permute-start(bf16[176,1024]{1,0:T(8,128)(2,1)S(1)} %get-tuple-element.91), channel_id=1, source_target_pairs={{0,8},{8,0},{16,24},{24,16},{1,9},{9,1},{17,25},{25,17},{2,10},{10... | collective-permute-start | bytes 1081352 | tf_op jit(solution)/shard_map/ppermute | solution.py:584
  35.8 4.2 %residual.4 = (bf16[176,1024]{1,0:T(8,128)(2,1)S(1)}, bf16[80,1024]{1,0:T(8,128)(2,1)S(1)}) custom-call(f32[8,128]{1,0:T(8,128)S(1)} %get-tuple-element.82.most, bf16[256,4096]{1,0:T(8,128)(2,1)S(1)} %get-tuple-element.83.own.own_all, bf16[192,2048]{1,0:T(8,128)(2,1)S(1)} %collective-permute-done.6.above_all, ...), custom_call_target="tpu_custom_call" | custom-call | flops 2000000000 | bytes 4194304 | tf_op jit(solution)/shard_map/residual/pallas_call | solution.py:446
  40.0 1.7 %collective-permute-done.9 = bf16[176,1024]{1,0:T(8,128)(2,1)S(1)} collective-permute-done((bf16[176,1024]{1,0:T(8,128)(2,1)S(1)}, bf16[176,1024]{1,0:T(8,128)(2,1)S(1)}, u32[]{:S(2)}, u32[]{:S(2)}) %collective-permute-start.9) | collective-permute-done | bytes 360480 | tf_op jit(solution)/shard_map/ppermute | solution.py:584
  41.7 1.1 %collective-permute-done.8 = bf16[176,1024]{1,0:T(8,128)(2,1)S(1)} collective-permute-done((bf16[176,1024]{1,0:T(8,128)(2,1)S(1)}, bf16[176,1024]{1,0:T(8,128)(2,1)S(1)}, u32[]{:S(2)}, u32[]{:S(2)}) %collective-permute-start.8) | collective-permute-done | bytes 360480 | tf_op jit(solution)/shard_map/ppermute | solution.py:584
  42.8 2.3 %conditional.1 = ((f32[32,16,1024]{2,1,0:T(8,128)}, f32[32,128]{1,0:T(8,128)S(1)})) conditional(s32[]{:T(128)} %bitcast, (bf16[4,512,256]{2,1,0:T(8,128)(2,1)S(1)}, f32[4,2,16,1024]{3,2,1,0:T(8,128)S(1)}, bf16[176,1024]{1,0:T(8,128)(2,1)S(1)}, bf16[176,1024]{1,0:T(8,128)(2,1)S(1)}, bf16[176,1024]{1,0:T(8,128)(2,1)S(1)}, ...), branch_computations={%region_0.0_spmd, %region_1.0_spmd} | conditional | flops 2000000000 | bytes 6160512 | solution.py:627
  42.8 2.3 %assemble.2 = (f32[32,16,1024]{2,1,0:T(8,128)}, f32[32,128]{1,0:T(8,128)S(1)}) custom-call(bf16[4,512,256]{2,1,0:T(8,128)(2,1)S(1)} %get-tuple-element.32.select, f32[4,2,16,1024]{3,2,1,0:T(8,128)S(1)} %get-tuple-element.33.share, bf16[176,1024]{1,0:T(8,128)(2,1)S(1)} %get-tuple-element.34.refs_0_, bf16[176,1024]{1,0:T(8,128)(2,1)S(1)} %get-tuple-element.35.refs_1_, ...), custom_call_target="tpu_custom_call" | custom-call | flops 2000000000 | bytes 4194304 | tf_op jit(solution)/shard_map/cond/branch_0_fun/assemble/pallas_call | solution.py:532
  45.2 2.7 %collective-permute-start.11 = (f32[32,128]{1,0:T(8,128)S(1)}, f32[32,128]{1,0:T(8,128)S(1)}, u32[]{:S(2)}, u32[]{:S(2)}) collective-permute-start(f32[32,128]{1,0:T(8,128)S(1)} %get-tuple-element.99), channel_id=1, source_target_pairs={{0,1},{1,0},{2,3},{3,2},{4,5},{5,4},{6,7},{7,6},{8,9},{9,8},{10,11... | collective-permute-start | bytes 49160 | tf_op jit(solution)/shard_map/ppermute | solution.py:584
  47.9 0.8 %collective-permute-done.11 = f32[32,128]{1,0:T(8,128)S(1)} collective-permute-done((f32[32,128]{1,0:T(8,128)S(1)}, f32[32,128]{1,0:T(8,128)S(1)}, u32[]{:S(2)}, u32[]{:S(2)}) %collective-permute-start.11) | collective-permute-done | bytes 16416 | tf_op jit(solution)/shard_map/ppermute | solution.py:584
  48.7 0.8 %collective-permute-start.14 = (f32[32,128]{1,0:T(8,128)S(1)}, f32[32,128]{1,0:T(8,128)S(1)}, u32[]{:S(2)}, u32[]{:S(2)}) collective-permute-start(f32[32,128]{1,0:T(8,128)S(1)} %add.21), channel_id=1, source_target_pairs={{0,24},{8,16},{16,8},{24,0},{1,25},{9,17},{17,9},{25,1},{2,26},{10... | collective-permute-start | bytes 49160 | tf_op jit(solution)/shard_map/ppermute | solution.py:584
  49.5 1.4 %collective-permute-start.13 = (f32[32,128]{1,0:T(8,128)S(1)}, f32[32,128]{1,0:T(8,128)S(1)}, u32[]{:S(2)}, u32[]{:S(2)}) collective-permute-start(f32[32,128]{1,0:T(8,128)S(1)} %add.21), channel_id=1, source_target_pairs={{0,16},{8,24},{16,0},{24,8},{1,17},{9,25},{17,1},{25,9},{2,18},{10... | collective-permute-start | bytes 49160 | tf_op jit(solution)/shard_map/ppermute | solution.py:584
  50.9 1.3 %collective-permute-start.12 = (f32[32,128]{1,0:T(8,128)S(1)}, f32[32,128]{1,0:T(8,128)S(1)}, u32[]{:S(2)}, u32[]{:S(2)}) collective-permute-start(f32[32,128]{1,0:T(8,128)S(1)} %add.21), channel_id=1, source_target_pairs={{0,8},{8,0},{16,24},{24,16},{1,9},{9,1},{17,25},{25,17},{2,10},{10... | collective-permute-start | bytes 49160 | tf_op jit(solution)/shard_map/ppermute | solution.py:584
  52.2 1.2 %collective-permute-done.14 = f32[32,128]{1,0:T(8,128)S(1)} collective-permute-done((f32[32,128]{1,0:T(8,128)S(1)}, f32[32,128]{1,0:T(8,128)S(1)}, u32[]{:S(2)}, u32[]{:S(2)}) %collective-permute-start.14) | collective-permute-done | bytes 16416 | tf_op jit(solution)/shard_map/ppermute | solution.py:584
  53.4 1.2 %collective-permute-done.12 = f32[32,128]{1,0:T(8,128)S(1)} collective-permute-done((f32[32,128]{1,0:T(8,128)S(1)}, f32[32,128]{1,0:T(8,128)S(1)}, u32[]{:S(2)}, u32[]{:S(2)}) %collective-permute-start.12) | collective-permute-done | bytes 16416 | tf_op jit(solution)/shard_map/ppermute | solution.py:584
  54.7 3.0 %collective-permute-start.17 = (f32[32,128]{1,0:T(8,128)S(1)}, f32[32,128]{1,0:T(8,128)S(1)}, u32[]{:S(2)}, u32[]{:S(2)}) collective-permute-start(f32[32,128]{1,0:T(8,128)S(1)} %add_add_fusion.1), channel_id=1, source_target_pairs={{0,6},{1,7},{2,4},{3,5},{4,2},{5,3},{6,0},{7,1},{8,14},{9,15},{10,... | collective-permute-start | bytes 49160 | tf_op jit(solution)/shard_map/ppermute | solution.py:584
  57.7 2.6 %collective-permute-start.16 = (f32[32,128]{1,0:T(8,128)S(1)}, f32[32,128]{1,0:T(8,128)S(1)}, u32[]{:S(2)}, u32[]{:S(2)}) collective-permute-start(f32[32,128]{1,0:T(8,128)S(1)} %add_add_fusion.1), channel_id=1, source_target_pairs={{0,4},{1,5},{2,6},{3,7},{4,0},{5,1},{6,2},{7,3},{8,12},{9,13},{10,... | collective-permute-start | bytes 49160 | tf_op jit(solution)/shard_map/ppermute | solution.py:584
  60.4 1.9 %collective-permute-done.16 = f32[32,128]{1,0:T(8,128)S(1)} collective-permute-done((f32[32,128]{1,0:T(8,128)S(1)}, f32[32,128]{1,0:T(8,128)S(1)}, u32[]{:S(2)}, u32[]{:S(2)}) %collective-permute-start.16) | collective-permute-done | bytes 16416 | tf_op jit(solution)/shard_map/ppermute | solution.py:584
  62.4 1.7 %collective-permute-done.15 = f32[32,128]{1,0:T(8,128)S(1)} collective-permute-done((f32[32,128]{1,0:T(8,128)S(1)}, f32[32,128]{1,0:T(8,128)S(1)}, u32[]{:S(2)}, u32[]{:S(2)}) %collective-permute-start.15) | collective-permute-done | bytes 16416 | tf_op jit(solution)/shard_map/ppermute | solution.py:584
  64.0 0.8 %correlate.1 = f32[32,32]{1,0:T(8,128)} custom-call(f32[32,128]{1,0:T(8,128)S(1)} %add_add_fusion.refs_0_), custom_call_target="tpu_custom_call" | custom-call | tf_op jit(solution)/shard_map/correlate/pallas_call | solution.py:574
  (15 shorter events, 1.4 us)
Async XLA Ops:
  0.6 1.6 %copy-start = (bf16[16,16,4096]{2,1,0:T(8,128)(2,1)S(1)}, bf16[16,16,4096]{2,1,0:T(8,128)(2,1)}, u32[]{:S(2)}) copy-start(bf16[16,16,4096]{2,1,0:T(8,128)(2,1)} %photos.1) | copy-start | bytes 6291460
  2.2 0.7 %copy-start.1 = (s32[16]{0:T(128)S(1)}, s32[16]{0:T(128)}, u32[]{:S(2)}) copy-start(s32[16]{0:T(128)} %ids.1) | copy-start | bytes 196
  4.5 14.1 %collective-permute-start.6 = (bf16[192,2048]{1,0:T(8,128)(2,1)S(1)}, bf16[192,2048]{1,0:T(8,128)(2,1)S(1)}, u32[]{:S(2)}, u32[]{:S(2)}) collective-permute-start(bf16[192,2048]{1,0:T(8,128)(2,1)S(1)} %get-tuple-element.84), channel_id=1, source_target_pairs={{0,1},{1,2},{2,3},{3,4},{4,5},{5,6},{6,7},{8,9},{9,10},{10,11},{11... | collective-permute-start | bytes 2359304 | tf_op jit(solution)/shard_map/ppermute | solution.py:598
  7.0 11.7 %collective-permute-start.7 = (bf16[192,2048]{1,0:T(8,128)(2,1)S(1)}, bf16[192,2048]{1,0:T(8,128)(2,1)S(1)}, u32[]{:S(2)}, u32[]{:S(2)}) collective-permute-start(bf16[192,2048]{1,0:T(8,128)(2,1)S(1)} %get-tuple-element.85), channel_id=1, source_target_pairs={{1,0},{2,1},{3,2},{4,3},{5,4},{6,5},{7,6},{9,8},{10,9},{11,10},{12... | collective-permute-start | bytes 2359304 | tf_op jit(solution)/shard_map/ppermute | solution.py:599
  8.3 6.5 %collective-permute-start.3 = (bf16[48,1024]{1,0:T(8,128)(2,1)S(1)}, bf16[48,1024]{1,0:T(8,128)(2,1)S(1)}, u32[]{:S(2)}, u32[]{:S(2)}) collective-permute-start(bf16[48,1024]{1,0:T(8,128)(2,1)S(1)} %get-tuple-element.76), channel_id=1, source_target_pairs={{0,8},{8,0},{16,24},{24,16},{1,9},{9,1},{17,25},{25,17},{2,10},{10... | collective-permute-start | bytes 294920 | tf_op jit(solution)/shard_map/ppermute | solution.py:584
  10.6 4.6 %collective-permute-start.4 = (bf16[48,1024]{1,0:T(8,128)(2,1)S(1)}, bf16[48,1024]{1,0:T(8,128)(2,1)S(1)}, u32[]{:S(2)}, u32[]{:S(2)}) collective-permute-start(bf16[48,1024]{1,0:T(8,128)(2,1)S(1)} %get-tuple-element.77), channel_id=1, source_target_pairs={{0,16},{8,24},{16,0},{24,8},{1,17},{9,25},{17,1},{25,9},{2,18},{10... | collective-permute-start | bytes 294920 | tf_op jit(solution)/shard_map/ppermute | solution.py:584
  12.1 5.7 %collective-permute-start.5 = (bf16[48,1024]{1,0:T(8,128)(2,1)S(1)}, bf16[48,1024]{1,0:T(8,128)(2,1)S(1)}, u32[]{:S(2)}, u32[]{:S(2)}) collective-permute-start(bf16[48,1024]{1,0:T(8,128)(2,1)S(1)} %get-tuple-element.78), channel_id=1, source_target_pairs={{0,24},{8,16},{16,8},{24,0},{1,25},{9,17},{17,9},{25,1},{2,26},{10... | collective-permute-start | bytes 294920 | tf_op jit(solution)/shard_map/ppermute | solution.py:584
  22.9 17.1 %collective-permute-start.10 = (bf16[176,1024]{1,0:T(8,128)(2,1)S(1)}, bf16[176,1024]{1,0:T(8,128)(2,1)S(1)}, u32[]{:S(2)}, u32[]{:S(2)}) collective-permute-start(bf16[176,1024]{1,0:T(8,128)(2,1)S(1)} %get-tuple-element.93), channel_id=1, source_target_pairs={{0,24},{8,16},{16,8},{24,0},{1,25},{9,17},{17,9},{25,1},{2,26},{10... | collective-permute-start | bytes 1081352 | tf_op jit(solution)/shard_map/ppermute | solution.py:584
  28.4 13.3 %collective-permute-start.9 = (bf16[176,1024]{1,0:T(8,128)(2,1)S(1)}, bf16[176,1024]{1,0:T(8,128)(2,1)S(1)}, u32[]{:S(2)}, u32[]{:S(2)}) collective-permute-start(bf16[176,1024]{1,0:T(8,128)(2,1)S(1)} %get-tuple-element.92), channel_id=1, source_target_pairs={{0,16},{8,24},{16,0},{24,8},{1,17},{9,25},{17,1},{25,9},{2,18},{10... | collective-permute-start | bytes 1081352 | tf_op jit(solution)/shard_map/ppermute | solution.py:584
  34.4 8.5 %collective-permute-start.8 = (bf16[176,1024]{1,0:T(8,128)(2,1)S(1)}, bf16[176,1024]{1,0:T(8,128)(2,1)S(1)}, u32[]{:S(2)}, u32[]{:S(2)}) collective-permute-start(bf16[176,1024]{1,0:T(8,128)(2,1)S(1)} %get-tuple-element.91), channel_id=1, source_target_pairs={{0,8},{8,0},{16,24},{24,16},{1,9},{9,1},{17,25},{25,17},{2,10},{10... | collective-permute-start | bytes 1081352 | tf_op jit(solution)/shard_map/ppermute | solution.py:584
  45.2 3.6 %collective-permute-start.11 = (f32[32,128]{1,0:T(8,128)S(1)}, f32[32,128]{1,0:T(8,128)S(1)}, u32[]{:S(2)}, u32[]{:S(2)}) collective-permute-start(f32[32,128]{1,0:T(8,128)S(1)} %get-tuple-element.99), channel_id=1, source_target_pairs={{0,1},{1,0},{2,3},{3,2},{4,5},{5,4},{6,7},{7,6},{8,9},{9,8},{10,11... | collective-permute-start | bytes 49160 | tf_op jit(solution)/shard_map/ppermute | solution.py:584
  48.7 4.7 %collective-permute-start.14 = (f32[32,128]{1,0:T(8,128)S(1)}, f32[32,128]{1,0:T(8,128)S(1)}, u32[]{:S(2)}, u32[]{:S(2)}) collective-permute-start(f32[32,128]{1,0:T(8,128)S(1)} %add.21), channel_id=1, source_target_pairs={{0,24},{8,16},{16,8},{24,0},{1,25},{9,17},{17,9},{25,1},{2,26},{10... | collective-permute-start | bytes 49160 | tf_op jit(solution)/shard_map/ppermute | solution.py:584
  49.5 3.9 %collective-permute-start.13 = (f32[32,128]{1,0:T(8,128)S(1)}, f32[32,128]{1,0:T(8,128)S(1)}, u32[]{:S(2)}, u32[]{:S(2)}) collective-permute-start(f32[32,128]{1,0:T(8,128)S(1)} %add.21), channel_id=1, source_target_pairs={{0,16},{8,24},{16,0},{24,8},{1,17},{9,25},{17,1},{25,9},{2,18},{10... | collective-permute-start | bytes 49160 | tf_op jit(solution)/shard_map/ppermute | solution.py:584
  50.9 3.7 %collective-permute-start.12 = (f32[32,128]{1,0:T(8,128)S(1)}, f32[32,128]{1,0:T(8,128)S(1)}, u32[]{:S(2)}, u32[]{:S(2)}) collective-permute-start(f32[32,128]{1,0:T(8,128)S(1)} %add.21), channel_id=1, source_target_pairs={{0,8},{8,0},{16,24},{24,16},{1,9},{9,1},{17,25},{25,17},{2,10},{10... | collective-permute-start | bytes 49160 | tf_op jit(solution)/shard_map/ppermute | solution.py:584
  54.7 5.8 %collective-permute-start.17 = (f32[32,128]{1,0:T(8,128)S(1)}, f32[32,128]{1,0:T(8,128)S(1)}, u32[]{:S(2)}, u32[]{:S(2)}) collective-permute-start(f32[32,128]{1,0:T(8,128)S(1)} %add_add_fusion.1), channel_id=1, source_target_pairs={{0,6},{1,7},{2,4},{3,5},{4,2},{5,3},{6,0},{7,1},{8,14},{9,15},{10,... | collective-permute-start | bytes 49160 | tf_op jit(solution)/shard_map/ppermute | solution.py:584
  57.7 4.7 %collective-permute-start.16 = (f32[32,128]{1,0:T(8,128)S(1)}, f32[32,128]{1,0:T(8,128)S(1)}, u32[]{:S(2)}, u32[]{:S(2)}) collective-permute-start(f32[32,128]{1,0:T(8,128)S(1)} %add_add_fusion.1), channel_id=1, source_target_pairs={{0,4},{1,5},{2,6},{3,7},{4,0},{5,1},{6,2},{7,3},{8,12},{9,13},{10,... | collective-permute-start | bytes 49160 | tf_op jit(solution)/shard_map/ppermute | solution.py:584
  60.3 3.7 %collective-permute-start.15 = (f32[32,128]{1,0:T(8,128)S(1)}, f32[32,128]{1,0:T(8,128)S(1)}, u32[]{:S(2)}, u32[]{:S(2)}) collective-permute-start(f32[32,128]{1,0:T(8,128)S(1)} %add_add_fusion.1), channel_id=1, source_target_pairs={{0,2},{1,3},{2,0},{3,1},{4,6},{5,7},{6,4},{7,5},{8,10},{9,11},{10,... | collective-permute-start | bytes 49160 | tf_op jit(solution)/shard_map/ppermute | solution.py:584

commit v8 on v7

--- a/solution.py
+++ b/solution.py
@@ -82,19 +82,31 @@
     return slots, last + 1
 
 
-def prepare_kernel(ids_all, photos, sorted_out, up_out, down_out, *refs):
-    extras, (ids, ready) = refs[:-2], refs[-2:]
+def prepare_kernel(ids_all, photos_all, sorted_all, near_all, far_all, *refs):
+    extras = refs[:-8]
+    photos, sorted_out, near_out, far_out, arrived, sent, ids, ready = refs[-8:]
     count, rows, width = photos.shape
     cells = rows // 2
     pieces = len(extras)
     step = width // pieces
     me = lax.axis_index("photo")
+    odd_tile = (lax.axis_index("tile") & 1) == 1
+    copies = []
+    for piece in range(pieces):
+        cols = pl.ds(piece * step, step)
+        copies.append(
+            pltpu.make_async_copy(
+                photos_all.at[:, :, cols], photos.at[:, :, cols], arrived.at[piece]
+            )
+        )
+        copies[-1].start()
     copy = pltpu.make_async_copy(ids_all, ids, ready)
     copy.start()
     perm = row_permutation(count, rows)
     split = column_split()
 
     for piece in range(pieces):
+        copies[piece].wait()
         flat = photos[:, :, piece * step : (piece + 1) * step].reshape(count * rows, step)
         by_row = jnp.dot(perm, flat, preferred_element_type=f32).astype(bf16)
         for inner in range(step // (2 * LANES)):
@@ -104,6 +116,7 @@
             pixels = by_row[:, inner * 2 * LANES : (inner + 1) * 2 * LANES]
             parted = jnp.dot(pixels, split, preferred_element_type=f32)
             sorted_out[:, cols] = parted.astype(bf16)
+            edges = {}
             for i in range(cells):
                 if RADII <= i < cells - RADII:
                     continue
@@ -111,13 +124,28 @@
                 low = parted[(2 * i + 1) * count : (2 * i + 2) * count]
                 bands = haar_rows(top[:, :LANES], top[:, LANES:], low[:, :LANES], low[:, LANES:])
                 for band in range(3):
-                    square = (bands[band] * bands[band]).astype(bf16)
-                    if i < RADII:
-                        start = (band * RADII + i) * count
-                        up_out[start : start + count, cell_cols] = square
-                    if i >= cells - RADII:
-                        start = (band * RADII + i - (cells - RADII)) * count
-                        down_out[start : start + count, cell_cols] = square
+                    edges[band, i] = bands[band] * bands[band]
+            for band in range(3):
+                for i in range(RADII):
+                    start = (band * RADII + i) * count
+                    upper, lower = edges[band, i], edges[band, cells - RADII + i]
+                    near_out[start : start + count, cell_cols] = jnp.where(
+                        odd_tile, upper, lower
+                    ).astype(bf16)
+                    far_out[start : start + count, cell_cols] = jnp.where(
+                        odd_tile, lower, upper
+                    ).astype(bf16)
+        for at, (local, whole) in enumerate(
+            ((sorted_out, sorted_all), (near_out, near_all), (far_out, far_all))
+        ):
+            length = whole.shape[1] // pieces
+            there = pl.ds(piece * length, length)
+            copies.append(
+                pltpu.make_async_copy(
+                    local.at[:, there], whole.at[:, there], sent.at[at * pieces + piece]
+                )
+            )
+            copies[-1].start()
 
     copy.wait()
     slots, cameras = slot_numbers(ids, count)
@@ -142,6 +170,8 @@
         extra[:rows, :] = lax.fori_loop(0, in_first, add, none).astype(bf16)
         extra[rows : 2 * rows, :] = lax.fori_loop(count - in_last, count, add, none).astype(bf16)
         extra[2 * rows :, :] = notes
+    for copy_out in copies[pieces:]:
+        copy_out.wait()
 
 
 def prepare(ids, photos, pieces):
@@ -152,23 +182,40 @@
     vmem = pl.BlockSpec(memory_space=pltpu.VMEM)
     return pl.pallas_call(
         prepare_kernel,
-        in_specs=[pl.BlockSpec(memory_space=pl.ANY), vmem],
-        out_specs=[vmem] * (3 + pieces),
+        in_specs=[pl.BlockSpec(memory_space=pl.ANY)] * 2,
+        out_specs=[pl.BlockSpec(memory_space=pl.ANY)] * 3 + [vmem] * pieces,
         out_shape=[
             jax.ShapeDtypeStruct((size, width), bf16),
             jax.ShapeDtypeStruct((halo, width // 2), bf16),
             jax.ShapeDtypeStruct((halo, width // 2), bf16),
         ]
         + [jax.ShapeDtypeStruct((3 * rows, step), bf16)] * pieces,
-        scratch_shapes=[pltpu.SMEM((count,), jnp.int32), pltpu.SemaphoreType.DMA(())],
-        compiler_params=pltpu.CompilerParams(vmem_limit_bytes=20 * 2**20),
+        scratch_shapes=[
+            pltpu.VMEM((count, rows, width), bf16),
+            pltpu.VMEM((size, width), bf16),
+            pltpu.VMEM((halo, width // 2), bf16),
+            pltpu.VMEM((halo, width // 2), bf16),
+            pltpu.SemaphoreType.DMA((pieces,)),
+            pltpu.SemaphoreType.DMA((3 * pieces,)),
+            pltpu.SMEM((count,), jnp.int32),
+            pltpu.SemaphoreType.DMA(()),
+        ],
+        compiler_params=pltpu.CompilerParams(vmem_limit_bytes=56 * 2**20),
         cost_estimate=pl.CostEstimate(flops=10**9, bytes_accessed=8 * 2**20, transcendentals=0),
         name="prepare",
     )(ids, photos)
 
 
-def energy_kernel(count, rows, ids, own, inverse, select_out, box_out, merge_out):
+def energy_kernel(
+    count, rows, ids_all, own, inverse, select_out, box_out, merge_out, ids, ready
+):
     size, width = own.shape
+    copy = pltpu.make_async_copy(ids_all, ids, ready)
+    copy.start()
+    for radius in range(1, RADII + 1):
+        box_out[radius - 1] = box_matrix(radius)
+    merge_out[...] = column_merge()
+    copy.wait()
     slots, _ = slot_numbers(ids, count)
     sub, lane = iotas((size, size))
     lane_photo = lane & (count - 1)
@@ -180,9 +227,6 @@
     select = indicator(in_slot & same_row)
     select = jnp.concatenate([select, select], axis=1)
     select_out[...] = select
-    for radius in range(1, RADII + 1):
-        box_out[radius - 1] = box_matrix(radius)
-    merge_out[...] = column_merge()
 
     for block in range(width // (2 * LANES)):
         cols = slice(block * 2 * LANES, (block + 1) * 2 * LANES)
@@ -195,10 +239,9 @@
 def energies(ids, own, rows):
     size, width = own.shape
     vmem = pl.BlockSpec(memory_space=pltpu.VMEM)
-    smem = pl.BlockSpec(memory_space=pltpu.SMEM)
     return pl.pallas_call(
         functools.partial(energy_kernel, size // rows, rows),
-        in_specs=[smem, vmem],
+        in_specs=[pl.BlockSpec(memory_space=pl.ANY), vmem],
         out_specs=[vmem] * 4,
         out_shape=[
             jax.ShapeDtypeStruct((size, width), f32),
@@ -206,6 +249,7 @@
             jax.ShapeDtypeStruct((RADII, 4 * LANES, 2 * LANES), bf16),
             jax.ShapeDtypeStruct((2 * LANES, 2 * LANES), bf16),
         ],
+        scratch_shapes=[pltpu.SMEM((size // rows,), jnp.int32), pltpu.SemaphoreType.DMA(())],
         compiler_params=pltpu.CompilerParams(vmem_limit_bytes=20 * 2**20),
         cost_estimate=pl.CostEstimate(flops=10**9, bytes_accessed=8 * 2**20, transcendentals=0),
         name="energies",
@@ -265,8 +309,8 @@
 
 
 def main_kernel(
-    count, rows, distance, most, own_all, above_all, below_all, inverse, select, box, merge,
-    out, other, own, above, below, sums, rest, least, product, scale, scale_other, select_in, box_in, merge_in,
+    count, rows, distance, most, own_all, near_all, far_all, inverse, select, box, merge,
+    out, other, own, halos, sums, rest, least, product, scale, scale_other, select_in, box_in, merge_in,
     arrived, ready,
 ):
     cells = rows // 2
@@ -276,13 +320,17 @@
     slot_rows = out.shape[0]
     chunk = lax.axis_index("photo") ^ distance
     base = chunk * width
+    odd_tile = lax.axis_index("tile") & 1
+    above, below = halos.at[0], halos.at[1]
     inner = []
     edges = ([], [])
     for at, (whole, local, lanes) in enumerate(
-        ((own_all, own, 2 * LANES), (above_all, above, LANES), (below_all, below, LANES))
+        ((own_all, own, 2 * LANES), (near_all, None, LANES), (far_all, None, LANES))
     ):
         length = blocks * lanes
         start = chunk * length
+        if local is None:
+            local = halos.at[1 - odd_tile if at == 1 else odd_tile]
         for place, size_here, offset, group in (
             (start, length, lanes, inner),
             (jnp.maximum(start - lanes, 0), lanes, 0, edges[0]),
@@ -437,11 +485,11 @@
             other[:, cols] = fingerprints(cols, slice(slot_rows, size), scale_other)
 
 
-def main_part(distance, most, own, above, below, inverse, select, box, merge, rows, pieces, slots):
+def main_part(distance, most, own, near, far, inverse, select, box, merge, rows, pieces, slots):
     size, width_all = own.shape
     count = size // rows
     width = width_all // pieces
-    halo = above.shape[0]
+    halo = near.shape[0]
     cell_rows = 3 * (rows // 2) * count
     return pl.pallas_call(
         functools.partial(main_kernel, count, rows, distance),
@@ -450,8 +498,7 @@
         out_specs=[pl.BlockSpec(memory_space=pltpu.VMEM)] * 2,
         scratch_shapes=[
             pltpu.VMEM((size, width + 4 * LANES), bf16),
-            pltpu.VMEM((halo, width // 2 + 2 * LANES), bf16),
-            pltpu.VMEM((halo, width // 2 + 2 * LANES), bf16),
+            pltpu.VMEM((2, halo, width // 2 + 2 * LANES), bf16),
             pltpu.VMEM((RADII, cell_rows, width // 2 + 2 * LANES), bf16),
             pltpu.VMEM((FINE, cell_rows, width // 2 + 2 * LANES), bf16),
             pltpu.VMEM((cell_rows, 2 * LANES), f32),
@@ -473,7 +520,7 @@
             flops=2 * 10**9, bytes_accessed=4 * 2**20, transcendentals=0
         ),
         name="residual",
-    )(most, own, above, below, inverse, select, box, merge)
+    )(most, own, near, far, inverse, select, box, merge)
 
 
 def assemble_kernel(rows, pieces, select, share, *refs):
@@ -594,9 +641,10 @@
 def on_device(photos, camera_id):
     count, rows, width = photos.shape
     pieces, tiles = lax.axis_size("photo"), lax.axis_size("tile")
-    own, up, down, *extras = prepare(camera_id, photos, pieces)
-    above = lax.ppermute(down, "tile", [(i, i + 1) for i in range(tiles - 1)])
-    below = lax.ppermute(up, "tile", [(i + 1, i) for i in range(tiles - 1)])
+    own, near, far, *extras = prepare(camera_id, photos, pieces)
+    near = exchange(near, "tile", 1)
+    across = [(i, i + 1) for i in range(1, tiles - 1, 2)]
+    far = lax.ppermute(far, "tile", across + [(j, i) for i, j in across])
     extras = [
         exchange(extra, "photo", distance) if distance else extra
         for distance, extra in enumerate(extras)
@@ -608,7 +656,7 @@
     parts, others = [None] * pieces, [None] * pieces
     for distance in reversed(range(pieces)):
         part, other = main_part(
-            distance, most_row, own, above, below, inverse, select, box, merge,
+            distance, most_row, own, near, far, inverse, select, box, merge,
             rows, pieces, few,
         )
         parts[distance] = exchange(part, "photo", distance) if distance else part

time: 65.1 us -> 63.8 us (0.980)
  starting transfers between devices: 23.4 us -> 20.1 us
  Pallas kernels: 25.1 us -> 28.1 us
    pallas_call x1, Pallas kernels: 1.66 us -> 4.84 us  [prepare(): pl.pallas_call(prepare_kernel, in_specs=[pl.BlockSpec(memory_space=pl.ANY...]
    ppermute x2 -> x1, starting transfers between devices: 3.7 us -> 0.7 us  [on_device(): far = lax.ppermute(far, 'tile', across + [(j, i) for i, j in across])]
    unnamed x4 -> x8, local copies, waits for them, and re-layouts: 2.24 us -> 1.6 us
    ppermute x13 -> x14, starting transfers between devices: 19.7 us -> 19.4 us  [exchange(): return lax.ppermute(array, axis, [(i, i ^ distance) for i in range(size)])]
    ppermute x13 -> x14, waiting for transfers between devices: 12.7 us -> 12.4 us  [exchange(): return lax.ppermute(array, axis, [(i, i ^ distance) for i in range(size)])]
  transfers between devices with their start and end apart: 15 -> 15, of which waited for: 9 -> 8; matrix products, arithmetic and copies ran while one was open for 0% -> 0% of each run, Pallas kernels for 25% -> 25%
where the time goes in v8:
time: 63.8 us; the launch traced here: 63.6 us
  Pallas kernels  28.1 us (44%)
  starting transfers between devices  20.1 us (32%)
  waiting for transfers between devices  12.4 us (19%)
  local copies, waits for them, and re-layouts  1.6 us (3%)
  between operations  1.43 us (2%)
    ppermute x14, starting transfers between devices, exchange(): return lax.ppermute(array, axis, [(i, i ^ distance) for i in range(size)])  19.4 us
    pallas_call x4, Pallas kernels, main_part(): pl.pallas_call(functools.partial(main_kernel, count, rows, distance), in_...  16.9 us
    ppermute x14, waiting for transfers between devices, exchange(): return lax.ppermute(array, axis, [(i, i ^ distance) for i in range(size)])  12.4 us
    pallas_call x1, Pallas kernels, prepare(): pl.pallas_call(prepare_kernel, in_specs=[pl.BlockSpec(memory_space=pl.ANY...  4.84 us
    pallas_call x1, Pallas kernels, energies(): pl.pallas_call(functools.partial(energy_kernel, size // rows, rows), in_s...  2.4 us
    pallas_call x1, Pallas kernels, assemble(): pl.pallas_call(functools.partial(assemble_kernel, rows, len(parts)), in_s...  2.3 us
    unnamed x8, local copies, waits for them, and re-layouts  1.6 us
  transfers between devices with their start and end apart: 15, of which 8 were waited for; matrix products, arithmetic and copies ran while one was open for 0% of the time, Pallas kernels for 25%

profile of v8, /device:TPU:0, one launch (start us, length us, event | category | flops | bytes accessed | tf_op | source)
XLA Modules:
  0.0 63.6 jit_solution(6014142658601042419)
XLA Ops:
  0.6 4.8 %prepare.1 = (bf16[256,4096]{1,0:T(8,128)(2,1)}, bf16[192,2048]{1,0:T(8,128)(2,1)}, bf16[192,2048]{1,0:T(8,128)(2,1)}, bf16[48,1024]{1,0:T(8,128)(2,1)}, bf16[48...) custom-call(s32[16]{0:T(128)} %ids_all.3, bf16[16,16,4096]{2,1,0:T(8,128)(2,1)} %photos_all.1), custom_call_target="tpu_custom_call" | custom-call | flops 1000000000 | bytes 8388608 | tf_op jit(solution)/shard_map/prepare/pallas_call | solution.py:183
  5.5 0.5 collective-permute-start.6
  6.0 0.7 %collective-permute-start.7 = (bf16[192,2048]{1,0:T(8,128)(2,1)}, bf16[192,2048]{1,0:T(8,128)(2,1)S(1)}, u32[]{:S(2)}, u32[]{:S(2)}) collective-permute-start(bf16[192,2048]{1,0:T(8,128)(2,1)} %get-tuple-element.85), channel_id=1, source_target_pairs={{1,2},{3,4},{5,6},{2,1},{4,3},{6,5},{9,10},{11,12},{13,14},{10,9},... | collective-permute-start | bytes 2359304 | tf_op jit(solution)/shard_map/ppermute | solution.py:647
  6.7 2.6 %collective-permute-start.3 = (bf16[48,1024]{1,0:T(8,128)(2,1)}, bf16[48,1024]{1,0:T(8,128)(2,1)S(1)}, u32[]{:S(2)}, u32[]{:S(2)}) collective-permute-start(bf16[48,1024]{1,0:T(8,128)(2,1)} %get-tuple-element.76), channel_id=1, source_target_pairs={{0,8},{8,0},{16,24},{24,16},{1,9},{9,1},{17,25},{25,17},{2,10},{10... | collective-permute-start | bytes 294920 | tf_op jit(solution)/shard_map/ppermute | solution.py:631
  9.3 1.5 %collective-permute-start.4 = (bf16[48,1024]{1,0:T(8,128)(2,1)}, bf16[48,1024]{1,0:T(8,128)(2,1)S(1)}, u32[]{:S(2)}, u32[]{:S(2)}) collective-permute-start(bf16[48,1024]{1,0:T(8,128)(2,1)} %get-tuple-element.77), channel_id=1, source_target_pairs={{0,16},{8,24},{16,0},{24,8},{1,17},{9,25},{17,1},{25,9},{2,18},{10... | collective-permute-start | bytes 294920 | tf_op jit(solution)/shard_map/ppermute | solution.py:631
  10.8 1.6 %copy-done = bf16[256,4096]{1,0:T(8,128)(2,1)S(1)} copy-done((bf16[256,4096]{1,0:T(8,128)(2,1)S(1)}, bf16[256,4096]{1,0:T(8,128)(2,1)}, u32[]{:S(2)}) %copy-start) | copy-done | bytes 2097176
  12.4 2.4 %energies.1 = (f32[256,4096]{1,0:T(8,128)S(1)}, bf16[256,512]{1,0:T(8,128)(2,1)S(1)}, bf16[4,512,256]{2,1,0:T(8,128)(2,1)S(1)}, bf16[256,256]{1,0:T(8,128)(2,1)S(1)}) custom-call(s32[16]{0:T(128)S(1)} %copy-done.3, bf16[256,4096]{1,0:T(8,128)(2,1)S(1)} %copy-done), custom_call_target="tpu_custom_call" | custom-call | flops 1000000000 | bytes 8388608 | tf_op jit(solution)/shard_map/energies/pallas_call | solution.py:242
  14.9 1.8 %collective-permute-done.5.refs_3_ = bf16[48,1024]{1,0:T(8,128)(2,1)S(1)} collective-permute-done((bf16[48,1024]{1,0:T(8,128)(2,1)}, bf16[48,1024]{1,0:T(8,128)(2,1)S(1)}, u32[]{:S(2)}, u32[]{:S(2)}) %collective-permute-start.5) | collective-permute-done | bytes 98336 | tf_op jit(solution)/shard_map/ppermute | solution.py:631
  16.7 0.9 %blend.1 = (bf16[4,512,256]{2,1,0:T(8,128)(2,1)S(1)}, f32[4,2,16,1024]{3,2,1,0:T(8,128)S(1)}, s32[1]{0:T(128)}, f32[8,128]{1,0:T(8,128)S(1)}) custom-call(bf16[48,1024]{1,0:T(8,128)(2,1)S(1)} %copy-done.2, bf16[48,1024]{1,0:T(8,128)(2,1)S(1)} %collective-permute-done.3.refs_1_, bf16[48,1024]{1,0:T(8,128)(2,1)S(1)} %collective-permute-done.4.refs_2_, ...), custom_call_target="tpu_custom_call" | custom-call | tf_op jit(solution)/shard_map/blend/pallas_call | solution.py:295
  17.6 4.2 %residual.7 = (bf16[176,1024]{1,0:T(8,128)(2,1)S(1)}, bf16[80,1024]{1,0:T(8,128)(2,1)S(1)}) custom-call(f32[8,128]{1,0:T(8,128)S(1)} %get-tuple-element.82.most, bf16[256,4096]{1,0:T(8,128)(2,1)S(1)} %copy-done.1, bf16[192,2048]{1,0:T(8,128)(2,1)S(1)} %collective-permute-done.6.near_all, bf16[192,2048]{1,0:T(8,128)(2,1)S(1)} %collective-permute-done.7.far_all, ...), custom_call_target="tpu_custom_call" | custom-call | flops 2000000000 | bytes 4194304 | tf_op jit(solution)/shard_map/residual/pallas_call | solution.py:494
  21.8 1.2 %collective-permute-start.10 = (bf16[176,1024]{1,0:T(8,128)(2,1)S(1)}, bf16[176,1024]{1,0:T(8,128)(2,1)S(1)}, u32[]{:S(2)}, u32[]{:S(2)}) collective-permute-start(bf16[176,1024]{1,0:T(8,128)(2,1)S(1)} %get-tuple-element.93), channel_id=1, source_target_pairs={{0,24},{8,16},{16,8},{24,0},{1,25},{9,17},{17,9},{25,1},{2,26},{10... | collective-permute-start | bytes 1081352 | tf_op jit(solution)/shard_map/ppermute | solution.py:631
  23.0 4.3 %residual.6 = (bf16[176,1024]{1,0:T(8,128)(2,1)S(1)}, bf16[80,1024]{1,0:T(8,128)(2,1)S(1)}) custom-call(f32[8,128]{1,0:T(8,128)S(1)} %get-tuple-element.82.most, bf16[256,4096]{1,0:T(8,128)(2,1)S(1)} %copy-done.1, bf16[192,2048]{1,0:T(8,128)(2,1)S(1)} %collective-permute-done.6.near_all, bf16[192,2048]{1,0:T(8,128)(2,1)S(1)} %collective-permute-done.7.far_all, ...), custom_call_target="tpu_custom_call" | custom-call | flops 2000000000 | bytes 4194304 | tf_op jit(solution)/shard_map/residual/pallas_call | solution.py:494
  27.3 1.9 %collective-permute-start.9 = (bf16[176,1024]{1,0:T(8,128)(2,1)S(1)}, bf16[176,1024]{1,0:T(8,128)(2,1)S(1)}, u32[]{:S(2)}, u32[]{:S(2)}) collective-permute-start(bf16[176,1024]{1,0:T(8,128)(2,1)S(1)} %get-tuple-element.92), channel_id=1, source_target_pairs={{0,16},{8,24},{16,0},{24,8},{1,17},{9,25},{17,1},{25,9},{2,18},{10... | collective-permute-start | bytes 1081352 | tf_op jit(solution)/shard_map/ppermute | solution.py:631
  29.2 4.1 %residual.5 = (bf16[176,1024]{1,0:T(8,128)(2,1)S(1)}, bf16[80,1024]{1,0:T(8,128)(2,1)S(1)}) custom-call(f32[8,128]{1,0:T(8,128)S(1)} %get-tuple-element.82.most, bf16[256,4096]{1,0:T(8,128)(2,1)S(1)} %copy-done.1, bf16[192,2048]{1,0:T(8,128)(2,1)S(1)} %collective-permute-done.6.near_all, bf16[192,2048]{1,0:T(8,128)(2,1)S(1)} %collective-permute-done.7.far_all, ...), custom_call_target="tpu_custom_call" | custom-call | flops 2000000000 | bytes 4194304 | tf_op jit(solution)/shard_map/residual/pallas_call | solution.py:494
  33.3 0.7 %collective-permute-start.8 = (bf16[176,1024]{1,0:T(8,128)(2,1)S(1)}, bf16[176,1024]{1,0:T(8,128)(2,1)S(1)}, u32[]{:S(2)}, u32[]{:S(2)}) collective-permute-start(bf16[176,1024]{1,0:T(8,128)(2,1)S(1)} %get-tuple-element.91), channel_id=1, source_target_pairs={{0,8},{8,0},{16,24},{24,16},{1,9},{9,1},{17,25},{25,17},{2,10},{10... | collective-permute-start | bytes 1081352 | tf_op jit(solution)/shard_map/ppermute | solution.py:631
  34.7 4.2 %residual.4 = (bf16[176,1024]{1,0:T(8,128)(2,1)S(1)}, bf16[80,1024]{1,0:T(8,128)(2,1)S(1)}) custom-call(f32[8,128]{1,0:T(8,128)S(1)} %get-tuple-element.82.most, bf16[256,4096]{1,0:T(8,128)(2,1)S(1)} %copy-done.1, bf16[192,2048]{1,0:T(8,128)(2,1)S(1)} %collective-permute-done.6.near_all, bf16[192,2048]{1,0:T(8,128)(2,1)S(1)} %collective-permute-done.7.far_all, ...), custom_call_target="tpu_custom_call" | custom-call | flops 2000000000 | bytes 4194304 | tf_op jit(solution)/shard_map/residual/pallas_call | solution.py:494
  38.9 2.4 %collective-permute-done.9 = bf16[176,1024]{1,0:T(8,128)(2,1)S(1)} collective-permute-done((bf16[176,1024]{1,0:T(8,128)(2,1)S(1)}, bf16[176,1024]{1,0:T(8,128)(2,1)S(1)}, u32[]{:S(2)}, u32[]{:S(2)}) %collective-permute-start.9) | collective-permute-done | bytes 360480 | tf_op jit(solution)/shard_map/ppermute | solution.py:631
  41.3 1.4 %collective-permute-done.8 = bf16[176,1024]{1,0:T(8,128)(2,1)S(1)} collective-permute-done((bf16[176,1024]{1,0:T(8,128)(2,1)S(1)}, bf16[176,1024]{1,0:T(8,128)(2,1)S(1)}, u32[]{:S(2)}, u32[]{:S(2)}) %collective-permute-start.8) | collective-permute-done | bytes 360480 | tf_op jit(solution)/shard_map/ppermute | solution.py:631
  42.7 2.3 %conditional.1 = ((f32[32,16,1024]{2,1,0:T(8,128)}, f32[32,128]{1,0:T(8,128)S(1)})) conditional(s32[]{:T(128)} %bitcast, (bf16[4,512,256]{2,1,0:T(8,128)(2,1)S(1)}, f32[4,2,16,1024]{3,2,1,0:T(8,128)S(1)}, bf16[176,1024]{1,0:T(8,128)(2,1)S(1)}, bf16[176,1024]{1,0:T(8,128)(2,1)S(1)}, bf16[176,1024]{1,0:T(8,128)(2,1)S(1)}, ...), branch_computations={%region_0.0_spmd, %region_1.0_spmd} | conditional | flops 2000000000 | bytes 6160512 | solution.py:675
  42.7 2.3 %assemble.2 = (f32[32,16,1024]{2,1,0:T(8,128)}, f32[32,128]{1,0:T(8,128)S(1)}) custom-call(bf16[4,512,256]{2,1,0:T(8,128)(2,1)S(1)} %get-tuple-element.32.select, f32[4,2,16,1024]{3,2,1,0:T(8,128)S(1)} %get-tuple-element.33.share, bf16[176,1024]{1,0:T(8,128)(2,1)S(1)} %get-tuple-element.34.refs_0_, bf16[176,1024]{1,0:T(8,128)(2,1)S(1)} %get-tuple-element.35.refs_1_, ...), custom_call_target="tpu_custom_call" | custom-call | flops 2000000000 | bytes 4194304 | tf_op jit(solution)/shard_map/cond/branch_0_fun/assemble/pallas_call | solution.py:579
  45.0 1.9 %collective-permute-start.11 = (f32[32,128]{1,0:T(8,128)S(1)}, f32[32,128]{1,0:T(8,128)S(1)}, u32[]{:S(2)}, u32[]{:S(2)}) collective-permute-start(f32[32,128]{1,0:T(8,128)S(1)} %get-tuple-element.99), channel_id=1, source_target_pairs={{0,1},{1,0},{2,3},{3,2},{4,5},{5,4},{6,7},{7,6},{8,9},{9,8},{10,11... | collective-permute-start | bytes 49160 | tf_op jit(solution)/shard_map/ppermute | solution.py:631
  46.9 0.8 %collective-permute-done.11 = f32[32,128]{1,0:T(8,128)S(1)} collective-permute-done((f32[32,128]{1,0:T(8,128)S(1)}, f32[32,128]{1,0:T(8,128)S(1)}, u32[]{:S(2)}, u32[]{:S(2)}) %collective-permute-start.11) | collective-permute-done | bytes 16416 | tf_op jit(solution)/shard_map/ppermute | solution.py:631
  47.7 0.5 collective-permute-start.14
  48.2 1.6 %collective-permute-start.13 = (f32[32,128]{1,0:T(8,128)S(1)}, f32[32,128]{1,0:T(8,128)S(1)}, u32[]{:S(2)}, u32[]{:S(2)}) collective-permute-start(f32[32,128]{1,0:T(8,128)S(1)} %add.21), channel_id=1, source_target_pairs={{0,16},{8,24},{16,0},{24,8},{1,17},{9,25},{17,1},{25,9},{2,18},{10... | collective-permute-start | bytes 49160 | tf_op jit(solution)/shard_map/ppermute | solution.py:631
  49.8 1.4 %collective-permute-start.12 = (f32[32,128]{1,0:T(8,128)S(1)}, f32[32,128]{1,0:T(8,128)S(1)}, u32[]{:S(2)}, u32[]{:S(2)}) collective-permute-start(f32[32,128]{1,0:T(8,128)S(1)} %add.21), channel_id=1, source_target_pairs={{0,8},{8,0},{16,24},{24,16},{1,9},{9,1},{17,25},{25,17},{2,10},{10... | collective-permute-start | bytes 49160 | tf_op jit(solution)/shard_map/ppermute | solution.py:631
  51.2 1.2 %collective-permute-done.14 = f32[32,128]{1,0:T(8,128)S(1)} collective-permute-done((f32[32,128]{1,0:T(8,128)S(1)}, f32[32,128]{1,0:T(8,128)S(1)}, u32[]{:S(2)}, u32[]{:S(2)}) %collective-permute-start.14) | collective-permute-done | bytes 16416 | tf_op jit(solution)/shard_map/ppermute | solution.py:631
  52.4 1.1 %collective-permute-done.12 = f32[32,128]{1,0:T(8,128)S(1)} collective-permute-done((f32[32,128]{1,0:T(8,128)S(1)}, f32[32,128]{1,0:T(8,128)S(1)}, u32[]{:S(2)}, u32[]{:S(2)}) %collective-permute-start.12) | collective-permute-done | bytes 16416 | tf_op jit(solution)/shard_map/ppermute | solution.py:631
  53.5 3.3 %collective-permute-start.17 = (f32[32,128]{1,0:T(8,128)S(1)}, f32[32,128]{1,0:T(8,128)S(1)}, u32[]{:S(2)}, u32[]{:S(2)}) collective-permute-start(f32[32,128]{1,0:T(8,128)S(1)} %add_add_fusion.1), channel_id=1, source_target_pairs={{0,6},{1,7},{2,4},{3,5},{4,2},{5,3},{6,0},{7,1},{8,14},{9,15},{10,... | collective-permute-start | bytes 49160 | tf_op jit(solution)/shard_map/ppermute | solution.py:631
  56.8 2.3 %collective-permute-start.16 = (f32[32,128]{1,0:T(8,128)S(1)}, f32[32,128]{1,0:T(8,128)S(1)}, u32[]{:S(2)}, u32[]{:S(2)}) collective-permute-start(f32[32,128]{1,0:T(8,128)S(1)} %add_add_fusion.1), channel_id=1, source_target_pairs={{0,4},{1,5},{2,6},{3,7},{4,0},{5,1},{6,2},{7,3},{8,12},{9,13},{10,... | collective-permute-start | bytes 49160 | tf_op jit(solution)/shard_map/ppermute | solution.py:631
  59.2 2.3 %collective-permute-done.16 = f32[32,128]{1,0:T(8,128)S(1)} collective-permute-done((f32[32,128]{1,0:T(8,128)S(1)}, f32[32,128]{1,0:T(8,128)S(1)}, u32[]{:S(2)}, u32[]{:S(2)}) %collective-permute-start.16) | collective-permute-done | bytes 16416 | tf_op jit(solution)/shard_map/ppermute | solution.py:631
  61.5 1.4 %collective-permute-done.15 = f32[32,128]{1,0:T(8,128)S(1)} collective-permute-done((f32[32,128]{1,0:T(8,128)S(1)}, f32[32,128]{1,0:T(8,128)S(1)}, u32[]{:S(2)}, u32[]{:S(2)}) %collective-permute-start.15) | collective-permute-done | bytes 16416 | tf_op jit(solution)/shard_map/ppermute | solution.py:631
  62.8 0.8 %correlate.1 = f32[32,32]{1,0:T(8,128)} custom-call(f32[32,128]{1,0:T(8,128)S(1)} %add_add_fusion.refs_0_), custom_call_target="tpu_custom_call" | custom-call | tf_op jit(solution)/shard_map/correlate/pallas_call | solution.py:621
  (19 shorter events, 0.2 us)
Async XLA Ops:
  0.6 10.2 %copy-start.3 = (s32[16]{0:T(128)S(1)}, s32[16]{0:T(128)}, u32[]{:S(2)}) copy-start(s32[16]{0:T(128)} %ids_all.3) | copy-start | bytes 196
  5.5 12.1 %collective-permute-start.6 = (bf16[192,2048]{1,0:T(8,128)(2,1)}, bf16[192,2048]{1,0:T(8,128)(2,1)S(1)}, u32[]{:S(2)}, u32[]{:S(2)}) collective-permute-start(bf16[192,2048]{1,0:T(8,128)(2,1)} %get-tuple-element.84), channel_id=1, source_target_pairs={{0,1},{1,0},{2,3},{3,2},{4,5},{5,4},{6,7},{7,6},{8,9},{9,8},{10,11... | collective-permute-start | bytes 2359304 | tf_op jit(solution)/shard_map/ppermute | solution.py:631
  6.0 11.5 %collective-permute-start.7 = (bf16[192,2048]{1,0:T(8,128)(2,1)}, bf16[192,2048]{1,0:T(8,128)(2,1)S(1)}, u32[]{:S(2)}, u32[]{:S(2)}) collective-permute-start(bf16[192,2048]{1,0:T(8,128)(2,1)} %get-tuple-element.85), channel_id=1, source_target_pairs={{1,2},{3,4},{5,6},{2,1},{4,3},{6,5},{9,10},{11,12},{13,14},{10,9},... | collective-permute-start | bytes 2359304 | tf_op jit(solution)/shard_map/ppermute | solution.py:647
  6.7 8.1 %collective-permute-start.3 = (bf16[48,1024]{1,0:T(8,128)(2,1)}, bf16[48,1024]{1,0:T(8,128)(2,1)S(1)}, u32[]{:S(2)}, u32[]{:S(2)}) collective-permute-start(bf16[48,1024]{1,0:T(8,128)(2,1)} %get-tuple-element.76), channel_id=1, source_target_pairs={{0,8},{8,0},{16,24},{24,16},{1,9},{9,1},{17,25},{25,17},{2,10},{10... | collective-permute-start | bytes 294920 | tf_op jit(solution)/shard_map/ppermute | solution.py:631
  9.3 5.6 %collective-permute-start.4 = (bf16[48,1024]{1,0:T(8,128)(2,1)}, bf16[48,1024]{1,0:T(8,128)(2,1)S(1)}, u32[]{:S(2)}, u32[]{:S(2)}) collective-permute-start(bf16[48,1024]{1,0:T(8,128)(2,1)} %get-tuple-element.77), channel_id=1, source_target_pairs={{0,16},{8,24},{16,0},{24,8},{1,17},{9,25},{17,1},{25,9},{2,18},{10... | collective-permute-start | bytes 294920 | tf_op jit(solution)/shard_map/ppermute | solution.py:631
  10.8 5.8 %collective-permute-start.5 = (bf16[48,1024]{1,0:T(8,128)(2,1)}, bf16[48,1024]{1,0:T(8,128)(2,1)S(1)}, u32[]{:S(2)}, u32[]{:S(2)}) collective-permute-start(bf16[48,1024]{1,0:T(8,128)(2,1)} %get-tuple-element.78), channel_id=1, source_target_pairs={{0,24},{8,16},{16,8},{24,0},{1,25},{9,17},{17,9},{25,1},{2,26},{10... | collective-permute-start | bytes 294920 | tf_op jit(solution)/shard_map/ppermute | solution.py:631
  10.8 1.6 %copy-start = (bf16[256,4096]{1,0:T(8,128)(2,1)S(1)}, bf16[256,4096]{1,0:T(8,128)(2,1)}, u32[]{:S(2)}) copy-start(bf16[256,4096]{1,0:T(8,128)(2,1)} %get-tuple-element.83.own.own_all) | copy-start | bytes 6291460
  12.4 4.2 %copy-start.2 = (bf16[48,1024]{1,0:T(8,128)(2,1)S(1)}, bf16[48,1024]{1,0:T(8,128)(2,1)}, u32[]{:S(2)}) copy-start(bf16[48,1024]{1,0:T(8,128)(2,1)} %get-tuple-element.75.refs_0_) | copy-start | bytes 294916
  12.4 5.1 %copy-start.1 = (bf16[256,4096]{1,0:T(8,128)(2,1)S(1)}, bf16[256,4096]{1,0:T(8,128)(2,1)}, u32[]{:S(2)}) copy-start(bf16[256,4096]{1,0:T(8,128)(2,1)} %get-tuple-element.83.own.own_all) | copy-start | bytes 6291460
  21.8 17.1 %collective-permute-start.10 = (bf16[176,1024]{1,0:T(8,128)(2,1)S(1)}, bf16[176,1024]{1,0:T(8,128)(2,1)S(1)}, u32[]{:S(2)}, u32[]{:S(2)}) collective-permute-start(bf16[176,1024]{1,0:T(8,128)(2,1)S(1)} %get-tuple-element.93), channel_id=1, source_target_pairs={{0,24},{8,16},{16,8},{24,0},{1,25},{9,17},{17,9},{25,1},{2,26},{10... | collective-permute-start | bytes 1081352 | tf_op jit(solution)/shard_map/ppermute | solution.py:631
  27.3 14.0 %collective-permute-start.9 = (bf16[176,1024]{1,0:T(8,128)(2,1)S(1)}, bf16[176,1024]{1,0:T(8,128)(2,1)S(1)}, u32[]{:S(2)}, u32[]{:S(2)}) collective-permute-start(bf16[176,1024]{1,0:T(8,128)(2,1)S(1)} %get-tuple-element.92), channel_id=1, source_target_pairs={{0,16},{8,24},{16,0},{24,8},{1,17},{9,25},{17,1},{25,9},{2,18},{10... | collective-permute-start | bytes 1081352 | tf_op jit(solution)/shard_map/ppermute | solution.py:631
  33.3 9.4 %collective-permute-start.8 = (bf16[176,1024]{1,0:T(8,128)(2,1)S(1)}, bf16[176,1024]{1,0:T(8,128)(2,1)S(1)}, u32[]{:S(2)}, u32[]{:S(2)}) collective-permute-start(bf16[176,1024]{1,0:T(8,128)(2,1)S(1)} %get-tuple-element.91), channel_id=1, source_target_pairs={{0,8},{8,0},{16,24},{24,16},{1,9},{9,1},{17,25},{25,17},{2,10},{10... | collective-permute-start | bytes 1081352 | tf_op jit(solution)/shard_map/ppermute | solution.py:631
  45.0 2.7 %collective-permute-start.11 = (f32[32,128]{1,0:T(8,128)S(1)}, f32[32,128]{1,0:T(8,128)S(1)}, u32[]{:S(2)}, u32[]{:S(2)}) collective-permute-start(f32[32,128]{1,0:T(8,128)S(1)} %get-tuple-element.99), channel_id=1, source_target_pairs={{0,1},{1,0},{2,3},{3,2},{4,5},{5,4},{6,7},{7,6},{8,9},{9,8},{10,11... | collective-permute-start | bytes 49160 | tf_op jit(solution)/shard_map/ppermute | solution.py:631
  47.7 4.7 %collective-permute-start.14 = (f32[32,128]{1,0:T(8,128)S(1)}, f32[32,128]{1,0:T(8,128)S(1)}, u32[]{:S(2)}, u32[]{:S(2)}) collective-permute-start(f32[32,128]{1,0:T(8,128)S(1)} %add.21), channel_id=1, source_target_pairs={{0,24},{8,16},{16,8},{24,0},{1,25},{9,17},{17,9},{25,1},{2,26},{10... | collective-permute-start | bytes 49160 | tf_op jit(solution)/shard_map/ppermute | solution.py:631
  48.2 4.2 %collective-permute-start.13 = (f32[32,128]{1,0:T(8,128)S(1)}, f32[32,128]{1,0:T(8,128)S(1)}, u32[]{:S(2)}, u32[]{:S(2)}) collective-permute-start(f32[32,128]{1,0:T(8,128)S(1)} %add.21), channel_id=1, source_target_pairs={{0,16},{8,24},{16,0},{24,8},{1,17},{9,25},{17,1},{25,9},{2,18},{10... | collective-permute-start | bytes 49160 | tf_op jit(solution)/shard_map/ppermute | solution.py:631
  49.8 3.7 %collective-permute-start.12 = (f32[32,128]{1,0:T(8,128)S(1)}, f32[32,128]{1,0:T(8,128)S(1)}, u32[]{:S(2)}, u32[]{:S(2)}) collective-permute-start(f32[32,128]{1,0:T(8,128)S(1)} %add.21), channel_id=1, source_target_pairs={{0,8},{8,0},{16,24},{24,16},{1,9},{9,1},{17,25},{25,17},{2,10},{10... | collective-permute-start | bytes 49160 | tf_op jit(solution)/shard_map/ppermute | solution.py:631
  53.5 5.7 %collective-permute-start.17 = (f32[32,128]{1,0:T(8,128)S(1)}, f32[32,128]{1,0:T(8,128)S(1)}, u32[]{:S(2)}, u32[]{:S(2)}) collective-permute-start(f32[32,128]{1,0:T(8,128)S(1)} %add_add_fusion.1), channel_id=1, source_target_pairs={{0,6},{1,7},{2,4},{3,5},{4,2},{5,3},{6,0},{7,1},{8,14},{9,15},{10,... | collective-permute-start | bytes 49160 | tf_op jit(solution)/shard_map/ppermute | solution.py:631
  56.8 4.6 %collective-permute-start.16 = (f32[32,128]{1,0:T(8,128)S(1)}, f32[32,128]{1,0:T(8,128)S(1)}, u32[]{:S(2)}, u32[]{:S(2)}) collective-permute-start(f32[32,128]{1,0:T(8,128)S(1)} %add_add_fusion.1), channel_id=1, source_target_pairs={{0,4},{1,5},{2,6},{3,7},{4,0},{5,1},{6,2},{7,3},{8,12},{9,13},{10,... | collective-permute-start | bytes 49160 | tf_op jit(solution)/shard_map/ppermute | solution.py:631
  59.1 3.7 %collective-permute-start.15 = (f32[32,128]{1,0:T(8,128)S(1)}, f32[32,128]{1,0:T(8,128)S(1)}, u32[]{:S(2)}, u32[]{:S(2)}) collective-permute-start(f32[32,128]{1,0:T(8,128)S(1)} %add_add_fusion.1), channel_id=1, source_target_pairs={{0,2},{1,3},{2,0},{3,1},{4,6},{5,7},{6,4},{7,5},{8,10},{9,11},{10,... | collective-permute-start | bytes 49160 | tf_op jit(solution)/shard_map/ppermute | solution.py:631

commit v9 on v8

--- a/solution.py
+++ b/solution.py
@@ -82,31 +82,20 @@
     return slots, last + 1
 
 
-def prepare_kernel(ids_all, photos_all, sorted_all, near_all, far_all, *refs):
-    extras = refs[:-8]
-    photos, sorted_out, near_out, far_out, arrived, sent, ids, ready = refs[-8:]
+def prepare_kernel(ids_all, photos, sorted_out, near_out, far_out, *refs):
+    extras, (ids, ready) = refs[:-2], refs[-2:]
     count, rows, width = photos.shape
     cells = rows // 2
     pieces = len(extras)
     step = width // pieces
     me = lax.axis_index("photo")
     odd_tile = (lax.axis_index("tile") & 1) == 1
-    copies = []
-    for piece in range(pieces):
-        cols = pl.ds(piece * step, step)
-        copies.append(
-            pltpu.make_async_copy(
-                photos_all.at[:, :, cols], photos.at[:, :, cols], arrived.at[piece]
-            )
-        )
-        copies[-1].start()
     copy = pltpu.make_async_copy(ids_all, ids, ready)
     copy.start()
     perm = row_permutation(count, rows)
     split = column_split()
 
     for piece in range(pieces):
-        copies[piece].wait()
         flat = photos[:, :, piece * step : (piece + 1) * step].reshape(count * rows, step)
         by_row = jnp.dot(perm, flat, preferred_element_type=f32).astype(bf16)
         for inner in range(step // (2 * LANES)):
@@ -135,17 +124,6 @@
                     far_out[start : start + count, cell_cols] = jnp.where(
                         odd_tile, lower, upper
                     ).astype(bf16)
-        for at, (local, whole) in enumerate(
-            ((sorted_out, sorted_all), (near_out, near_all), (far_out, far_all))
-        ):
-            length = whole.shape[1] // pieces
-            there = pl.ds(piece * length, length)
-            copies.append(
-                pltpu.make_async_copy(
-                    local.at[:, there], whole.at[:, there], sent.at[at * pieces + piece]
-                )
-            )
-            copies[-1].start()
 
     copy.wait()
     slots, cameras = slot_numbers(ids, count)
@@ -170,8 +148,6 @@
         extra[:rows, :] = lax.fori_loop(0, in_first, add, none).astype(bf16)
         extra[rows : 2 * rows, :] = lax.fori_loop(count - in_last, count, add, none).astype(bf16)
         extra[2 * rows :, :] = notes
-    for copy_out in copies[pieces:]:
-        copy_out.wait()
 
 
 def prepare(ids, photos, pieces):
@@ -182,8 +158,8 @@
     vmem = pl.BlockSpec(memory_space=pltpu.VMEM)
     return pl.pallas_call(
         prepare_kernel,
-        in_specs=[pl.BlockSpec(memory_space=pl.ANY)] * 2,
-        out_specs=[pl.BlockSpec(memory_space=pl.ANY)] * 3 + [vmem] * pieces,
+        in_specs=[pl.BlockSpec(memory_space=pl.ANY), vmem],
+        out_specs=[vmem] * (3 + pieces),
         out_shape=[
             jax.ShapeDtypeStruct((size, width), bf16),
             jax.ShapeDtypeStruct((halo, width // 2), bf16),
@@ -191,16 +167,10 @@
         ]
         + [jax.ShapeDtypeStruct((3 * rows, step), bf16)] * pieces,
         scratch_shapes=[
-            pltpu.VMEM((count, rows, width), bf16),
-            pltpu.VMEM((size, width), bf16),
-            pltpu.VMEM((halo, width // 2), bf16),
-            pltpu.VMEM((halo, width // 2), bf16),
-            pltpu.SemaphoreType.DMA((pieces,)),
-            pltpu.SemaphoreType.DMA((3 * pieces,)),
             pltpu.SMEM((count,), jnp.int32),
             pltpu.SemaphoreType.DMA(()),
         ],
-        compiler_params=pltpu.CompilerParams(vmem_limit_bytes=56 * 2**20),
+        compiler_params=pltpu.CompilerParams(vmem_limit_bytes=20 * 2**20),
         cost_estimate=pl.CostEstimate(flops=10**9, bytes_accessed=8 * 2**20, transcendentals=0),
         name="prepare",
     )(ids, photos)

time: 63.8 us -> 62.8 us (0.984)
  Pallas kernels: 28.1 us -> 25.1 us
  waiting for transfers between devices: 12.4 us -> 13.7 us
  local copies, waits for them, and re-layouts: 1.6 us -> 2.24 us
    pallas_call x1, Pallas kernels: 4.84 us -> 1.89 us  [prepare(): pl.pallas_call(prepare_kernel, in_specs=[pl.BlockSpec(memory_space=pl.ANY...]
    ppermute x14, waiting for transfers between devices: 12.4 us -> 13.7 us  [exchange(): return lax.ppermute(array, axis, [(i, i ^ distance) for i in range(size)])]
    unnamed x8 -> x4, local copies, waits for them, and re-layouts: 1.6 us -> 2.24 us
  transfers between devices with their start and end apart: 15 -> 15, of which waited for: 8 -> 9; matrix products, arithmetic and copies ran while one was open for 0% -> 0% of each run, Pallas kernels for 25% -> 25%
where the time goes in v9:
time: 62.8 us; the launch traced here: 62.7 us
  Pallas kernels  25.1 us (40%)
  starting transfers between devices  20.2 us (32%)
  waiting for transfers between devices  13.7 us (22%)
  local copies, waits for them, and re-layouts  2.24 us (4%)
  between operations  1.41 us (2%)
    ppermute x14, starting transfers between devices, exchange(): return lax.ppermute(array, axis, [(i, i ^ distance) for i in range(size)])  19.5 us
    pallas_call x4, Pallas kernels, main_part(): pl.pallas_call(functools.partial(main_kernel, count, rows, distance), in_...  16.9 us
    ppermute x14, waiting for transfers between devices, exchange(): return lax.ppermute(array, axis, [(i, i ^ distance) for i in range(size)])  13.7 us
    pallas_call x1, Pallas kernels, energies(): pl.pallas_call(functools.partial(energy_kernel, size // rows, rows), in_s...  2.39 us
    pallas_call x1, Pallas kernels, assemble(): pl.pallas_call(functools.partial(assemble_kernel, rows, len(parts)), in_s...  2.3 us
    unnamed x4, local copies, waits for them, and re-layouts  2.24 us
    pallas_call x1, Pallas kernels, prepare(): pl.pallas_call(prepare_kernel, in_specs=[pl.BlockSpec(memory_space=pl.ANY...  1.89 us
  transfers between devices with their start and end apart: 15, of which 9 were waited for; matrix products, arithmetic and copies ran while one was open for 0% of the time, Pallas kernels for 25%

profile of v9, /device:TPU:0, one launch (start us, length us, event | category | flops | bytes accessed | tf_op | source)
XLA Modules:
  0.0 62.7 jit_solution(8091425668728742508)
XLA Ops:
  0.6 1.6 %copy-done = bf16[16,16,4096]{2,1,0:T(8,128)(2,1)S(1)} copy-done((bf16[16,16,4096]{2,1,0:T(8,128)(2,1)S(1)}, bf16[16,16,4096]{2,1,0:T(8,128)(2,1)}, u32[]{:S(2)}) %copy-start) | copy-done | bytes 2097176
  2.2 0.7 %copy-done.1 = s32[16]{0:T(128)S(1)} copy-done((s32[16]{0:T(128)S(1)}, s32[16]{0:T(128)}, u32[]{:S(2)}) %copy-start.1) | copy-done | bytes 88
  2.9 1.9 %prepare.1 = (bf16[256,4096]{1,0:T(8,128)(2,1)S(1)}, bf16[192,2048]{1,0:T(8,128)(2,1)S(1)}, bf16[192,2048]{1,0:T(8,128)(2,1)S(1)}, bf16[48,1024]{1,0:T(8,128)(2,...) custom-call(s32[16]{0:T(128)S(1)} %copy-done.1, ...), custom_call_target="tpu_custom_call" | custom-call | flops 1000000000 | bytes 8388608 | tf_op jit(solution)/shard_map/prepare/pallas_call | solution.py:159
  5.3 0.7 %collective-permute-start.7 = (bf16[192,2048]{1,0:T(8,128)(2,1)S(1)}, bf16[192,2048]{1,0:T(8,128)(2,1)S(1)}, u32[]{:S(2)}, u32[]{:S(2)}) collective-permute-start(bf16[192,2048]{1,0:T(8,128)(2,1)S(1)} %get-tuple-element.85), channel_id=1, source_target_pairs={{1,2},{3,4},{5,6},{2,1},{4,3},{6,5},{9,10},{11,12},{13,14},{10,9},... | collective-permute-start | bytes 2359304 | tf_op jit(solution)/shard_map/ppermute | solution.py:617
  6.0 2.5 %collective-permute-start.3 = (bf16[48,1024]{1,0:T(8,128)(2,1)S(1)}, bf16[48,1024]{1,0:T(8,128)(2,1)S(1)}, u32[]{:S(2)}, u32[]{:S(2)}) collective-permute-start(bf16[48,1024]{1,0:T(8,128)(2,1)S(1)} %get-tuple-element.76), channel_id=1, source_target_pairs={{0,8},{8,0},{16,24},{24,16},{1,9},{9,1},{17,25},{25,17},{2,10},{10... | collective-permute-start | bytes 294920 | tf_op jit(solution)/shard_map/ppermute | solution.py:601
  8.5 1.6 %collective-permute-start.4 = (bf16[48,1024]{1,0:T(8,128)(2,1)S(1)}, bf16[48,1024]{1,0:T(8,128)(2,1)S(1)}, u32[]{:S(2)}, u32[]{:S(2)}) collective-permute-start(bf16[48,1024]{1,0:T(8,128)(2,1)S(1)} %get-tuple-element.77), channel_id=1, source_target_pairs={{0,16},{8,24},{16,0},{24,8},{1,17},{9,25},{17,1},{25,9},{2,18},{10... | collective-permute-start | bytes 294920 | tf_op jit(solution)/shard_map/ppermute | solution.py:601
  10.1 2.4 %energies.1 = (f32[256,4096]{1,0:T(8,128)S(1)}, bf16[256,512]{1,0:T(8,128)(2,1)S(1)}, bf16[4,512,256]{2,1,0:T(8,128)(2,1)S(1)}, bf16[256,256]{1,0:T(8,128)(2,1)S(1)}) custom-call(s32[16]{0:T(128)S(1)} %copy-done.1, bf16[256,4096]{1,0:T(8,128)(2,1)S(1)} %get-tuple-element.83.own.own_all), custom_call_target="tpu_custom_call" | custom-call | flops 1000000000 | bytes 8388608 | tf_op jit(solution)/shard_map/energies/pallas_call | solution.py:212
  13.1 2.6 %collective-permute-done.5.refs_3_ = bf16[48,1024]{1,0:T(8,128)(2,1)S(1)} collective-permute-done((bf16[48,1024]{1,0:T(8,128)(2,1)S(1)}, bf16[48,1024]{1,0:T(8,128)(2,1)S(1)}, u32[]{:S(2)}, u32[]{:S(2)}) %collective-permute-start.5) | collective-permute-done | bytes 98336 | tf_op jit(solution)/shard_map/ppermute | solution.py:601
  15.7 0.9 %blend.1 = (bf16[4,512,256]{2,1,0:T(8,128)(2,1)S(1)}, f32[4,2,16,1024]{3,2,1,0:T(8,128)S(1)}, s32[1]{0:T(128)}, f32[8,128]{1,0:T(8,128)S(1)}) custom-call(bf16[48,1024]{1,0:T(8,128)(2,1)S(1)} %get-tuple-element.75.refs_0_, bf16[48,1024]{1,0:T(8,128)(2,1)S(1)} %collective-permute-done.3.refs_1_, bf16[48,1024]{1,0:T(8,128)(2,1)S(1)} %collective-permute-done.4.refs_2_, ...), custom_call_target="tpu_custom_call" | custom-call | tf_op jit(solution)/shard_map/blend/pallas_call | solution.py:265
  16.6 4.2 %residual.7 = (bf16[176,1024]{1,0:T(8,128)(2,1)S(1)}, bf16[80,1024]{1,0:T(8,128)(2,1)S(1)}) custom-call(f32[8,128]{1,0:T(8,128)S(1)} %get-tuple-element.82.most, bf16[256,4096]{1,0:T(8,128)(2,1)S(1)} %get-tuple-element.83.own.own_all, bf16[192,2048]{1,0:T(8,128)(2,1)S(1)} %collective-permute-done.6.near_all, ...), custom_call_target="tpu_custom_call" | custom-call | flops 2000000000 | bytes 4194304 | tf_op jit(solution)/shard_map/residual/pallas_call | solution.py:464
  20.8 0.7 %collective-permute-start.10 = (bf16[176,1024]{1,0:T(8,128)(2,1)S(1)}, bf16[176,1024]{1,0:T(8,128)(2,1)S(1)}, u32[]{:S(2)}, u32[]{:S(2)}) collective-permute-start(bf16[176,1024]{1,0:T(8,128)(2,1)S(1)} %get-tuple-element.93), channel_id=1, source_target_pairs={{0,24},{8,16},{16,8},{24,0},{1,25},{9,17},{17,9},{25,1},{2,26},{10... | collective-permute-start | bytes 1081352 | tf_op jit(solution)/shard_map/ppermute | solution.py:601
  21.5 4.3 %residual.6 = (bf16[176,1024]{1,0:T(8,128)(2,1)S(1)}, bf16[80,1024]{1,0:T(8,128)(2,1)S(1)}) custom-call(f32[8,128]{1,0:T(8,128)S(1)} %get-tuple-element.82.most, bf16[256,4096]{1,0:T(8,128)(2,1)S(1)} %get-tuple-element.83.own.own_all, bf16[192,2048]{1,0:T(8,128)(2,1)S(1)} %collective-permute-done.6.near_all, ...), custom_call_target="tpu_custom_call" | custom-call | flops 2000000000 | bytes 4194304 | tf_op jit(solution)/shard_map/residual/pallas_call | solution.py:464
  25.8 2.3 %collective-permute-start.9 = (bf16[176,1024]{1,0:T(8,128)(2,1)S(1)}, bf16[176,1024]{1,0:T(8,128)(2,1)S(1)}, u32[]{:S(2)}, u32[]{:S(2)}) collective-permute-start(bf16[176,1024]{1,0:T(8,128)(2,1)S(1)} %get-tuple-element.92), channel_id=1, source_target_pairs={{0,16},{8,24},{16,0},{24,8},{1,17},{9,25},{17,1},{25,9},{2,18},{10... | collective-permute-start | bytes 1081352 | tf_op jit(solution)/shard_map/ppermute | solution.py:601
  28.1 4.1 %residual.5 = (bf16[176,1024]{1,0:T(8,128)(2,1)S(1)}, bf16[80,1024]{1,0:T(8,128)(2,1)S(1)}) custom-call(f32[8,128]{1,0:T(8,128)S(1)} %get-tuple-element.82.most, bf16[256,4096]{1,0:T(8,128)(2,1)S(1)} %get-tuple-element.83.own.own_all, bf16[192,2048]{1,0:T(8,128)(2,1)S(1)} %collective-permute-done.6.near_all, ...), custom_call_target="tpu_custom_call" | custom-call | flops 2000000000 | bytes 4194304 | tf_op jit(solution)/shard_map/residual/pallas_call | solution.py:464
  32.2 0.8 %collective-permute-start.8 = (bf16[176,1024]{1,0:T(8,128)(2,1)S(1)}, bf16[176,1024]{1,0:T(8,128)(2,1)S(1)}, u32[]{:S(2)}, u32[]{:S(2)}) collective-permute-start(bf16[176,1024]{1,0:T(8,128)(2,1)S(1)} %get-tuple-element.91), channel_id=1, source_target_pairs={{0,8},{8,0},{16,24},{24,16},{1,9},{9,1},{17,25},{25,17},{2,10},{10... | collective-permute-start | bytes 1081352 | tf_op jit(solution)/shard_map/ppermute | solution.py:601
  33.7 4.2 %residual.4 = (bf16[176,1024]{1,0:T(8,128)(2,1)S(1)}, bf16[80,1024]{1,0:T(8,128)(2,1)S(1)}) custom-call(f32[8,128]{1,0:T(8,128)S(1)} %get-tuple-element.82.most, bf16[256,4096]{1,0:T(8,128)(2,1)S(1)} %get-tuple-element.83.own.own_all, bf16[192,2048]{1,0:T(8,128)(2,1)S(1)} %collective-permute-done.6.near_all, ...), custom_call_target="tpu_custom_call" | custom-call | flops 2000000000 | bytes 4194304 | tf_op jit(solution)/shard_map/residual/pallas_call | solution.py:464
  37.9 2.4 %collective-permute-done.9 = bf16[176,1024]{1,0:T(8,128)(2,1)S(1)} collective-permute-done((bf16[176,1024]{1,0:T(8,128)(2,1)S(1)}, bf16[176,1024]{1,0:T(8,128)(2,1)S(1)}, u32[]{:S(2)}, u32[]{:S(2)}) %collective-permute-start.9) | collective-permute-done | bytes 360480 | tf_op jit(solution)/shard_map/ppermute | solution.py:601
  40.3 1.2 %collective-permute-done.8 = bf16[176,1024]{1,0:T(8,128)(2,1)S(1)} collective-permute-done((bf16[176,1024]{1,0:T(8,128)(2,1)S(1)}, bf16[176,1024]{1,0:T(8,128)(2,1)S(1)}, u32[]{:S(2)}, u32[]{:S(2)}) %collective-permute-start.8) | collective-permute-done | bytes 360480 | tf_op jit(solution)/shard_map/ppermute | solution.py:601
  41.5 2.3 %conditional.1 = ((f32[32,16,1024]{2,1,0:T(8,128)}, f32[32,128]{1,0:T(8,128)S(1)})) conditional(s32[]{:T(128)} %bitcast, (bf16[4,512,256]{2,1,0:T(8,128)(2,1)S(1)}, f32[4,2,16,1024]{3,2,1,0:T(8,128)S(1)}, bf16[176,1024]{1,0:T(8,128)(2,1)S(1)}, bf16[176,1024]{1,0:T(8,128)(2,1)S(1)}, bf16[176,1024]{1,0:T(8,128)(2,1)S(1)}, ...), branch_computations={%region_0.0_spmd, %region_1.0_spmd} | conditional | flops 2000000000 | bytes 6160512 | solution.py:645
  41.5 2.3 %assemble.2 = (f32[32,16,1024]{2,1,0:T(8,128)}, f32[32,128]{1,0:T(8,128)S(1)}) custom-call(bf16[4,512,256]{2,1,0:T(8,128)(2,1)S(1)} %get-tuple-element.32.select, f32[4,2,16,1024]{3,2,1,0:T(8,128)S(1)} %get-tuple-element.33.share, bf16[176,1024]{1,0:T(8,128)(2,1)S(1)} %get-tuple-element.34.refs_0_, bf16[176,1024]{1,0:T(8,128)(2,1)S(1)} %get-tuple-element.35.refs_1_, ...), custom_call_target="tpu_custom_call" | custom-call | flops 2000000000 | bytes 4194304 | tf_op jit(solution)/shard_map/cond/branch_0_fun/assemble/pallas_call | solution.py:549
  43.8 1.9 %collective-permute-start.11 = (f32[32,128]{1,0:T(8,128)S(1)}, f32[32,128]{1,0:T(8,128)S(1)}, u32[]{:S(2)}, u32[]{:S(2)}) collective-permute-start(f32[32,128]{1,0:T(8,128)S(1)} %get-tuple-element.99), channel_id=1, source_target_pairs={{0,1},{1,0},{2,3},{3,2},{4,5},{5,4},{6,7},{7,6},{8,9},{9,8},{10,11... | collective-permute-start | bytes 49160 | tf_op jit(solution)/shard_map/ppermute | solution.py:601
  45.8 0.8 %collective-permute-done.11 = f32[32,128]{1,0:T(8,128)S(1)} collective-permute-done((f32[32,128]{1,0:T(8,128)S(1)}, f32[32,128]{1,0:T(8,128)S(1)}, u32[]{:S(2)}, u32[]{:S(2)}) %collective-permute-start.11) | collective-permute-done | bytes 16416 | tf_op jit(solution)/shard_map/ppermute | solution.py:601
  46.6 0.7 %collective-permute-start.14 = (f32[32,128]{1,0:T(8,128)S(1)}, f32[32,128]{1,0:T(8,128)S(1)}, u32[]{:S(2)}, u32[]{:S(2)}) collective-permute-start(f32[32,128]{1,0:T(8,128)S(1)} %add.21), channel_id=1, source_target_pairs={{0,24},{8,16},{16,8},{24,0},{1,25},{9,17},{17,9},{25,1},{2,26},{10... | collective-permute-start | bytes 49160 | tf_op jit(solution)/shard_map/ppermute | solution.py:601
  47.3 1.5 %collective-permute-start.13 = (f32[32,128]{1,0:T(8,128)S(1)}, f32[32,128]{1,0:T(8,128)S(1)}, u32[]{:S(2)}, u32[]{:S(2)}) collective-permute-start(f32[32,128]{1,0:T(8,128)S(1)} %add.21), channel_id=1, source_target_pairs={{0,16},{8,24},{16,0},{24,8},{1,17},{9,25},{17,1},{25,9},{2,18},{10... | collective-permute-start | bytes 49160 | tf_op jit(solution)/shard_map/ppermute | solution.py:601
  48.8 1.3 %collective-permute-start.12 = (f32[32,128]{1,0:T(8,128)S(1)}, f32[32,128]{1,0:T(8,128)S(1)}, u32[]{:S(2)}, u32[]{:S(2)}) collective-permute-start(f32[32,128]{1,0:T(8,128)S(1)} %add.21), channel_id=1, source_target_pairs={{0,8},{8,0},{16,24},{24,16},{1,9},{9,1},{17,25},{25,17},{2,10},{10... | collective-permute-start | bytes 49160 | tf_op jit(solution)/shard_map/ppermute | solution.py:601
  50.1 1.3 %collective-permute-done.14 = f32[32,128]{1,0:T(8,128)S(1)} collective-permute-done((f32[32,128]{1,0:T(8,128)S(1)}, f32[32,128]{1,0:T(8,128)S(1)}, u32[]{:S(2)}, u32[]{:S(2)}) %collective-permute-start.14) | collective-permute-done | bytes 16416 | tf_op jit(solution)/shard_map/ppermute | solution.py:601
  51.4 1.1 %collective-permute-done.12 = f32[32,128]{1,0:T(8,128)S(1)} collective-permute-done((f32[32,128]{1,0:T(8,128)S(1)}, f32[32,128]{1,0:T(8,128)S(1)}, u32[]{:S(2)}, u32[]{:S(2)}) %collective-permute-start.12) | collective-permute-done | bytes 16416 | tf_op jit(solution)/shard_map/ppermute | solution.py:601
  52.6 3.3 %collective-permute-start.17 = (f32[32,128]{1,0:T(8,128)S(1)}, f32[32,128]{1,0:T(8,128)S(1)}, u32[]{:S(2)}, u32[]{:S(2)}) collective-permute-start(f32[32,128]{1,0:T(8,128)S(1)} %add_add_fusion.1), channel_id=1, source_target_pairs={{0,6},{1,7},{2,4},{3,5},{4,2},{5,3},{6,0},{7,1},{8,14},{9,15},{10,... | collective-permute-start | bytes 49160 | tf_op jit(solution)/shard_map/ppermute | solution.py:601
  55.9 2.3 %collective-permute-start.16 = (f32[32,128]{1,0:T(8,128)S(1)}, f32[32,128]{1,0:T(8,128)S(1)}, u32[]{:S(2)}, u32[]{:S(2)}) collective-permute-start(f32[32,128]{1,0:T(8,128)S(1)} %add_add_fusion.1), channel_id=1, source_target_pairs={{0,4},{1,5},{2,6},{3,7},{4,0},{5,1},{6,2},{7,3},{8,12},{9,13},{10,... | collective-permute-start | bytes 49160 | tf_op jit(solution)/shard_map/ppermute | solution.py:601
  58.3 2.3 %collective-permute-done.16 = f32[32,128]{1,0:T(8,128)S(1)} collective-permute-done((f32[32,128]{1,0:T(8,128)S(1)}, f32[32,128]{1,0:T(8,128)S(1)}, u32[]{:S(2)}, u32[]{:S(2)}) %collective-permute-start.16) | collective-permute-done | bytes 16416 | tf_op jit(solution)/shard_map/ppermute | solution.py:601
  60.5 1.4 %collective-permute-done.15 = f32[32,128]{1,0:T(8,128)S(1)} collective-permute-done((f32[32,128]{1,0:T(8,128)S(1)}, f32[32,128]{1,0:T(8,128)S(1)}, u32[]{:S(2)}, u32[]{:S(2)}) %collective-permute-start.15) | collective-permute-done | bytes 16416 | tf_op jit(solution)/shard_map/ppermute | solution.py:601
  61.9 0.8 %correlate.1 = f32[32,32]{1,0:T(8,128)} custom-call(f32[32,128]{1,0:T(8,128)S(1)} %add_add_fusion.refs_0_), custom_call_target="tpu_custom_call" | custom-call | tf_op jit(solution)/shard_map/correlate/pallas_call | solution.py:591
  (15 shorter events, 1.3 us)
Async XLA Ops:
  0.6 1.6 %copy-start = (bf16[16,16,4096]{2,1,0:T(8,128)(2,1)S(1)}, bf16[16,16,4096]{2,1,0:T(8,128)(2,1)}, u32[]{:S(2)}) copy-start(bf16[16,16,4096]{2,1,0:T(8,128)(2,1)} %photos.1) | copy-start | bytes 6291460
  2.2 0.7 %copy-start.1 = (s32[16]{0:T(128)S(1)}, s32[16]{0:T(128)}, u32[]{:S(2)}) copy-start(s32[16]{0:T(128)} %ids_all.3) | copy-start | bytes 196
  4.8 11.8 %collective-permute-start.6 = (bf16[192,2048]{1,0:T(8,128)(2,1)S(1)}, bf16[192,2048]{1,0:T(8,128)(2,1)S(1)}, u32[]{:S(2)}, u32[]{:S(2)}) collective-permute-start(bf16[192,2048]{1,0:T(8,128)(2,1)S(1)} %get-tuple-element.84), channel_id=1, source_target_pairs={{0,1},{1,0},{2,3},{3,2},{4,5},{5,4},{6,7},{7,6},{8,9},{9,8},{10,11... | collective-permute-start | bytes 2359304 | tf_op jit(solution)/shard_map/ppermute | solution.py:601
  5.3 11.3 %collective-permute-start.7 = (bf16[192,2048]{1,0:T(8,128)(2,1)S(1)}, bf16[192,2048]{1,0:T(8,128)(2,1)S(1)}, u32[]{:S(2)}, u32[]{:S(2)}) collective-permute-start(bf16[192,2048]{1,0:T(8,128)(2,1)S(1)} %get-tuple-element.85), channel_id=1, source_target_pairs={{1,2},{3,4},{5,6},{2,1},{4,3},{6,5},{9,10},{11,12},{13,14},{10,9},... | collective-permute-start | bytes 2359304 | tf_op jit(solution)/shard_map/ppermute | solution.py:617
  6.0 6.5 %collective-permute-start.3 = (bf16[48,1024]{1,0:T(8,128)(2,1)S(1)}, bf16[48,1024]{1,0:T(8,128)(2,1)S(1)}, u32[]{:S(2)}, u32[]{:S(2)}) collective-permute-start(bf16[48,1024]{1,0:T(8,128)(2,1)S(1)} %get-tuple-element.76), channel_id=1, source_target_pairs={{0,8},{8,0},{16,24},{24,16},{1,9},{9,1},{17,25},{25,17},{2,10},{10... | collective-permute-start | bytes 294920 | tf_op jit(solution)/shard_map/ppermute | solution.py:601
  8.5 4.6 %collective-permute-start.4 = (bf16[48,1024]{1,0:T(8,128)(2,1)S(1)}, bf16[48,1024]{1,0:T(8,128)(2,1)S(1)}, u32[]{:S(2)}, u32[]{:S(2)}) collective-permute-start(bf16[48,1024]{1,0:T(8,128)(2,1)S(1)} %get-tuple-element.77), channel_id=1, source_target_pairs={{0,16},{8,24},{16,0},{24,8},{1,17},{9,25},{17,1},{25,9},{2,18},{10... | collective-permute-start | bytes 294920 | tf_op jit(solution)/shard_map/ppermute | solution.py:601
  10.1 5.6 %collective-permute-start.5 = (bf16[48,1024]{1,0:T(8,128)(2,1)S(1)}, bf16[48,1024]{1,0:T(8,128)(2,1)S(1)}, u32[]{:S(2)}, u32[]{:S(2)}) collective-permute-start(bf16[48,1024]{1,0:T(8,128)(2,1)S(1)} %get-tuple-element.78), channel_id=1, source_target_pairs={{0,24},{8,16},{16,8},{24,0},{1,25},{9,17},{17,9},{25,1},{2,26},{10... | collective-permute-start | bytes 294920 | tf_op jit(solution)/shard_map/ppermute | solution.py:601
  20.8 17.1 %collective-permute-start.10 = (bf16[176,1024]{1,0:T(8,128)(2,1)S(1)}, bf16[176,1024]{1,0:T(8,128)(2,1)S(1)}, u32[]{:S(2)}, u32[]{:S(2)}) collective-permute-start(bf16[176,1024]{1,0:T(8,128)(2,1)S(1)} %get-tuple-element.93), channel_id=1, source_target_pairs={{0,24},{8,16},{16,8},{24,0},{1,25},{9,17},{17,9},{25,1},{2,26},{10... | collective-permute-start | bytes 1081352 | tf_op jit(solution)/shard_map/ppermute | solution.py:601
  25.8 14.5 %collective-permute-start.9 = (bf16[176,1024]{1,0:T(8,128)(2,1)S(1)}, bf16[176,1024]{1,0:T(8,128)(2,1)S(1)}, u32[]{:S(2)}, u32[]{:S(2)}) collective-permute-start(bf16[176,1024]{1,0:T(8,128)(2,1)S(1)} %get-tuple-element.92), channel_id=1, source_target_pairs={{0,16},{8,24},{16,0},{24,8},{1,17},{9,25},{17,1},{25,9},{2,18},{10... | collective-permute-start | bytes 1081352 | tf_op jit(solution)/shard_map/ppermute | solution.py:601
  32.2 9.3 %collective-permute-start.8 = (bf16[176,1024]{1,0:T(8,128)(2,1)S(1)}, bf16[176,1024]{1,0:T(8,128)(2,1)S(1)}, u32[]{:S(2)}, u32[]{:S(2)}) collective-permute-start(bf16[176,1024]{1,0:T(8,128)(2,1)S(1)} %get-tuple-element.91), channel_id=1, source_target_pairs={{0,8},{8,0},{16,24},{24,16},{1,9},{9,1},{17,25},{25,17},{2,10},{10... | collective-permute-start | bytes 1081352 | tf_op jit(solution)/shard_map/ppermute | solution.py:601
  43.8 2.8 %collective-permute-start.11 = (f32[32,128]{1,0:T(8,128)S(1)}, f32[32,128]{1,0:T(8,128)S(1)}, u32[]{:S(2)}, u32[]{:S(2)}) collective-permute-start(f32[32,128]{1,0:T(8,128)S(1)} %get-tuple-element.99), channel_id=1, source_target_pairs={{0,1},{1,0},{2,3},{3,2},{4,5},{5,4},{6,7},{7,6},{8,9},{9,8},{10,11... | collective-permute-start | bytes 49160 | tf_op jit(solution)/shard_map/ppermute | solution.py:601
  46.6 4.8 %collective-permute-start.14 = (f32[32,128]{1,0:T(8,128)S(1)}, f32[32,128]{1,0:T(8,128)S(1)}, u32[]{:S(2)}, u32[]{:S(2)}) collective-permute-start(f32[32,128]{1,0:T(8,128)S(1)} %add.21), channel_id=1, source_target_pairs={{0,24},{8,16},{16,8},{24,0},{1,25},{9,17},{17,9},{25,1},{2,26},{10... | collective-permute-start | bytes 49160 | tf_op jit(solution)/shard_map/ppermute | solution.py:601
  47.3 4.1 %collective-permute-start.13 = (f32[32,128]{1,0:T(8,128)S(1)}, f32[32,128]{1,0:T(8,128)S(1)}, u32[]{:S(2)}, u32[]{:S(2)}) collective-permute-start(f32[32,128]{1,0:T(8,128)S(1)} %add.21), channel_id=1, source_target_pairs={{0,16},{8,24},{16,0},{24,8},{1,17},{9,25},{17,1},{25,9},{2,18},{10... | collective-permute-start | bytes 49160 | tf_op jit(solution)/shard_map/ppermute | solution.py:601
  48.8 3.7 %collective-permute-start.12 = (f32[32,128]{1,0:T(8,128)S(1)}, f32[32,128]{1,0:T(8,128)S(1)}, u32[]{:S(2)}, u32[]{:S(2)}) collective-permute-start(f32[32,128]{1,0:T(8,128)S(1)} %add.21), channel_id=1, source_target_pairs={{0,8},{8,0},{16,24},{24,16},{1,9},{9,1},{17,25},{25,17},{2,10},{10... | collective-permute-start | bytes 49160 | tf_op jit(solution)/shard_map/ppermute | solution.py:601
  52.6 5.7 %collective-permute-start.17 = (f32[32,128]{1,0:T(8,128)S(1)}, f32[32,128]{1,0:T(8,128)S(1)}, u32[]{:S(2)}, u32[]{:S(2)}) collective-permute-start(f32[32,128]{1,0:T(8,128)S(1)} %add_add_fusion.1), channel_id=1, source_target_pairs={{0,6},{1,7},{2,4},{3,5},{4,2},{5,3},{6,0},{7,1},{8,14},{9,15},{10,... | collective-permute-start | bytes 49160 | tf_op jit(solution)/shard_map/ppermute | solution.py:601
  55.9 4.6 %collective-permute-start.16 = (f32[32,128]{1,0:T(8,128)S(1)}, f32[32,128]{1,0:T(8,128)S(1)}, u32[]{:S(2)}, u32[]{:S(2)}) collective-permute-start(f32[32,128]{1,0:T(8,128)S(1)} %add_add_fusion.1), channel_id=1, source_target_pairs={{0,4},{1,5},{2,6},{3,7},{4,0},{5,1},{6,2},{7,3},{8,12},{9,13},{10,... | collective-permute-start | bytes 49160 | tf_op jit(solution)/shard_map/ppermute | solution.py:601
  58.2 3.7 %collective-permute-start.15 = (f32[32,128]{1,0:T(8,128)S(1)}, f32[32,128]{1,0:T(8,128)S(1)}, u32[]{:S(2)}, u32[]{:S(2)}) collective-permute-start(f32[32,128]{1,0:T(8,128)S(1)} %add_add_fusion.1), channel_id=1, source_target_pairs={{0,2},{1,3},{2,0},{3,1},{4,6},{5,7},{6,4},{7,5},{8,10},{9,11},{10,... | collective-permute-start | bytes 49160 | tf_op jit(solution)/shard_map/ppermute | solution.py:601

commit v10 on v9

--- a/solution.py
+++ b/solution.py
@@ -497,7 +497,6 @@
     parts, others = refs[:pieces], refs[pieces:-7]
     prints, partial, flat, scaled, wide, total, sent = refs[-7:]
     width = parts[0].shape[1]
-    size = parts[0].shape[0] + sum(other.shape[0] for other in others[:1])
     tall = CAMS * rows
     for place, part in enumerate(parts):
         edges = part[: 2 * rows, :].astype(f32) * share[place].reshape(2 * rows, width)
@@ -506,15 +505,18 @@
     copies = []
     for block in range(width // (2 * LANES)):
         cols = slice(block * 2 * LANES, (block + 1) * 2 * LANES)
-        joined = jnp.zeros((tall, 2 * LANES), f32)
+        sources = []
         for place, part in enumerate(parts):
-            pieces_of = [scaled[place, :, cols], part[2 * rows :, cols]]
+            sources += [scaled[place, :, cols], part[2 * rows :, cols]]
             if others:
-                pieces_of.append(others[place][:, cols])
-            source = jnp.concatenate(pieces_of, axis=0)
-            joined = joined + jnp.dot(
-                select[place, :, :size], source, preferred_element_type=f32
-            )
+                sources.append(others[place][:, cols])
+            else:
+                sources.append(jnp.zeros((select.shape[2] - part.shape[0], 2 * LANES), bf16))
+        joined = jnp.dot(
+            jnp.concatenate([select[place] for place in range(pieces)], axis=1),
+            jnp.concatenate(sources, axis=0),
+            preferred_element_type=f32,
+        )
         flat[:, cols] = joined.astype(bf16)
         total[...] += joined[:, :LANES] + joined[:, LANES:]
         wide[:, :, cols] = joined.reshape(CAMS, rows, 2 * LANES)

time: 62.8 us -> 62.9 us (level)
  no operation moved by 1% of the time
where the time goes in v10:
time: 62.9 us; the launch traced here: 62.6 us
  Pallas kernels  25.1 us (40%)
  starting transfers between devices  19.9 us (32%)
  waiting for transfers between devices  13.9 us (22%)
  local copies, waits for them, and re-layouts  2.24 us (4%)
  between operations  1.41 us (2%)
    ppermute x14, starting transfers between devices, exchange(): return lax.ppermute(array, axis, [(i, i ^ distance) for i in range(size)])  19.3 us
    pallas_call x4, Pallas kernels, main_part(): pl.pallas_call(functools.partial(main_kernel, count, rows, distance), in_...  16.9 us
    ppermute x14, waiting for transfers between devices, exchange(): return lax.ppermute(array, axis, [(i, i ^ distance) for i in range(size)])  13.9 us
    pallas_call x1, Pallas kernels, energies(): pl.pallas_call(functools.partial(energy_kernel, size // rows, rows), in_s...  2.4 us
    pallas_call x1, Pallas kernels, assemble(): pl.pallas_call(functools.partial(assemble_kernel, rows, len(parts)), in_s...  2.3 us
    unnamed x4, local copies, waits for them, and re-layouts  2.24 us
    pallas_call x1, Pallas kernels, prepare(): pl.pallas_call(prepare_kernel, in_specs=[pl.BlockSpec(memory_space=pl.ANY...  1.8 us
  transfers between devices with their start and end apart: 15, of which 9 were waited for; matrix products, arithmetic and copies ran while one was open for 0% of the time, Pallas kernels for 25%

profile of v10, /device:TPU:0, one launch (start us, length us, event | category | flops | bytes accessed | tf_op | source)
XLA Modules:
  0.0 62.6 jit_solution(11158318506793366174)
XLA Ops:
  0.6 1.6 %copy-done = bf16[16,16,4096]{2,1,0:T(8,128)(2,1)S(1)} copy-done((bf16[16,16,4096]{2,1,0:T(8,128)(2,1)S(1)}, bf16[16,16,4096]{2,1,0:T(8,128)(2,1)}, u32[]{:S(2)}) %copy-start) | copy-done | bytes 2097176
  2.2 0.7 %copy-done.1 = s32[16]{0:T(128)S(1)} copy-done((s32[16]{0:T(128)S(1)}, s32[16]{0:T(128)}, u32[]{:S(2)}) %copy-start.1) | copy-done | bytes 88
  2.9 1.8 %prepare.1 = (bf16[256,4096]{1,0:T(8,128)(2,1)S(1)}, bf16[192,2048]{1,0:T(8,128)(2,1)S(1)}, bf16[192,2048]{1,0:T(8,128)(2,1)S(1)}, bf16[48,1024]{1,0:T(8,128)(2,...) custom-call(s32[16]{0:T(128)S(1)} %copy-done.1, ...), custom_call_target="tpu_custom_call" | custom-call | flops 1000000000 | bytes 8388608 | tf_op jit(solution)/shard_map/prepare/pallas_call | solution.py:159
  5.2 0.7 %collective-permute-start.7 = (bf16[192,2048]{1,0:T(8,128)(2,1)S(1)}, bf16[192,2048]{1,0:T(8,128)(2,1)S(1)}, u32[]{:S(2)}, u32[]{:S(2)}) collective-permute-start(bf16[192,2048]{1,0:T(8,128)(2,1)S(1)} %get-tuple-element.85), channel_id=1, source_target_pairs={{1,2},{3,4},{5,6},{2,1},{4,3},{6,5},{9,10},{11,12},{13,14},{10,9},... | collective-permute-start | bytes 2359304 | tf_op jit(solution)/shard_map/ppermute | solution.py:619
  5.9 2.5 %collective-permute-start.3 = (bf16[48,1024]{1,0:T(8,128)(2,1)S(1)}, bf16[48,1024]{1,0:T(8,128)(2,1)S(1)}, u32[]{:S(2)}, u32[]{:S(2)}) collective-permute-start(bf16[48,1024]{1,0:T(8,128)(2,1)S(1)} %get-tuple-element.76), channel_id=1, source_target_pairs={{0,8},{8,0},{16,24},{24,16},{1,9},{9,1},{17,25},{25,17},{2,10},{10... | collective-permute-start | bytes 294920 | tf_op jit(solution)/shard_map/ppermute | solution.py:603
  8.4 1.7 %collective-permute-start.4 = (bf16[48,1024]{1,0:T(8,128)(2,1)S(1)}, bf16[48,1024]{1,0:T(8,128)(2,1)S(1)}, u32[]{:S(2)}, u32[]{:S(2)}) collective-permute-start(bf16[48,1024]{1,0:T(8,128)(2,1)S(1)} %get-tuple-element.77), channel_id=1, source_target_pairs={{0,16},{8,24},{16,0},{24,8},{1,17},{9,25},{17,1},{25,9},{2,18},{10... | collective-permute-start | bytes 294920 | tf_op jit(solution)/shard_map/ppermute | solution.py:603
  10.1 2.4 %energies.1 = (f32[256,4096]{1,0:T(8,128)S(1)}, bf16[256,512]{1,0:T(8,128)(2,1)S(1)}, bf16[4,512,256]{2,1,0:T(8,128)(2,1)S(1)}, bf16[256,256]{1,0:T(8,128)(2,1)S(1)}) custom-call(s32[16]{0:T(128)S(1)} %copy-done.1, bf16[256,4096]{1,0:T(8,128)(2,1)S(1)} %get-tuple-element.83.own.own_all), custom_call_target="tpu_custom_call" | custom-call | flops 1000000000 | bytes 8388608 | tf_op jit(solution)/shard_map/energies/pallas_call | solution.py:212
  12.5 0.5 collective-permute-done.4.refs_2_
  13.1 2.7 %collective-permute-done.5.refs_3_ = bf16[48,1024]{1,0:T(8,128)(2,1)S(1)} collective-permute-done((bf16[48,1024]{1,0:T(8,128)(2,1)S(1)}, bf16[48,1024]{1,0:T(8,128)(2,1)S(1)}, u32[]{:S(2)}, u32[]{:S(2)}) %collective-permute-start.5) | collective-permute-done | bytes 98336 | tf_op jit(solution)/shard_map/ppermute | solution.py:603
  15.7 0.9 %blend.1 = (bf16[4,512,256]{2,1,0:T(8,128)(2,1)S(1)}, f32[4,2,16,1024]{3,2,1,0:T(8,128)S(1)}, s32[1]{0:T(128)}, f32[8,128]{1,0:T(8,128)S(1)}) custom-call(bf16[48,1024]{1,0:T(8,128)(2,1)S(1)} %get-tuple-element.75.refs_0_, bf16[48,1024]{1,0:T(8,128)(2,1)S(1)} %collective-permute-done.3.refs_1_, bf16[48,1024]{1,0:T(8,128)(2,1)S(1)} %collective-permute-done.4.refs_2_, ...), custom_call_target="tpu_custom_call" | custom-call | tf_op jit(solution)/shard_map/blend/pallas_call | solution.py:265
  16.6 4.2 %residual.7 = (bf16[176,1024]{1,0:T(8,128)(2,1)S(1)}, bf16[80,1024]{1,0:T(8,128)(2,1)S(1)}) custom-call(f32[8,128]{1,0:T(8,128)S(1)} %get-tuple-element.82.most, bf16[256,4096]{1,0:T(8,128)(2,1)S(1)} %get-tuple-element.83.own.own_all, bf16[192,2048]{1,0:T(8,128)(2,1)S(1)} %collective-permute-done.6.near_all, ...), custom_call_target="tpu_custom_call" | custom-call | flops 2000000000 | bytes 4194304 | tf_op jit(solution)/shard_map/residual/pallas_call | solution.py:464
  20.9 0.7 %collective-permute-start.10 = (bf16[176,1024]{1,0:T(8,128)(2,1)S(1)}, bf16[176,1024]{1,0:T(8,128)(2,1)S(1)}, u32[]{:S(2)}, u32[]{:S(2)}) collective-permute-start(bf16[176,1024]{1,0:T(8,128)(2,1)S(1)} %get-tuple-element.93), channel_id=1, source_target_pairs={{0,24},{8,16},{16,8},{24,0},{1,25},{9,17},{17,9},{25,1},{2,26},{10... | collective-permute-start | bytes 1081352 | tf_op jit(solution)/shard_map/ppermute | solution.py:603
  21.6 4.3 %residual.6 = (bf16[176,1024]{1,0:T(8,128)(2,1)S(1)}, bf16[80,1024]{1,0:T(8,128)(2,1)S(1)}) custom-call(f32[8,128]{1,0:T(8,128)S(1)} %get-tuple-element.82.most, bf16[256,4096]{1,0:T(8,128)(2,1)S(1)} %get-tuple-element.83.own.own_all, bf16[192,2048]{1,0:T(8,128)(2,1)S(1)} %collective-permute-done.6.near_all, ...), custom_call_target="tpu_custom_call" | custom-call | flops 2000000000 | bytes 4194304 | tf_op jit(solution)/shard_map/residual/pallas_call | solution.py:464
  25.9 2.3 %collective-permute-start.9 = (bf16[176,1024]{1,0:T(8,128)(2,1)S(1)}, bf16[176,1024]{1,0:T(8,128)(2,1)S(1)}, u32[]{:S(2)}, u32[]{:S(2)}) collective-permute-start(bf16[176,1024]{1,0:T(8,128)(2,1)S(1)} %get-tuple-element.92), channel_id=1, source_target_pairs={{0,16},{8,24},{16,0},{24,8},{1,17},{9,25},{17,1},{25,9},{2,18},{10... | collective-permute-start | bytes 1081352 | tf_op jit(solution)/shard_map/ppermute | solution.py:603
  28.2 4.1 %residual.5 = (bf16[176,1024]{1,0:T(8,128)(2,1)S(1)}, bf16[80,1024]{1,0:T(8,128)(2,1)S(1)}) custom-call(f32[8,128]{1,0:T(8,128)S(1)} %get-tuple-element.82.most, bf16[256,4096]{1,0:T(8,128)(2,1)S(1)} %get-tuple-element.83.own.own_all, bf16[192,2048]{1,0:T(8,128)(2,1)S(1)} %collective-permute-done.6.near_all, ...), custom_call_target="tpu_custom_call" | custom-call | flops 2000000000 | bytes 4194304 | tf_op jit(solution)/shard_map/residual/pallas_call | solution.py:464
  32.4 0.7 %collective-permute-start.8 = (bf16[176,1024]{1,0:T(8,128)(2,1)S(1)}, bf16[176,1024]{1,0:T(8,128)(2,1)S(1)}, u32[]{:S(2)}, u32[]{:S(2)}) collective-permute-start(bf16[176,1024]{1,0:T(8,128)(2,1)S(1)} %get-tuple-element.91), channel_id=1, source_target_pairs={{0,8},{8,0},{16,24},{24,16},{1,9},{9,1},{17,25},{25,17},{2,10},{10... | collective-permute-start | bytes 1081352 | tf_op jit(solution)/shard_map/ppermute | solution.py:603
  33.7 4.2 %residual.4 = (bf16[176,1024]{1,0:T(8,128)(2,1)S(1)}, bf16[80,1024]{1,0:T(8,128)(2,1)S(1)}) custom-call(f32[8,128]{1,0:T(8,128)S(1)} %get-tuple-element.82.most, bf16[256,4096]{1,0:T(8,128)(2,1)S(1)} %get-tuple-element.83.own.own_all, bf16[192,2048]{1,0:T(8,128)(2,1)S(1)} %collective-permute-done.6.near_all, ...), custom_call_target="tpu_custom_call" | custom-call | flops 2000000000 | bytes 4194304 | tf_op jit(solution)/shard_map/residual/pallas_call | solution.py:464
  38.0 2.4 %collective-permute-done.9 = bf16[176,1024]{1,0:T(8,128)(2,1)S(1)} collective-permute-done((bf16[176,1024]{1,0:T(8,128)(2,1)S(1)}, bf16[176,1024]{1,0:T(8,128)(2,1)S(1)}, u32[]{:S(2)}, u32[]{:S(2)}) %collective-permute-start.9) | collective-permute-done | bytes 360480 | tf_op jit(solution)/shard_map/ppermute | solution.py:603
  40.4 1.5 %collective-permute-done.8 = bf16[176,1024]{1,0:T(8,128)(2,1)S(1)} collective-permute-done((bf16[176,1024]{1,0:T(8,128)(2,1)S(1)}, bf16[176,1024]{1,0:T(8,128)(2,1)S(1)}, u32[]{:S(2)}, u32[]{:S(2)}) %collective-permute-start.8) | collective-permute-done | bytes 360480 | tf_op jit(solution)/shard_map/ppermute | solution.py:603
  41.9 2.3 %conditional.1 = ((f32[32,16,1024]{2,1,0:T(8,128)}, f32[32,128]{1,0:T(8,128)S(1)})) conditional(s32[]{:T(128)} %bitcast, (bf16[4,512,256]{2,1,0:T(8,128)(2,1)S(1)}, f32[4,2,16,1024]{3,2,1,0:T(8,128)S(1)}, bf16[176,1024]{1,0:T(8,128)(2,1)S(1)}, bf16[176,1024]{1,0:T(8,128)(2,1)S(1)}, bf16[176,1024]{1,0:T(8,128)(2,1)S(1)}, ...), branch_computations={%region_0.0_spmd, %region_1.0_spmd} | conditional | flops 2000000000 | bytes 6160512 | solution.py:647
  41.9 2.3 %assemble.2 = (f32[32,16,1024]{2,1,0:T(8,128)}, f32[32,128]{1,0:T(8,128)S(1)}) custom-call(bf16[4,512,256]{2,1,0:T(8,128)(2,1)S(1)} %get-tuple-element.32.select, f32[4,2,16,1024]{3,2,1,0:T(8,128)S(1)} %get-tuple-element.33.share, bf16[176,1024]{1,0:T(8,128)(2,1)S(1)} %get-tuple-element.34.refs_0_, bf16[176,1024]{1,0:T(8,128)(2,1)S(1)} %get-tuple-element.35.refs_1_, ...), custom_call_target="tpu_custom_call" | custom-call | flops 2000000000 | bytes 4194304 | tf_op jit(solution)/shard_map/cond/branch_0_fun/assemble/pallas_call | solution.py:551
  44.2 1.8 %collective-permute-start.11 = (f32[32,128]{1,0:T(8,128)S(1)}, f32[32,128]{1,0:T(8,128)S(1)}, u32[]{:S(2)}, u32[]{:S(2)}) collective-permute-start(f32[32,128]{1,0:T(8,128)S(1)} %get-tuple-element.99), channel_id=1, source_target_pairs={{0,1},{1,0},{2,3},{3,2},{4,5},{5,4},{6,7},{7,6},{8,9},{9,8},{10,11... | collective-permute-start | bytes 49160 | tf_op jit(solution)/shard_map/ppermute | solution.py:603
  45.9 0.8 %collective-permute-done.11 = f32[32,128]{1,0:T(8,128)S(1)} collective-permute-done((f32[32,128]{1,0:T(8,128)S(1)}, f32[32,128]{1,0:T(8,128)S(1)}, u32[]{:S(2)}, u32[]{:S(2)}) %collective-permute-start.11) | collective-permute-done | bytes 16416 | tf_op jit(solution)/shard_map/ppermute | solution.py:603
  47.2 1.7 %collective-permute-start.13 = (f32[32,128]{1,0:T(8,128)S(1)}, f32[32,128]{1,0:T(8,128)S(1)}, u32[]{:S(2)}, u32[]{:S(2)}) collective-permute-start(f32[32,128]{1,0:T(8,128)S(1)} %add.21), channel_id=1, source_target_pairs={{0,16},{8,24},{16,0},{24,8},{1,17},{9,25},{17,1},{25,9},{2,18},{10... | collective-permute-start | bytes 49160 | tf_op jit(solution)/shard_map/ppermute | solution.py:603
  48.9 1.4 %collective-permute-start.12 = (f32[32,128]{1,0:T(8,128)S(1)}, f32[32,128]{1,0:T(8,128)S(1)}, u32[]{:S(2)}, u32[]{:S(2)}) collective-permute-start(f32[32,128]{1,0:T(8,128)S(1)} %add.21), channel_id=1, source_target_pairs={{0,8},{8,0},{16,24},{24,16},{1,9},{9,1},{17,25},{25,17},{2,10},{10... | collective-permute-start | bytes 49160 | tf_op jit(solution)/shard_map/ppermute | solution.py:603
  50.3 1.1 %collective-permute-done.14 = f32[32,128]{1,0:T(8,128)S(1)} collective-permute-done((f32[32,128]{1,0:T(8,128)S(1)}, f32[32,128]{1,0:T(8,128)S(1)}, u32[]{:S(2)}, u32[]{:S(2)}) %collective-permute-start.14) | collective-permute-done | bytes 16416 | tf_op jit(solution)/shard_map/ppermute | solution.py:603
  51.4 1.2 %collective-permute-done.12 = f32[32,128]{1,0:T(8,128)S(1)} collective-permute-done((f32[32,128]{1,0:T(8,128)S(1)}, f32[32,128]{1,0:T(8,128)S(1)}, u32[]{:S(2)}, u32[]{:S(2)}) %collective-permute-start.12) | collective-permute-done | bytes 16416 | tf_op jit(solution)/shard_map/ppermute | solution.py:603
  52.6 3.2 %collective-permute-start.17 = (f32[32,128]{1,0:T(8,128)S(1)}, f32[32,128]{1,0:T(8,128)S(1)}, u32[]{:S(2)}, u32[]{:S(2)}) collective-permute-start(f32[32,128]{1,0:T(8,128)S(1)} %add_add_fusion.1), channel_id=1, source_target_pairs={{0,6},{1,7},{2,4},{3,5},{4,2},{5,3},{6,0},{7,1},{8,14},{9,15},{10,... | collective-permute-start | bytes 49160 | tf_op jit(solution)/shard_map/ppermute | solution.py:603
  55.8 2.2 %collective-permute-start.16 = (f32[32,128]{1,0:T(8,128)S(1)}, f32[32,128]{1,0:T(8,128)S(1)}, u32[]{:S(2)}, u32[]{:S(2)}) collective-permute-start(f32[32,128]{1,0:T(8,128)S(1)} %add_add_fusion.1), channel_id=1, source_target_pairs={{0,4},{1,5},{2,6},{3,7},{4,0},{5,1},{6,2},{7,3},{8,12},{9,13},{10,... | collective-permute-start | bytes 49160 | tf_op jit(solution)/shard_map/ppermute | solution.py:603
  58.2 2.2 %collective-permute-done.16 = f32[32,128]{1,0:T(8,128)S(1)} collective-permute-done((f32[32,128]{1,0:T(8,128)S(1)}, f32[32,128]{1,0:T(8,128)S(1)}, u32[]{:S(2)}, u32[]{:S(2)}) %collective-permute-start.16) | collective-permute-done | bytes 16416 | tf_op jit(solution)/shard_map/ppermute | solution.py:603
  60.5 1.3 %collective-permute-done.15 = f32[32,128]{1,0:T(8,128)S(1)} collective-permute-done((f32[32,128]{1,0:T(8,128)S(1)}, f32[32,128]{1,0:T(8,128)S(1)}, u32[]{:S(2)}, u32[]{:S(2)}) %collective-permute-start.15) | collective-permute-done | bytes 16416 | tf_op jit(solution)/shard_map/ppermute | solution.py:603
  61.8 0.8 %correlate.1 = f32[32,32]{1,0:T(8,128)} custom-call(f32[32,128]{1,0:T(8,128)S(1)} %add_add_fusion.refs_0_), custom_call_target="tpu_custom_call" | custom-call | tf_op jit(solution)/shard_map/correlate/pallas_call | solution.py:593
  (15 shorter events, 1.1 us)
Async XLA Ops:
  0.6 1.6 %copy-start = (bf16[16,16,4096]{2,1,0:T(8,128)(2,1)S(1)}, bf16[16,16,4096]{2,1,0:T(8,128)(2,1)}, u32[]{:S(2)}) copy-start(bf16[16,16,4096]{2,1,0:T(8,128)(2,1)} %photos.1) | copy-start | bytes 6291460
  2.2 0.7 %copy-start.1 = (s32[16]{0:T(128)S(1)}, s32[16]{0:T(128)}, u32[]{:S(2)}) copy-start(s32[16]{0:T(128)} %ids_all.3) | copy-start | bytes 196
  4.7 11.9 %collective-permute-start.6 = (bf16[192,2048]{1,0:T(8,128)(2,1)S(1)}, bf16[192,2048]{1,0:T(8,128)(2,1)S(1)}, u32[]{:S(2)}, u32[]{:S(2)}) collective-permute-start(bf16[192,2048]{1,0:T(8,128)(2,1)S(1)} %get-tuple-element.84), channel_id=1, source_target_pairs={{0,1},{1,0},{2,3},{3,2},{4,5},{5,4},{6,7},{7,6},{8,9},{9,8},{10,11... | collective-permute-start | bytes 2359304 | tf_op jit(solution)/shard_map/ppermute | solution.py:603
  5.2 11.4 %collective-permute-start.7 = (bf16[192,2048]{1,0:T(8,128)(2,1)S(1)}, bf16[192,2048]{1,0:T(8,128)(2,1)S(1)}, u32[]{:S(2)}, u32[]{:S(2)}) collective-permute-start(bf16[192,2048]{1,0:T(8,128)(2,1)S(1)} %get-tuple-element.85), channel_id=1, source_target_pairs={{1,2},{3,4},{5,6},{2,1},{4,3},{6,5},{9,10},{11,12},{13,14},{10,9},... | collective-permute-start | bytes 2359304 | tf_op jit(solution)/shard_map/ppermute | solution.py:619
  5.9 6.6 %collective-permute-start.3 = (bf16[48,1024]{1,0:T(8,128)(2,1)S(1)}, bf16[48,1024]{1,0:T(8,128)(2,1)S(1)}, u32[]{:S(2)}, u32[]{:S(2)}) collective-permute-start(bf16[48,1024]{1,0:T(8,128)(2,1)S(1)} %get-tuple-element.76), channel_id=1, source_target_pairs={{0,8},{8,0},{16,24},{24,16},{1,9},{9,1},{17,25},{25,17},{2,10},{10... | collective-permute-start | bytes 294920 | tf_op jit(solution)/shard_map/ppermute | solution.py:603
  8.4 4.6 %collective-permute-start.4 = (bf16[48,1024]{1,0:T(8,128)(2,1)S(1)}, bf16[48,1024]{1,0:T(8,128)(2,1)S(1)}, u32[]{:S(2)}, u32[]{:S(2)}) collective-permute-start(bf16[48,1024]{1,0:T(8,128)(2,1)S(1)} %get-tuple-element.77), channel_id=1, source_target_pairs={{0,16},{8,24},{16,0},{24,8},{1,17},{9,25},{17,1},{25,9},{2,18},{10... | collective-permute-start | bytes 294920 | tf_op jit(solution)/shard_map/ppermute | solution.py:603
  10.1 5.6 %collective-permute-start.5 = (bf16[48,1024]{1,0:T(8,128)(2,1)S(1)}, bf16[48,1024]{1,0:T(8,128)(2,1)S(1)}, u32[]{:S(2)}, u32[]{:S(2)}) collective-permute-start(bf16[48,1024]{1,0:T(8,128)(2,1)S(1)} %get-tuple-element.78), channel_id=1, source_target_pairs={{0,24},{8,16},{16,8},{24,0},{1,25},{9,17},{17,9},{25,1},{2,26},{10... | collective-permute-start | bytes 294920 | tf_op jit(solution)/shard_map/ppermute | solution.py:603
  20.9 17.1 %collective-permute-start.10 = (bf16[176,1024]{1,0:T(8,128)(2,1)S(1)}, bf16[176,1024]{1,0:T(8,128)(2,1)S(1)}, u32[]{:S(2)}, u32[]{:S(2)}) collective-permute-start(bf16[176,1024]{1,0:T(8,128)(2,1)S(1)} %get-tuple-element.93), channel_id=1, source_target_pairs={{0,24},{8,16},{16,8},{24,0},{1,25},{9,17},{17,9},{25,1},{2,26},{10... | collective-permute-start | bytes 1081352 | tf_op jit(solution)/shard_map/ppermute | solution.py:603
  25.9 14.4 %collective-permute-start.9 = (bf16[176,1024]{1,0:T(8,128)(2,1)S(1)}, bf16[176,1024]{1,0:T(8,128)(2,1)S(1)}, u32[]{:S(2)}, u32[]{:S(2)}) collective-permute-start(bf16[176,1024]{1,0:T(8,128)(2,1)S(1)} %get-tuple-element.92), channel_id=1, source_target_pairs={{0,16},{8,24},{16,0},{24,8},{1,17},{9,25},{17,1},{25,9},{2,18},{10... | collective-permute-start | bytes 1081352 | tf_op jit(solution)/shard_map/ppermute | solution.py:603
  32.4 9.5 %collective-permute-start.8 = (bf16[176,1024]{1,0:T(8,128)(2,1)S(1)}, bf16[176,1024]{1,0:T(8,128)(2,1)S(1)}, u32[]{:S(2)}, u32[]{:S(2)}) collective-permute-start(bf16[176,1024]{1,0:T(8,128)(2,1)S(1)} %get-tuple-element.91), channel_id=1, source_target_pairs={{0,8},{8,0},{16,24},{24,16},{1,9},{9,1},{17,25},{25,17},{2,10},{10... | collective-permute-start | bytes 1081352 | tf_op jit(solution)/shard_map/ppermute | solution.py:603
  44.2 2.6 %collective-permute-start.11 = (f32[32,128]{1,0:T(8,128)S(1)}, f32[32,128]{1,0:T(8,128)S(1)}, u32[]{:S(2)}, u32[]{:S(2)}) collective-permute-start(f32[32,128]{1,0:T(8,128)S(1)} %get-tuple-element.99), channel_id=1, source_target_pairs={{0,1},{1,0},{2,3},{3,2},{4,5},{5,4},{6,7},{7,6},{8,9},{9,8},{10,11... | collective-permute-start | bytes 49160 | tf_op jit(solution)/shard_map/ppermute | solution.py:603
  46.8 4.6 %collective-permute-start.14 = (f32[32,128]{1,0:T(8,128)S(1)}, f32[32,128]{1,0:T(8,128)S(1)}, u32[]{:S(2)}, u32[]{:S(2)}) collective-permute-start(f32[32,128]{1,0:T(8,128)S(1)} %add.21), channel_id=1, source_target_pairs={{0,24},{8,16},{16,8},{24,0},{1,25},{9,17},{17,9},{25,1},{2,26},{10... | collective-permute-start | bytes 49160 | tf_op jit(solution)/shard_map/ppermute | solution.py:603
  47.2 4.3 %collective-permute-start.13 = (f32[32,128]{1,0:T(8,128)S(1)}, f32[32,128]{1,0:T(8,128)S(1)}, u32[]{:S(2)}, u32[]{:S(2)}) collective-permute-start(f32[32,128]{1,0:T(8,128)S(1)} %add.21), channel_id=1, source_target_pairs={{0,16},{8,24},{16,0},{24,8},{1,17},{9,25},{17,1},{25,9},{2,18},{10... | collective-permute-start | bytes 49160 | tf_op jit(solution)/shard_map/ppermute | solution.py:603
  48.9 3.7 %collective-permute-start.12 = (f32[32,128]{1,0:T(8,128)S(1)}, f32[32,128]{1,0:T(8,128)S(1)}, u32[]{:S(2)}, u32[]{:S(2)}) collective-permute-start(f32[32,128]{1,0:T(8,128)S(1)} %add.21), channel_id=1, source_target_pairs={{0,8},{8,0},{16,24},{24,16},{1,9},{9,1},{17,25},{25,17},{2,10},{10... | collective-permute-start | bytes 49160 | tf_op jit(solution)/shard_map/ppermute | solution.py:603
  52.6 5.6 %collective-permute-start.17 = (f32[32,128]{1,0:T(8,128)S(1)}, f32[32,128]{1,0:T(8,128)S(1)}, u32[]{:S(2)}, u32[]{:S(2)}) collective-permute-start(f32[32,128]{1,0:T(8,128)S(1)} %add_add_fusion.1), channel_id=1, source_target_pairs={{0,6},{1,7},{2,4},{3,5},{4,2},{5,3},{6,0},{7,1},{8,14},{9,15},{10,... | collective-permute-start | bytes 49160 | tf_op jit(solution)/shard_map/ppermute | solution.py:603
  55.8 4.6 %collective-permute-start.16 = (f32[32,128]{1,0:T(8,128)S(1)}, f32[32,128]{1,0:T(8,128)S(1)}, u32[]{:S(2)}, u32[]{:S(2)}) collective-permute-start(f32[32,128]{1,0:T(8,128)S(1)} %add_add_fusion.1), channel_id=1, source_target_pairs={{0,4},{1,5},{2,6},{3,7},{4,0},{5,1},{6,2},{7,3},{8,12},{9,13},{10,... | collective-permute-start | bytes 49160 | tf_op jit(solution)/shard_map/ppermute | solution.py:603
  58.1 3.7 %collective-permute-start.15 = (f32[32,128]{1,0:T(8,128)S(1)}, f32[32,128]{1,0:T(8,128)S(1)}, u32[]{:S(2)}, u32[]{:S(2)}) collective-permute-start(f32[32,128]{1,0:T(8,128)S(1)} %add_add_fusion.1), channel_id=1, source_target_pairs={{0,2},{1,3},{2,0},{3,1},{4,6},{5,7},{6,4},{7,5},{8,10},{9,11},{10,... | collective-permute-start | bytes 49160 | tf_op jit(solution)/shard_map/ppermute | solution.py:603
